TPU v7x, 32 devices: a whole 2x2x4 slice. The times are simulated.
32 devices in a mesh: lon: 8 (over y, x, core), lat: 4 (over z).
Axes of the slice: x: 2, y: 2, z: 4, core: 2. Of those that a mesh axis runs over, the one named last changes fastest.
Arguments:
- record_values: bfloat16 [64, 16, 2, 128], P('lon', 'lat'), may hold values from -6 to 6
- record_cell: int32 [64, 16, 2], P('lon', 'lat'), may hold values from 0 to 287
- record_instrument: int32 [64, 16, 2], P('lon', 'lat'), may hold values from 0 to 7
- block_counts: int32 [64, 16], P('lon', 'lat'), may hold values from 0 to 2, as said below
- background: bfloat16 [48, 192, 2, 192], P('lat', 'lon'), may hold values from -6 to 6
- input_weight: bfloat16 [128, 192], replicated, may hold values from -0.5 to 0.5
- instrument_table: bfloat16 [8, 192], replicated, may hold values from -4 to 4
- lift_weight: bfloat16 [192, 384], replicated, may hold values from -0.4375 to 0.4375
- first_gain: bfloat16 [192], replicated, may hold values from 0.5 to 1.5
- attn_weight: bfloat16 [192, 576], replicated
- mix_weight: bfloat16 [192, 192], replicated, may hold values from -0.4375 to 0.4375
- second_gain: bfloat16 [192], replicated, may hold values from 0.5 to 1.5
- up_weight: bfloat16 [192, 768], replicated, may hold values from -0.4375 to 0.4375
- down_weight: bfloat16 [768, 192], replicated, may hold values from -0.21875 to 0.21875
Outputs:
- result: bfloat16 [48, 192, 2, 192], P('lat', 'lon')
Inputs may be any that keep to these rules, and one draw needn't show every extreme that they name: `block_counts`: each block's count is at most 2; for some tiles every source fills all 2 slots.
All inputs are finite; a program needn't handle non-finite values.
Results may differ from a plain program's by a relative error of at most 0.017.
Values may be sent and summed in bfloat16 or wider, within the bound.
No kernel may reach another device: no remote copies, remote signals or barrier semaphores. Data moves between devices by JAX's collectives and lax.ppermute only.
A program may use at most 64 MiB of HBM per device.

v0:
```python
import jax
import jax.numpy as jnp
from jax import lax
from jax.sharding import PartitionSpec as P

HEADS = 6
INSTR = 8
LEV = 2
WLAT = 6
WLON = 12


def shifted(value, axis, steps):
    count = lax.axis_size(axis)
    pairs = [(source, (source + steps) % count) for source in range(count)]
    return lax.ppermute(value, axis, pairs)


def layer_norm(tensor, norm_gain):
    wide = tensor.astype(jnp.float32)
    average = jnp.mean(wide, axis=-1, keepdims=True)
    centred = wide - average
    spread = jnp.mean(centred * centred, axis=-1, keepdims=True)
    return (centred * lax.rsqrt(spread + 1e-05) * norm_gain.astype(jnp.float32)).astype(
        jnp.bfloat16
    )


def to_windows(tensor):
    height, breadth, levels, width = tensor.shape
    shaped = tensor.reshape(height // WLAT, WLAT, breadth // WLON, WLON, levels, width)
    shaped = shaped.transpose(0, 2, 1, 3, 4, 5)
    return shaped.reshape(height // WLAT * (breadth // WLON), WLAT * WLON * levels, width)


def from_windows(tensor, height, breadth):
    width = tensor.shape[-1]
    shaped = tensor.reshape(height // WLAT, breadth // WLON, WLAT, WLON, LEV, width)
    return shaped.transpose(0, 2, 1, 3, 4, 5).reshape(height, breadth, LEV, width)


def encode_records(values, instrument_tag, input_weight, instrument_table):
    flat = values.reshape(-1, values.shape[-1])
    tags = instrument_tag.reshape(-1)
    chooser = (tags[:, None] == jnp.arange(INSTR, dtype=jnp.float32)[None, :]).astype(jnp.bfloat16)
    before = jnp.dot(flat, input_weight, preferred_element_type=jnp.float32)
    before = before + jnp.dot(chooser, instrument_table, preferred_element_type=jnp.float32)
    encoded = jax.nn.gelu(before).astype(jnp.bfloat16)
    return encoded.reshape(values.shape[:-1] + (input_weight.shape[1],))


def attend_windows(tokens, rows_global, grid_rows, attn_weight):
    height, breadth, levels, width = tokens.shape
    head_size = width // HEADS
    projected = jnp.dot(tokens.reshape(-1, width), attn_weight, preferred_element_type=jnp.float32)
    projected = projected.reshape(height, breadth, levels, 3 * width)
    query = (projected[..., :width] * head_size ** (-0.5)).astype(jnp.bfloat16)
    keys = projected[..., width : 2 * width].astype(jnp.bfloat16)
    value_rows = projected[..., 2 * width :].astype(jnp.bfloat16)
    region = (rows_global >= grid_rows - WLAT // 2).astype(jnp.float32)
    region = jnp.broadcast_to(region[:, None, None, None], (height, breadth, levels, 1))
    region_w = to_windows(region)[..., 0]
    windows = region_w.shape[0]
    count_tok = region_w.shape[1]
    query_w = to_windows(query).reshape(windows, count_tok, HEADS, head_size)
    keys_w = to_windows(keys).reshape(windows, count_tok, HEADS, head_size)
    values_w = to_windows(value_rows).reshape(windows, count_tok, HEADS, head_size)
    scores = jnp.einsum("wqhd,wkhd->whqk", query_w, keys_w, preferred_element_type=jnp.float32)
    allowed = region_w[:, None, :, None] == region_w[:, None, None, :]
    scores = jnp.where(allowed, scores, jnp.float32(-1e30))
    largest = jnp.max(scores, axis=-1, keepdims=True)
    raised = jnp.exp(scores - largest)
    attn_weights = (raised / jnp.sum(raised, axis=-1, keepdims=True)).astype(jnp.bfloat16)
    output = jnp.einsum(
        "whqk,wkhd->wqhd", attn_weights, values_w, preferred_element_type=jnp.float32
    )
    output = output.astype(jnp.bfloat16).reshape(windows, count_tok, width)
    return from_windows(output, height, breadth)


def local(
    record_values,
    record_cell,
    record_instrument,
    block_counts,
    background,
    input_weight,
    instrument_table,
    lift_weight,
    first_gain,
    attn_weight,
    mix_weight,
    second_gain,
    up_weight,
    down_weight,
):
    lat_cells = background.shape[0]
    lon_cells = background.shape[1]
    width = background.shape[3]
    capacity = record_values.shape[2]
    is_live = jnp.arange(capacity, dtype=jnp.int32)[None, None, :] < block_counts[:, :, None]
    row_index = jnp.where(is_live, record_cell // lon_cells, -1).astype(jnp.bfloat16)
    col_index = (record_cell % lon_cells).astype(jnp.bfloat16)
    encoded = encode_records(
        record_values, record_instrument.astype(jnp.float32), input_weight, instrument_table
    )
    encoded, row_index, col_index = (
        lax.all_to_all(
            lax.all_to_all(encoded, "lon", split_axis=0, concat_axis=0, tiled=True),
            "lat",
            split_axis=1,
            concat_axis=1,
            tiled=True,
        ),
        lax.all_to_all(
            lax.all_to_all(row_index, "lon", split_axis=0, concat_axis=0, tiled=True),
            "lat",
            split_axis=1,
            concat_axis=1,
            tiled=True,
        ),
        lax.all_to_all(
            lax.all_to_all(col_index, "lon", split_axis=0, concat_axis=0, tiled=True),
            "lat",
            split_axis=1,
            concat_axis=1,
            tiled=True,
        ),
    )
    lifted = jnp.dot(encoded.reshape(-1, width), lift_weight, preferred_element_type=jnp.float32)
    lifted = jax.nn.gelu(lifted).astype(jnp.bfloat16)
    row_float = row_index.reshape(-1).astype(jnp.float32)
    col_float = col_index.reshape(-1).astype(jnp.float32)
    cell_value = jnp.where(row_float < 0.0, -1.0, row_float * lon_cells + col_float)
    cell_ids = jnp.arange(lat_cells * lon_cells, dtype=jnp.float32)
    onehot = (cell_ids[:, None] == cell_value[None, :]).astype(jnp.bfloat16)
    summed = jnp.dot(onehot, lifted, preferred_element_type=jnp.float32)
    tallies = jnp.sum(onehot, axis=1, dtype=jnp.float32)
    latent = (background.astype(jnp.float32) + summed.reshape(lat_cells, lon_cells, LEV, width)) / (
        1.0 + tallies
    ).reshape(lat_cells, lon_cells, 1, 1)
    latent = latent.astype(jnp.bfloat16)
    normed = layer_norm(latent, first_gain)
    grid_rows = lat_cells * lax.axis_size("lat")
    lat_start = lax.axis_index("lat") * lat_cells
    half_lat = WLAT // 2
    half_lon = WLON // 2
    ahead = shifted(normed[:, :half_lon], "lon", -1)
    moved = jnp.concatenate([normed[:, half_lon:], ahead], axis=1)
    above = shifted(moved[:half_lat], "lat", -1)
    moved = jnp.concatenate([moved[half_lat:], above], axis=0)
    rows_global = (lat_start + jnp.arange(lat_cells, dtype=jnp.int32) + half_lat) % grid_rows
    mixed_rolled = attend_windows(moved, rows_global, grid_rows, attn_weight)
    below = shifted(mixed_rolled[lat_cells - half_lat :], "lat", 1)
    returned = jnp.concatenate([below, mixed_rolled[: lat_cells - half_lat]], axis=0)
    behind = shifted(returned[:, lon_cells - half_lon :], "lon", 1)
    mixed = jnp.concatenate([behind, returned[:, : lon_cells - half_lon]], axis=1)
    after_attn = latent.astype(jnp.float32) + jnp.dot(
        mixed.reshape(-1, width), mix_weight, preferred_element_type=jnp.float32
    ).reshape(lat_cells, lon_cells, LEV, width)
    after_attn = after_attn.astype(jnp.bfloat16)
    normed_two = layer_norm(after_attn, second_gain)
    hidden = jax.nn.gelu(
        jnp.dot(normed_two.reshape(-1, width), up_weight, preferred_element_type=jnp.float32)
    ).astype(jnp.bfloat16)
    result = after_attn.astype(jnp.float32) + jnp.dot(
        hidden, down_weight, preferred_element_type=jnp.float32
    ).reshape(lat_cells, lon_cells, LEV, width)
    return result.astype(jnp.bfloat16)


def solution(mesh):
    placed = (
        P("lon", "lat", None, None),
        P("lon", "lat", None),
        P("lon", "lat", None),
        P("lon", "lat"),
        P("lat", "lon", None, None),
        P(),
        P(),
        P(),
        P(),
        P(),
        P(),
        P(),
        P(),
        P(),
    )
    return jax.shard_map(
        local, mesh=mesh, in_specs=placed, out_specs=P("lat", "lon", None, None), check_vma=False
    )
```

profile of v0, /device:TPU:0, one launch (start us, length us, event | category | flops | bytes accessed | tf_op | source)
XLA Modules:
  0.0 92.8 jit_solution(4242301654169193499)
XLA Ops:
  0.0 0.8 copy.132
  0.8 0.8 copy.131
  1.6 0.6 fusion.73
  2.2 5.2 %all-to-all-start = ((bf16[8,4,2]{1,2,0:T(2,128)(2,1)}), bf16[8,4,2]{1,2,0:T(2,128)(2,1)S(1)}, u32[]{:S(2)}, u32[]{:S(2)}) async-start(bf16[8,4,2]{1,2,0:T(2,128)(2,1)} %get-tuple-element.10), calls=%async_computation | async-start | bytes 8192 | tf_op jit(solution)/shard_map/all_to_all | solution.py:116
  7.4 0.7 convert_element_type.99
  8.3 1.0 %fusion.93 = f32[64,192]{1,0:T(8,128)S(1)} fusion(bf16[64,128]{1,0:T(8,128)(2,1)} %bitcast.44, bf16[128,192]{0,1:T(8,128)(2,1)} %param.19), kind=kOutput, calls=%fused_computation.125 | convolution fusion | flops 3145728 | bytes 114688 | tf_op jit(solution)/shard_map/dot_general | solution.py:46
  9.3 0.9 %fusion.64 = bf16[64,192]{1,0:T(8,128)(2,1)S(1)} fusion(f32[64,192]{1,0:T(8,128)S(1)} %fusion.93, bf16[8,192]{1,0:T(8,128)(2,1)} %param.20, f32[64]{0:T(128)S(1)} %eq.53), kind=kOutput, calls=%fused_computation.84 | convolution fusion | flops 320000 | bytes 77056 | tf_op jit(solution)/shard_map/dot_general | solution.py:47
  10.2 1.8 %all-to-all-done = bf16[8,4,2]{1,2,0:T(2,128)(2,1)S(1)} async-done(((bf16[8,4,2]{1,2,0:T(2,128)(2,1)}), bf16[8,4,2]{1,2,0:T(2,128)(2,1)S(1)}, u32[]{:S(2)}, u32[]{:S(2)}) %all-to-all-start) | async-done | bytes 160 | tf_op jit(solution)/shard_map/all_to_all | solution.py:116
  12.1 3.3 %all-to-all-start.2 = ((bf16[8,4,2]{1,2,0:T(2,128)(2,1)}), bf16[8,4,2]{1,2,0:T(2,128)(2,1)S(1)}, u32[]{:S(2)}, u32[]{:S(2)}) async-start(bf16[8,4,2]{1,2,0:T(2,128)(2,1)} %get-tuple-element.9), calls=%async_computation.2 | async-start | bytes 8192 | tf_op jit(solution)/shard_map/all_to_all | solution.py:123
  15.4 0.7 copy.135
  16.0 3.9 %all-to-all-done.2 = bf16[8,4,2]{1,2,0:T(2,128)(2,1)S(1)} async-done(((bf16[8,4,2]{1,2,0:T(2,128)(2,1)}), bf16[8,4,2]{1,2,0:T(2,128)(2,1)S(1)}, u32[]{:S(2)}, u32[]{:S(2)}) %all-to-all-start.2) | async-done | bytes 160 | tf_op jit(solution)/shard_map/all_to_all | solution.py:123
  19.9 4.9 %all-to-all-start.1 = ((bf16[8,4,2]{0,2,1:T(2,128)(2,1)}), bf16[8,4,2]{0,2,1:T(2,128)(2,1)S(1)}, u32[]{:S(2)}, u32[]{:S(2)}) async-start(bf16[8,4,2]{0,2,1:T(2,128)(2,1)} %copy.135), calls=%async_computation.1 | async-start | bytes 4096 | tf_op jit(solution)/shard_map/all_to_all | solution.py:115
  24.8 0.6 reshape.129
  25.4 0.7 copy.136
  26.1 4.1 %all-to-all-done.1 = bf16[8,4,2]{0,2,1:T(2,128)(2,1)S(1)} async-done(((bf16[8,4,2]{0,2,1:T(2,128)(2,1)}), bf16[8,4,2]{0,2,1:T(2,128)(2,1)S(1)}, u32[]{:S(2)}, u32[]{:S(2)}) %all-to-all-start.1) | async-done | bytes 160 | tf_op jit(solution)/shard_map/all_to_all | solution.py:115
  30.2 3.2 %all-to-all-start.3 = ((bf16[8,4,2]{0,2,1:T(2,128)(2,1)}), bf16[8,4,2]{0,2,1:T(2,128)(2,1)S(1)}, u32[]{:S(2)}, u32[]{:S(2)}) async-start(bf16[8,4,2]{0,2,1:T(2,128)(2,1)} %copy.136), calls=%async_computation.3 | async-start | bytes 4096 | tf_op jit(solution)/shard_map/all_to_all | solution.py:122
  33.4 0.7 convert_element_type.106
  34.1 0.1 transpose.42
  34.2 4.6 %all-to-all-done.3 = bf16[8,4,2]{0,2,1:T(2,128)(2,1)S(1)} async-done(((bf16[8,4,2]{0,2,1:T(2,128)(2,1)}), bf16[8,4,2]{0,2,1:T(2,128)(2,1)S(1)}, u32[]{:S(2)}, u32[]{:S(2)}) %all-to-all-start.3) | async-done | bytes 160 | tf_op jit(solution)/shard_map/all_to_all | solution.py:122
  38.9 3.3 %all-to-all-start.4 = ((bf16[8,4,2,192]{3,2,1,0:T(2,128)(2,1)}), bf16[8,4,2,192]{3,2,1,0:T(2,128)(2,1)S(1)}, u32[]{:S(2)}, u32[]{:S(2)}) async-start(bf16[8,4,2,192]{3,2,1,0:T(2,128)(2,1)} %reshape.129), calls=%async_computation.4 | async-start | bytes 65536 | tf_op jit(solution)/shard_map/all_to_all | solution.py:109
  42.6 4.4 %all-to-all-done.4 = bf16[8,4,2,192]{3,2,1,0:T(2,128)(2,1)S(1)} async-done(((bf16[8,4,2,192]{3,2,1,0:T(2,128)(2,1)}), bf16[8,4,2,192]{3,2,1,0:T(2,128)(2,1)S(1)}, u32[]{:S(2)}, u32[]{:S(2)}) %all-to-all-start.4) | async-done | bytes 24608 | tf_op jit(solution)/shard_map/all_to_all | solution.py:109
  47.0 0.6 copy.139
  47.6 3.3 %all-to-all-start.5 = ((bf16[8,4,2,192]{3,2,0,1:T(2,128)(2,1)}), bf16[8,4,2,192]{3,2,0,1:T(2,128)(2,1)S(1)}, u32[]{:S(2)}, u32[]{:S(2)}) async-start(bf16[8,4,2,192]{3,2,0,1:T(2,128)(2,1)} %copy.139), calls=%async_computation.5 | async-start | bytes 65536 | tf_op jit(solution)/shard_map/all_to_all | solution.py:108
  51.0 5.5 %all-to-all-done.5 = bf16[8,4,2,192]{3,2,0,1:T(2,128)(2,1)S(1)} async-done(((bf16[8,4,2,192]{3,2,0,1:T(2,128)(2,1)}), bf16[8,4,2,192]{3,2,0,1:T(2,128)(2,1)S(1)}, u32[]{:S(2)}, u32[]{:S(2)}) %all-to-all-start.5) | async-done | bytes 24608 | tf_op jit(solution)/shard_map/all_to_all | solution.py:108
  56.6 1.3 %fusion.56 = f32[288,384]{1,0:T(8,128)S(1)} fusion(f32[64]{0:T(128)S(1)} %select_n.45, bf16[64,192]{1,0:T(8,128)(2,1)S(1)} %reshape.130, bf16[192,384]{1,0:T(8,128)(2,1)} %param.21), kind=kOutput, calls=%fused_computation.75 | convolution fusion | flops 23832576 | bytes 614656 | tf_op jit(solution)/shard_map/dot_general | solution.py:137
  57.9 0.4 reshape.131
  58.3 0.3 convert_reduce_fusion
  58.6 0.3 fusion.30
  59.0 0.2 fusion.32
  59.3 0.8 broadcast_compare_fusion
  60.2 1.3 %collective-permute-done = bf16[12,6,2,192]{3,1,2,0:T(8,128)(2,1)S(1)} collective-permute-done((bf16[12,6,2,192]{3,1,2,0:T(8,128)(2,1)S(1)}, bf16[12,6,2,192]{3,1,2,0:T(8,128)(2,1)S(1)}, u32[]{:S(2)}, u32[]{:S(2)}) %collective-permute-start) | collective-permute-done | bytes 55328 | tf_op jit(solution)/shard_map/ppermute | solution.py:16
  61.5 0.7 collective-permute-start.1
  62.3 4.2 %collective-permute-done.1 = bf16[3,24,2,192]{3,1,2,0:T(8,128)(2,1)S(1)} collective-permute-done((bf16[3,24,2,192]{3,1,2,0:T(8,128)(2,1)S(1)}, bf16[3,24,2,192]{3,1,2,0:T(8,128)(2,1)S(1)}, u32[]{:S(2)}, u32[]{:S(2)}) %collective-permute-start.1) | collective-permute-done | bytes 55328 | tf_op jit(solution)/shard_map/ppermute | solution.py:16
  66.5 0.4 fusion.88
  66.9 0.2 fusion.87
  67.0 0.2 copy.146
  67.3 0.9 copy.147
  68.2 1.9 %reshape_reshape.14 = bf16[4,144,6,32]{3,2,1,0:T(8,128)(2,1)S(1)} reshape(bf16[2,2,6,12,2,192]{5,4,3,2,1,0:T(2,128)(2,1)} %copy.147) | data formatting | bytes 442368 | tf_op jit(solution)/shard_map/reshape;reshape | solution.py:66
  70.2 0.2 copy.144
  70.4 0.2 copy.145
  70.6 0.6 reshape_reshape.13
  71.2 0.2 copy.142
  71.5 0.2 copy.143
  71.7 1.6 %reshape_reshape.12 = bf16[4,144,6,32]{3,2,1,0:T(8,128)(2,1)} reshape(bf16[2,2,6,12,2,192]{5,4,3,2,1,0:T(2,128)(2,1)S(1)} %copy.143) | data formatting | bytes 442368 | tf_op jit(solution)/shard_map/reshape;reshape | solution.py:67
  73.3 0.6 fusion.21
  73.9 0.3 copy-done.2
  74.2 1.2 %fusion.89 = (f32[4,6,144]{2,1,0:T(8,128)S(1)}, f32[4,6,144,144]{2,3,1,0:T(8,128)S(1)}) fusion(f32[4,6,144,144]{2,3,1,0:T(8,128)S(1)} %fusion.21, pred[4,144,144]{1,2,0:T(8,128)(4,1)S(1)} %copy-done.2), kind=kOutput, calls=%fused_computation.122 | output fusion | flops 1990799 | bytes 4078080 | tf_op jit(solution)/shard_map/sub | solution.py:72
  75.4 0.5 fusion.19
  75.9 0.6 copy.152
  76.5 0.7 reshape_reshape.15
  77.3 0.2 copy.153
  77.6 0.8 collective-permute-start.2
  78.4 0.2 slice.54
  78.5 5.3 %collective-permute-done.2 = bf16[3,24,2,192]{3,1,2,0:T(8,128)(2,1)S(1)} collective-permute-done((bf16[3,24,2,192]{3,1,2,0:T(8,128)(2,1)S(1)}, bf16[3,24,2,192]{3,1,2,0:T(8,128)(2,1)S(1)}, u32[]{:S(2)}, u32[]{:S(2)}) %collective-permute-start.2) | collective-permute-done | bytes 55328 | tf_op jit(solution)/shard_map/ppermute | solution.py:16
  83.9 0.2 collective-permute-start.3
  84.1 4.9 %collective-permute-done.3 = bf16[12,6,2,192]{3,1,2,0:T(8,128)(2,1)S(1)} collective-permute-done((bf16[12,6,2,192]{3,1,2,0:T(8,128)(2,1)S(1)}, bf16[12,6,2,192]{3,1,2,0:T(8,128)(2,1)S(1)}, u32[]{:S(2)}, u32[]{:S(2)}) %collective-permute-start.3) | collective-permute-done | bytes 55328 | tf_op jit(solution)/shard_map/ppermute | solution.py:16
  89.0 0.4 fusion.90
  89.4 0.3 multiply_reduce_fusion
  89.8 0.2 multiply_convert_fusion
  90.0 0.2 copy.156
  90.2 0.3 reshape.136
  90.5 0.9 fusion.15
  91.4 0.3 reshape.137
  91.8 0.9 %copy.159 = bf16[12,24,2,192]{3,2,1,0:T(2,128)(2,1)} copy(bf16[12,24,2,192]{3,1,2,0:T(8,128)(2,1)S(1)} %fusion.34) | data formatting | bytes 442368 | tf_op jit(solution)/shard_map/convert_element_type | solution.py:169
  (44 shorter events, 1.4 us)
Async XLA Ops:
  0.0 90.5 %copy-start = (bf16[768,192]{0,1:T(8,128)(2,1)S(1)}, bf16[768,192]{0,1:T(8,128)(2,1)}, u32[]{:S(2)}) copy-start(bf16[768,192]{0,1:T(8,128)(2,1)} %param.27) | copy-start | bytes 884740
  0.0 58.3 %copy-start.3 = (bf16[12,24,2,192]{3,2,1,0:T(2,128)(2,1)S(1)}, bf16[12,24,2,192]{3,2,1,0:T(2,128)(2,1)}, u32[]{:S(2)}) copy-start(bf16[12,24,2,192]{3,2,1,0:T(2,128)(2,1)} %param.18) | copy-start | bytes 663556
  2.2 9.8 %all-to-all-start = ((bf16[8,4,2]{1,2,0:T(2,128)(2,1)}), bf16[8,4,2]{1,2,0:T(2,128)(2,1)S(1)}, u32[]{:S(2)}, u32[]{:S(2)}) async-start(bf16[8,4,2]{1,2,0:T(2,128)(2,1)} %get-tuple-element.10), calls=%async_computation | async-start | bytes 8192 | tf_op jit(solution)/shard_map/all_to_all | solution.py:116
  12.1 7.8 %all-to-all-start.2 = ((bf16[8,4,2]{1,2,0:T(2,128)(2,1)}), bf16[8,4,2]{1,2,0:T(2,128)(2,1)S(1)}, u32[]{:S(2)}, u32[]{:S(2)}) async-start(bf16[8,4,2]{1,2,0:T(2,128)(2,1)} %get-tuple-element.9), calls=%async_computation.2 | async-start | bytes 8192 | tf_op jit(solution)/shard_map/all_to_all | solution.py:123
  19.9 10.3 %all-to-all-start.1 = ((bf16[8,4,2]{0,2,1:T(2,128)(2,1)}), bf16[8,4,2]{0,2,1:T(2,128)(2,1)S(1)}, u32[]{:S(2)}, u32[]{:S(2)}) async-start(bf16[8,4,2]{0,2,1:T(2,128)(2,1)} %copy.135), calls=%async_computation.1 | async-start | bytes 4096 | tf_op jit(solution)/shard_map/all_to_all | solution.py:115
  30.2 8.7 %all-to-all-start.3 = ((bf16[8,4,2]{0,2,1:T(2,128)(2,1)}), bf16[8,4,2]{0,2,1:T(2,128)(2,1)S(1)}, u32[]{:S(2)}, u32[]{:S(2)}) async-start(bf16[8,4,2]{0,2,1:T(2,128)(2,1)} %copy.136), calls=%async_computation.3 | async-start | bytes 4096 | tf_op jit(solution)/shard_map/all_to_all | solution.py:122
  38.9 8.1 %all-to-all-start.4 = ((bf16[8,4,2,192]{3,2,1,0:T(2,128)(2,1)}), bf16[8,4,2,192]{3,2,1,0:T(2,128)(2,1)S(1)}, u32[]{:S(2)}, u32[]{:S(2)}) async-start(bf16[8,4,2,192]{3,2,1,0:T(2,128)(2,1)} %reshape.129), calls=%async_computation.4 | async-start | bytes 65536 | tf_op jit(solution)/shard_map/all_to_all | solution.py:109
  47.6 8.9 %all-to-all-start.5 = ((bf16[8,4,2,192]{3,2,0,1:T(2,128)(2,1)}), bf16[8,4,2,192]{3,2,0,1:T(2,128)(2,1)S(1)}, u32[]{:S(2)}, u32[]{:S(2)}) async-start(bf16[8,4,2,192]{3,2,0,1:T(2,128)(2,1)} %copy.139), calls=%async_computation.5 | async-start | bytes 65536 | tf_op jit(solution)/shard_map/all_to_all | solution.py:108
  58.6 7.9 %copy-start.4 = (bf16[192,576]{1,0:T(8,128)(2,1)S(1)}, bf16[192,576]{1,0:T(8,128)(2,1)}, u32[]{:S(2)}) copy-start(bf16[192,576]{1,0:T(8,128)(2,1)} %param.23) | copy-start | bytes 663556
  59.2 2.3 %collective-permute-start = (bf16[12,6,2,192]{3,1,2,0:T(8,128)(2,1)S(1)}, bf16[12,6,2,192]{3,1,2,0:T(8,128)(2,1)S(1)}, u32[]{:S(2)}, u32[]{:S(2)}) collective-permute-start(bf16[12,6,2,192]{3,1,2,0:T(8,128)(2,1)S(1)} %slice.47), channel_id=1, source_target_pairs={{0,28},{4,0},{8,4},{12,8},{16,12},{20,16},{24,20},{28,24},{1,29},{... | collective-permute-start | bytes 165896 | tf_op jit(solution)/shard_map/ppermute | solution.py:16
  61.5 5.0 %collective-permute-start.1 = (bf16[3,24,2,192]{3,1,2,0:T(8,128)(2,1)S(1)}, bf16[3,24,2,192]{3,1,2,0:T(8,128)(2,1)S(1)}, u32[]{:S(2)}, u32[]{:S(2)}) collective-permute-start(bf16[3,24,2,192]{3,1,2,0:T(8,128)(2,1)S(1)} %pad_maximum_fusion), channel_id=1, source_target_pairs={{0,3},{1,0},{2,1},{3,2},{4,7},{5,4},{6,5},{7,6},{8,11},{9,8},{10,9... | collective-permute-start | bytes 165896 | tf_op jit(solution)/shard_map/ppermute | solution.py:16
  73.3 0.9 copy-start.2
  74.2 1.3 %copy-start.1 = (bf16[4,144,6,32]{3,2,1,0:T(8,128)(2,1)S(1)}, bf16[4,144,6,32]{3,2,1,0:T(8,128)(2,1)}, u32[]{:S(2)}) copy-start(bf16[4,144,6,32]{3,2,1,0:T(8,128)(2,1)} %reshape_reshape.12) | copy-start | bytes 663556
  76.5 7.6 %copy-start.7 = (bf16[192]{0:T(256)(128)(2,1)S(1)}, bf16[192]{0:T(256)(128)(2,1)}, u32[]{:S(2)}) copy-start(bf16[192]{0:T(256)(128)(2,1)} %param.25) | copy-start | bytes 1156
  76.5 12.5 %copy-start.5 = (bf16[192,192]{1,0:T(8,128)(2,1)S(1)}, bf16[192,192]{1,0:T(8,128)(2,1)}, u32[]{:S(2)}) copy-start(bf16[192,192]{1,0:T(8,128)(2,1)} %param.24) | copy-start | bytes 221188
  77.6 6.2 %collective-permute-start.2 = (bf16[3,24,2,192]{3,1,2,0:T(8,128)(2,1)S(1)}, bf16[3,24,2,192]{3,1,2,0:T(8,128)(2,1)S(1)}, u32[]{:S(2)}, u32[]{:S(2)}) collective-permute-start(bf16[3,24,2,192]{3,1,2,0:T(8,128)(2,1)S(1)} %copy.164), channel_id=1, source_target_pairs={{0,1},{1,2},{2,3},{3,0},{4,5},{5,6},{6,7},{7,4},{8,9},{9,10},{10,1... | collective-permute-start | bytes 165896 | tf_op jit(solution)/shard_map/ppermute | solution.py:16
  83.9 5.2 %collective-permute-start.3 = (bf16[12,6,2,192]{3,1,2,0:T(8,128)(2,1)S(1)}, bf16[12,6,2,192]{3,1,2,0:T(8,128)(2,1)S(1)}, u32[]{:S(2)}, u32[]{:S(2)}) collective-permute-start(bf16[12,6,2,192]{3,1,2,0:T(8,128)(2,1)S(1)} %slice.55), channel_id=1, source_target_pairs={{0,4},{4,8},{8,12},{12,16},{16,20},{20,24},{24,28},{28,0},{1,5},{5... | collective-permute-start | bytes 165896 | tf_op jit(solution)/shard_map/ppermute | solution.py:16
  89.0 1.5 %copy-start.6 = (bf16[192,768]{1,0:T(8,128)(2,1)S(1)}, bf16[192,768]{1,0:T(8,128)(2,1)}, u32[]{:S(2)}) copy-start(bf16[192,768]{1,0:T(8,128)(2,1)} %param.26) | copy-start | bytes 884740
where the time goes:
time: 93.5 us; the launch traced here: 92.8 us
  waiting for transfers between devices  40 us (43%)
  starting transfers between devices  24.9 us (27%)
  local copies, waits for them, and re-layouts  15.7 us (17%)
  matrix products  5.9 us (6%)
  other arithmetic  5.78 us (6%)
    ppermute x4, waiting for transfers between devices, shifted(): return lax.ppermute(value, axis, pairs)  15.7 us
    all_to_all x1, waiting for transfers between devices, local(): lax.all_to_all(lax.all_to_all(encoded, 'lon', split_axis=0, concat_axis=0...  5.53 us
    all_to_all x1, starting transfers between devices, local(): lax.all_to_all(row_index, 'lon', split_axis=0, concat_axis=0, tiled=True)  5.17 us
    all_to_all x1, starting transfers between devices, local(): lax.all_to_all(lax.all_to_all(row_index, 'lon', split_axis=0, concat_axis...  4.87 us
    all_to_all x1, waiting for transfers between devices, local(): lax.all_to_all(lax.all_to_all(col_index, 'lon', split_axis=0, concat_axis...  4.63 us
    all_to_all x1, waiting for transfers between devices, local(): lax.all_to_all(encoded, 'lon', split_axis=0, concat_axis=0, tiled=True)  4.44 us
    all_to_all x1, waiting for transfers between devices, local(): lax.all_to_all(lax.all_to_all(row_index, 'lon', split_axis=0, concat_axis...  4.07 us
    all_to_all x1, waiting for transfers between devices, local(): lax.all_to_all(col_index, 'lon', split_axis=0, concat_axis=0, tiled=True)  3.85 us
  transfers between devices with their start and end apart: 10, of which 10 were waited for; matrix products, arithmetic and copies ran while one was open for 8% of the time, Pallas kernels for 0%

commit v1 on v0

v1 whole, which is shorter than its diff:
```python
import functools

import jax
import jax.numpy as jnp
import ml_dtypes
import numpy as np
from jax import lax
from jax.experimental import pallas as pl
from jax.experimental.pallas import tpu as pltpu
from jax.sharding import PartitionSpec as P

HEADS = 6
INSTR = 8
LEV = 2
WLAT = 6
WLON = 12
HLAT = WLAT // 2
HLON = WLON // 2
PAD = 256
FIELDS = 4
GROUP = 8
CHUNK = 32
BF16 = jnp.bfloat16
F32 = jnp.float32

AROUND = [(dy, dx) for dy in (-1, 0, 1) for dx in (-1, 0, 1)]


def shifted(value, axis, steps):
    count = lax.axis_size(axis)
    pairs = [(source, (source + steps) % count) for source in range(count)]
    return lax.ppermute(value, axis, pairs)


def window_cells(lat_cells, lon_cells):
    high, wide = lat_cells + WLAT, lon_cells + WLON
    windows = []
    for top in range(0, high, WLAT):
        for left in range(0, wide, WLON):
            cells = [(r, c) for r in range(top, top + WLAT) for c in range(left, left + WLON)]
            own = [
                (r, c)
                for r, c in cells
                if HLAT <= r < HLAT + lat_cells and HLON <= c < HLON + lon_cells
            ]
            rest = [cell for cell in cells if cell not in own]
            windows.append((own, rest))
    return windows


def gelu(x):
    return jax.nn.gelu(x)


def normalise(wide, gain):
    average = jnp.mean(wide, axis=-1, keepdims=True)
    centred = wide - average
    spread = jnp.mean(centred * centred, axis=-1, keepdims=True)
    return centred * lax.rsqrt(spread + 1e-05) * gain


def dot(a, b):
    return jnp.dot(a, b, preferred_element_type=F32)


def dot_nt(a, b):
    return lax.dot_general(a, b, (((1,), (1,)), ((), ())), preferred_element_type=F32)


def block_kernel(
    plan,
    pole_ref,
    recv_ref,
    bg_ref,
    find_ref,
    pick_ref,
    coef_ref,
    place_ref,
    code_ref,
    keep_ref,
    sel_ref,
    win_ref,
    tab_ref,
    lift_ref,
    g1_ref,
    wq_ref,
    wk_ref,
    wv_ref,
    wm_ref,
    g2_ref,
    wu_ref,
    wd_ref,
    out_ref,
    lifted_ref,
    hot_ref,
    sum_ref,
):
    width = win_ref.shape[0]
    stride = find_ref.shape[0]
    per_chunk = lifted_ref.shape[0]
    chunks = recv_ref.shape[0] // per_chunk
    cells = bg_ref.shape[0]
    in_window = WLAT * WLON

    def scatter(base):
        for group in range(per_chunk // stride):
            at = group * stride
            recs = recv_ref[pl.ds(base + at, stride), :]
            meta = (dot(find_ref[...], recs) * pick_ref[...].astype(F32)).astype(BF16)
            lane = lax.broadcasted_iota(jnp.int32, (stride, 128), 1).astype(F32)
            tag = dot(meta, coef_ref[8:, :])
            chooser = jnp.where(tag == lane, 1.0, 0.0).astype(BF16)
            before = dot_nt(recs, win_ref[...]) + dot(chooser[:, :INSTR], tab_ref[...])
            encoded = gelu(before).astype(BF16)
            lifted = gelu(dot(encoded, lift_ref[...]))
            lanes = lax.broadcasted_iota(jnp.int32, lifted.shape, 1) % PAD
            lifted_ref[at : at + stride, :] = jnp.where(lanes >= width, 1.0, lifted).astype(BF16)
            code = dot_nt(coef_ref[:8, :], meta)[:1, :] + place_ref[:, at : at + stride]
            hot_ref[:, at : at + stride] = jnp.where(code_ref[...] == code, 1.0, 0.0).astype(BF16)
        return dot(hot_ref[...], lifted_ref[...])

    if chunks == 1:
        sum_ref[...] = scatter(0)
    else:
        sum_ref[...] = jnp.zeros_like(sum_ref)

        @pl.loop(0, chunks)
        def _(step):
            sum_ref[...] += scatter(pl.multiple_of(step * per_chunk, per_chunk))

    gain_one = g1_ref[...].astype(F32)
    latents, normeds = [], []
    for level in range(LEV):
        piece = sum_ref[:, level * PAD : (level + 1) * PAD]
        share = 1.0 / (1.0 + piece[:, width : width + 1])
        back = bg_ref[:, level * PAD : level * PAD + width].astype(F32)
        latent = ((back + piece[:, :width]) * share).astype(BF16).astype(F32)
        latents.append(latent)
        normeds.append(normalise(latent, gain_one))

    def gathered(tensors, counts):
        return jnp.concatenate(
            [t[w * in_window : w * in_window + n] for w, n in enumerate(counts) for t in tensors],
            axis=0,
        )

    all_n = gathered(normeds, [in_window] * len(plan)).astype(BF16)
    own_n = gathered(normeds, plan).astype(BF16)
    own_latent = gathered(latents, plan)
    keys = dot(all_n, wk_ref[...]).astype(BF16)
    values = dot(all_n, wv_ref[...])
    lanes = lax.broadcasted_iota(jnp.int32, values.shape, 1)
    values = jnp.where(lanes >= width, 1.0, values).astype(BF16)
    head = width // HEADS
    query = (dot(own_n, wq_ref[...]) * head ** (-0.5)).astype(BF16)

    head_of = lax.broadcasted_iota(jnp.int32, (1, width), 1) // head
    tokens = LEV * in_window
    mixed, start = [], 0
    for w, count in enumerate(plan):
        rows = LEV * count
        part = query[start : start + rows]
        start += rows
        stacked = jnp.concatenate(
            [jnp.where(head_of == h, part, jnp.zeros_like(part)) for h in range(HEADS)], axis=0
        )
        scores = dot_nt(stacked, keys[w * tokens : (w + 1) * tokens])
        side = w // 3
        if side != 1:
            kept = keep_ref[w : w + 1, :] > pole_ref[side // 2].astype(F32)
            scores = jnp.where(kept, scores, -1e30)
        largest = jnp.max(scores, axis=-1, keepdims=True)
        raised = jnp.exp(scores - largest).astype(BF16)
        product = dot(raised, values[w * tokens : (w + 1) * tokens])
        product = product[:, :width] * (1.0 / product[:, width : width + 1])
        total = jnp.zeros((rows, width), F32)
        for h in range(HEADS):
            total = jnp.where(head_of == h, product[h * rows : (h + 1) * rows], total)
        mixed.append(total.astype(BF16))
    mixed = jnp.concatenate(mixed, axis=0)

    after = (own_latent + dot(mixed, wm_ref[...])).astype(BF16).astype(F32)
    normed_two = normalise(after, g2_ref[...].astype(F32)).astype(BF16)
    hidden = gelu(dot(normed_two, wu_ref[...])).astype(BF16)
    result = (after + dot_nt(hidden, wd_ref[...])).astype(BF16)
    out_ref[...] = dot(sel_ref[...], result).astype(BF16)


def constants(lat_cells, lon_cells, capacity, sources):
    windows = window_cells(lat_cells, lon_cells)
    order = [cell for own, rest in windows for cell in own + rest]
    plan = [-(-len(own) // 8) * 8 for own, _ in windows]
    code = np.array([[r * 64 + c] for r, c in order], np.float32)
    wide = lon_cells + WLON
    perm = np.zeros((len(order), len(order)), ml_dtypes.bfloat16)
    for place, (r, c) in enumerate(order):
        perm[place, r * wide + c] = 1
    keep = np.zeros((16, LEV * WLAT * WLON), np.float32)
    for w, (own, rest) in enumerate(windows):
        for k, (r, c) in enumerate(own + rest):
            inside = HLAT <= r < HLAT + lat_cells
            keep[w, [k, k + WLAT * WLON]] = 1.0 if inside else 0.0
    sel = np.zeros((lat_cells * lon_cells * LEV, LEV * sum(plan)), ml_dtypes.bfloat16)
    start = 0
    for (own, _), count in zip(windows, plan):
        for level in range(LEV):
            for k, (r, c) in enumerate(own):
                row = ((r - HLAT) * lon_cells + c - HLON) * LEV + level
                sel[row, start + level * count + k] = 1
        start += LEV * count
    per_source = (len(AROUND) + 1) * capacity
    stride = GROUP * per_source
    find = np.zeros((stride, stride), ml_dtypes.bfloat16)
    pick = np.zeros((stride, 128), ml_dtypes.bfloat16)
    for row in range(stride):
        source, tile, slot = row // per_source, row % per_source // capacity, row % capacity
        find[row, source * per_source + len(AROUND) * capacity + slot] = 1
        if tile < len(AROUND):
            pick[row, tile * FIELDS : (tile + 1) * FIELDS] = 1
    place = np.full((1, sources * per_source), 1e6, np.float32)
    for row in range(place.shape[1]):
        tile = row % per_source // capacity
        if tile < len(AROUND):
            dy, dx = AROUND[tile]
            place[0, row] = (dy * lat_cells + HLAT) * 64 + dx * lon_cells + HLON
    coef = np.zeros((8 + 128, 128), ml_dtypes.bfloat16)
    coef[0, 0::FIELDS] = 64
    coef[0, 1::FIELDS] = 1
    coef[8 + 2 :: FIELDS, :] = 1
    return plan, code, perm, keep, sel, find, pick, coef, place


def packed(record_values, record_cell, record_instrument, block_counts, lon_cells):
    capacity = record_values.shape[2]
    is_live = jnp.arange(capacity, dtype=jnp.int32)[None, None, :] < block_counts[:, :, None]
    row = jnp.where(is_live, record_cell // lon_cells, 255)[..., None]
    col = (record_cell % lon_cells)[..., None]
    lane = jnp.arange(128, dtype=jnp.int32)
    field = lane % FIELDS
    tags = jnp.where(
        field == 0, row, jnp.where(field == 1, col, record_instrument[..., None])
    ).astype(BF16)
    pieces, meta = [], jnp.zeros(record_values.shape, BF16)
    for n, (dy, dx) in enumerate(AROUND):
        pieces.append(jnp.roll(record_values, (-dx, -dy), (0, 1)))
        meta = jnp.where(lane // FIELDS == n, jnp.roll(tags, (-dx, -dy), (0, 1)), meta)
    stacked = jnp.stack(pieces + [meta], axis=2)
    return stacked.reshape((-1,) + stacked.shape[2:])


def local(
    record_values,
    record_cell,
    record_instrument,
    block_counts,
    background,
    input_weight,
    instrument_table,
    lift_weight,
    first_gain,
    attn_weight,
    mix_weight,
    second_gain,
    up_weight,
    down_weight,
):
    lat_cells, lon_cells, _, width = background.shape
    capacity = record_values.shape[2]
    sources = record_values.shape[0] * record_values.shape[1]
    chunk = min(CHUNK, sources)
    plan, code, perm, keep, sel, find, pick, coef, place = constants(
        lat_cells, lon_cells, capacity, chunk
    )

    west = shifted(background[:, lon_cells - HLON :], "lon", 1)
    east = shifted(background[:, :HLON], "lon", -1)
    bordered = jnp.concatenate([west, background, east], axis=1)
    north = shifted(bordered[lat_cells - HLAT :], "lat", 1)
    south = shifted(bordered[:HLAT], "lat", -1)
    bordered = jnp.concatenate([north, bordered, south], axis=0)
    bordered = jnp.pad(bordered, ((0, 0), (0, 0), (0, 0), (0, PAD - width)))
    prior = dot(jnp.asarray(perm), bordered.reshape(len(code), LEV * PAD)).astype(BF16)

    sent = packed(record_values, record_cell, record_instrument, block_counts, lon_cells)
    received = lax.all_to_all(sent, ("lon", "lat"), split_axis=0, concat_axis=0, tiled=True)
    received = received.reshape(-1, received.shape[-1])

    lift = jnp.pad(
        lift_weight.reshape(width, LEV, width), ((0, 0), (0, 0), (0, PAD - width))
    ).reshape(width, LEV * PAD)
    values_weight = jnp.pad(attn_weight[:, 2 * width :], ((0, 0), (0, PAD - width)))
    where = lax.axis_index("lat")
    last = lax.axis_size("lat") - 1
    pole = jnp.stack([where == 0, where == last]).astype(jnp.int32)
    pole = pole - 1

    cells = len(code)
    rows = chunk * (len(AROUND) + 1) * capacity
    vmem = pl.BlockSpec(memory_space=pltpu.VMEM)
    out = pl.pallas_call(
        functools.partial(block_kernel, plan),
        out_shape=jax.ShapeDtypeStruct((lat_cells * lon_cells * LEV, width), BF16),
        in_specs=[pl.BlockSpec(memory_space=pltpu.SMEM)] + [vmem] * 20,
        out_specs=vmem,
        scratch_shapes=[
            pltpu.VMEM((rows, LEV * PAD), BF16),
            pltpu.VMEM((cells, rows), BF16),
            pltpu.VMEM((cells, LEV * PAD), F32),
        ],
        compiler_params=pltpu.CompilerParams(vmem_limit_bytes=40 * 2**20),
        cost_estimate=pl.CostEstimate(
            flops=4 * 10**9, bytes_accessed=6 * 10**6, transcendentals=2 * 10**6
        ),
    )(
        pole,
        received,
        prior,
        jnp.asarray(find),
        jnp.asarray(pick),
        jnp.asarray(coef),
        jnp.asarray(place),
        jnp.asarray(code),
        jnp.asarray(keep),
        jnp.asarray(sel),
        input_weight.T,
        instrument_table,
        lift,
        first_gain.reshape(1, width),
        attn_weight[:, :width],
        attn_weight[:, width : 2 * width],
        values_weight,
        mix_weight,
        second_gain.reshape(1, width),
        up_weight,
        down_weight.T,
    )
    return out.reshape(lat_cells, lon_cells, LEV, width)


def solution(mesh):
    placed = (
        P("lon", "lat", None, None),
        P("lon", "lat", None),
        P("lon", "lat", None),
        P("lon", "lat"),
        P("lat", "lon", None, None),
        P(),
        P(),
        P(),
        P(),
        P(),
        P(),
        P(),
        P(),
        P(),
    )
    return jax.shard_map(
        local, mesh=mesh, in_specs=placed, out_specs=P("lat", "lon", None, None), check_vma=False
    )
```

time: 93.5 us -> 54.9 us (0.59)
  waiting for transfers between devices: 40 us -> 7.41 us
  Pallas kernels: 0 us -> 13.4 us
  starting transfers between devices: 24.9 us -> 14.2 us
  matrix products: 5.9 us -> 1.54 us
  other arithmetic: 5.78 us -> 3.34 us
  local copies, waits for them, and re-layouts: 15.7 us -> 14 us
    all_to_all x6 -> x1, waiting for transfers between devices: 24.4 us -> 0.01 us  [local(): lax.all_to_all(sent, ('lon', 'lat'), split_axis=0, concat_axis=0, tiled=T...]
    all_to_all x6 -> x1, starting transfers between devices: 23.1 us -> 7.3 us  [local(): lax.all_to_all(sent, ('lon', 'lat'), split_axis=0, concat_axis=0, tiled=T...]
    pallas_call x0 -> x1, Pallas kernels: none -> 13.4 us  [local(): pl.pallas_call(functools.partial(block_kernel, plan), out_shape=jax.Shape...]
    ppermute x4, waiting for transfers between devices: 15.7 us -> 7.41 us  [shifted(): return lax.ppermute(value, axis, pairs)]
    unnamed x20 -> x54, local copies, waits for them, and re-layouts: 1.96 us -> 9.04 us
    ppermute x4, starting transfers between devices: 1.79 us -> 6.93 us  [shifted(): return lax.ppermute(value, axis, pairs)]
    another operation x4 -> x0, local copies, waits for them, and re-layouts: 4.83 us -> none  [the longest x1 1.92 us: attend_windows(): keys_w = to_windows(keys).reshape(windows, count_tok, HEADS, head_size)]
    dot_general x8 -> x1, matrix products: 5.9 us -> 1.54 us  [dot(): return jnp.dot(a, b, preferred_element_type=F32)]
  transfers between devices with their start and end apart: 10 -> 5, of which waited for: 10 -> 3; matrix products, arithmetic and copies ran while one was open for 8% -> 7% of each run, Pallas kernels for 0% -> 0%
where the time goes in v1:
time: 54.9 us; the launch traced here: 54.5 us
  starting transfers between devices  14.2 us (26%)
  local copies, waits for them, and re-layouts  14 us (26%)
  Pallas kernels  13.4 us (24%)
  waiting for transfers between devices  7.41 us (13%)
  other arithmetic  3.34 us (6%)
  matrix products  1.54 us (3%)
  between operations  0.57 us (1%)
    pallas_call x1, Pallas kernels, local(): pl.pallas_call(functools.partial(block_kernel, plan), out_shape=jax.Shape...  13.4 us
    unnamed x54, local copies, waits for them, and re-layouts  9.04 us
    ppermute x4, waiting for transfers between devices, shifted(): return lax.ppermute(value, axis, pairs)  7.41 us
    all_to_all x1, starting transfers between devices, local(): lax.all_to_all(sent, ('lon', 'lat'), split_axis=0, concat_axis=0, tiled=T...  7.3 us
    ppermute x4, starting transfers between devices, shifted(): return lax.ppermute(value, axis, pairs)  6.93 us
    slice x4, local copies, waits for them, and re-layouts, packed(): pieces.append(jnp.roll(record_values, (-dx, -dy), (0, 1)))  3.07 us
    dot_general x1, matrix products, dot(): return jnp.dot(a, b, preferred_element_type=F32)  1.54 us
  transfers between devices with their start and end apart: 5, of which 3 were waited for; matrix products, arithmetic and copies ran while one was open for 7% of the time, Pallas kernels for 0%

profile of v1, /device:TPU:0, one launch (start us, length us, event | category | flops | bytes accessed | tf_op | source)
XLA Modules:
  0.0 54.5 jit_solution(4841874798899137010)
XLA Ops:
  0.0 0.8 %fusion.35 = (bf16[7,4,2,128]{3,2,1,0:T(2,128)(2,1)S(1)}, bf16[7,4,2,128]{3,2,1,0:T(2,128)(2,1)S(1)}) fusion(bf16[8,4,2,128]{3,2,1,0:T(2,128)(2,1)} %param.22), kind=kLoop, calls=%fused_computation.121 | loop fusion | bytes 57344 | tf_op jit(solution)/shard_map/jit(_roll_static)/slice | solution.py:245
  0.8 0.7 %fusion.36 = (bf16[1,4,2,128]{3,2,1,0:T(2,128)(2,1)S(1)}, bf16[1,4,2,128]{3,2,1,0:T(2,128)(2,1)S(1)}) fusion(bf16[8,4,2,128]{3,2,1,0:T(2,128)(2,1)} %param.22), kind=kLoop, calls=%fused_computation.122 | loop fusion | bytes 8192 | tf_op jit(solution)/shard_map/jit(_roll_static)/slice | solution.py:245
  1.6 0.1 fusion.7
  1.7 0.0 copy-start.13
  1.7 0.8 %fusion.33 = (bf16[8,3,2,128]{3,2,1,0:T(2,128)(2,1)S(1)}, bf16[8,3,2,128]{3,2,1,0:T(2,128)(2,1)S(1)}) fusion(bf16[8,4,2,128]{3,2,1,0:T(2,128)(2,1)} %param.22), kind=kLoop, calls=%fused_computation.119 | loop fusion | bytes 49152 | tf_op jit(solution)/shard_map/jit(_roll_static)/slice | solution.py:245
  2.5 0.7 %fusion.34 = (bf16[8,1,2,128]{3,2,1,0:T(2,128)(2,1)S(1)}, bf16[8,1,2,128]{3,2,1,0:T(2,128)(2,1)S(1)}) fusion(bf16[8,4,2,128]{3,2,1,0:T(2,128)(2,1)} %param.22), kind=kLoop, calls=%fused_computation.120 | loop fusion | bytes 16384 | tf_op jit(solution)/shard_map/jit(_roll_static)/slice | solution.py:245
  3.3 0.7 %compare_select_fusion = (s32[8,4,2]{0,2,1:T(2,128)S(1)}, s32[8,4,2]{0,2,1:T(2,128)S(1)}) fusion(s32[8,4,2]{0,2,1:T(2,128)} %param.23, s32[8,4]{0,1:T(4,128)} %param.25), kind=kLoop, calls=%fused_computation.78 | loop fusion | flops 896 | bytes 896 | tf_op jit(solution)/shard_map/jit(_where)/select_n | solution.py:236
  4.0 0.1 copy.48
  4.1 0.1 copy.49
  4.2 0.8 %copy.50 = s32[8,4,2]{2,1,0:T(4,128)S(1)} copy(s32[8,4,2]{0,2,1:T(2,128)} %param.24) | data formatting | bytes 512 | tf_op args[2]
  5.0 0.2 select_convert_fusion.1
  5.2 0.0 copy-start.15
  5.5 0.6 %constant_dynamic-update-slice_fusion.9 = bf16[32,10,2,128]{3,2,1,0:T(2,128)(2,1)} fusion(bf16[32,1,2,128]{3,2,1,0:T(2,128)(2,1)S(1)} %bitcast.120), kind=kLoop, calls=%fused_computation.28 | loop fusion | bytes 32768
  6.2 0.6 %constant_dynamic-update-slice_fusion.8 = bf16[32,10,2,128]{3,2,1,0:T(2,128)(2,1)} fusion(bf16[32,10,2,128]{3,2,1,0:T(2,128)(2,1)} %constant_dynamic-update-slice_fusion.9, bf16[32,1,2,128]{3,2,1,0:T(2,128)(2,1)S(1)} %bitcast.124), kind=kLoop, calls=%fused_computation.27 | loop fusion | bytes 32768
  6.8 0.6 %constant_dynamic-update-slice_fusion.7 = bf16[32,10,2,128]{3,2,1,0:T(2,128)(2,1)} fusion(bf16[32,10,2,128]{3,2,1,0:T(2,128)(2,1)} %constant_dynamic-update-slice_fusion.8, bf16[32,1,2,128]{3,2,1,0:T(2,128)(2,1)S(1)} %bitcast.117), kind=kLoop, calls=%fused_computation.26 | loop fusion | bytes 32768
  7.4 0.6 %constant_dynamic-update-slice_fusion.6 = bf16[32,10,2,128]{3,2,1,0:T(2,128)(2,1)} fusion(bf16[32,10,2,128]{3,2,1,0:T(2,128)(2,1)} %constant_dynamic-update-slice_fusion.7, bf16[32,1,2,128]{3,2,1,0:T(2,128)(2,1)S(1)} %bitcast.122), kind=kLoop, calls=%fused_computation.25 | loop fusion | bytes 32768
  8.1 0.0 copy-done.14
  8.1 0.6 %constant_dynamic-update-slice_fusion.5 = bf16[32,10,2,128]{3,2,1,0:T(2,128)(2,1)} fusion(bf16[32,10,2,128]{3,2,1,0:T(2,128)(2,1)} %constant_dynamic-update-slice_fusion.6, bf16[32,1,2,128]{3,2,1,0:T(2,128)(2,1)S(1)} %bitcast.105), kind=kLoop, calls=%fused_computation.24 | loop fusion | bytes 32768
  8.7 0.6 %constant_dynamic-update-slice_fusion.4 = bf16[32,10,2,128]{3,2,1,0:T(2,128)(2,1)} fusion(bf16[32,10,2,128]{3,2,1,0:T(2,128)(2,1)} %constant_dynamic-update-slice_fusion.5, bf16[32,1,2,128]{3,2,1,0:T(2,128)(2,1)S(1)} %bitcast.121), kind=kLoop, calls=%fused_computation.23 | loop fusion | bytes 32768
  9.3 0.6 %constant_dynamic-update-slice_fusion.3 = bf16[32,10,2,128]{3,2,1,0:T(2,128)(2,1)} fusion(bf16[32,10,2,128]{3,2,1,0:T(2,128)(2,1)} %constant_dynamic-update-slice_fusion.4, bf16[32,1,2,128]{3,2,1,0:T(2,128)(2,1)S(1)} %bitcast.118), kind=kLoop, calls=%fused_computation.22 | loop fusion | bytes 32768
  10.0 0.6 %constant_dynamic-update-slice_fusion.2 = bf16[32,10,2,128]{3,2,1,0:T(2,128)(2,1)} fusion(bf16[32,10,2,128]{3,2,1,0:T(2,128)(2,1)} %constant_dynamic-update-slice_fusion.3, bf16[32,1,2,128]{3,2,1,0:T(2,128)(2,1)S(1)} %bitcast.123), kind=kLoop, calls=%fused_computation.21 | loop fusion | bytes 32768
  10.6 0.6 %constant_dynamic-update-slice_fusion.1 = bf16[32,10,2,128]{3,2,1,0:T(2,128)(2,1)} fusion(bf16[32,10,2,128]{3,2,1,0:T(2,128)(2,1)} %constant_dynamic-update-slice_fusion.2, bf16[32,1,2,128]{3,2,1,0:T(2,128)(2,1)S(1)} %bitcast.119), kind=kLoop, calls=%fused_computation.20 | loop fusion | bytes 32768
  11.5 0.8 %constant_dynamic-update-slice_fusion = bf16[32,10,2,128]{3,2,1,0:T(2,128)(2,1)} fusion(bf16[32,10,2,128]{3,2,1,0:T(2,128)(2,1)} %constant_dynamic-update-slice_fusion.1, bf16[32,1,2,128]{3,2,1,0:T(2,128)(2,1)S(1)} %bitcast.109, pred[128]{0:T(512)(128)(4,1)S(1)} %get-tuple-element.64, bf16[32,1,2,128]{3,2,1,0:T(2,128)(2,1)S(1)} %bitcast.115, ...), kind=kLoop, calls=%fused_computation.19 | loop fusion | flops 98304 | bytes 149632 | tf_op jit(solution)/shard_map/stack | solution.py:247
  12.3 7.3 %all-to-all-start = ((bf16[32,10,2,128]{3,2,1,0:T(2,128)(2,1)}), bf16[32,10,2,128]{3,2,1,0:T(2,128)(2,1)S(1)}, u32[]{:S(2)}, u32[]{:S(2)}) async-start(bf16[32,10,2,128]{3,2,1,0:T(2,128)(2,1)} %constant_dynamic-update-slice_fusion), calls=%async_computation | async-start | bytes 327680 | tf_op jit(solution)/shard_map/all_to_all | solution.py:285
  19.6 0.0 copy-done.13
  19.6 0.1 fusion.31
  19.7 0.0 copy-start.17
  19.7 0.0 copy-start.18
  19.7 0.3 collective-permute-start
  20.0 2.4 %collective-permute-start.1 = (bf16[12,6,2,192]{3,2,1,0:T(2,128)(2,1)S(1)}, bf16[12,6,2,192]{3,2,1,0:T(2,128)(2,1)S(1)}, u32[]{:S(2)}, u32[]{:S(2)}) collective-permute-start(bf16[12,6,2,192]{3,2,1,0:T(2,128)(2,1)S(1)} %get-tuple-element.7), channel_id=1, source_target_pairs={{0,28},{4,0},{8,4},{12,8},{16,12},{20,16},{24,20},{28,24},{1,29},{... | collective-permute-start | bytes 165896 | tf_op jit(solution)/shard_map/ppermute | solution.py:32
  22.4 0.0 copy-done.15
  22.4 0.1 fusion.32
  22.5 0.0 copy-done.16
  22.6 0.1 reshape.158
  22.7 0.2 pad.13
  23.0 0.0 copy-done.17
  23.0 2.1 %collective-permute-done = bf16[12,6,2,192]{3,2,1,0:T(2,128)(2,1)S(1)} collective-permute-done((bf16[12,6,2,192]{3,2,1,0:T(2,128)(2,1)S(1)}, bf16[12,6,2,192]{3,2,1,0:T(2,128)(2,1)S(1)}, u32[]{:S(2)}, u32[]{:S(2)}) %collective-permute-start) | collective-permute-done | bytes 55328 | tf_op jit(solution)/shard_map/ppermute | solution.py:32
  25.1 0.1 constant_dynamic-update-slice_fusion.12
  25.1 0.2 constant_dynamic-update-slice_fusion.11
  25.4 0.0 collective-permute-done.1
  25.4 0.1 constant_dynamic-update-slice_fusion.10
  25.5 0.2 fusion.30
  25.6 2.1 %collective-permute-start.2 = (bf16[3,36,2,192]{3,2,1,0:T(2,128)(2,1)S(1)}, bf16[3,36,2,192]{3,2,1,0:T(2,128)(2,1)S(1)}, u32[]{:S(2)}, u32[]{:S(2)}) collective-permute-start(bf16[3,36,2,192]{3,2,1,0:T(2,128)(2,1)S(1)} %get-tuple-element.5), channel_id=1, source_target_pairs={{0,1},{1,2},{2,3},{3,0},{4,5},{5,6},{6,7},{7,4},{8,9},{9,10},{10,1... | collective-permute-start | bytes 248840 | tf_op jit(solution)/shard_map/ppermute | solution.py:32
  27.7 2.2 %collective-permute-start.3 = (bf16[3,36,2,192]{3,2,1,0:T(2,128)(2,1)S(1)}, bf16[3,36,2,192]{3,2,1,0:T(2,128)(2,1)S(1)}, u32[]{:S(2)}, u32[]{:S(2)}) collective-permute-start(bf16[3,36,2,192]{3,2,1,0:T(2,128)(2,1)S(1)} %get-tuple-element.6), channel_id=1, source_target_pairs={{0,3},{1,0},{2,1},{3,2},{4,7},{5,4},{6,5},{7,6},{8,11},{9,8},{10,9... | collective-permute-start | bytes 248840 | tf_op jit(solution)/shard_map/ppermute | solution.py:32
  29.9 0.1 fusion.28.pole_ref
  29.9 3.6 %collective-permute-done.2 = bf16[3,36,2,192]{3,2,1,0:T(2,128)(2,1)S(1)} collective-permute-done((bf16[3,36,2,192]{3,2,1,0:T(2,128)(2,1)S(1)}, bf16[3,36,2,192]{3,2,1,0:T(2,128)(2,1)S(1)}, u32[]{:S(2)}, u32[]{:S(2)}) %collective-permute-start.2) | collective-permute-done | bytes 82976 | tf_op jit(solution)/shard_map/ppermute | solution.py:32
  33.5 1.7 %collective-permute-done.3 = bf16[3,36,2,192]{3,2,1,0:T(2,128)(2,1)S(1)} collective-permute-done((bf16[3,36,2,192]{3,2,1,0:T(2,128)(2,1)S(1)}, bf16[3,36,2,192]{3,2,1,0:T(2,128)(2,1)S(1)}, u32[]{:S(2)}, u32[]{:S(2)}) %collective-permute-start.3) | collective-permute-done | bytes 82976 | tf_op jit(solution)/shard_map/ppermute | solution.py:32
  35.3 0.9 %fusion.5 = bf16[18,36,2,256]{3,2,1,0:T(2,128)(2,1)S(1)} fusion(bf16[3,36,2,192]{3,2,1,0:T(2,128)(2,1)S(1)} %collective-permute-done.3, bf16[12,36,2,192]{3,2,1,0:T(2,128)(2,1)S(1)} %constant_dynamic-update-slice_fusion.10, bf16[3,36,2,192]{3,2,1,0:T(2,128)(2,1)S(1)} %collective-permute-done.2), kind=kLoop, calls=%fused_computation.7 | loop fusion | flops 3317760 | bytes 1161216 | tf_op jit(solution)/shard_map/concatenate | solution.py:280
  36.2 0.0 copy-start.19
  36.2 0.1 copy.81
  36.3 1.1 %copy-done.19 = bf16[648,648]{1,0:T(8,128)(2,1)S(1)} copy-done((bf16[648,648]{1,0:T(8,128)(2,1)S(1)}, bf16[648,648]{1,0:T(8,128)(2,1)}, u32[]{:S(2)}) %copy-start.19) | copy-done | bytes 839832
  37.4 0.0 copy-start.4
  37.4 0.0 copy-start.5
  37.4 0.0 copy-start.6
  37.4 0.0 copy-start.7
  37.4 0.0 copy-start.8
  37.5 0.0 copy-start.9
  37.5 0.0 copy-start.10
  37.5 0.0 copy-start.11
  37.5 1.5 %fusion.3.bg_ref = bf16[648,512]{1,0:T(8,128)(2,1)} fusion(bf16[648,512]{1,0:T(8,128)(2,1)S(1)} %bitcast.104, bf16[648,648]{1,0:T(8,128)(2,1)S(1)} %copy-done.19), kind=kOutput, calls=%fused_computation.5 | convolution fusion | flops 430313472 | bytes 2166912 | tf_op jit(solution)/shard_map/dot_general | solution.py:63
  39.0 0.0 all-to-all-done
  39.2 1.1 %copy-done.12 = bf16[648,512]{1,0:T(8,128)(2,1)S(1)} copy-done((bf16[648,512]{1,0:T(8,128)(2,1)S(1)}, bf16[648,512]{1,0:T(8,128)(2,1)}, u32[]{:S(2)}) %copy-start.12) | copy-done | bytes 663576
  40.2 13.4 %shard_map.208 = bf16[576,192]{1,0:T(8,128)(2,1)S(1)} custom-call(s32[2]{0:T(128)S(1)} %fusion.28.pole_ref, bf16[640,128]{1,0:T(8,128)(2,1)S(1)} %bitcast.99, bf16[648,512]{1,0:T(8,128)(2,1)S(1)} %copy-done.12, bf16[160,160]{1,0:T(8,128)(2,1)S(1)} %copy-done.7, bf16[160,128]{1,0:T(8,128)(2,1)S(1)} %copy-done.8, bf16[136,128]{1,0:T(8,128)(2,1)S(1)} %copy-done.9, ...), custom_call_target="tpu_custom_call" | custom-call | flops 4000000000 | bytes 6000000 | tf_op jit(solution)/shard_map/pallas_call | solution.py:300
  53.6 0.9 %reshape.162 = bf16[12,24,2,192]{3,2,1,0:T(2,128)(2,1)} reshape(bf16[576,192]{1,0:T(8,128)(2,1)S(1)} %shard_map.208) | data formatting | bytes 442368 | tf_op jit(solution)/shard_map/reshape | solution.py:337
  (53 shorter events, 0.8 us)
Async XLA Ops:
  0.0 8.1 %copy-start.14 = (bf16[8,4,2,128]{3,2,1,0:T(2,128)(2,1)S(1)}, bf16[8,4,2,128]{3,2,1,0:T(2,128)(2,1)}, u32[]{:S(2)}) copy-start(bf16[8,4,2,128]{3,2,1,0:T(2,128)(2,1)} %param.22) | copy-start | bytes 49156
  1.7 17.9 %copy-start.13 = (bf16[12,24,2,192]{3,2,1,0:T(2,128)(2,1)S(1)}, bf16[12,24,2,192]{3,2,1,0:T(2,128)(2,1)}, u32[]{:S(2)}) copy-start(bf16[12,24,2,192]{3,2,1,0:T(2,128)(2,1)} %param.26) | copy-start | bytes 663556
  5.2 17.3 %copy-start.15 = (bf16[192,576]{1,0:T(8,128)(2,1)S(1)}, bf16[192,576]{1,0:T(8,128)(2,1)}, u32[]{:S(2)}) copy-start(bf16[192,576]{1,0:T(8,128)(2,1)} %param.31) | copy-start | bytes 663556
  8.7 13.9 %copy-start.16 = (bf16[192,384]{1,0:T(8,128)(2,1)S(1)}, bf16[192,384]{1,0:T(8,128)(2,1)}, u32[]{:S(2)}) copy-start(bf16[192,384]{1,0:T(8,128)(2,1)} %param.29) | copy-start | bytes 442372
  12.3 26.8 %all-to-all-start = ((bf16[32,10,2,128]{3,2,1,0:T(2,128)(2,1)}), bf16[32,10,2,128]{3,2,1,0:T(2,128)(2,1)S(1)}, u32[]{:S(2)}, u32[]{:S(2)}) async-start(bf16[32,10,2,128]{3,2,1,0:T(2,128)(2,1)} %constant_dynamic-update-slice_fusion), calls=%async_computation | async-start | bytes 327680 | tf_op jit(solution)/shard_map/all_to_all | solution.py:285
  19.7 3.2 %copy-start.17 = (bf16[192]{0:T(256)(128)(2,1)S(1)}, bf16[192]{0:T(256)(128)(2,1)}, u32[]{:S(2)}) copy-start(bf16[192]{0:T(256)(128)(2,1)} %param.30) | copy-start | bytes 1156
  19.7 3.3 %copy-start.18 = (bf16[192]{0:T(256)(128)(2,1)S(1)}, bf16[192]{0:T(256)(128)(2,1)}, u32[]{:S(2)}) copy-start(bf16[192]{0:T(256)(128)(2,1)} %param.33) | copy-start | bytes 1156
  19.7 5.3 %collective-permute-start = (bf16[12,6,2,192]{3,2,1,0:T(2,128)(2,1)S(1)}, bf16[12,6,2,192]{3,2,1,0:T(2,128)(2,1)S(1)}, u32[]{:S(2)}, u32[]{:S(2)}) collective-permute-start(bf16[12,6,2,192]{3,2,1,0:T(2,128)(2,1)S(1)} %get-tuple-element.8), channel_id=1, source_target_pairs={{0,4},{4,8},{8,12},{12,16},{16,20},{20,24},{24,28},{28,0},{1,5},{5... | collective-permute-start | bytes 165896 | tf_op jit(solution)/shard_map/ppermute | solution.py:32
  20.0 5.3 %collective-permute-start.1 = (bf16[12,6,2,192]{3,2,1,0:T(2,128)(2,1)S(1)}, bf16[12,6,2,192]{3,2,1,0:T(2,128)(2,1)S(1)}, u32[]{:S(2)}, u32[]{:S(2)}) collective-permute-start(bf16[12,6,2,192]{3,2,1,0:T(2,128)(2,1)S(1)} %get-tuple-element.7), channel_id=1, source_target_pairs={{0,28},{4,0},{8,4},{12,8},{16,12},{20,16},{24,20},{28,24},{1,29},{... | collective-permute-start | bytes 165896 | tf_op jit(solution)/shard_map/ppermute | solution.py:32
  25.6 7.9 %collective-permute-start.2 = (bf16[3,36,2,192]{3,2,1,0:T(2,128)(2,1)S(1)}, bf16[3,36,2,192]{3,2,1,0:T(2,128)(2,1)S(1)}, u32[]{:S(2)}, u32[]{:S(2)}) collective-permute-start(bf16[3,36,2,192]{3,2,1,0:T(2,128)(2,1)S(1)} %get-tuple-element.5), channel_id=1, source_target_pairs={{0,1},{1,2},{2,3},{3,0},{4,5},{5,6},{6,7},{7,4},{8,9},{9,10},{10,1... | collective-permute-start | bytes 248840 | tf_op jit(solution)/shard_map/ppermute | solution.py:32
  27.7 7.5 %collective-permute-start.3 = (bf16[3,36,2,192]{3,2,1,0:T(2,128)(2,1)S(1)}, bf16[3,36,2,192]{3,2,1,0:T(2,128)(2,1)S(1)}, u32[]{:S(2)}, u32[]{:S(2)}) collective-permute-start(bf16[3,36,2,192]{3,2,1,0:T(2,128)(2,1)S(1)} %get-tuple-element.6), channel_id=1, source_target_pairs={{0,3},{1,0},{2,1},{3,2},{4,7},{5,4},{6,5},{7,6},{8,11},{9,8},{10,9... | collective-permute-start | bytes 248840 | tf_op jit(solution)/shard_map/ppermute | solution.py:32
  36.2 1.2 %copy-start.19 = (bf16[648,648]{1,0:T(8,128)(2,1)S(1)}, bf16[648,648]{1,0:T(8,128)(2,1)}, u32[]{:S(2)}) copy-start(bf16[648,648]{1,0:T(8,128)(2,1)} %constant.106.clone) | copy-start | bytes 2519428
  37.4 1.7 %copy-start = (bf16[192,768]{1,0:T(8,128)(2,1)S(1)}, bf16[192,768]{1,0:T(8,128)(2,1)}, u32[]{:S(2)}) copy-start(bf16[192,768]{1,0:T(8,128)(2,1)} %wu_ref.1) | copy-start | bytes 884740
  37.4 1.7 %copy-start.1 = (bf16[768,192]{0,1:T(8,128)(2,1)S(1)}, bf16[768,192]{0,1:T(8,128)(2,1)}, u32[]{:S(2)}) copy-start(bf16[768,192]{0,1:T(8,128)(2,1)} %param.35) | copy-start | bytes 884740
  37.4 1.7 %copy-start.2 = (bf16[192,192]{1,0:T(8,128)(2,1)S(1)}, bf16[192,192]{1,0:T(8,128)(2,1)}, u32[]{:S(2)}) copy-start(bf16[192,192]{1,0:T(8,128)(2,1)} %wm_ref.1) | copy-start | bytes 221188
  37.4 1.7 %copy-start.3 = (bf16[128,192]{0,1:T(8,128)(2,1)S(1)}, bf16[128,192]{0,1:T(8,128)(2,1)}, u32[]{:S(2)}) copy-start(bf16[128,192]{0,1:T(8,128)(2,1)} %param.27) | copy-start | bytes 147460
  37.4 1.7 %copy-start.4 = (bf16[8,192]{1,0:T(8,128)(2,1)S(1)}, bf16[8,192]{1,0:T(8,128)(2,1)}, u32[]{:S(2)}) copy-start(bf16[8,192]{1,0:T(8,128)(2,1)} %tab_ref.1) | copy-start | bytes 9220
  37.4 1.7 %copy-start.5 = (bf16[576,656]{1,0:T(8,128)(2,1)S(1)}, bf16[576,656]{1,0:T(8,128)(2,1)}, u32[]{:S(2)}) copy-start(bf16[576,656]{1,0:T(8,128)(2,1)} %constant.113.clone.sel_ref) | copy-start | bytes 2267140
  37.4 1.7 %copy-start.6 = (f32[648,1]{1,0:T(8,128)S(1)}, f32[648,1]{1,0:T(8,128)}, u32[]{:S(2)}) copy-start(f32[648,1]{1,0:T(8,128)} %constant.111.clone.code_ref) | copy-start | bytes 7780
  37.4 1.7 %copy-start.7 = (bf16[160,160]{1,0:T(8,128)(2,1)S(1)}, bf16[160,160]{1,0:T(8,128)(2,1)}, u32[]{:S(2)}) copy-start(bf16[160,160]{1,0:T(8,128)(2,1)} %constant.107.clone.find_ref) | copy-start | bytes 153604
  37.4 1.7 %copy-start.8 = (bf16[160,128]{1,0:T(8,128)(2,1)S(1)}, bf16[160,128]{1,0:T(8,128)(2,1)}, u32[]{:S(2)}) copy-start(bf16[160,128]{1,0:T(8,128)(2,1)} %constant.108.clone.pick_ref) | copy-start | bytes 122884
  37.5 1.7 %copy-start.9 = (bf16[136,128]{1,0:T(8,128)(2,1)S(1)}, bf16[136,128]{1,0:T(8,128)(2,1)}, u32[]{:S(2)}) copy-start(bf16[136,128]{1,0:T(8,128)(2,1)} %constant.109.clone.coef_ref) | copy-start | bytes 104452
  37.5 1.7 %copy-start.10 = (f32[16,144]{1,0:T(8,128)S(1)}, f32[16,144]{1,0:T(8,128)}, u32[]{:S(2)}) copy-start(f32[16,144]{1,0:T(8,128)} %constant.112.clone.keep_ref) | copy-start | bytes 27652
  37.5 1.7 %copy-start.11 = (f32[1,640]{1,0:T(1,128)S(1)}, f32[1,640]{1,0:T(1,128)}, u32[]{:S(2)}) copy-start(f32[1,640]{1,0:T(1,128)} %constant.110.clone.place_ref) | copy-start | bytes 7684
  39.2 1.1 %copy-start.12 = (bf16[648,512]{1,0:T(8,128)(2,1)S(1)}, bf16[648,512]{1,0:T(8,128)(2,1)}, u32[]{:S(2)}) copy-start(bf16[648,512]{1,0:T(8,128)(2,1)} %fusion.3.bg_ref) | copy-start | bytes 1990660

commit v2 on v1

--- a/solution.py
+++ b/solution.py
@@ -71,7 +71,12 @@
     plan,
     pole_ref,
     recv_ref,
-    bg_ref,
+    own_ref,
+    north_ref,
+    south_ref,
+    west_ref,
+    east_ref,
+    perm_ref,
     find_ref,
     pick_ref,
     coef_ref,
@@ -93,14 +98,25 @@
     out_ref,
     lifted_ref,
     hot_ref,
+    prior_ref,
     sum_ref,
 ):
     width = win_ref.shape[0]
     stride = find_ref.shape[0]
     per_chunk = lifted_ref.shape[0]
     chunks = recv_ref.shape[0] // per_chunk
-    cells = bg_ref.shape[0]
     in_window = WLAT * WLON
+
+    start = 0
+    for strip in (own_ref, north_ref, south_ref, west_ref, east_ref):
+        count = strip.shape[0]
+        held = -(-count // 16) * 16
+        value = strip[...].astype(F32)
+        if held > count:
+            value = jnp.concatenate([value, jnp.zeros((held - count, value.shape[1]), F32)], axis=0)
+        prior_ref[start : start + held, :] = value.astype(BF16)
+        start += held
+    prior = dot(perm_ref[...], prior_ref[...])
 
     def scatter(base):
         for group in range(per_chunk // stride):
@@ -120,9 +136,9 @@
         return dot(hot_ref[...], lifted_ref[...])
 
     if chunks == 1:
-        sum_ref[...] = scatter(0)
+        sum_ref[...] = prior + scatter(0)
     else:
-        sum_ref[...] = jnp.zeros_like(sum_ref)
+        sum_ref[...] = prior
 
         @pl.loop(0, chunks)
         def _(step):
@@ -133,8 +149,7 @@
     for level in range(LEV):
         piece = sum_ref[:, level * PAD : (level + 1) * PAD]
         share = 1.0 / (1.0 + piece[:, width : width + 1])
-        back = bg_ref[:, level * PAD : level * PAD + width].astype(F32)
-        latent = ((back + piece[:, :width]) * share).astype(BF16).astype(F32)
+        latent = (piece[:, :width] * share).astype(BF16).astype(F32)
         latents.append(latent)
         normeds.append(normalise(latent, gain_one))
 
@@ -191,10 +206,24 @@
     order = [cell for own, rest in windows for cell in own + rest]
     plan = [-(-len(own) // 8) * 8 for own, _ in windows]
     code = np.array([[r * 64 + c] for r, c in order], np.float32)
-    wide = lon_cells + WLON
-    perm = np.zeros((len(order), len(order)), ml_dtypes.bfloat16)
+    up16 = lambda count: -(-count // 16) * 16
+    high = lat_cells + WLAT
+    strips = [lat_cells * lon_cells, HLAT * lon_cells, HLAT * lon_cells, high * HLON, high * HLON]
+    begins = np.cumsum([0] + [up16(count) for count in strips])
+    perm = np.zeros((len(order), begins[-1]), ml_dtypes.bfloat16)
     for place, (r, c) in enumerate(order):
-        perm[place, r * wide + c] = 1
+        row, col = r - HLAT, c - HLON
+        if col < 0:
+            at = begins[3] + r * HLON + c
+        elif col >= lon_cells:
+            at = begins[4] + r * HLON + col - lon_cells
+        elif row < 0:
+            at = begins[1] + r * lon_cells + col
+        elif row >= lat_cells:
+            at = begins[2] + (row - lat_cells) * lon_cells + col
+        else:
+            at = begins[0] + row * lon_cells + col
+        perm[place, at] = 1
     keep = np.zeros((16, LEV * WLAT * WLON), np.float32)
     for w, (own, rest) in enumerate(windows):
         for k, (r, c) in enumerate(own + rest):
@@ -230,22 +259,76 @@
     return plan, code, perm, keep, sel, find, pick, coef, place
 
 
+def pack_kernel(values_ref, cell_ref, tag_ref, count_ref, spread_ref, out_ref, *, lon_cells):
+    tiles_lon, tiles_lat, capacity, _ = values_ref.shape
+    for n, (dy, dx) in enumerate(AROUND):
+        lat_parts = [(0, tiles_lat)] if dy == 0 else [(0, tiles_lat - 1), (tiles_lat - 1, tiles_lat)]
+        if dy < 0:
+            lat_parts = [(0, 1), (1, tiles_lat)]
+
+        def copy_tiles(lon, n=n, dx=dx, dy=dy, lat_parts=lat_parts):
+            source = lax.rem(lon + dx + tiles_lon, tiles_lon)
+            for low, end in lat_parts:
+                first = (low + dy) % tiles_lat
+                out_ref[lon, low:end, n] = values_ref[source, first : first + end - low]
+
+        if tiles_lon <= 8:
+            for lon in range(tiles_lon):
+                copy_tiles(lon)
+        else:
+            pl.loop(0, tiles_lon)(copy_tiles)
+
+    cell = cell_ref[...]
+    counts = count_ref[...]
+    counts = jnp.concatenate(
+        [counts[tile : tile + 1] for tile in range(tiles_lat) for _ in range(capacity)], axis=0
+    )
+    slot = lax.broadcasted_iota(jnp.int32, cell.shape, 0) % capacity
+    row = cell // lon_cells
+    fields = [jnp.where(slot < counts, row, 255), cell - row * lon_cells, tag_ref[...]]
+    fields = [field.astype(F32) for field in fields]
+    block = 8
+    for begin in range(0, tiles_lon, block):
+        parts = []
+        for field in fields:
+            around = jnp.concatenate([field[:, -1:], field, field[:, :1]], axis=1)
+            around = around[:, begin : begin + block + 2]
+            for dy in (-1, 0, 1):
+                by = dy * capacity % field.shape[0]
+                parts.append(
+                    jnp.concatenate([around[by:], around[:by]], axis=0) if by else around
+                )
+        meta = dot(jnp.concatenate(parts, axis=1).astype(BF16), spread_ref[...])
+        for lon in range(block):
+            piece = meta[:, lon * 128 : (lon + 1) * 128].astype(BF16)
+            for lat in range(tiles_lat):
+                out_ref[begin + lon, lat, len(AROUND)] = piece[lat * capacity : (lat + 1) * capacity]
+
+
 def packed(record_values, record_cell, record_instrument, block_counts, lon_cells):
-    capacity = record_values.shape[2]
-    is_live = jnp.arange(capacity, dtype=jnp.int32)[None, None, :] < block_counts[:, :, None]
-    row = jnp.where(is_live, record_cell // lon_cells, 255)[..., None]
-    col = (record_cell % lon_cells)[..., None]
-    lane = jnp.arange(128, dtype=jnp.int32)
-    field = lane % FIELDS
-    tags = jnp.where(
-        field == 0, row, jnp.where(field == 1, col, record_instrument[..., None])
-    ).astype(BF16)
-    pieces, meta = [], jnp.zeros(record_values.shape, BF16)
-    for n, (dy, dx) in enumerate(AROUND):
-        pieces.append(jnp.roll(record_values, (-dx, -dy), (0, 1)))
-        meta = jnp.where(lane // FIELDS == n, jnp.roll(tags, (-dx, -dy), (0, 1)), meta)
-    stacked = jnp.stack(pieces + [meta], axis=2)
-    return stacked.reshape((-1,) + stacked.shape[2:])
+    tiles_lon, tiles_lat, capacity, wide = record_values.shape
+    block = 8
+    spread = np.zeros((9 * (block + 2), block * 128), ml_dtypes.bfloat16)
+    for lon in range(block):
+        for n, (dy, dx) in enumerate(AROUND):
+            for field in range(3):
+                spread[(field * 3 + dy + 1) * (block + 2) + lon + 1 + dx, lon * 128 + n * FIELDS + field] = 1
+    vmem = pl.BlockSpec(memory_space=pltpu.VMEM)
+    shape = (tiles_lon, tiles_lat, len(AROUND) + 1, capacity, wide)
+    out = pl.pallas_call(
+        functools.partial(pack_kernel, lon_cells=lon_cells),
+        out_shape=jax.ShapeDtypeStruct(shape, BF16),
+        in_specs=[vmem] * 5,
+        out_specs=vmem,
+        compiler_params=pltpu.CompilerParams(vmem_limit_bytes=32 * 2**20),
+    )(
+        record_values,
+        record_cell.transpose(1, 2, 0).reshape(-1, tiles_lon),
+        record_instrument.transpose(1, 2, 0).reshape(-1, tiles_lon),
+        block_counts.T,
+        jnp.asarray(spread),
+    )
+    return out.reshape((-1,) + shape[2:])
 
 
 def local(
@@ -272,14 +355,17 @@
         lat_cells, lon_cells, capacity, chunk
     )
 
-    west = shifted(background[:, lon_cells - HLON :], "lon", 1)
-    east = shifted(background[:, :HLON], "lon", -1)
-    bordered = jnp.concatenate([west, background, east], axis=1)
-    north = shifted(bordered[lat_cells - HLAT :], "lat", 1)
-    south = shifted(bordered[:HLAT], "lat", -1)
-    bordered = jnp.concatenate([north, bordered, south], axis=0)
-    bordered = jnp.pad(bordered, ((0, 0), (0, 0), (0, 0), (0, PAD - width)))
-    prior = dot(jnp.asarray(perm), bordered.reshape(len(code), LEV * PAD)).astype(BF16)
+    laid = jnp.pad(background, ((0, 0), (0, 0), (0, 0), (0, PAD - width)))
+    laid = lax.optimization_barrier(laid.reshape(lat_cells, lon_cells, LEV * PAD))
+    north = shifted(laid[lat_cells - HLAT :], "lat", 1)
+    south = shifted(laid[:HLAT], "lat", -1)
+
+    def columns(low, end):
+        return jnp.concatenate([north[:, low:end], laid[:, low:end], south[:, low:end]], axis=0)
+
+    west = shifted(columns(lon_cells - HLON, lon_cells), "lon", 1)
+    east = shifted(columns(0, HLON), "lon", -1)
+    strips = [strip.reshape(-1, LEV * PAD) for strip in (laid, north, south, west, east)]
 
     sent = packed(record_values, record_cell, record_instrument, block_counts, lon_cells)
     received = lax.all_to_all(sent, ("lon", "lat"), split_axis=0, concat_axis=0, tiled=True)
@@ -300,11 +386,12 @@
     out = pl.pallas_call(
         functools.partial(block_kernel, plan),
         out_shape=jax.ShapeDtypeStruct((lat_cells * lon_cells * LEV, width), BF16),
-        in_specs=[pl.BlockSpec(memory_space=pltpu.SMEM)] + [vmem] * 20,
+        in_specs=[pl.BlockSpec(memory_space=pltpu.SMEM)] + [vmem] * 25,
         out_specs=vmem,
         scratch_shapes=[
             pltpu.VMEM((rows, LEV * PAD), BF16),
             pltpu.VMEM((cells, rows), BF16),
+            pltpu.VMEM((perm.shape[1], LEV * PAD), BF16),
             pltpu.VMEM((cells, LEV * PAD), F32),
         ],
         compiler_params=pltpu.CompilerParams(vmem_limit_bytes=40 * 2**20),
@@ -314,7 +401,8 @@
     )(
         pole,
         received,
-        prior,
+        *strips,
+        jnp.asarray(perm),
         jnp.asarray(find),
         jnp.asarray(pick),
         jnp.asarray(coef),

time: 54.9 us -> 48.3 us (0.88)
  the two profiles are of different devices: /device:TPU:0 before, /device:TPU:1 now
where the time goes in v2:
time: 48.3 us; the launch traced here: 47.8 us
  Pallas kernels  14.9 us (31%)
  starting transfers between devices  12.6 us (26%)
  local copies, waits for them, and re-layouts  10.7 us (22%)
  waiting for transfers between devices  9.12 us (19%)
    pallas_call x1, Pallas kernels, local(): pl.pallas_call(functools.partial(block_kernel, plan), out_shape=jax.Shape...  13.9 us
    ppermute x4, waiting for transfers between devices, shifted(): return lax.ppermute(value, axis, pairs)  9.11 us
    unnamed x47, local copies, waits for them, and re-layouts  7.86 us
    all_to_all x1, starting transfers between devices, local(): lax.all_to_all(sent, ('lon', 'lat'), split_axis=0, concat_axis=0, tiled=T...  7.1 us
    ppermute x4, starting transfers between devices, shifted(): return lax.ppermute(value, axis, pairs)  5.53 us
    reshape x2, local copies, waits for them, and re-layouts, local(): strip.reshape(-1, LEV * PAD)  1.01 us
  transfers between devices with their start and end apart: 5, of which 4 were waited for; matrix products, arithmetic and copies ran while one was open for 4% of the time, Pallas kernels for 0%

profile of v2, /device:TPU:1, one launch (start us, length us, event | category | flops | bytes accessed | tf_op | source)
XLA Modules:
  0.0 47.8 jit_solution(2072562514270578542)
XLA Ops:
  0.0 0.0 copy-start.2
  0.0 0.7 %copy-done.2 = s32[8,4,2]{0,2,1:T(2,128)S(1)} copy-done((s32[8,4,2]{0,2,1:T(2,128)S(1)}, s32[8,4,2]{0,2,1:T(2,128)}, u32[]{:S(2)}) %copy-start.2) | copy-done | bytes 280
  0.7 0.0 copy-start
  0.7 0.9 %copy-done = bf16[90,1024]{1,0:T(8,128)(2,1)S(1)} copy-done((bf16[90,1024]{1,0:T(8,128)(2,1)S(1)}, bf16[90,1024]{1,0:T(8,128)(2,1)}, u32[]{:S(2)}) %copy-start) | copy-done | bytes 184344
  1.6 0.0 copy-start.1
  1.6 0.7 %copy-done.1 = bf16[8,4,2,128]{3,2,1,0:T(2,128)(2,1)S(1)} copy-done((bf16[8,4,2,128]{3,2,1,0:T(2,128)(2,1)S(1)}, bf16[8,4,2,128]{3,2,1,0:T(2,128)(2,1)}, u32[]{:S(2)}) %copy-start.1) | copy-done | bytes 16408
  2.3 0.7 %copy-done.3 = s32[8,4,2]{0,2,1:T(2,128)S(1)} copy-done((s32[8,4,2]{0,2,1:T(2,128)S(1)}, s32[8,4,2]{0,2,1:T(2,128)}, u32[]{:S(2)}) %copy-start.3) | copy-done | bytes 280
  3.0 0.0 copy-start.4
  3.0 0.7 %copy-done.4 = s32[8,4]{0,1:T(4,128)S(1)} copy-done((s32[8,4]{0,1:T(4,128)S(1)}, s32[8,4]{0,1:T(4,128)}, u32[]{:S(2)}) %copy-start.4) | copy-done | bytes 152
  3.7 0.0 copy-start.19
  3.7 1.0 %shard_map.217 = bf16[8,4,10,2,128]{4,3,2,1,0:T(2,128)(2,1)} custom-call(bf16[8,4,2,128]{3,2,1,0:T(2,128)(2,1)S(1)} %copy-done.1, s32[8,8]{1,0:T(8,128)S(1)} %bitcast.23, s32[8,8]{1,0:T(8,128)S(1)} %bitcast.24, s32[4,8]{1,0:T(4,128)S(1)} %bitcast.25, bf16[90,1024]{1,0:T(8,128)(2,1)S(1)} %copy-done), custom_call_target="tpu_custom_call" | custom-call | tf_op jit(solution)/shard_map/pallas_call | solution.py:318
  4.7 7.1 %all-to-all-start = ((bf16[32,10,2,128]{3,2,1,0:T(2,128)(2,1)}), bf16[32,10,2,128]{3,2,1,0:T(2,128)(2,1)S(1)}, u32[]{:S(2)}, u32[]{:S(2)}) async-start(bf16[32,10,2,128]{3,2,1,0:T(2,128)(2,1)} %bitcast.7), calls=%async_computation | async-start | bytes 327680 | tf_op jit(solution)/shard_map/all_to_all | solution.py:371
  11.8 0.0 copy-done.19
  11.8 0.3 pad.12
  12.1 0.2 reshape.49
  12.3 0.0 copy-start.18
  12.3 3.3 %collective-permute-start.1 = (bf16[3,24,512]{2,1,0:T(8,128)(2,1)S(1)}, bf16[3,24,512]{2,1,0:T(8,128)(2,1)S(1)}, u32[]{:S(2)}, u32[]{:S(2)}) collective-permute-start(bf16[3,24,512]{2,1,0:T(8,128)(2,1)S(1)} %get-tuple-element.7), channel_id=1, source_target_pairs={{0,3},{1,0},{2,1},{3,2},{4,7},{5,4},{6,5},{7,6},{8,11},{9,8},{10,9... | collective-permute-start | bytes 221192 | tf_op jit(solution)/shard_map/ppermute | solution.py:32
  15.6 0.0 collective-permute-start
  15.6 0.0 copy-done.18
  15.6 0.1 fusion.3
  15.7 0.0 copy-start.20
  15.7 0.0 copy-start.21
  15.8 0.7 %copy-done.21 = bf16[192]{0:T(256)(128)(2,1)S(1)} copy-done((bf16[192]{0:T(256)(128)(2,1)S(1)}, bf16[192]{0:T(256)(128)(2,1)}, u32[]{:S(2)}) %copy-start.21) | copy-done | bytes 408
  16.4 0.0 copy-start.22
  16.4 0.6 %copy-done.22 = bf16[192]{0:T(256)(128)(2,1)S(1)} copy-done((bf16[192]{0:T(256)(128)(2,1)S(1)}, bf16[192]{0:T(256)(128)(2,1)}, u32[]{:S(2)}) %copy-start.22) | copy-done | bytes 408
  17.1 0.0 copy-done.20
  17.1 0.1 reshape.55
  17.2 0.2 pad.13
  17.4 0.0 copy-start.10
  17.5 0.3 collective-permute-done.1
  17.8 3.7 %collective-permute-done = bf16[3,24,512]{2,1,0:T(8,128)(2,1)S(1)} collective-permute-done((bf16[3,24,512]{2,1,0:T(8,128)(2,1)S(1)}, bf16[3,24,512]{2,1,0:T(8,128)(2,1)S(1)}, u32[]{:S(2)}, u32[]{:S(2)}) %collective-permute-start) | collective-permute-done | bytes 73760 | tf_op jit(solution)/shard_map/ppermute | solution.py:32
  21.5 0.0 copy-start.14
  21.5 0.0 copy-start.15
  21.6 2.2 %collective-permute-start.2 = (bf16[18,6,512]{2,1,0:T(8,128)(2,1)S(1)}, bf16[18,6,512]{2,1,0:T(8,128)(2,1)S(1)}, u32[]{:S(2)}, u32[]{:S(2)}) collective-permute-start(bf16[18,6,512]{2,1,0:T(8,128)(2,1)S(1)} %pad_maximum_fusion), channel_id=1, source_target_pairs={{0,4},{4,8},{8,12},{12,16},{16,20},{20,24},{24,28},{28,0},{1,5},{5... | collective-permute-start | bytes 331784 | tf_op jit(solution)/shard_map/ppermute | solution.py:32
  23.8 0.0 copy-start.6
  23.8 0.0 copy-start.5
  23.8 0.1 collective-permute-start.3
  23.9 0.1 fusion.pole_ref
  24.0 1.9 %collective-permute-done.2 = bf16[18,6,512]{2,1,0:T(8,128)(2,1)S(1)} collective-permute-done((bf16[18,6,512]{2,1,0:T(8,128)(2,1)S(1)}, bf16[18,6,512]{2,1,0:T(8,128)(2,1)S(1)}, u32[]{:S(2)}, u32[]{:S(2)}) %collective-permute-start.2) | collective-permute-done | bytes 110624 | tf_op jit(solution)/shard_map/ppermute | solution.py:32
  25.9 0.0 copy-start.7
  25.9 0.0 copy-start.8
  25.9 0.0 copy-start.13
  25.9 3.2 %collective-permute-done.3 = bf16[18,6,512]{2,1,0:T(8,128)(2,1)} collective-permute-done((bf16[18,6,512]{2,1,0:T(8,128)(2,1)S(1)}, bf16[18,6,512]{2,1,0:T(8,128)(2,1)}, u32[]{:S(2)}, u32[]{:S(2)}) %collective-permute-start.3) | collective-permute-done | bytes 110624 | tf_op jit(solution)/shard_map/ppermute | solution.py:32
  29.2 0.0 copy-start.16
  29.2 1.0 %reshape.54.east_ref = bf16[108,512]{1,0:T(8,128)(2,1)S(1)} reshape(bf16[18,6,512]{2,1,0:T(8,128)(2,1)} %collective-permute-done.3) | data formatting | bytes 221184 | tf_op jit(solution)/shard_map/reshape | solution.py:368
  30.1 0.0 all-to-all-done
  30.1 0.0 copy-start.9
  30.2 0.0 copy-start.17
  30.2 0.0 copy-done.10
  30.2 0.0 copy-done.14
  30.2 0.0 copy-done.15
  30.2 0.0 copy-done.6
  30.2 0.0 copy-done.5
  30.2 0.0 copy-done.7
  30.2 0.0 copy-done.8
  30.2 0.0 copy-done.13
  30.3 0.0 copy-done.16
  30.3 0.6 %copy-done.9 = bf16[8,192]{1,0:T(8,128)(2,1)S(1)} copy-done((bf16[8,192]{1,0:T(8,128)(2,1)S(1)}, bf16[8,192]{1,0:T(8,128)(2,1)}, u32[]{:S(2)}) %copy-start.9) | copy-done | bytes 3096
  30.8 0.0 copy-done.17
  30.9 0.0 copy-start.11
  30.9 1.2 %copy-done.11 = bf16[576,656]{1,0:T(8,128)(2,1)S(1)} copy-done((bf16[576,656]{1,0:T(8,128)(2,1)S(1)}, bf16[576,656]{1,0:T(8,128)(2,1)}, u32[]{:S(2)}) %copy-start.11) | copy-done | bytes 755736
  32.0 1.0 %copy-done.12 = f32[648,1]{1,0:T(8,128)S(1)} copy-done((f32[648,1]{1,0:T(8,128)S(1)}, f32[648,1]{1,0:T(8,128)}, u32[]{:S(2)}) %copy-start.12) | copy-done | bytes 2616
  33.0 13.9 %shard_map.218 = bf16[576,192]{1,0:T(8,128)(2,1)S(1)} custom-call(s32[2]{0:T(128)S(1)} %fusion.pole_ref, bf16[640,128]{1,0:T(8,128)(2,1)S(1)} %bitcast.20, bf16[288,512]{1,0:T(8,128)(2,1)S(1)} %bitcast.18, bf16[72,512]{1,0:T(8,128)(2,1)S(1)} %bitcast.22, bf16[72,512]{1,0:T(8,128)(2,1)S(1)} %bitcast.21, bf16[108,512]{1,0:T(8,128)(2,1)S(1)} %reshape.53.west_ref, ...), custom_call_target="tpu_custom_call" | custom-call | flops 4000000000 | bytes 6000000 | tf_op jit(solution)/shard_map/pallas_call | solution.py:386
  46.9 0.9 %reshape.59 = bf16[12,24,2,192]{3,2,1,0:T(2,128)(2,1)} reshape(bf16[576,192]{1,0:T(8,128)(2,1)S(1)} %shard_map.218) | data formatting | bytes 442368 | tf_op jit(solution)/shard_map/reshape | solution.py:425
  (13 shorter events, 0.2 us)
Async XLA Ops:
  0.0 0.7 %copy-start.2 = (s32[8,4,2]{0,2,1:T(2,128)S(1)}, s32[8,4,2]{0,2,1:T(2,128)}, u32[]{:S(2)}) copy-start(s32[8,4,2]{0,2,1:T(2,128)} %param.24) | copy-start | bytes 772
  0.7 0.9 %copy-start = (bf16[90,1024]{1,0:T(8,128)(2,1)S(1)}, bf16[90,1024]{1,0:T(8,128)(2,1)}, u32[]{:S(2)}) copy-start(bf16[90,1024]{1,0:T(8,128)(2,1)} %constant.31.clone.spread_ref) | copy-start | bytes 552964
  1.6 0.7 %copy-start.1 = (bf16[8,4,2,128]{3,2,1,0:T(2,128)(2,1)S(1)}, bf16[8,4,2,128]{3,2,1,0:T(2,128)(2,1)}, u32[]{:S(2)}) copy-start(bf16[8,4,2,128]{3,2,1,0:T(2,128)(2,1)} %values_ref.1) | copy-start | bytes 49156
  2.3 0.7 %copy-start.3 = (s32[8,4,2]{0,2,1:T(2,128)S(1)}, s32[8,4,2]{0,2,1:T(2,128)}, u32[]{:S(2)}) copy-start(s32[8,4,2]{0,2,1:T(2,128)} %param.25) | copy-start | bytes 772
  3.0 0.7 %copy-start.4 = (s32[8,4]{0,1:T(4,128)S(1)}, s32[8,4]{0,1:T(4,128)}, u32[]{:S(2)}) copy-start(s32[8,4]{0,1:T(4,128)} %param.26) | copy-start | bytes 388
  3.7 8.1 %copy-start.19 = (bf16[12,24,2,192]{3,2,1,0:T(2,128)(2,1)S(1)}, bf16[12,24,2,192]{3,2,1,0:T(2,128)(2,1)}, u32[]{:S(2)}) copy-start(bf16[12,24,2,192]{3,2,1,0:T(2,128)(2,1)} %param.27) | copy-start | bytes 663556
  4.7 25.5 %all-to-all-start = ((bf16[32,10,2,128]{3,2,1,0:T(2,128)(2,1)}), bf16[32,10,2,128]{3,2,1,0:T(2,128)(2,1)S(1)}, u32[]{:S(2)}, u32[]{:S(2)}) async-start(bf16[32,10,2,128]{3,2,1,0:T(2,128)(2,1)} %bitcast.7), calls=%async_computation | async-start | bytes 327680 | tf_op jit(solution)/shard_map/all_to_all | solution.py:371
  12.3 3.3 %copy-start.18 = (bf16[192,576]{1,0:T(8,128)(2,1)S(1)}, bf16[192,576]{1,0:T(8,128)(2,1)}, u32[]{:S(2)}) copy-start(bf16[192,576]{1,0:T(8,128)(2,1)} %param.32) | copy-start | bytes 663556
  12.3 5.5 %collective-permute-start.1 = (bf16[3,24,512]{2,1,0:T(8,128)(2,1)S(1)}, bf16[3,24,512]{2,1,0:T(8,128)(2,1)S(1)}, u32[]{:S(2)}, u32[]{:S(2)}) collective-permute-start(bf16[3,24,512]{2,1,0:T(8,128)(2,1)S(1)} %get-tuple-element.7), channel_id=1, source_target_pairs={{0,3},{1,0},{2,1},{3,2},{4,7},{5,4},{6,5},{7,6},{8,11},{9,8},{10,9... | collective-permute-start | bytes 221192 | tf_op jit(solution)/shard_map/ppermute | solution.py:32
  15.6 5.9 %collective-permute-start = (bf16[3,24,512]{2,1,0:T(8,128)(2,1)S(1)}, bf16[3,24,512]{2,1,0:T(8,128)(2,1)S(1)}, u32[]{:S(2)}, u32[]{:S(2)}) collective-permute-start(bf16[3,24,512]{2,1,0:T(8,128)(2,1)S(1)} %get-tuple-element.8), channel_id=1, source_target_pairs={{0,1},{1,2},{2,3},{3,0},{4,5},{5,6},{6,7},{7,4},{8,9},{9,10},{10,1... | collective-permute-start | bytes 221192 | tf_op jit(solution)/shard_map/ppermute | solution.py:32
  15.7 1.4 %copy-start.20 = (bf16[192,384]{1,0:T(8,128)(2,1)S(1)}, bf16[192,384]{1,0:T(8,128)(2,1)}, u32[]{:S(2)}) copy-start(bf16[192,384]{1,0:T(8,128)(2,1)} %param.30) | copy-start | bytes 442372
  15.7 0.7 %copy-start.21 = (bf16[192]{0:T(256)(128)(2,1)S(1)}, bf16[192]{0:T(256)(128)(2,1)}, u32[]{:S(2)}) copy-start(bf16[192]{0:T(256)(128)(2,1)} %param.31) | copy-start | bytes 1156
  16.4 0.7 %copy-start.22 = (bf16[192]{0:T(256)(128)(2,1)S(1)}, bf16[192]{0:T(256)(128)(2,1)}, u32[]{:S(2)}) copy-start(bf16[192]{0:T(256)(128)(2,1)} %param.34) | copy-start | bytes 1156
  17.4 12.7 %copy-start.10 = (bf16[648,672]{1,0:T(8,128)(2,1)S(1)}, bf16[648,672]{1,0:T(8,128)(2,1)}, u32[]{:S(2)}) copy-start(bf16[648,672]{1,0:T(8,128)(2,1)} %constant.32.clone.perm_ref) | copy-start | bytes 2612740
  21.5 8.7 %copy-start.14 = (bf16[160,128]{1,0:T(8,128)(2,1)S(1)}, bf16[160,128]{1,0:T(8,128)(2,1)}, u32[]{:S(2)}) copy-start(bf16[160,128]{1,0:T(8,128)(2,1)} %constant.34.clone.pick_ref) | copy-start | bytes 122884
  21.5 8.7 %copy-start.15 = (bf16[136,128]{1,0:T(8,128)(2,1)S(1)}, bf16[136,128]{1,0:T(8,128)(2,1)}, u32[]{:S(2)}) copy-start(bf16[136,128]{1,0:T(8,128)(2,1)} %constant.35.clone.coef_ref) | copy-start | bytes 104452
  21.6 4.3 %collective-permute-start.2 = (bf16[18,6,512]{2,1,0:T(8,128)(2,1)S(1)}, bf16[18,6,512]{2,1,0:T(8,128)(2,1)S(1)}, u32[]{:S(2)}, u32[]{:S(2)}) collective-permute-start(bf16[18,6,512]{2,1,0:T(8,128)(2,1)S(1)} %pad_maximum_fusion), channel_id=1, source_target_pairs={{0,4},{4,8},{8,12},{12,16},{16,20},{20,24},{24,28},{28,0},{1,5},{5... | collective-permute-start | bytes 331784 | tf_op jit(solution)/shard_map/ppermute | solution.py:32
  23.8 6.4 %copy-start.6 = (bf16[768,192]{0,1:T(8,128)(2,1)S(1)}, bf16[768,192]{0,1:T(8,128)(2,1)}, u32[]{:S(2)}) copy-start(bf16[768,192]{0,1:T(8,128)(2,1)} %param.36) | copy-start | bytes 884740
  23.8 6.4 %copy-start.5 = (bf16[192,768]{1,0:T(8,128)(2,1)S(1)}, bf16[192,768]{1,0:T(8,128)(2,1)}, u32[]{:S(2)}) copy-start(bf16[192,768]{1,0:T(8,128)(2,1)} %wu_ref.1) | copy-start | bytes 884740
  23.8 5.4 %collective-permute-start.3 = (bf16[18,6,512]{2,1,0:T(8,128)(2,1)S(1)}, bf16[18,6,512]{2,1,0:T(8,128)(2,1)}, u32[]{:S(2)}, u32[]{:S(2)}) collective-permute-start(bf16[18,6,512]{2,1,0:T(8,128)(2,1)S(1)} %pad_maximum_fusion.1), channel_id=1, source_target_pairs={{0,28},{4,0},{8,4},{12,8},{16,12},{20,16},{24,20},{28,24},{1,29},{... | collective-permute-start | bytes 331784 | tf_op jit(solution)/shard_map/ppermute | solution.py:32
  25.9 4.3 %copy-start.7 = (bf16[192,192]{1,0:T(8,128)(2,1)S(1)}, bf16[192,192]{1,0:T(8,128)(2,1)}, u32[]{:S(2)}) copy-start(bf16[192,192]{1,0:T(8,128)(2,1)} %wm_ref.1) | copy-start | bytes 221188
  25.9 4.3 %copy-start.8 = (bf16[128,192]{0,1:T(8,128)(2,1)S(1)}, bf16[128,192]{0,1:T(8,128)(2,1)}, u32[]{:S(2)}) copy-start(bf16[128,192]{0,1:T(8,128)(2,1)} %param.28) | copy-start | bytes 147460
  25.9 4.3 %copy-start.13 = (bf16[160,160]{1,0:T(8,128)(2,1)S(1)}, bf16[160,160]{1,0:T(8,128)(2,1)}, u32[]{:S(2)}) copy-start(bf16[160,160]{1,0:T(8,128)(2,1)} %constant.33.clone.find_ref) | copy-start | bytes 153604
  29.2 1.1 %copy-start.16 = (f32[16,144]{1,0:T(8,128)S(1)}, f32[16,144]{1,0:T(8,128)}, u32[]{:S(2)}) copy-start(f32[16,144]{1,0:T(8,128)} %constant.38.clone.keep_ref) | copy-start | bytes 27652
  30.1 0.7 %copy-start.9 = (bf16[8,192]{1,0:T(8,128)(2,1)S(1)}, bf16[8,192]{1,0:T(8,128)(2,1)}, u32[]{:S(2)}) copy-start(bf16[8,192]{1,0:T(8,128)(2,1)} %tab_ref.1) | copy-start | bytes 9220
  30.2 0.7 %copy-start.17 = (f32[1,640]{1,0:T(1,128)S(1)}, f32[1,640]{1,0:T(1,128)}, u32[]{:S(2)}) copy-start(f32[1,640]{1,0:T(1,128)} %constant.36.clone.place_ref) | copy-start | bytes 7684
  30.9 1.2 %copy-start.11 = (bf16[576,656]{1,0:T(8,128)(2,1)S(1)}, bf16[576,656]{1,0:T(8,128)(2,1)}, u32[]{:S(2)}) copy-start(bf16[576,656]{1,0:T(8,128)(2,1)} %constant.39.clone.sel_ref) | copy-start | bytes 2267140
  32.0 1.0 %copy-start.12 = (f32[648,1]{1,0:T(8,128)S(1)}, f32[648,1]{1,0:T(8,128)}, u32[]{:S(2)}) copy-start(f32[648,1]{1,0:T(8,128)} %constant.37.clone.code_ref) | copy-start | bytes 7780

commit v3 on v2

--- a/solution.py
+++ b/solution.py
@@ -20,15 +20,19 @@
 FIELDS = 4
 GROUP = 8
 CHUNK = 32
+LIMIT = 56 * 2**20
+FEW = 32
 BF16 = jnp.bfloat16
 F32 = jnp.float32
 
 AROUND = [(dy, dx) for dy in (-1, 0, 1) for dx in (-1, 0, 1)]
 
 
-def shifted(value, axis, steps):
+def shifted(value, axis, steps, wraps=True):
     count = lax.axis_size(axis)
     pairs = [(source, (source + steps) % count) for source in range(count)]
+    if not wraps:
+        pairs = [pair for pair in pairs if pair[1] == pair[0] + steps]
     return lax.ppermute(value, axis, pairs)
 
 
@@ -67,91 +71,144 @@
     return lax.dot_general(a, b, (((1,), (1,)), ((), ())), preferred_element_type=F32)
 
 
-def block_kernel(
-    plan,
-    pole_ref,
-    recv_ref,
-    own_ref,
-    north_ref,
-    south_ref,
-    west_ref,
-    east_ref,
-    perm_ref,
-    find_ref,
-    pick_ref,
-    coef_ref,
-    place_ref,
-    code_ref,
-    keep_ref,
-    sel_ref,
-    win_ref,
-    tab_ref,
-    lift_ref,
-    g1_ref,
-    wq_ref,
-    wk_ref,
-    wv_ref,
-    wm_ref,
-    g2_ref,
-    wu_ref,
-    wd_ref,
-    out_ref,
-    lifted_ref,
-    hot_ref,
-    prior_ref,
-    sum_ref,
-):
-    width = win_ref.shape[0]
-    stride = find_ref.shape[0]
+def put_ones(lifted, width):
+    lanes = lax.broadcasted_iota(jnp.int32, lifted.shape, 1) % PAD
+    return jnp.where(lanes >= width, 1.0, lifted).astype(BF16)
+
+
+def sums_gathered(scalars_ref, all_ref, take, work):
+    tiles_ref, meta_ref, hot_ref, lifted_ref, sem = work
+    sources, tiles = all_ref.shape[0], all_ref.shape[1] - 1
+    per_tile = sources * all_ref.shape[2]
+    copies = [pltpu.make_async_copy(all_ref.at[:, tiles], meta_ref, sem.at[0])]
+    for n in range(len(AROUND)):
+        source = all_ref.at[:, scalars_ref[2 + n]]
+        copies.append(pltpu.make_async_copy(source, tiles_ref.at[n], sem.at[1 + n]))
+    for copy in copies:
+        copy.start()
+
+    def finish(place):
+        copies[0].wait()
+        meta = meta_ref.reshape(per_tile, 128)[...]
+        lane = lax.broadcasted_iota(jnp.int32, (16, 128), 1)
+        sub = lax.broadcasted_iota(jnp.int32, (16, 128), 0)
+        wanted = jnp.zeros((16, 128), F32)
+        lane_two = lax.broadcasted_iota(jnp.int32, (128, 128), 1)
+        sub_two = lax.broadcasted_iota(jnp.int32, (128, 128), 0)
+        tag_at = jnp.full((128, 128), -1, jnp.int32)
+        for n in range(len(AROUND)):
+            at = scalars_ref[2 + len(AROUND) + n]
+            wanted = jnp.where((sub == n) & (lane == at), 64.0, wanted)
+            wanted = jnp.where((sub == n) & (lane == tiles + at), 1.0, wanted)
+            tag_at = jnp.where(lane_two // INSTR == n, 2 * tiles + at, tag_at)
+        codes = dot_nt(wanted.astype(BF16), meta)
+        code_row = jnp.concatenate([codes[n : n + 1] + place[n] for n in range(len(AROUND))], axis=1)
+        tag = dot(meta, jnp.where(tag_at == sub_two, 1.0, 0.0).astype(BF16))
+        lane = lax.broadcasted_iota(jnp.int32, tag.shape, 1)
+        chosen = jnp.where(tag == (lane % INSTR).astype(F32), 1.0, 0.0)
+        hot_ref[...] = jnp.where(take("code")[...] == code_row, 1.0, 0.0).astype(BF16)
+        weight, lift = take("first")[...], take("lift")[...]
+        width = weight.shape[1]
+        for group in range(0, len(AROUND), 3):
+            rows = []
+            for n in range(group, group + 3):
+                copies[1 + n].wait()
+                records = tiles_ref.at[n].reshape(per_tile, 128)[...]
+                own = jnp.where(lane // INSTR == n, chosen, 0.0).astype(BF16)
+                rows.append(jnp.concatenate([records, own], axis=1))
+            encoded = gelu(dot(jnp.concatenate(rows, axis=0), weight)).astype(BF16)
+            lifted = put_ones(gelu(dot(encoded, lift)), width)
+            lifted_ref[group * per_tile : (group + 3) * per_tile, :] = lifted
+        return dot(hot_ref[...], lifted_ref[...])
+
+    return finish
+
+
+def sums_exchanged(recv_ref, take, work):
+    hot_ref, lifted_ref, total_ref = work
     per_chunk = lifted_ref.shape[0]
     chunks = recv_ref.shape[0] // per_chunk
+
+    def finish(_):
+        find, pick, coef = take("find")[...], take("pick")[...], take("coef")
+        win, tab, lift, place = take("win")[...], take("tab")[...], take("lift")[...], take("place")
+        code_column = take("code")[...]
+        stride = find.shape[0]
+
+        def scatter(base):
+            for at in range(0, per_chunk, stride):
+                recs = recv_ref[pl.ds(base + at, stride), :]
+                meta = (dot(find, recs) * pick.astype(F32)).astype(BF16)
+                lane = lax.broadcasted_iota(jnp.int32, (stride, 128), 1).astype(F32)
+                tag = dot(meta, coef[8:, :])
+                chooser = jnp.where(tag == lane, 1.0, 0.0).astype(BF16)
+                before = dot_nt(recs, win) + dot(chooser[:, :INSTR], tab)
+                encoded = gelu(before).astype(BF16)
+                lifted_ref[at : at + stride, :] = put_ones(gelu(dot(encoded, lift)), win.shape[0])
+                code = dot_nt(coef[:8, :], meta)[:1, :] + place[:, at : at + stride]
+                hot_ref[:, at : at + stride] = jnp.where(code_column == code, 1.0, 0.0).astype(BF16)
+            return dot(hot_ref[...], lifted_ref[...])
+
+        total_ref[...] = scatter(0)
+
+        @pl.loop(1, chunks)
+        def _(step):
+            total_ref[...] += scatter(pl.multiple_of(step * per_chunk, per_chunk))
+
+        return total_ref[...]
+
+    return finish
+
+
+def block_kernel(plan, names, gathers, place, *refs):
+    refs = list(refs)
+    scalars_ref, records_ref, *strips = refs[:7]
+    kept = dict(zip(names, refs[7 : 7 + len(names)]))
+    out_ref, prior_ref, load_sem = refs[7 + len(names) : 10 + len(names)]
+    held = dict(zip(names, refs[10 + len(names) : 10 + 2 * len(names)]))
+    work = refs[10 + 2 * len(names) :]
+    loads = {
+        name: pltpu.make_async_copy(kept[name], held[name], load_sem.at[n])
+        for n, name in enumerate(names)
+    }
+    waiting = set(names)
+
+    def take(name):
+        if name in waiting:
+            loads[name].wait()
+            waiting.remove(name)
+        return held[name]
+
+    if gathers:
+        finish = sums_gathered(scalars_ref, records_ref, take, work)
+    else:
+        finish = sums_exchanged(records_ref, take, work)
+    for name in names:
+        loads[name].start()
+
     in_window = WLAT * WLON
-
     start = 0
-    for strip in (own_ref, north_ref, south_ref, west_ref, east_ref):
+    for strip in strips:
         count = strip.shape[0]
-        held = -(-count // 16) * 16
+        full = -(-count // 16) * 16
         value = strip[...].astype(F32)
-        if held > count:
-            value = jnp.concatenate([value, jnp.zeros((held - count, value.shape[1]), F32)], axis=0)
-        prior_ref[start : start + held, :] = value.astype(BF16)
-        start += held
-    prior = dot(perm_ref[...], prior_ref[...])
-
-    def scatter(base):
-        for group in range(per_chunk // stride):
-            at = group * stride
-            recs = recv_ref[pl.ds(base + at, stride), :]
-            meta = (dot(find_ref[...], recs) * pick_ref[...].astype(F32)).astype(BF16)
-            lane = lax.broadcasted_iota(jnp.int32, (stride, 128), 1).astype(F32)
-            tag = dot(meta, coef_ref[8:, :])
-            chooser = jnp.where(tag == lane, 1.0, 0.0).astype(BF16)
-            before = dot_nt(recs, win_ref[...]) + dot(chooser[:, :INSTR], tab_ref[...])
-            encoded = gelu(before).astype(BF16)
-            lifted = gelu(dot(encoded, lift_ref[...]))
-            lanes = lax.broadcasted_iota(jnp.int32, lifted.shape, 1) % PAD
-            lifted_ref[at : at + stride, :] = jnp.where(lanes >= width, 1.0, lifted).astype(BF16)
-            code = dot_nt(coef_ref[:8, :], meta)[:1, :] + place_ref[:, at : at + stride]
-            hot_ref[:, at : at + stride] = jnp.where(code_ref[...] == code, 1.0, 0.0).astype(BF16)
-        return dot(hot_ref[...], lifted_ref[...])
-
-    if chunks == 1:
-        sum_ref[...] = prior + scatter(0)
-    else:
-        sum_ref[...] = prior
-
-        @pl.loop(0, chunks)
-        def _(step):
-            sum_ref[...] += scatter(pl.multiple_of(step * per_chunk, per_chunk))
-
-    gain_one = g1_ref[...].astype(F32)
+        if full > count:
+            value = jnp.concatenate([value, jnp.zeros((full - count, value.shape[1]), F32)], axis=0)
+        prior_ref[start : start + full, :] = value.astype(BF16)
+        start += full
+    sums = finish(place)
+    prior = dot(take("perm")[...], prior_ref[...])
+
+    width = held["wm"].shape[0]
+    gains = take("gains")[...]
     latents, normeds = [], []
     for level in range(LEV):
-        piece = sum_ref[:, level * PAD : (level + 1) * PAD]
+        piece = sums[:, level * PAD : (level + 1) * PAD]
         share = 1.0 / (1.0 + piece[:, width : width + 1])
-        latent = (piece[:, :width] * share).astype(BF16).astype(F32)
+        latent = (prior[:, level * PAD : (level + 1) * PAD] + piece)[:, :width] * share
+        latent = latent.astype(BF16).astype(F32)
         latents.append(latent)
-        normeds.append(normalise(latent, gain_one))
+        normeds.append(normalise(latent, gains[:1]))
 
     def gathered(tensors, counts):
         return jnp.concatenate(
@@ -162,15 +219,14 @@
     all_n = gathered(normeds, [in_window] * len(plan)).astype(BF16)
     own_n = gathered(normeds, plan).astype(BF16)
     own_latent = gathered(latents, plan)
-    keys = dot(all_n, wk_ref[...]).astype(BF16)
-    values = dot(all_n, wv_ref[...])
-    lanes = lax.broadcasted_iota(jnp.int32, values.shape, 1)
-    values = jnp.where(lanes >= width, 1.0, values).astype(BF16)
+    keys = dot(all_n, take("wk")[...]).astype(BF16)
+    values = put_ones(dot(all_n, take("wv")[...]), width)
     head = width // HEADS
-    query = (dot(own_n, wq_ref[...]) * head ** (-0.5)).astype(BF16)
+    query = (dot(own_n, take("wq")[...]) * head ** (-0.5)).astype(BF16)
 
     head_of = lax.broadcasted_iota(jnp.int32, (1, width), 1) // head
     tokens = LEV * in_window
+    keep = take("keep")[...]
     mixed, start = [], 0
     for w, count in enumerate(plan):
         rows = LEV * count
@@ -182,8 +238,8 @@
         scores = dot_nt(stacked, keys[w * tokens : (w + 1) * tokens])
         side = w // 3
         if side != 1:
-            kept = keep_ref[w : w + 1, :] > pole_ref[side // 2].astype(F32)
-            scores = jnp.where(kept, scores, -1e30)
+            allowed = keep[w : w + 1, :] > scalars_ref[side // 2].astype(F32)
+            scores = jnp.where(allowed, scores, -1e30)
         largest = jnp.max(scores, axis=-1, keepdims=True)
         raised = jnp.exp(scores - largest).astype(BF16)
         product = dot(raised, values[w * tokens : (w + 1) * tokens])
@@ -194,11 +250,11 @@
         mixed.append(total.astype(BF16))
     mixed = jnp.concatenate(mixed, axis=0)
 
-    after = (own_latent + dot(mixed, wm_ref[...])).astype(BF16).astype(F32)
-    normed_two = normalise(after, g2_ref[...].astype(F32)).astype(BF16)
-    hidden = gelu(dot(normed_two, wu_ref[...])).astype(BF16)
-    result = (after + dot_nt(hidden, wd_ref[...])).astype(BF16)
-    out_ref[...] = dot(sel_ref[...], result).astype(BF16)
+    after = (own_latent + dot(mixed, take("wm")[...])).astype(BF16).astype(F32)
+    normed_two = normalise(after, gains[1:2]).astype(BF16)
+    hidden = gelu(dot(normed_two, take("wu")[...])).astype(BF16)
+    result = (after + dot_nt(hidden, take("wd")[...])).astype(BF16)
+    out_ref[...] = dot(take("sel")[...], result).astype(BF16)
 
 
 def constants(lat_cells, lon_cells, capacity, sources):
@@ -305,6 +361,63 @@
                 out_ref[begin + lon, lat, len(AROUND)] = piece[lat * capacity : (lat + 1) * capacity]
 
 
+def shard_kernel(values_ref, cell_ref, tag_ref, count_ref, out_ref, cells, tags, held, sem, *, lon_cells):
+    tiles, capacity, _ = values_ref.shape
+    copies = [
+        pltpu.make_async_copy(values_ref, out_ref.at[pl.ds(0, tiles)], sem.at[0]),
+        pltpu.make_async_copy(cell_ref, cells, sem.at[1]),
+        pltpu.make_async_copy(tag_ref, tags, sem.at[2]),
+        pltpu.make_async_copy(count_ref, held, sem.at[3]),
+    ]
+    for copy in copies:
+        copy.start()
+    for copy in copies[1:]:
+        copy.wait()
+    tiles_lat = held.shape[0]
+    counts = jnp.concatenate(
+        [held[tile : tile + 1, :] for tile in range(tiles_lat) for _ in range(capacity)], axis=0
+    )
+    cell = cells[...]
+    slot = lax.broadcasted_iota(jnp.int32, cell.shape, 0) % capacity
+    row = cell // lon_cells
+    fields = [jnp.where(slot < counts, row, 255), cell - row * lon_cells, tags[...]]
+    parts = [
+        field[tile * capacity : (tile + 1) * capacity].astype(F32)
+        for field in fields
+        for tile in range(tiles_lat)
+    ]
+    used = len(fields) * tiles
+    if used < 128:
+        parts.append(jnp.zeros((capacity, 128 - used), F32))
+    out_ref[tiles] = jnp.concatenate(parts, axis=1).astype(BF16)
+    copies[0].wait()
+
+
+def shard(record_values, record_cell, record_instrument, block_counts, lon_cells):
+    tiles_lon, tiles_lat, capacity, wide = record_values.shape
+    tiles = tiles_lon * tiles_lat
+    anywhere = pl.BlockSpec(memory_space=pl.ANY)
+    ints = pltpu.VMEM((tiles_lat * capacity, tiles_lon), jnp.int32)
+    return pl.pallas_call(
+        functools.partial(shard_kernel, lon_cells=lon_cells),
+        out_shape=jax.ShapeDtypeStruct((tiles + 1, capacity, wide), BF16),
+        in_specs=[anywhere] * 4,
+        out_specs=pl.BlockSpec(memory_space=pltpu.VMEM),
+        scratch_shapes=[
+            ints,
+            ints,
+            pltpu.VMEM((tiles_lat, tiles_lon), jnp.int32),
+            pltpu.SemaphoreType.DMA((4,)),
+        ],
+        compiler_params=pltpu.CompilerParams(vmem_limit_bytes=LIMIT),
+    )(
+        record_values.reshape(tiles, capacity, wide),
+        record_cell.transpose(1, 2, 0).reshape(-1, tiles_lon),
+        record_instrument.transpose(1, 2, 0).reshape(-1, tiles_lon),
+        block_counts.T,
+    )
+
+
 def packed(record_values, record_cell, record_instrument, block_counts, lon_cells):
     tiles_lon, tiles_lat, capacity, wide = record_values.shape
     block = 8
@@ -350,15 +463,30 @@
     lat_cells, lon_cells, _, width = background.shape
     capacity = record_values.shape[2]
     sources = record_values.shape[0] * record_values.shape[1]
+    tiles_lon, tiles_lat = record_values.shape[:2]
+    gathers = sources <= FEW
     chunk = min(CHUNK, sources)
     plan, code, perm, keep, sel, find, pick, coef, place = constants(
         lat_cells, lon_cells, capacity, chunk
     )
 
+    if gathers:
+        mine = shard(record_values, record_cell, record_instrument, block_counts, lon_cells)
+        records = lax.all_gather(mine, ("lon", "lat"), axis=0, tiled=True)
+        records = records.reshape((sources,) + mine.shape)
+        grown = jnp.tile(instrument_table, (128 // INSTR, 1))
+        special = {"code": code, "first": jnp.concatenate([input_weight, grown], axis=0)}
+    else:
+        sent = packed(record_values, record_cell, record_instrument, block_counts, lon_cells)
+        records = lax.all_to_all(sent, ("lon", "lat"), split_axis=0, concat_axis=0, tiled=True)
+        records = records.reshape(-1, records.shape[-1])
+        special = {"find": find, "pick": pick, "coef": coef, "place": place, "code": code}
+        special.update(win=input_weight.T, tab=instrument_table)
+
     laid = jnp.pad(background, ((0, 0), (0, 0), (0, 0), (0, PAD - width)))
     laid = lax.optimization_barrier(laid.reshape(lat_cells, lon_cells, LEV * PAD))
-    north = shifted(laid[lat_cells - HLAT :], "lat", 1)
-    south = shifted(laid[:HLAT], "lat", -1)
+    north = shifted(laid[lat_cells - HLAT :], "lat", 1, wraps=False)
+    south = shifted(laid[:HLAT], "lat", -1, wraps=False)
 
     def columns(low, end):
         return jnp.concatenate([north[:, low:end], laid[:, low:end], south[:, low:end]], axis=0)
@@ -367,61 +495,71 @@
     east = shifted(columns(0, HLON), "lon", -1)
     strips = [strip.reshape(-1, LEV * PAD) for strip in (laid, north, south, west, east)]
 
-    sent = packed(record_values, record_cell, record_instrument, block_counts, lon_cells)
-    received = lax.all_to_all(sent, ("lon", "lat"), split_axis=0, concat_axis=0, tiled=True)
-    received = received.reshape(-1, received.shape[-1])
-
     lift = jnp.pad(
         lift_weight.reshape(width, LEV, width), ((0, 0), (0, 0), (0, PAD - width))
     ).reshape(width, LEV * PAD)
-    values_weight = jnp.pad(attn_weight[:, 2 * width :], ((0, 0), (0, PAD - width)))
-    where = lax.axis_index("lat")
-    last = lax.axis_size("lat") - 1
-    pole = jnp.stack([where == 0, where == last]).astype(jnp.int32)
-    pole = pole - 1
+    gains = jnp.pad(jnp.stack([first_gain, second_gain]).astype(F32), ((0, 6), (0, 0)))
+    loaded = special | {
+        "lift": lift,
+        "perm": perm,
+        "gains": gains,
+        "wk": attn_weight[:, width : 2 * width],
+        "wv": jnp.pad(attn_weight[:, 2 * width :], ((0, 0), (0, PAD - width))),
+        "wq": attn_weight[:, :width],
+        "keep": keep,
+        "wm": mix_weight,
+        "wu": up_weight,
+        "wd": down_weight.T,
+        "sel": sel,
+    }
+    loaded = {name: jnp.asarray(value) for name, value in loaded.items()}
+
+    lon, lat = lax.axis_index("lon"), lax.axis_index("lat")
+    scalars = [(lat == 0).astype(jnp.int32) - 1, (lat == tiles_lat - 1).astype(jnp.int32) - 1]
+    near = [((lon + dx) % tiles_lon, (lat + dy) % tiles_lat) for dy, dx in AROUND]
+    scalars += [x * tiles_lat + y for x, y in near] + [y * tiles_lon + x for x, y in near]
 
     cells = len(code)
-    rows = chunk * (len(AROUND) + 1) * capacity
     vmem = pl.BlockSpec(memory_space=pltpu.VMEM)
+    anywhere = pl.BlockSpec(memory_space=pl.ANY)
+    if gathers:
+        rows = sources * len(AROUND) * capacity
+        work = [
+            pltpu.VMEM((len(AROUND), sources, capacity, 128), BF16),
+            pltpu.VMEM((sources, capacity, 128), BF16),
+            pltpu.VMEM((cells, rows), BF16),
+            pltpu.VMEM((rows, LEV * PAD), BF16),
+            pltpu.SemaphoreType.DMA((1 + len(AROUND),)),
+        ]
+    else:
+        rows = chunk * (len(AROUND) + 1) * capacity
+        work = [
+            pltpu.VMEM((cells, rows), BF16),
+            pltpu.VMEM((rows, LEV * PAD), BF16),
+            pltpu.VMEM((cells, LEV * PAD), F32),
+        ]
+    starts = [
+        float((dy * lat_cells + HLAT) * 64 + dx * lon_cells + HLON) for dy, dx in AROUND
+    ]
     out = pl.pallas_call(
-        functools.partial(block_kernel, plan),
+        functools.partial(block_kernel, plan, list(loaded), gathers, starts),
         out_shape=jax.ShapeDtypeStruct((lat_cells * lon_cells * LEV, width), BF16),
-        in_specs=[pl.BlockSpec(memory_space=pltpu.SMEM)] + [vmem] * 25,
+        in_specs=[pl.BlockSpec(memory_space=pltpu.SMEM)]
+        + [anywhere if gathers else vmem]
+        + [vmem] * len(strips)
+        + [anywhere] * len(loaded),
         out_specs=vmem,
         scratch_shapes=[
-            pltpu.VMEM((rows, LEV * PAD), BF16),
-            pltpu.VMEM((cells, rows), BF16),
             pltpu.VMEM((perm.shape[1], LEV * PAD), BF16),
-            pltpu.VMEM((cells, LEV * PAD), F32),
+            pltpu.SemaphoreType.DMA((len(loaded),)),
+            *[pltpu.VMEM(value.shape, value.dtype) for value in loaded.values()],
+            *work,
         ],
-        compiler_params=pltpu.CompilerParams(vmem_limit_bytes=40 * 2**20),
+        compiler_params=pltpu.CompilerParams(vmem_limit_bytes=LIMIT),
         cost_estimate=pl.CostEstimate(
             flops=4 * 10**9, bytes_accessed=6 * 10**6, transcendentals=2 * 10**6
         ),
-    )(
-        pole,
-        received,
-        *strips,
-        jnp.asarray(perm),
-        jnp.asarray(find),
-        jnp.asarray(pick),
-        jnp.asarray(coef),
-        jnp.asarray(place),
-        jnp.asarray(code),
-        jnp.asarray(keep),
-        jnp.asarray(sel),
-        input_weight.T,
-        instrument_table,
-        lift,
-        first_gain.reshape(1, width),
-        attn_weight[:, :width],
-        attn_weight[:, width : 2 * width],
-        values_weight,
-        mix_weight,
-        second_gain.reshape(1, width),
-        up_weight,
-        down_weight.T,
-    )
+    )(jnp.stack(scalars), records, *strips, *loaded.values())
     return out.reshape(lat_cells, lon_cells, LEV, width)
 
 

time: 48.3 us -> 116 us (2.40)
  the two profiles are of different devices: /device:TPU:1 before, /device:TPU:0 now
where the time goes in v3:
time: 116 us; the launch traced here: 115 us
  blocking collectives  75.7 us (65%)
  Pallas kernels  16.8 us (14%)
  starting transfers between devices  9.59 us (8%)
  local copies, waits for them, and re-layouts  9.56 us (8%)
  waiting for transfers between devices  2.14 us (2%)
  other arithmetic  1.35 us (1%)
    all_gather x1, blocking collectives, local(): records = lax.all_gather(mine, ('lon', 'lat'), axis=0, tiled=True)  75.7 us
    pallas_call x1, Pallas kernels, local(): pl.pallas_call(functools.partial(block_kernel, plan, list(loaded), gather...  15.3 us
    ppermute x4, starting transfers between devices, shifted(): return lax.ppermute(value, axis, pairs)  9.59 us
    unnamed x20, local copies, waits for them, and re-layouts  2.47 us
  transfers between devices with their start and end apart: 4, of which 1 were waited for; matrix products, arithmetic and copies ran while one was open for 5% of the time, Pallas kernels for 1%

profile of v3, /device:TPU:0, one launch (start us, length us, event | category | flops | bytes accessed | tf_op | source)
XLA Modules:
  0.0 115.4 jit_solution(6134054408049407989)
XLA Ops:
  0.0 0.0 copy-start
  0.0 1.2 %pad.18 = bf16[12,24,2,256]{3,2,1,0:T(2,128)(2,1)S(1)} pad(bf16[12,24,2,192]{3,2,1,0:T(2,128)(2,1)} %param.22, bf16[]{:T(256)} %constant.91.clone.1), padding=0_0x0_0x0_0x0_64 | pad | bytes 516098 | tf_op jit(solution)/shard_map/jit(_pad)/pad | solution.py:486
  1.2 0.2 reshape.47
  1.4 0.0 copy-start.1
  1.5 1.3 %collective-permute-start.1 = (bf16[3,24,512]{2,1,0:T(8,128)(2,1)S(1)}, bf16[3,24,512]{2,1,0:T(8,128)(2,1)S(1)}, u32[]{:S(2)}, u32[]{:S(2)}) collective-permute-start(bf16[3,24,512]{2,1,0:T(8,128)(2,1)S(1)} %get-tuple-element.7), channel_id=1, source_target_pairs={{1,0},{2,1},{3,2},{5,4},{6,5},{7,6},{9,8},{10,9},{11,10},{13,12},{... | collective-permute-start | bytes 221192 | tf_op jit(solution)/shard_map/ppermute | solution.py:36
  2.8 5.6 %collective-permute-start = (bf16[3,24,512]{2,1,0:T(8,128)(2,1)S(1)}, bf16[3,24,512]{2,1,0:T(8,128)(2,1)S(1)}, u32[]{:S(2)}, u32[]{:S(2)}) collective-permute-start(bf16[3,24,512]{2,1,0:T(8,128)(2,1)S(1)} %get-tuple-element.8), channel_id=1, source_target_pairs={{0,1},{1,2},{2,3},{4,5},{5,6},{6,7},{8,9},{9,10},{10,11},{12,13},{... | collective-permute-start | bytes 221192 | tf_op jit(solution)/shard_map/ppermute | solution.py:36
  8.4 0.0 copy-start.7
  8.4 0.0 copy-start.8
  8.5 0.0 copy-start.4
  8.5 0.0 copy-done.1
  8.5 0.0 copy-start.3
  8.5 0.6 copy-done.7
  9.1 0.0 copy-done.8
  9.1 0.2 copy-done.4
  9.3 0.1 copy.21
  9.4 0.0 copy-done
  9.4 0.0 copy-done.3
  9.4 0.1 reshape.53
  9.6 0.2 pad.19
  9.8 0.0 copy-start.2
  9.8 0.7 copy.22
  10.5 0.3 copy-done.2
  10.8 0.7 fusion.6
  11.5 0.7 pad.22.refs_13_
  12.2 1.5 %shard_map.172 = bf16[33,2,128]{2,1,0:T(2,128)(2,1)} custom-call(bf16[32,2,128]{2,1,0:T(2,128)(2,1)} %bitcast.43, s32[8,8]{1,0:T(8,128)} %bitcast.44, s32[8,8]{1,0:T(8,128)} %bitcast.45, s32[4,8]{1,0:T(4,128)} %bitcast.46), custom_call_target="tpu_custom_call" | custom-call | tf_op jit(solution)/shard_map/pallas_call | solution.py:401
  13.6 75.7 %all_gather.3 = bf16[1056,2,128]{2,1,0:T(2,128)(2,1)} all-gather(bf16[33,2,128]{2,1,0:T(2,128)(2,1)} %shard_map.172), channel_id=1, replica_groups=mesh['lon'=8,'lat'=4] {'lon','lat'}, dimensions={0}, use_global_device_ids=true | all-gather | bytes 557568 | tf_op jit(solution)/shard_map/all_gather | solution.py:475
  89.3 0.7 stack.92.refs_0_
  90.0 0.7 pad_maximum_fusion.2.refs_8_
  90.6 0.0 collective-permute-done.1
  90.6 0.0 copy-start.5
  90.7 0.0 collective-permute-done
  90.7 0.0 copy-start.6
  90.7 0.6 copy-done.5
  91.3 0.0 copy-done.6
  91.3 0.1 collective-permute-start.2
  91.4 2.7 %collective-permute-start.3 = (bf16[18,6,512]{2,1,0:T(8,128)(2,1)S(1)}, bf16[18,6,512]{2,1,0:T(8,128)(2,1)S(1)}, u32[]{:S(2)}, u32[]{:S(2)}) collective-permute-start(bf16[18,6,512]{2,1,0:T(8,128)(2,1)S(1)} %pad_maximum_fusion.1), channel_id=1, source_target_pairs={{0,28},{4,0},{8,4},{12,8},{16,12},{20,16},{24,20},{28,24},{1,29},{... | collective-permute-start | bytes 331784 | tf_op jit(solution)/shard_map/ppermute | solution.py:36
  94.1 0.6 fusion.3.refs_11_
  94.7 2.1 %collective-permute-done.2 = bf16[18,6,512]{2,1,0:T(8,128)(2,1)S(1)} collective-permute-done((bf16[18,6,512]{2,1,0:T(8,128)(2,1)S(1)}, bf16[18,6,512]{2,1,0:T(8,128)(2,1)S(1)}, u32[]{:S(2)}, u32[]{:S(2)}) %collective-permute-start.2) | collective-permute-done | bytes 110624 | tf_op jit(solution)/shard_map/ppermute | solution.py:36
  96.8 0.7 reshape.51.refs_5_
  97.5 0.0 collective-permute-done.3
  97.5 0.7 reshape.52.refs_6_
  98.2 15.3 %shard_map.173 = bf16[576,192]{1,0:T(8,128)(2,1)} custom-call(s32[20]{0:T(128)} %stack.92.refs_0_, bf16[32,33,2,128]{3,2,1,0:T(2,128)(2,1)} %bitcast.39, bf16[288,512]{1,0:T(8,128)(2,1)} %bitcast.37, bf16[72,512]{1,0:T(8,128)(2,1)} %bitcast.42, bf16[72,512]{1,0:T(8,128)(2,1)} %bitcast.41, bf16[108,512]{1,0:T(8,128)(2,1)} %reshape.51.refs_5_, ...), custom_call_target="tpu_custom_call" | custom-call | flops 4000000000 | bytes 6000000 | tf_op jit(solution)/shard_map/pallas_call | solution.py:544
  113.5 1.8 %reshape.55 = bf16[12,24,2,192]{3,2,1,0:T(2,128)(2,1)} reshape(bf16[576,192]{1,0:T(8,128)(2,1)} %shard_map.173) | data formatting | bytes 442368 | tf_op jit(solution)/shard_map/reshape | solution.py:563
  (9 shorter events, 0.1 us)
Async XLA Ops:
  0.0 9.4 %copy-start = (bf16[8,192]{1,0:T(8,128)(2,1)S(1)}, bf16[8,192]{1,0:T(8,128)(2,1)}, u32[]{:S(2)}) copy-start(bf16[8,192]{1,0:T(8,128)(2,1)} %param.24) | copy-start | bytes 9220
  1.4 7.1 %copy-start.1 = (bf16[12,24,512]{2,1,0:T(8,128)(2,1)}, bf16[12,24,512]{2,1,0:T(8,128)(2,1)S(1)}, u32[]{:S(2)}) copy-start(bf16[12,24,512]{2,1,0:T(8,128)(2,1)S(1)} %reshape.47) | copy-start | bytes 884740
  1.5 89.2 %collective-permute-start.1 = (bf16[3,24,512]{2,1,0:T(8,128)(2,1)S(1)}, bf16[3,24,512]{2,1,0:T(8,128)(2,1)S(1)}, u32[]{:S(2)}, u32[]{:S(2)}) collective-permute-start(bf16[3,24,512]{2,1,0:T(8,128)(2,1)S(1)} %get-tuple-element.7), channel_id=1, source_target_pairs={{1,0},{2,1},{3,2},{5,4},{6,5},{7,6},{9,8},{10,9},{11,10},{13,12},{... | collective-permute-start | bytes 221192 | tf_op jit(solution)/shard_map/ppermute | solution.py:36
  2.8 87.9 %collective-permute-start = (bf16[3,24,512]{2,1,0:T(8,128)(2,1)S(1)}, bf16[3,24,512]{2,1,0:T(8,128)(2,1)S(1)}, u32[]{:S(2)}, u32[]{:S(2)}) collective-permute-start(bf16[3,24,512]{2,1,0:T(8,128)(2,1)S(1)} %get-tuple-element.8), channel_id=1, source_target_pairs={{0,1},{1,2},{2,3},{4,5},{5,6},{6,7},{8,9},{9,10},{10,11},{12,13},{... | collective-permute-start | bytes 221192 | tf_op jit(solution)/shard_map/ppermute | solution.py:36
  8.4 0.7 copy-start.7
  8.4 0.7 copy-start.8
  8.5 0.8 copy-start.4
  8.5 0.9 copy-start.3
  9.8 1.0 copy-start.2
  90.6 0.6 copy-start.5
  90.7 0.6 copy-start.6
  91.3 5.5 %collective-permute-start.2 = (bf16[18,6,512]{2,1,0:T(8,128)(2,1)S(1)}, bf16[18,6,512]{2,1,0:T(8,128)(2,1)S(1)}, u32[]{:S(2)}, u32[]{:S(2)}) collective-permute-start(bf16[18,6,512]{2,1,0:T(8,128)(2,1)S(1)} %pad_maximum_fusion), channel_id=1, source_target_pairs={{0,4},{4,8},{8,12},{12,16},{16,20},{20,24},{24,28},{28,0},{1,5},{5... | collective-permute-start | bytes 331784 | tf_op jit(solution)/shard_map/ppermute | solution.py:36
  91.4 6.1 %collective-permute-start.3 = (bf16[18,6,512]{2,1,0:T(8,128)(2,1)S(1)}, bf16[18,6,512]{2,1,0:T(8,128)(2,1)S(1)}, u32[]{:S(2)}, u32[]{:S(2)}) collective-permute-start(bf16[18,6,512]{2,1,0:T(8,128)(2,1)S(1)} %pad_maximum_fusion.1), channel_id=1, source_target_pairs={{0,28},{4,0},{8,4},{12,8},{16,12},{20,16},{24,20},{28,24},{1,29},{... | collective-permute-start | bytes 331784 | tf_op jit(solution)/shard_map/ppermute | solution.py:36

commit v4 on v0

v4 whole, which is shorter than its diff:
```python
import functools

import jax
import jax.numpy as jnp
import numpy as np
from jax import lax
from jax.experimental import pallas as pl
from jax.experimental.pallas import tpu as pltpu
from jax.sharding import PartitionSpec as P

HEADS = 6
INSTR = 8
LEV = 2
WLAT = 6
WLON = 12
HLAT = WLAT // 2
HLON = WLON // 2
LANES = 128
PAD = 256
CHUNK = 32
BF16 = jnp.bfloat16
F32 = jnp.float32


def shifted(value, axis, steps, wraps=True):
    count = lax.axis_size(axis)
    pairs = [(source, (source + steps) % count) for source in range(count)]
    if not wraps:
        pairs = [pair for pair in pairs if pair[1] == pair[0] + steps]
    return lax.ppermute(value, axis, pairs)


def rectangles(lat_cells, lon_cells):
    parts = []
    for top, high in ((0, HLAT), (HLAT, lat_cells - WLAT), (lat_cells - HLAT, HLAT)):
        for left, wide in ((0, HLON), (HLON, lon_cells - WLON), (lon_cells - HLON, HLON)):
            tokens = high * wide * LEV
            parts.append((top, high, left, wide, -(-tokens // 16) * 16))
    return parts


def gelu(x):
    return jax.nn.gelu(x)


def normalise(wide, gain):
    average = jnp.mean(wide, axis=-1, keepdims=True)
    centred = wide - average
    spread = jnp.mean(centred * centred, axis=-1, keepdims=True)
    return centred * lax.rsqrt(spread + 1e-05) * gain


def dot(a, b):
    return jnp.dot(a, b, preferred_element_type=F32)


def dot_nt(a, b):
    return lax.dot_general(a, b, (((1,), (1,)), ((), ())), preferred_element_type=F32)


def put_ones(tensor, width):
    lanes = lax.broadcasted_iota(jnp.int32, tensor.shape, 1) % PAD
    return jnp.where(lanes >= width, 1.0, tensor).astype(BF16)


def pack_kernel(values_ref, cell_ref, tag_ref, count_ref, out_ref, cells, tags, held, sem, *, lon_cells):
    tiles_lon, tiles_lat, capacity, _ = values_ref.shape
    copies = [
        pltpu.make_async_copy(values_ref, out_ref.at[:, :, 0], sem.at[0]),
        pltpu.make_async_copy(cell_ref, cells, sem.at[1]),
        pltpu.make_async_copy(tag_ref, tags, sem.at[2]),
        pltpu.make_async_copy(count_ref, held, sem.at[3]),
    ]
    for copy in copies:
        copy.start()
    for copy in copies[1:]:
        copy.wait()
    counts = jnp.concatenate(
        [held[tile : tile + 1, :] for tile in range(tiles_lat) for _ in range(capacity)], axis=0
    )
    cell = cells[...]
    slot = lax.broadcasted_iota(jnp.int32, cell.shape, 0) % capacity
    row = cell // lon_cells
    fields = [jnp.where(slot < counts, row, 255), cell - row * lon_cells, tags[...]]
    rows, columns, kinds = (field.astype(F32) for field in fields)
    lane = lax.broadcasted_iota(jnp.int32, (cell.shape[0], LANES), 1)
    for lon in range(tiles_lon):
        kind = jnp.where(lane.astype(F32) == kinds[:, lon : lon + 1], 1.0, 0.0)
        meta = jnp.where(lane == INSTR, rows[:, lon : lon + 1], kind)
        meta = jnp.where(lane == INSTR + 1, columns[:, lon : lon + 1], meta).astype(BF16)
        out_ref[lon, :, 1] = meta.reshape(tiles_lat, capacity, LANES)
    copies[0].wait()


def packed(record_values, record_cell, record_instrument, block_counts, lon_cells):
    tiles_lon, tiles_lat, capacity, wide = record_values.shape
    anywhere = pl.BlockSpec(memory_space=pl.ANY)
    ints = pltpu.VMEM((tiles_lat * capacity, tiles_lon), jnp.int32)
    shape = (tiles_lon, tiles_lat, 2, capacity, wide)
    out = pl.pallas_call(
        functools.partial(pack_kernel, lon_cells=lon_cells),
        out_shape=jax.ShapeDtypeStruct(shape, BF16),
        in_specs=[anywhere] * 4,
        out_specs=pl.BlockSpec(memory_space=pltpu.VMEM),
        scratch_shapes=[
            ints,
            ints,
            pltpu.VMEM((tiles_lat, tiles_lon), jnp.int32),
            pltpu.SemaphoreType.DMA((4,)),
        ],
        compiler_params=pltpu.CompilerParams(vmem_limit_bytes=56 * 2**20),
    )(
        record_values,
        record_cell.transpose(1, 2, 0).reshape(-1, tiles_lon),
        record_instrument.transpose(1, 2, 0).reshape(-1, tiles_lon),
        block_counts.T,
    )
    return out.reshape((-1,) + shape[2:])


def latent_kernel(
    parts, recv_ref, back_ref, code_ref, first_ref, lift_ref, gain_ref, latent_ref, normed_ref, lifted_ref
):
    sources, _, capacity, _ = recv_ref.shape
    width = first_ref.shape[1]
    lon_cells = back_ref.shape[1]
    chunk = min(CHUNK, sources)
    slots = chunk * capacity

    def scatter(begin):
        records = recv_ref[pl.ds(begin, chunk), 0].reshape(slots, LANES)
        meta = recv_ref[pl.ds(begin, chunk), 1].reshape(slots, LANES)
        encoded = dot(jnp.concatenate([records, meta], axis=1), first_ref[...])
        lifted = put_ones(gelu(dot(gelu(encoded).astype(BF16), lift_ref[...])), width)
        for level in range(LEV):
            lifted_ref[level * slots : (level + 1) * slots, :] = lifted[:, level * PAD : (level + 1) * PAD]
        lane = lax.broadcasted_iota(jnp.int32, (16, LANES), 1)
        weigh = jnp.where(lane == INSTR, float(lon_cells * LEV), 0.0)
        weigh = jnp.where(lane == INSTR + 1, float(LEV), weigh).astype(BF16)
        token = dot_nt(weigh, meta)[:1]
        token = jnp.concatenate([token + float(level) for level in range(LEV)], axis=1)
        hot = jnp.where(code_ref[...] == token, 1.0, 0.0).astype(BF16)
        return dot(hot, lifted_ref[...])

    sums = scatter(0)
    if sources > chunk:
        sums = lax.fori_loop(
            1, sources // chunk, lambda step, total: total + scatter(step * chunk), sums
        )
    back = []
    for top, high, left, wide, padded in parts:
        tokens = high * wide * LEV
        part = back_ref[top : top + high, left : left + wide].reshape(tokens, width).astype(F32)
        if padded > tokens:
            part = jnp.concatenate([part, jnp.zeros((padded - tokens, width), F32)], axis=0)
        back.append(part)
    latent = jnp.concatenate(back, axis=0) + sums[:, :width]
    latent = (latent * (1.0 / (1.0 + sums[:, width : width + 1]))).astype(BF16)
    latent_ref[...] = latent
    normed_ref[...] = normalise(latent.astype(F32), gain_ref[...].astype(F32)).astype(BF16)


def window_pieces(parts):
    own = np.cumsum([0] + [part[4] for part in parts])
    edge = [np.cumsum([0] + [parts[n][4] for n in group]) for group in ((0, 1, 2), (0, 0, 3, 6, 6))]

    def piece(array, first, part):
        return array, int(first), parts[part][4], parts[part][1] * parts[part][3] * LEV

    windows = []
    for i in range(3):
        for j in range(3):
            pieces = [piece("own", own[3 * i + j], 3 * i + j)]
            if i != 1:
                pieces.append(piece("north" if i == 0 else "south", edge[0][j], j))
            if j != 1:
                side = "west" if j == 0 else "east"
                pieces.append(piece(side, edge[1][i + 1], 3 * i))
                if i != 1:
                    pieces.append(piece(side, edge[1][0 if i == 0 else 4], 0))
            windows.append(pieces)
    return windows


def block_kernel(
    parts,
    scalars_ref,
    latent_ref,
    own_ref,
    north_ref,
    south_ref,
    west_ref,
    east_ref,
    keep_ref,
    wk_ref,
    wv_ref,
    wq_ref,
    wm_ref,
    gain_ref,
    wu_ref,
    wd_ref,
    out_ref,
):
    width = wm_ref.shape[0]
    head = width // HEADS
    arrays = dict(own=own_ref, north=north_ref, south=south_ref, west=west_ref, east=east_ref)
    windows = window_pieces(parts)
    tokens = [
        arrays[array][first : first + rows] for pieces in windows for array, first, rows, _ in pieces
    ]
    tokens = jnp.concatenate(tokens, axis=0)
    keys = dot(tokens, wk_ref[...]).astype(BF16)
    values = put_ones(dot(tokens, wv_ref[...]), width)
    query = (dot(own_ref[...], wq_ref[...]) * head ** (-0.5)).astype(BF16)

    head_of = lax.broadcasted_iota(jnp.int32, (1, width), 1) // head
    mixed, start, begin = [], 0, 0
    for w, pieces in enumerate(windows):
        rows = parts[w][4]
        held = sum(piece[2] for piece in pieces)
        part = query[start : start + rows]
        stacked = jnp.concatenate(
            [jnp.where(head_of == h, part, jnp.zeros_like(part)) for h in range(HEADS)], axis=0
        )
        scores = dot_nt(stacked, keys[begin : begin + held])
        if len(pieces) > 1:
            floor = scalars_ref[w // 3].astype(F32)
            scores = jnp.where(keep_ref[w : w + 1, :held] > floor, scores, -1e30)
        largest = jnp.max(scores, axis=-1, keepdims=True)
        raised = jnp.exp(scores - largest).astype(BF16)
        product = dot(raised, values[begin : begin + held])
        product = product[:, :width] * (1.0 / product[:, width : width + 1])
        total = jnp.zeros((rows, width), F32)
        for h in range(HEADS):
            total = jnp.where(head_of == h, product[h * rows : (h + 1) * rows], total)
        mixed.append(total.astype(BF16))
        start += rows
        begin += held
    mixed = jnp.concatenate(mixed, axis=0)

    after = (latent_ref[...].astype(F32) + dot(mixed, wm_ref[...])).astype(BF16).astype(F32)
    normed_two = normalise(after, gain_ref[...].astype(F32)).astype(BF16)
    hidden = gelu(dot(normed_two, wu_ref[...])).astype(BF16)
    result = (after + dot_nt(hidden, wd_ref[...])).astype(BF16)
    start = 0
    for top, high, left, wide, padded in parts:
        part = result[start : start + padded][: high * wide * LEV]
        out_ref[top : top + high, left : left + wide] = part.reshape(high, wide, LEV, width)
        start += padded


def local(
    record_values,
    record_cell,
    record_instrument,
    block_counts,
    background,
    input_weight,
    instrument_table,
    lift_weight,
    first_gain,
    attn_weight,
    mix_weight,
    second_gain,
    up_weight,
    down_weight,
):
    lat_cells, lon_cells, _, width = background.shape
    capacity = record_values.shape[2]
    tiles_lat = record_values.shape[1]
    parts = rectangles(lat_cells, lon_cells)
    starts = np.cumsum([0] + [part[4] for part in parts])
    padded = int(starts[-1])
    code = np.full((padded, 1), -8, np.float32)
    for start, (top, high, left, wide, _) in zip(starts, parts):
        for n in range(high * wide * LEV):
            cell, level = divmod(n, LEV)
            code[start + n] = ((top + cell // wide) * lon_cells + left + cell % wide) * LEV + level
    windows = window_pieces(parts)
    keep = np.zeros((16, max(sum(piece[2] for piece in pieces) for pieces in windows)), np.float32)
    for w, pieces in enumerate(windows):
        at = 0
        for n, (array, _, rows, tokens) in enumerate(pieces):
            beyond = array in ("north", "south") or n == 3
            keep[w, at : at + tokens] = 1 if beyond else 2
            at += rows

    sent = packed(record_values, record_cell, record_instrument, block_counts, lon_cells)
    received = lax.all_to_all(sent, ("lon", "lat"), split_axis=0, concat_axis=0, tiled=True)

    first = jnp.concatenate(
        [input_weight, instrument_table, jnp.zeros((LANES - INSTR, width), BF16)], axis=0
    )
    lift = jnp.pad(
        lift_weight.reshape(width, LEV, width), ((0, 0), (0, 0), (0, PAD - width))
    ).reshape(width, LEV * PAD)
    vmem = pl.BlockSpec(memory_space=pltpu.VMEM)
    latent, normed = pl.pallas_call(
        functools.partial(latent_kernel, parts),
        out_shape=[jax.ShapeDtypeStruct((padded, width), BF16)] * 2,
        in_specs=[vmem] * 6,
        out_specs=[vmem] * 2,
        scratch_shapes=[pltpu.VMEM((min(CHUNK, sent.shape[0]) * capacity * LEV, PAD), BF16)],
        compiler_params=pltpu.CompilerParams(vmem_limit_bytes=24 * 2**20),
    )(received, background, jnp.asarray(code), first, lift, first_gain.reshape(1, width))

    north = shifted(normed[starts[6] :], "lat", 1, wraps=False)
    south = shifted(normed[: starts[3]], "lat", -1, wraps=False)

    def side(j):
        low, end = starts[j] , starts[j + 1]
        own = [normed[starts[3 * i + j] : starts[3 * i + j + 1]] for i in range(3)]
        return jnp.concatenate([north[low:end], *own, south[low:end]], axis=0)

    west = shifted(side(2), "lon", 1)
    east = shifted(side(0), "lon", -1)

    lat = lax.axis_index("lat")
    scalars = jnp.stack([lat == 0, lat < 0, lat == tiles_lat - 1]).astype(jnp.int32)
    return pl.pallas_call(
        functools.partial(block_kernel, parts),
        out_shape=jax.ShapeDtypeStruct(background.shape, BF16),
        in_specs=[pl.BlockSpec(memory_space=pltpu.SMEM)] + [vmem] * 14,
        out_specs=vmem,
        compiler_params=pltpu.CompilerParams(vmem_limit_bytes=40 * 2**20),
    )(
        scalars,
        latent,
        normed,
        north,
        south,
        west,
        east,
        jnp.asarray(keep),
        attn_weight[:, width : 2 * width],
        jnp.pad(attn_weight[:, 2 * width :], ((0, 0), (0, PAD - width))),
        attn_weight[:, :width],
        mix_weight,
        second_gain.reshape(1, width),
        up_weight,
        down_weight.T,
    )


def solution(mesh):
    placed = (
        P("lon", "lat", None, None),
        P("lon", "lat", None),
        P("lon", "lat", None),
        P("lon", "lat"),
        P("lat", "lon", None, None),
        P(),
        P(),
        P(),
        P(),
        P(),
        P(),
        P(),
        P(),
        P(),
    )
    return jax.shard_map(
        local, mesh=mesh, in_specs=placed, out_specs=P("lat", "lon", None, None), check_vma=False
    )
```

time: 93.5 us -> 41.1 us (0.44)
  waiting for transfers between devices: 40 us -> 15.9 us
  local copies, waits for them, and re-layouts: 15.7 us -> 1.99 us
  starting transfers between devices: 24.9 us -> 11.7 us
  Pallas kernels: 0 us -> 10.8 us
  matrix products: 5.9 us -> 0 us
  other arithmetic: 5.78 us -> 0.17 us
    all_to_all x6 -> x1, waiting for transfers between devices: 24.4 us -> 5.97 us  [local(): lax.all_to_all(sent, ('lon', 'lat'), split_axis=0, concat_axis=0, tiled=T...]
    all_to_all x6 -> x1, starting transfers between devices: 23.1 us -> 7.3 us  [local(): lax.all_to_all(sent, ('lon', 'lat'), split_axis=0, concat_axis=0, tiled=T...]
    pallas_call x0 -> x3, Pallas kernels: none -> 10.8 us  [the longest x1 8.41 us: local(): pl.pallas_call(functools.partial(block_kernel, parts), out_shape=jax.Shap...]
    dot_general x8 -> x0, matrix products: 5.9 us -> none  [the longest x1 1.27 us: local(): summed = jnp.dot(onehot, lifted, preferred_element_type=jnp.float32)]
    ppermute x4, waiting for transfers between devices: 15.7 us -> 9.91 us  [shifted(): return lax.ppermute(value, axis, pairs)]
    another operation x4 -> x0, local copies, waits for them, and re-layouts: 4.83 us -> none  [the longest x1 1.92 us: attend_windows(): keys_w = to_windows(keys).reshape(windows, count_tok, HEADS, head_size)]
    ppermute x4, starting transfers between devices: 1.79 us -> 4.37 us  [shifted(): return lax.ppermute(value, axis, pairs)]
    convert_element_type x9 -> x1, other arithmetic: 2.6 us -> 0.08 us  [local(): jnp.stack([lat == 0, lat < 0, lat == tiles_lat - 1]).astype(jnp.int32)]
  transfers between devices with their start and end apart: 10 -> 5, of which waited for: 10 -> 4; matrix products, arithmetic and copies ran while one was open for 8% -> 2% of each run, Pallas kernels for 0% -> 0%
where the time goes in v4:
time: 41.1 us; the launch traced here: 40.8 us
  waiting for transfers between devices  15.9 us (39%)
  starting transfers between devices  11.7 us (28%)
  Pallas kernels  10.8 us (26%)
  local copies, waits for them, and re-layouts  1.99 us (5%)
    ppermute x4, waiting for transfers between devices, shifted(): return lax.ppermute(value, axis, pairs)  9.91 us
    pallas_call x1, Pallas kernels, local(): pl.pallas_call(functools.partial(block_kernel, parts), out_shape=jax.Shap...  8.41 us
    all_to_all x1, starting transfers between devices, local(): lax.all_to_all(sent, ('lon', 'lat'), split_axis=0, concat_axis=0, tiled=T...  7.3 us
    all_to_all x1, waiting for transfers between devices, local(): lax.all_to_all(sent, ('lon', 'lat'), split_axis=0, concat_axis=0, tiled=T...  5.97 us
    ppermute x4, starting transfers between devices, shifted(): return lax.ppermute(value, axis, pairs)  4.37 us
    pallas_call x1, Pallas kernels, packed(): pl.pallas_call(functools.partial(pack_kernel, lon_cells=lon_cells), out_s...  1.49 us
    unnamed x30, local copies, waits for them, and re-layouts  1.45 us
    pallas_call x1, Pallas kernels, local(): pl.pallas_call(functools.partial(latent_kernel, parts), out_shape=[jax.Sh...  0.94 us
  transfers between devices with their start and end apart: 5, of which 4 were waited for; matrix products, arithmetic and copies ran while one was open for 2% of the time, Pallas kernels for 0%

profile of v4, /device:TPU:0, one launch (start us, length us, event | category | flops | bytes accessed | tf_op | source)
XLA Modules:
  0.0 40.8 jit_solution(12075192462238242274)
XLA Ops:
  0.0 0.0 copy-start.8
  0.0 1.5 %shard_map.154 = bf16[8,4,2,2,128]{4,3,2,1,0:T(2,128)(2,1)} custom-call(bf16[8,4,2,128]{3,2,1,0:T(2,128)(2,1)} %values_ref.1, s32[8,8]{1,0:T(8,128)} %bitcast.18, s32[8,8]{1,0:T(8,128)} %bitcast.19, s32[4,8]{1,0:T(4,128)} %bitcast.20), custom_call_target="tpu_custom_call" | custom-call | tf_op jit(solution)/shard_map/pallas_call | solution.py:100
  1.5 0.0 copy-start.9
  1.5 7.3 %all-to-all-start = ((bf16[32,2,2,128]{3,2,1,0:T(2,128)(2,1)}), bf16[32,2,2,128]{3,2,1,0:T(2,128)(2,1)S(1)}, u32[]{:S(2)}, u32[]{:S(2)}) async-start(bf16[32,2,2,128]{3,2,1,0:T(2,128)(2,1)} %bitcast.17), calls=%async_computation | async-start | bytes 65536 | tf_op jit(solution)/shard_map/all_to_all | solution.py:289
  8.8 0.0 copy-done.8
  8.8 0.0 copy-start.7
  8.8 0.1 copy.17
  9.0 0.1 pad.12.clone
  9.0 0.0 copy-done.9
  9.0 0.0 copy-start.10
  9.0 0.1 maximum_maximum_fusion.first_ref
  9.2 0.6 %copy-done.10 = bf16[192]{0:T(256)(128)(2,1)S(1)} copy-done((bf16[192]{0:T(256)(128)(2,1)S(1)}, bf16[192]{0:T(256)(128)(2,1)}, u32[]{:S(2)}) %copy-start.10) | copy-done | bytes 408
  9.7 0.0 copy-done.7
  9.7 0.1 reshape.24
  9.9 0.0 copy-start
  9.9 0.2 pad.8
  10.1 0.0 copy-start.3
  10.1 6.0 %all-to-all-done.recv_ref = bf16[32,2,2,128]{3,2,1,0:T(2,128)(2,1)S(1)} async-done(((bf16[32,2,2,128]{3,2,1,0:T(2,128)(2,1)}), bf16[32,2,2,128]{3,2,1,0:T(2,128)(2,1)S(1)}, u32[]{:S(2)}, u32[]{:S(2)}) %all-to-all-start) | async-done | bytes 32800 | tf_op jit(solution)/shard_map/all_to_all | solution.py:289
  16.1 0.0 copy-done
  16.1 0.0 copy-done.3
  16.1 0.9 %shard_map.155 = (bf16[656,192]{1,0:T(8,128)(2,1)S(1)}, bf16[656,192]{1,0:T(8,128)(2,1)S(1)}) custom-call(bf16[32,2,2,128]{3,2,1,0:T(2,128)(2,1)S(1)} %all-to-all-done.recv_ref, bf16[12,24,2,192]{3,2,1,0:T(2,128)(2,1)S(1)} %copy-done.3, f32[656,1]{1,0:T(8,128)S(1)} %copy-done, bf16[256,192]{1,0:T(8,128)(2,1)S(1)} %maximum_maximum_fusion.first_ref, ...), custom_call_target="tpu_custom_call" | custom-call | tf_op jit(solution)/shard_map/pallas_call | solution.py:298
  17.1 0.0 copy-start.6
  17.1 2.4 %collective-permute-start = (bf16[176,192]{1,0:T(8,128)(2,1)S(1)}, bf16[176,192]{1,0:T(8,128)(2,1)S(1)}, u32[]{:S(2)}, u32[]{:S(2)}) collective-permute-start(bf16[176,192]{1,0:T(8,128)(2,1)S(1)} %get-tuple-element.16), channel_id=1, source_target_pairs={{0,1},{1,2},{2,3},{4,5},{5,6},{6,7},{8,9},{9,10},{10,11},{12,13},{... | collective-permute-start | bytes 202760 | tf_op jit(solution)/shard_map/ppermute | solution.py:30
  19.6 0.0 copy-done.6
  19.6 0.1 fusion.1
  19.7 0.0 copy-start.11
  19.7 0.6 %copy-done.11 = bf16[192]{0:T(256)(128)(2,1)S(1)} copy-done((bf16[192]{0:T(256)(128)(2,1)S(1)}, bf16[192]{0:T(256)(128)(2,1)}, u32[]{:S(2)}) %copy-start.11) | copy-done | bytes 408
  20.3 0.0 copy-start.4
  20.3 0.0 copy-start.5
  20.4 0.0 copy-start.1
  20.4 0.0 copy-start.2
  20.4 1.4 %collective-permute-start.1 = (bf16[176,192]{1,0:T(8,128)(2,1)S(1)}, bf16[176,192]{1,0:T(8,128)(2,1)S(1)}, u32[]{:S(2)}, u32[]{:S(2)}) collective-permute-start(bf16[176,192]{1,0:T(8,128)(2,1)S(1)} %get-tuple-element.15), channel_id=1, source_target_pairs={{1,0},{2,1},{3,2},{5,4},{6,5},{7,6},{9,8},{10,9},{11,10},{13,12},{... | collective-permute-start | bytes 202760 | tf_op jit(solution)/shard_map/ppermute | solution.py:30
  21.8 0.0 collective-permute-done.north_ref
  21.9 5.1 %collective-permute-done.1.south_ref = bf16[176,192]{1,0:T(8,128)(2,1)S(1)} collective-permute-done((bf16[176,192]{1,0:T(8,128)(2,1)S(1)}, bf16[176,192]{1,0:T(8,128)(2,1)S(1)}, u32[]{:S(2)}, u32[]{:S(2)}) %collective-permute-start.1) | collective-permute-done | bytes 67616 | tf_op jit(solution)/shard_map/ppermute | solution.py:30
  26.9 0.0 collective-permute-start.3
  26.9 0.5 %collective-permute-start.2 = (bf16[272,192]{1,0:T(8,128)(2,1)S(1)}, bf16[272,192]{1,0:T(8,128)(2,1)S(1)}, u32[]{:S(2)}, u32[]{:S(2)}) collective-permute-start(bf16[272,192]{1,0:T(8,128)(2,1)S(1)} %get-tuple-element.21), channel_id=1, source_target_pairs={{0,4},{4,8},{8,12},{12,16},{16,20},{20,24},{24,28},{28,0},{1,5},{5... | collective-permute-start | bytes 313352 | tf_op jit(solution)/shard_map/ppermute | solution.py:30
  27.5 0.1 add_convert_fusion.scalars_ref
  27.5 3.4 %collective-permute-done.3.east_ref = bf16[272,192]{1,0:T(8,128)(2,1)S(1)} collective-permute-done((bf16[272,192]{1,0:T(8,128)(2,1)S(1)}, bf16[272,192]{1,0:T(8,128)(2,1)S(1)}, u32[]{:S(2)}, u32[]{:S(2)}) %collective-permute-start.3) | collective-permute-done | bytes 104480 | tf_op jit(solution)/shard_map/ppermute | solution.py:30
  30.9 1.5 %collective-permute-done.2.west_ref = bf16[272,192]{1,0:T(8,128)(2,1)S(1)} collective-permute-done((bf16[272,192]{1,0:T(8,128)(2,1)S(1)}, bf16[272,192]{1,0:T(8,128)(2,1)S(1)}, u32[]{:S(2)}, u32[]{:S(2)}) %collective-permute-start.2) | collective-permute-done | bytes 104480 | tf_op jit(solution)/shard_map/ppermute | solution.py:30
  32.4 0.0 copy-done.4
  32.4 0.0 copy-done.5
  32.4 0.0 copy-done.1
  32.4 0.0 copy-done.2
  32.4 8.4 %shard_map.156 = bf16[12,24,2,192]{3,2,1,0:T(2,128)(2,1)} custom-call(s32[3]{0:T(128)S(1)} %add_convert_fusion.scalars_ref, bf16[656,192]{1,0:T(8,128)(2,1)S(1)} %get-tuple-element.7.latent_ref, bf16[656,192]{1,0:T(8,128)(2,1)S(1)} %get-tuple-element.8.own_ref, bf16[176,192]{1,0:T(8,128)(2,1)S(1)} %collective-permute-done.north_ref, ...), custom_call_target="tpu_custom_call" | custom-call | tf_op jit(solution)/shard_map/pallas_call | solution.py:320
  (11 shorter events, 0.1 us)
Async XLA Ops:
  0.0 8.8 %copy-start.8 = (bf16[128,192]{0,1:T(8,128)(2,1)S(1)}, bf16[128,192]{0,1:T(8,128)(2,1)}, u32[]{:S(2)}) copy-start(bf16[128,192]{0,1:T(8,128)(2,1)} %param.21) | copy-start | bytes 147460
  1.5 7.5 %copy-start.9 = (bf16[8,192]{1,0:T(8,128)(2,1)S(1)}, bf16[8,192]{1,0:T(8,128)(2,1)}, u32[]{:S(2)}) copy-start(bf16[8,192]{1,0:T(8,128)(2,1)} %param.22) | copy-start | bytes 9220
  1.5 14.6 %all-to-all-start = ((bf16[32,2,2,128]{3,2,1,0:T(2,128)(2,1)}), bf16[32,2,2,128]{3,2,1,0:T(2,128)(2,1)S(1)}, u32[]{:S(2)}, u32[]{:S(2)}) async-start(bf16[32,2,2,128]{3,2,1,0:T(2,128)(2,1)} %bitcast.17), calls=%async_computation | async-start | bytes 65536 | tf_op jit(solution)/shard_map/all_to_all | solution.py:289
  8.8 0.9 %copy-start.7 = (bf16[192,384]{1,0:T(8,128)(2,1)S(1)}, bf16[192,384]{1,0:T(8,128)(2,1)}, u32[]{:S(2)}) copy-start(bf16[192,384]{1,0:T(8,128)(2,1)} %param.23) | copy-start | bytes 442372
  9.0 0.7 %copy-start.10 = (bf16[192]{0:T(256)(128)(2,1)S(1)}, bf16[192]{0:T(256)(128)(2,1)}, u32[]{:S(2)}) copy-start(bf16[192]{0:T(256)(128)(2,1)} %param.24) | copy-start | bytes 1156
  9.9 6.2 %copy-start = (f32[656,1]{1,0:T(8,128)S(1)}, f32[656,1]{1,0:T(8,128)}, u32[]{:S(2)}) copy-start(f32[656,1]{1,0:T(8,128)} %constant.15.clone.code_ref) | copy-start | bytes 7876
  10.1 6.0 %copy-start.3 = (bf16[12,24,2,192]{3,2,1,0:T(2,128)(2,1)S(1)}, bf16[12,24,2,192]{3,2,1,0:T(2,128)(2,1)}, u32[]{:S(2)}) copy-start(bf16[12,24,2,192]{3,2,1,0:T(2,128)(2,1)} %back_ref.1) | copy-start | bytes 663556
  17.1 2.5 %copy-start.6 = (bf16[192,576]{1,0:T(8,128)(2,1)S(1)}, bf16[192,576]{1,0:T(8,128)(2,1)}, u32[]{:S(2)}) copy-start(bf16[192,576]{1,0:T(8,128)(2,1)} %param.25) | copy-start | bytes 663556
  17.1 4.7 %collective-permute-start = (bf16[176,192]{1,0:T(8,128)(2,1)S(1)}, bf16[176,192]{1,0:T(8,128)(2,1)S(1)}, u32[]{:S(2)}, u32[]{:S(2)}) collective-permute-start(bf16[176,192]{1,0:T(8,128)(2,1)S(1)} %get-tuple-element.16), channel_id=1, source_target_pairs={{0,1},{1,2},{2,3},{4,5},{5,6},{6,7},{8,9},{9,10},{10,11},{12,13},{... | collective-permute-start | bytes 202760 | tf_op jit(solution)/shard_map/ppermute | solution.py:30
  19.7 0.7 %copy-start.11 = (bf16[192]{0:T(256)(128)(2,1)S(1)}, bf16[192]{0:T(256)(128)(2,1)}, u32[]{:S(2)}) copy-start(bf16[192]{0:T(256)(128)(2,1)} %param.27) | copy-start | bytes 1156
  20.3 12.0 %copy-start.4 = (bf16[192,192]{1,0:T(8,128)(2,1)S(1)}, bf16[192,192]{1,0:T(8,128)(2,1)}, u32[]{:S(2)}) copy-start(bf16[192,192]{1,0:T(8,128)(2,1)} %wm_ref.1) | copy-start | bytes 221188
  20.3 12.0 %copy-start.5 = (f32[16,192]{1,0:T(8,128)S(1)}, f32[16,192]{1,0:T(8,128)}, u32[]{:S(2)}) copy-start(f32[16,192]{1,0:T(8,128)} %constant.16.clone.keep_ref) | copy-start | bytes 36868
  20.4 12.0 %copy-start.1 = (bf16[192,768]{1,0:T(8,128)(2,1)S(1)}, bf16[192,768]{1,0:T(8,128)(2,1)}, u32[]{:S(2)}) copy-start(bf16[192,768]{1,0:T(8,128)(2,1)} %wu_ref.1) | copy-start | bytes 884740
  20.4 12.0 %copy-start.2 = (bf16[768,192]{0,1:T(8,128)(2,1)S(1)}, bf16[768,192]{0,1:T(8,128)(2,1)}, u32[]{:S(2)}) copy-start(bf16[768,192]{0,1:T(8,128)(2,1)} %param.29) | copy-start | bytes 884740
  20.4 6.6 %collective-permute-start.1 = (bf16[176,192]{1,0:T(8,128)(2,1)S(1)}, bf16[176,192]{1,0:T(8,128)(2,1)S(1)}, u32[]{:S(2)}, u32[]{:S(2)}) collective-permute-start(bf16[176,192]{1,0:T(8,128)(2,1)S(1)} %get-tuple-element.15), channel_id=1, source_target_pairs={{1,0},{2,1},{3,2},{5,4},{6,5},{7,6},{9,8},{10,9},{11,10},{13,12},{... | collective-permute-start | bytes 202760 | tf_op jit(solution)/shard_map/ppermute | solution.py:30
  26.9 4.0 %collective-permute-start.3 = (bf16[272,192]{1,0:T(8,128)(2,1)S(1)}, bf16[272,192]{1,0:T(8,128)(2,1)S(1)}, u32[]{:S(2)}, u32[]{:S(2)}) collective-permute-start(bf16[272,192]{1,0:T(8,128)(2,1)S(1)} %get-tuple-element.20), channel_id=1, source_target_pairs={{0,28},{4,0},{8,4},{12,8},{16,12},{20,16},{24,20},{28,24},{1,29},{... | collective-permute-start | bytes 313352 | tf_op jit(solution)/shard_map/ppermute | solution.py:30
  26.9 5.4 %collective-permute-start.2 = (bf16[272,192]{1,0:T(8,128)(2,1)S(1)}, bf16[272,192]{1,0:T(8,128)(2,1)S(1)}, u32[]{:S(2)}, u32[]{:S(2)}) collective-permute-start(bf16[272,192]{1,0:T(8,128)(2,1)S(1)} %get-tuple-element.21), channel_id=1, source_target_pairs={{0,4},{4,8},{8,12},{12,16},{16,20},{20,24},{24,28},{28,0},{1,5},{5... | collective-permute-start | bytes 313352 | tf_op jit(solution)/shard_map/ppermute | solution.py:30

commit v5 on v4

--- a/solution.py
+++ b/solution.py
@@ -58,9 +58,17 @@
     return lax.dot_general(a, b, (((1,), (1,)), ((), ())), preferred_element_type=F32)
 
 
-def put_ones(tensor, width):
-    lanes = lax.broadcasted_iota(jnp.int32, tensor.shape, 1) % PAD
-    return jnp.where(lanes >= width, 1.0, tensor).astype(BF16)
+def with_ones(tensor):
+    ones = jnp.ones((tensor.shape[0], PAD - tensor.shape[1]), F32)
+    return jnp.concatenate([tensor, ones], axis=1).astype(BF16)
+
+
+def beside(left, right):
+    return jnp.concatenate([left, right], axis=1)
+
+
+def below(*pieces):
+    return jnp.concatenate(pieces, axis=0)
 
 
 def pack_kernel(values_ref, cell_ref, tag_ref, count_ref, out_ref, cells, tags, held, sem, *, lon_cells):
@@ -119,10 +127,23 @@
 
 
 def latent_kernel(
-    parts, recv_ref, back_ref, code_ref, first_ref, lift_ref, gain_ref, latent_ref, normed_ref, lifted_ref
+    parts,
+    recv_ref,
+    back_ref,
+    code_ref,
+    first_ref,
+    table_ref,
+    lift_ref,
+    gain_ref,
+    latent_ref,
+    normed_ref,
+    up_ref,
+    down_ref,
+    left_ref,
+    right_ref,
 ):
     sources, _, capacity, _ = recv_ref.shape
-    width = first_ref.shape[1]
+    width = table_ref.shape[1]
     lon_cells = back_ref.shape[1]
     chunk = min(CHUNK, sources)
     slots = chunk * capacity
@@ -130,17 +151,18 @@
     def scatter(begin):
         records = recv_ref[pl.ds(begin, chunk), 0].reshape(slots, LANES)
         meta = recv_ref[pl.ds(begin, chunk), 1].reshape(slots, LANES)
-        encoded = dot(jnp.concatenate([records, meta], axis=1), first_ref[...])
-        lifted = put_ones(gelu(dot(gelu(encoded).astype(BF16), lift_ref[...])), width)
-        for level in range(LEV):
-            lifted_ref[level * slots : (level + 1) * slots, :] = lifted[:, level * PAD : (level + 1) * PAD]
+        encoded = dot_nt(records, first_ref[...]) + dot(meta[:, :INSTR], table_ref[...])
+        lifted = gelu(dot(gelu(encoded).astype(BF16), lift_ref[...]))
+        lifted = with_ones(
+            below(*[lifted[:, level * width : (level + 1) * width] for level in range(LEV)])
+        )
         lane = lax.broadcasted_iota(jnp.int32, (16, LANES), 1)
         weigh = jnp.where(lane == INSTR, float(lon_cells * LEV), 0.0)
         weigh = jnp.where(lane == INSTR + 1, float(LEV), weigh).astype(BF16)
         token = dot_nt(weigh, meta)[:1]
         token = jnp.concatenate([token + float(level) for level in range(LEV)], axis=1)
         hot = jnp.where(code_ref[...] == token, 1.0, 0.0).astype(BF16)
-        return dot(hot, lifted_ref[...])
+        return dot(hot, lifted)
 
     sums = scatter(0)
     if sources > chunk:
@@ -157,29 +179,22 @@
     latent = jnp.concatenate(back, axis=0) + sums[:, :width]
     latent = (latent * (1.0 / (1.0 + sums[:, width : width + 1]))).astype(BF16)
     latent_ref[...] = latent
-    normed_ref[...] = normalise(latent.astype(F32), gain_ref[...].astype(F32)).astype(BF16)
-
-
-def window_pieces(parts):
-    own = np.cumsum([0] + [part[4] for part in parts])
-    edge = [np.cumsum([0] + [parts[n][4] for n in group]) for group in ((0, 1, 2), (0, 0, 3, 6, 6))]
-
-    def piece(array, first, part):
-        return array, int(first), parts[part][4], parts[part][1] * parts[part][3] * LEV
-
-    windows = []
-    for i in range(3):
-        for j in range(3):
-            pieces = [piece("own", own[3 * i + j], 3 * i + j)]
-            if i != 1:
-                pieces.append(piece("north" if i == 0 else "south", edge[0][j], j))
-            if j != 1:
-                side = "west" if j == 0 else "east"
-                pieces.append(piece(side, edge[1][i + 1], 3 * i))
-                if i != 1:
-                    pieces.append(piece(side, edge[1][0 if i == 0 else 4], 0))
-            windows.append(pieces)
-    return windows
+    normed = normalise(latent.astype(F32), gain_ref[...].astype(F32))
+    normed_ref[...] = normed.astype(BF16)
+
+    own, start = [], 0
+    for top, high, left, wide, padded in parts:
+        own.append(normed[start : start + high * wide * LEV])
+        start += padded
+    half = own[0].shape[0]
+
+    def halves(n):
+        return beside(own[n][:half], own[n][half:])
+
+    down_ref[...] = below(beside(own[6], own[8]), halves(7)).astype(BF16)
+    up_ref[...] = below(beside(own[2], own[0]), halves(1)).astype(BF16)
+    left_ref[...] = below(beside(own[0], own[3][:half]), beside(own[6], own[3][half:])).astype(BF16)
+    right_ref[...] = below(beside(own[2], own[5][:half]), beside(own[8], own[5][half:])).astype(BF16)
 
 
 def block_kernel(
@@ -192,9 +207,7 @@
     west_ref,
     east_ref,
     keep_ref,
-    wk_ref,
-    wv_ref,
-    wq_ref,
+    attn_ref,
     wm_ref,
     gain_ref,
     wu_ref,
@@ -203,40 +216,61 @@
 ):
     width = wm_ref.shape[0]
     head = width // HEADS
-    arrays = dict(own=own_ref, north=north_ref, south=south_ref, west=west_ref, east=east_ref)
-    windows = window_pieces(parts)
-    tokens = [
-        arrays[array][first : first + rows] for pieces in windows for array, first, rows, _ in pieces
+    half = parts[0][1] * parts[0][3] * LEV
+    own, start = [], 0
+    for top, high, left, wide, padded in parts:
+        own.append(own_ref[start : start + padded, :].astype(F32)[: high * wide * LEV])
+        start += padded
+
+    def pieces(ref):
+        value = ref[...].astype(F32)
+        rows = [value[at : at + half] for at in range(0, value.shape[0], half)]
+        return [part[:, at : at + width] for part in rows for at in (0, width)]
+
+    north_w, north_e, north_1, north_2 = pieces(north_ref)
+    south_e, south_w, south_1, south_2 = pieces(south_ref)
+    west_n, west_1, west_s, west_2, west_far_s, west_far_n = pieces(west_ref)
+    east_n, east_1, east_s, east_2, east_far_n, east_far_s = pieces(east_ref)
+    windows = [
+        (own[0], north_w, west_n, west_far_n),
+        (own[1], north_1, north_2),
+        (own[2], north_e, east_n, east_far_n),
+        (own[3], west_1, west_2),
+        (own[4],),
+        (own[5], east_1, east_2),
+        (own[6], south_w, west_s, west_far_s),
+        (own[7], south_1, south_2),
+        (own[8], south_e, east_s, east_far_s),
     ]
-    tokens = jnp.concatenate(tokens, axis=0)
-    keys = dot(tokens, wk_ref[...]).astype(BF16)
-    values = put_ones(dot(tokens, wv_ref[...]), width)
-    query = (dot(own_ref[...], wq_ref[...]) * head ** (-0.5)).astype(BF16)
+    tokens = below(*[piece for window in windows for piece in window]).astype(BF16)
+    weight = attn_ref[...]
+    keys = dot(tokens, weight[:, width : 2 * width]).astype(BF16)
+    values = with_ones(dot(tokens, weight[:, 2 * width :]))
+    query = (dot(own_ref[...], weight[:, :width]) * head ** (-0.5)).astype(BF16)
 
     head_of = lax.broadcasted_iota(jnp.int32, (1, width), 1) // head
-    mixed, start, begin = [], 0, 0
-    for w, pieces in enumerate(windows):
+    held = WLAT * WLON * LEV
+    mixed, start = [], 0
+    for w in range(len(parts)):
         rows = parts[w][4]
-        held = sum(piece[2] for piece in pieces)
         part = query[start : start + rows]
-        stacked = jnp.concatenate(
-            [jnp.where(head_of == h, part, jnp.zeros_like(part)) for h in range(HEADS)], axis=0
+        stacked = below(
+            *[jnp.where(head_of == h, part, jnp.zeros_like(part)) for h in range(HEADS)]
         )
-        scores = dot_nt(stacked, keys[begin : begin + held])
-        if len(pieces) > 1:
+        scores = dot_nt(stacked, keys[w * held : (w + 1) * held])
+        if w // 3 != 1:
             floor = scalars_ref[w // 3].astype(F32)
-            scores = jnp.where(keep_ref[w : w + 1, :held] > floor, scores, -1e30)
+            scores = jnp.where(keep_ref[w : w + 1, :] > floor, scores, -1e30)
         largest = jnp.max(scores, axis=-1, keepdims=True)
         raised = jnp.exp(scores - largest).astype(BF16)
-        product = dot(raised, values[begin : begin + held])
+        product = dot(raised, values[w * held : (w + 1) * held])
         product = product[:, :width] * (1.0 / product[:, width : width + 1])
         total = jnp.zeros((rows, width), F32)
         for h in range(HEADS):
             total = jnp.where(head_of == h, product[h * rows : (h + 1) * rows], total)
         mixed.append(total.astype(BF16))
         start += rows
-        begin += held
-    mixed = jnp.concatenate(mixed, axis=0)
+    mixed = below(*mixed)
 
     after = (latent_ref[...].astype(F32) + dot(mixed, wm_ref[...])).astype(BF16).astype(F32)
     normed_two = normalise(after, gain_ref[...].astype(F32)).astype(BF16)
@@ -276,51 +310,47 @@
         for n in range(high * wide * LEV):
             cell, level = divmod(n, LEV)
             code[start + n] = ((top + cell // wide) * lon_cells + left + cell % wide) * LEV + level
-    windows = window_pieces(parts)
-    keep = np.zeros((16, max(sum(piece[2] for piece in pieces) for pieces in windows)), np.float32)
-    for w, pieces in enumerate(windows):
-        at = 0
-        for n, (array, _, rows, tokens) in enumerate(pieces):
-            beyond = array in ("north", "south") or n == 3
-            keep[w, at : at + tokens] = 1 if beyond else 2
-            at += rows
+    half = HLAT * HLON * LEV
+    keep = np.zeros((16, WLAT * WLON * LEV), np.float32)
+    keep[:, :half] = 1
+    keep[[1, 7], : 2 * half] = 1
+    keep[[0, 2, 6, 8], 2 * half : 3 * half] = 1
 
     sent = packed(record_values, record_cell, record_instrument, block_counts, lon_cells)
     received = lax.all_to_all(sent, ("lon", "lat"), split_axis=0, concat_axis=0, tiled=True)
 
-    first = jnp.concatenate(
-        [input_weight, instrument_table, jnp.zeros((LANES - INSTR, width), BF16)], axis=0
-    )
-    lift = jnp.pad(
-        lift_weight.reshape(width, LEV, width), ((0, 0), (0, 0), (0, PAD - width))
-    ).reshape(width, LEV * PAD)
     vmem = pl.BlockSpec(memory_space=pltpu.VMEM)
-    latent, normed = pl.pallas_call(
+    whole = jax.ShapeDtypeStruct((padded, width), BF16)
+    strip = jax.ShapeDtypeStruct((2 * half, 2 * width), BF16)
+    latent, normed, up, down, left, right = pl.pallas_call(
         functools.partial(latent_kernel, parts),
-        out_shape=[jax.ShapeDtypeStruct((padded, width), BF16)] * 2,
-        in_specs=[vmem] * 6,
-        out_specs=[vmem] * 2,
-        scratch_shapes=[pltpu.VMEM((min(CHUNK, sent.shape[0]) * capacity * LEV, PAD), BF16)],
+        out_shape=[whole, whole, strip, strip, strip, strip],
+        in_specs=[vmem] * 7,
+        out_specs=[vmem] * 6,
         compiler_params=pltpu.CompilerParams(vmem_limit_bytes=24 * 2**20),
-    )(received, background, jnp.asarray(code), first, lift, first_gain.reshape(1, width))
-
-    north = shifted(normed[starts[6] :], "lat", 1, wraps=False)
-    south = shifted(normed[: starts[3]], "lat", -1, wraps=False)
-
-    def side(j):
-        low, end = starts[j] , starts[j + 1]
-        own = [normed[starts[3 * i + j] : starts[3 * i + j + 1]] for i in range(3)]
-        return jnp.concatenate([north[low:end], *own, south[low:end]], axis=0)
-
-    west = shifted(side(2), "lon", 1)
-    east = shifted(side(0), "lon", -1)
+    )(
+        received,
+        background,
+        jnp.asarray(code),
+        input_weight.T,
+        instrument_table,
+        lift_weight,
+        first_gain.reshape(1, width),
+    )
+
+    north = shifted(down, "lat", 1, wraps=False)
+    south = shifted(up, "lat", -1, wraps=False)
+    right = below(right, beside(south[:half, :width], north[:half, width:]))
+    left = below(left, beside(north[:half, :width], south[:half, width:]))
+    west = shifted(right, "lon", 1)
+    east = shifted(left, "lon", -1)
 
     lat = lax.axis_index("lat")
-    scalars = jnp.stack([lat == 0, lat < 0, lat == tiles_lat - 1]).astype(jnp.int32)
+    scalars = jnp.stack([lat == 0, lat < 0, lat == tiles_lat - 1]).astype(jnp.int32) - 1
     return pl.pallas_call(
         functools.partial(block_kernel, parts),
         out_shape=jax.ShapeDtypeStruct(background.shape, BF16),
-        in_specs=[pl.BlockSpec(memory_space=pltpu.SMEM)] + [vmem] * 14,
+        in_specs=[pl.BlockSpec(memory_space=pltpu.SMEM)] + [vmem] * 12,
         out_specs=vmem,
         compiler_params=pltpu.CompilerParams(vmem_limit_bytes=40 * 2**20),
     )(
@@ -332,9 +362,7 @@
         west,
         east,
         jnp.asarray(keep),
-        attn_weight[:, width : 2 * width],
-        jnp.pad(attn_weight[:, 2 * width :], ((0, 0), (0, PAD - width))),
-        attn_weight[:, :width],
+        attn_weight,
         mix_weight,
         second_gain.reshape(1, width),
         up_weight,

time: 41.1 us -> 43.1 us (1.049)
  starting transfers between devices: 11.7 us -> 13.7 us
  waiting for transfers between devices: 15.9 us -> 14.7 us
  local copies, waits for them, and re-layouts: 1.99 us -> 3.06 us
    ppermute x4, waiting for transfers between devices: 9.91 us -> 7.45 us  [shifted(): return lax.ppermute(value, axis, pairs)]
    ppermute x4, starting transfers between devices: 4.37 us -> 6.36 us  [shifted(): return lax.ppermute(value, axis, pairs)]
    unnamed x30 -> x24, local copies, waits for them, and re-layouts: 1.45 us -> 2.89 us
    all_to_all x1, waiting for transfers between devices: 5.97 us -> 7.27 us  [local(): lax.all_to_all(sent, ('lon', 'lat'), split_axis=0, concat_axis=0, tiled=T...]
  transfers between devices with their start and end apart: 5 -> 5, of which waited for: 4 -> 4; matrix products, arithmetic and copies ran while one was open for 2% -> 1% of each run, Pallas kernels for 0% -> 0%
where the time goes in v5:
time: 43.1 us; the launch traced here: 42.7 us
  waiting for transfers between devices  14.7 us (34%)
  starting transfers between devices  13.7 us (32%)
  Pallas kernels  10.8 us (25%)
  local copies, waits for them, and re-layouts  3.06 us (7%)
    pallas_call x1, Pallas kernels, local(): pl.pallas_call(functools.partial(block_kernel, parts), out_shape=jax.Shap...  8.21 us
    ppermute x4, waiting for transfers between devices, shifted(): return lax.ppermute(value, axis, pairs)  7.45 us
    all_to_all x1, starting transfers between devices, local(): lax.all_to_all(sent, ('lon', 'lat'), split_axis=0, concat_axis=0, tiled=T...  7.3 us
    all_to_all x1, waiting for transfers between devices, local(): lax.all_to_all(sent, ('lon', 'lat'), split_axis=0, concat_axis=0, tiled=T...  7.27 us
    ppermute x4, starting transfers between devices, shifted(): return lax.ppermute(value, axis, pairs)  6.36 us
    unnamed x24, local copies, waits for them, and re-layouts  2.89 us
    pallas_call x1, Pallas kernels, packed(): pl.pallas_call(functools.partial(pack_kernel, lon_cells=lon_cells), out_s...  1.48 us
    pallas_call x1, Pallas kernels, local(): pl.pallas_call(functools.partial(latent_kernel, parts), out_shape=[whole,...  1.15 us
  transfers between devices with their start and end apart: 5, of which 4 were waited for; matrix products, arithmetic and copies ran while one was open for 1% of the time, Pallas kernels for 0%

profile of v5, /device:TPU:0, one launch (start us, length us, event | category | flops | bytes accessed | tf_op | source)
XLA Modules:
  0.0 42.7 jit_solution(15885596462400648341)
XLA Ops:
  0.0 1.5 %shard_map.154 = bf16[8,4,2,2,128]{4,3,2,1,0:T(2,128)(2,1)} custom-call(bf16[8,4,2,128]{3,2,1,0:T(2,128)(2,1)} %values_ref.1, s32[8,8]{1,0:T(8,128)} %bitcast.16, s32[8,8]{1,0:T(8,128)} %bitcast.17, s32[4,8]{1,0:T(4,128)} %bitcast.18), custom_call_target="tpu_custom_call" | custom-call | tf_op jit(solution)/shard_map/pallas_call | solution.py:108
  1.5 0.0 copy-start.7
  1.5 0.0 copy-start.10
  1.5 0.0 copy-start.9
  1.5 7.3 %all-to-all-start = ((bf16[32,2,2,128]{3,2,1,0:T(2,128)(2,1)}), bf16[32,2,2,128]{3,2,1,0:T(2,128)(2,1)S(1)}, u32[]{:S(2)}, u32[]{:S(2)}) async-start(bf16[32,2,2,128]{3,2,1,0:T(2,128)(2,1)} %bitcast.15), calls=%async_computation | async-start | bytes 65536 | tf_op jit(solution)/shard_map/all_to_all | solution.py:320
  8.8 0.0 copy-done.10
  8.9 7.3 %all-to-all-done.recv_ref = bf16[32,2,2,128]{3,2,1,0:T(2,128)(2,1)S(1)} async-done(((bf16[32,2,2,128]{3,2,1,0:T(2,128)(2,1)}), bf16[32,2,2,128]{3,2,1,0:T(2,128)(2,1)S(1)}, u32[]{:S(2)}, u32[]{:S(2)}) %all-to-all-start) | async-done | bytes 32800 | tf_op jit(solution)/shard_map/all_to_all | solution.py:320
  16.1 0.0 copy-done.7
  16.1 0.0 copy-done.9
  16.1 0.0 copy-start
  16.1 1.0 %copy-done = f32[656,1]{1,0:T(8,128)S(1)} copy-done((f32[656,1]{1,0:T(8,128)S(1)}, f32[656,1]{1,0:T(8,128)}, u32[]{:S(2)}) %copy-start) | copy-done | bytes 2648
  17.1 0.0 copy-start.3
  17.1 1.0 %copy-done.3 = bf16[12,24,2,192]{3,2,1,0:T(2,128)(2,1)S(1)} copy-done((bf16[12,24,2,192]{3,2,1,0:T(2,128)(2,1)S(1)}, bf16[12,24,2,192]{3,2,1,0:T(2,128)(2,1)}, u32[]{:S(2)}) %copy-start.3) | copy-done | bytes 221208
  18.1 0.0 copy-start.5
  18.1 0.9 %copy-done.5 = bf16[192,384]{1,0:T(8,128)(2,1)S(1)} copy-done((bf16[192,384]{1,0:T(8,128)(2,1)S(1)}, bf16[192,384]{1,0:T(8,128)(2,1)}, u32[]{:S(2)}) %copy-start.5) | copy-done | bytes 147480
  19.0 0.0 copy-start.11
  19.0 0.0 copy-start.2
  19.0 0.0 copy-start.6
  19.0 1.2 %shard_map.155 = (bf16[656,192]{1,0:T(8,128)(2,1)S(1)}, bf16[656,192]{1,0:T(8,128)(2,1)S(1)}, bf16[72,384]{1,0:T(8,128)(2,1)S(1)}, bf16[72,384]{1,0:T(8,128)(2,1...) custom-call(bf16[32,2,2,128]{3,2,1,0:T(2,128)(2,1)S(1)} %all-to-all-done.recv_ref, ...), custom_call_target="tpu_custom_call" | custom-call | tf_op jit(solution)/shard_map/pallas_call | solution.py:325
  20.2 0.0 copy-start.1
  20.2 2.4 %collective-permute-start = (bf16[72,384]{1,0:T(8,128)(2,1)S(1)}, bf16[72,384]{1,0:T(8,128)(2,1)S(1)}, u32[]{:S(2)}, u32[]{:S(2)}) collective-permute-start(bf16[72,384]{1,0:T(8,128)(2,1)S(1)} %get-tuple-element.13), channel_id=1, source_target_pairs={{0,1},{1,2},{2,3},{4,5},{5,6},{6,7},{8,9},{9,10},{10,11},{12,13},{... | collective-permute-start | bytes 165896 | tf_op jit(solution)/shard_map/ppermute | solution.py:30
  22.6 0.0 copy-done.11
  22.6 1.3 %collective-permute-start.1 = (bf16[72,384]{1,0:T(8,128)(2,1)S(1)}, bf16[72,384]{1,0:T(8,128)(2,1)S(1)}, u32[]{:S(2)}, u32[]{:S(2)}) collective-permute-start(bf16[72,384]{1,0:T(8,128)(2,1)S(1)} %get-tuple-element.14), channel_id=1, source_target_pairs={{1,0},{2,1},{3,2},{5,4},{6,5},{7,6},{9,8},{10,9},{11,10},{13,12},{... | collective-permute-start | bytes 165896 | tf_op jit(solution)/shard_map/ppermute | solution.py:30
  23.9 0.5 %collective-permute-done.north_ref = bf16[72,384]{1,0:T(8,128)(2,1)S(1)} collective-permute-done((bf16[72,384]{1,0:T(8,128)(2,1)S(1)}, bf16[72,384]{1,0:T(8,128)(2,1)S(1)}, u32[]{:S(2)}, u32[]{:S(2)}) %collective-permute-start) | collective-permute-done | bytes 55328 | tf_op jit(solution)/shard_map/ppermute | solution.py:30
  24.4 0.1 fusion.1
  24.5 0.0 copy-start.4
  24.5 4.2 %collective-permute-done.1.south_ref = bf16[72,384]{1,0:T(8,128)(2,1)S(1)} collective-permute-done((bf16[72,384]{1,0:T(8,128)(2,1)S(1)}, bf16[72,384]{1,0:T(8,128)(2,1)S(1)}, u32[]{:S(2)}, u32[]{:S(2)}) %collective-permute-start.1) | collective-permute-done | bytes 55328 | tf_op jit(solution)/shard_map/ppermute | solution.py:30
  28.7 0.1 fusion.2
  28.8 0.1 maximum_maximum_fusion
  28.8 0.0 collective-permute-start.2
  28.9 0.0 copy-start.8
  28.9 0.1 maximum_maximum_fusion.1
  29.0 2.6 %collective-permute-start.3 = (bf16[108,384]{1,0:T(8,128)(2,1)S(1)}, bf16[108,384]{1,0:T(8,128)(2,1)S(1)}, u32[]{:S(2)}, u32[]{:S(2)}) collective-permute-start(bf16[108,384]{1,0:T(8,128)(2,1)S(1)} %maximum_maximum_fusion.1), channel_id=1, source_target_pairs={{0,28},{4,0},{8,4},{12,8},{16,12},{20,16},{24,20},{28,24},{1,29},{... | collective-permute-start | bytes 248840 | tf_op jit(solution)/shard_map/ppermute | solution.py:30
  31.6 0.1 fusion.scalars_ref
  31.7 2.8 %collective-permute-done.2.west_ref = bf16[108,384]{1,0:T(8,128)(2,1)S(1)} collective-permute-done((bf16[108,384]{1,0:T(8,128)(2,1)S(1)}, bf16[108,384]{1,0:T(8,128)(2,1)S(1)}, u32[]{:S(2)}, u32[]{:S(2)}) %collective-permute-start.2) | collective-permute-done | bytes 82976 | tf_op jit(solution)/shard_map/ppermute | solution.py:30
  34.4 0.0 collective-permute-done.3.east_ref
  34.4 0.0 copy-done.2
  34.4 0.0 copy-done.6
  34.4 0.0 copy-done.1
  34.5 0.0 copy-done.4
  34.5 0.0 copy-done.8
  34.5 8.2 %shard_map.156 = bf16[12,24,2,192]{3,2,1,0:T(2,128)(2,1)} custom-call(s32[3]{0:T(128)S(1)} %fusion.scalars_ref, bf16[656,192]{1,0:T(8,128)(2,1)S(1)} %get-tuple-element.11.latent_ref, bf16[656,192]{1,0:T(8,128)(2,1)S(1)} %get-tuple-element.12.own_ref, bf16[72,384]{1,0:T(8,128)(2,1)S(1)} %collective-permute-done.north_ref, ...), custom_call_target="tpu_custom_call" | custom-call | tf_op jit(solution)/shard_map/pallas_call | solution.py:350
  (2 shorter events, 0.0 us)
Async XLA Ops:
  1.5 14.6 %copy-start.7 = (bf16[128,192]{0,1:T(8,128)(2,1)S(1)}, bf16[128,192]{0,1:T(8,128)(2,1)}, u32[]{:S(2)}) copy-start(bf16[128,192]{0,1:T(8,128)(2,1)} %param.21) | copy-start | bytes 147460
  1.5 7.3 %copy-start.10 = (bf16[192]{0:T(256)(128)(2,1)S(1)}, bf16[192]{0:T(256)(128)(2,1)}, u32[]{:S(2)}) copy-start(bf16[192]{0:T(256)(128)(2,1)} %param.24) | copy-start | bytes 1156
  1.5 14.6 %copy-start.9 = (bf16[8,192]{1,0:T(8,128)(2,1)S(1)}, bf16[8,192]{1,0:T(8,128)(2,1)}, u32[]{:S(2)}) copy-start(bf16[8,192]{1,0:T(8,128)(2,1)} %table_ref.1) | copy-start | bytes 9220
  1.5 14.6 %all-to-all-start = ((bf16[32,2,2,128]{3,2,1,0:T(2,128)(2,1)}), bf16[32,2,2,128]{3,2,1,0:T(2,128)(2,1)S(1)}, u32[]{:S(2)}, u32[]{:S(2)}) async-start(bf16[32,2,2,128]{3,2,1,0:T(2,128)(2,1)} %bitcast.15), calls=%async_computation | async-start | bytes 65536 | tf_op jit(solution)/shard_map/all_to_all | solution.py:320
  16.1 1.0 %copy-start = (f32[656,1]{1,0:T(8,128)S(1)}, f32[656,1]{1,0:T(8,128)}, u32[]{:S(2)}) copy-start(f32[656,1]{1,0:T(8,128)} %constant.15.clone.code_ref) | copy-start | bytes 7876
  17.1 1.0 %copy-start.3 = (bf16[12,24,2,192]{3,2,1,0:T(2,128)(2,1)S(1)}, bf16[12,24,2,192]{3,2,1,0:T(2,128)(2,1)}, u32[]{:S(2)}) copy-start(bf16[12,24,2,192]{3,2,1,0:T(2,128)(2,1)} %back_ref.1) | copy-start | bytes 663556
  18.1 0.9 %copy-start.5 = (bf16[192,384]{1,0:T(8,128)(2,1)S(1)}, bf16[192,384]{1,0:T(8,128)(2,1)}, u32[]{:S(2)}) copy-start(bf16[192,384]{1,0:T(8,128)(2,1)} %lift_ref.1) | copy-start | bytes 442372
  19.0 3.6 %copy-start.11 = (bf16[192]{0:T(256)(128)(2,1)S(1)}, bf16[192]{0:T(256)(128)(2,1)}, u32[]{:S(2)}) copy-start(bf16[192]{0:T(256)(128)(2,1)} %param.27) | copy-start | bytes 1156
  19.0 15.5 %copy-start.2 = (bf16[768,192]{0,1:T(8,128)(2,1)S(1)}, bf16[768,192]{0,1:T(8,128)(2,1)}, u32[]{:S(2)}) copy-start(bf16[768,192]{0,1:T(8,128)(2,1)} %param.29) | copy-start | bytes 884740
  19.0 15.5 %copy-start.6 = (bf16[192,192]{1,0:T(8,128)(2,1)S(1)}, bf16[192,192]{1,0:T(8,128)(2,1)}, u32[]{:S(2)}) copy-start(bf16[192,192]{1,0:T(8,128)(2,1)} %wm_ref.1) | copy-start | bytes 221188
  20.2 14.3 %copy-start.1 = (bf16[192,768]{1,0:T(8,128)(2,1)S(1)}, bf16[192,768]{1,0:T(8,128)(2,1)}, u32[]{:S(2)}) copy-start(bf16[192,768]{1,0:T(8,128)(2,1)} %wu_ref.1) | copy-start | bytes 884740
  20.2 4.2 %collective-permute-start = (bf16[72,384]{1,0:T(8,128)(2,1)S(1)}, bf16[72,384]{1,0:T(8,128)(2,1)S(1)}, u32[]{:S(2)}, u32[]{:S(2)}) collective-permute-start(bf16[72,384]{1,0:T(8,128)(2,1)S(1)} %get-tuple-element.13), channel_id=1, source_target_pairs={{0,1},{1,2},{2,3},{4,5},{5,6},{6,7},{8,9},{9,10},{10,11},{12,13},{... | collective-permute-start | bytes 165896 | tf_op jit(solution)/shard_map/ppermute | solution.py:30
  22.6 6.0 %collective-permute-start.1 = (bf16[72,384]{1,0:T(8,128)(2,1)S(1)}, bf16[72,384]{1,0:T(8,128)(2,1)S(1)}, u32[]{:S(2)}, u32[]{:S(2)}) collective-permute-start(bf16[72,384]{1,0:T(8,128)(2,1)S(1)} %get-tuple-element.14), channel_id=1, source_target_pairs={{1,0},{2,1},{3,2},{5,4},{6,5},{7,6},{9,8},{10,9},{11,10},{13,12},{... | collective-permute-start | bytes 165896 | tf_op jit(solution)/shard_map/ppermute | solution.py:30
  24.5 10.0 %copy-start.4 = (bf16[192,576]{1,0:T(8,128)(2,1)S(1)}, bf16[192,576]{1,0:T(8,128)(2,1)}, u32[]{:S(2)}) copy-start(bf16[192,576]{1,0:T(8,128)(2,1)} %attn_ref.1) | copy-start | bytes 663556
  28.8 5.6 %collective-permute-start.2 = (bf16[108,384]{1,0:T(8,128)(2,1)S(1)}, bf16[108,384]{1,0:T(8,128)(2,1)S(1)}, u32[]{:S(2)}, u32[]{:S(2)}) collective-permute-start(bf16[108,384]{1,0:T(8,128)(2,1)S(1)} %maximum_maximum_fusion), channel_id=1, source_target_pairs={{0,4},{4,8},{8,12},{12,16},{16,20},{20,24},{24,28},{28,0},{1,5},{5... | collective-permute-start | bytes 248840 | tf_op jit(solution)/shard_map/ppermute | solution.py:30
  28.9 5.6 %copy-start.8 = (f32[16,144]{1,0:T(8,128)S(1)}, f32[16,144]{1,0:T(8,128)}, u32[]{:S(2)}) copy-start(f32[16,144]{1,0:T(8,128)} %constant.16.clone.keep_ref) | copy-start | bytes 27652
  29.0 5.5 %collective-permute-start.3 = (bf16[108,384]{1,0:T(8,128)(2,1)S(1)}, bf16[108,384]{1,0:T(8,128)(2,1)S(1)}, u32[]{:S(2)}, u32[]{:S(2)}) collective-permute-start(bf16[108,384]{1,0:T(8,128)(2,1)S(1)} %maximum_maximum_fusion.1), channel_id=1, source_target_pairs={{0,28},{4,0},{8,4},{12,8},{16,12},{20,16},{24,20},{28,24},{1,29},{... | collective-permute-start | bytes 248840 | tf_op jit(solution)/shard_map/ppermute | solution.py:30

commit v6 on v5

v6 whole, which is shorter than its diff:
```python
import functools

import jax
import jax.numpy as jnp
from jax import lax
from jax.experimental import pallas as pl
from jax.experimental.pallas import tpu as pltpu
from jax.sharding import PartitionSpec as P

HEADS = 6
INSTR = 8
LEV = 2
WLAT = 6
WLON = 12
HLAT = WLAT // 2
HLON = WLON // 2
LANES = 128
PAD = 256
CHUNK = 32
LIMIT = 40 * 2**20
BF16 = jnp.bfloat16
F32 = jnp.float32

AROUND = [(dy, dx) for dy in (-1, 0, 1) for dx in (-1, 0, 1)]
ROWS = INSTR * len(AROUND)
COLS = ROWS + len(AROUND)


def shifted(value, axis, steps, wraps=True):
    count = lax.axis_size(axis)
    pairs = [(source, (source + steps) % count) for source in range(count)]
    if not wraps:
        pairs = [pair for pair in pairs if pair[1] == pair[0] + steps]
    return lax.ppermute(value, axis, pairs)


def rectangles(lat_cells, lon_cells):
    lat = {-1: [(lat_cells - HLAT, HLAT)], 1: [(0, HLAT)]}
    lat[0] = [(0, HLAT), (HLAT, lat_cells - WLAT), (lat_cells - HLAT, HLAT)]
    lon = {-1: [(lon_cells - HLON, HLON)], 1: [(0, HLON)]}
    lon[0] = [(0, HLON), (HLON, lon_cells - WLON), (lon_cells - HLON, HLON)]
    return [
        [(top, high, left, wide) for top, high in lat[dy] for left, wide in lon[dx]]
        for dy, dx in AROUND
    ]


def tokens_of(part):
    return part[1] * part[3] * LEV


def padded(count):
    return -(-count // 8) * 8


def gelu(x):
    return jax.nn.gelu(x)


def normalise(wide, gain):
    average = jnp.mean(wide, axis=-1, keepdims=True)
    centred = wide - average
    spread = jnp.mean(centred * centred, axis=-1, keepdims=True)
    return centred * lax.rsqrt(spread + 1e-05) * gain


def dot(a, b):
    return jnp.dot(a, b, preferred_element_type=F32)


def dot_nt(a, b):
    return lax.dot_general(a, b, (((1,), (1,)), ((), ())), preferred_element_type=F32)


def with_ones(tensor):
    ones = jnp.ones((tensor.shape[0], PAD - tensor.shape[1]), F32)
    return jnp.concatenate([tensor, ones], axis=1).astype(BF16)


def below(*pieces):
    return jnp.concatenate(pieces, axis=0) if len(pieces) > 1 else pieces[0]


def pack_kernel(
    values_ref, cell_ref, tag_ref, count_ref, out_ref, values, cells, tags, held, sem, *, lon_cells
):
    tiles_lon, tiles_lat, capacity, _ = values_ref.shape
    copies = [
        pltpu.make_async_copy(cell_ref, cells, sem.at[0]),
        pltpu.make_async_copy(tag_ref, tags, sem.at[1]),
        pltpu.make_async_copy(count_ref, held, sem.at[2]),
        pltpu.make_async_copy(values_ref, values, sem.at[3]),
    ]
    for copy in copies:
        copy.start()
    for copy in copies[:3]:
        copy.wait()
    counts = below(*[held[tile : tile + 1, :] for tile in range(tiles_lat) for _ in range(capacity)])
    cell = cells[...]
    slot = lax.broadcasted_iota(jnp.int32, cell.shape, 0) % capacity
    row = cell // lon_cells
    fields = [jnp.where(slot < counts, row, 255), cell - row * lon_cells, tags[...]]
    rows, columns, kinds = (field.astype(F32) for field in fields)
    lane = lax.broadcasted_iota(jnp.int32, (cell.shape[0], LANES), 1)
    kind_of = (lane % INSTR).astype(F32)
    marks = [
        ((lane < ROWS) & (lane // INSTR == n)) | (lane == ROWS + n) | (lane == COLS + n)
        for n in range(len(AROUND))
    ]
    turned = []
    for lon in range(tiles_lon):
        meta = jnp.where(kind_of == kinds[:, lon : lon + 1], 1.0, 0.0)
        meta = jnp.where(lane >= ROWS, rows[:, lon : lon + 1], meta)
        meta = jnp.where(lane >= COLS, columns[:, lon : lon + 1], meta)
        turns = {0: meta}
        for dy in (-1, 1):
            by = dy * capacity % meta.shape[0]
            turns[dy] = below(meta[by:], meta[:by])
        turned.append(turns)
    for lon in range(tiles_lon):
        meta = jnp.zeros(lane.shape, F32)
        for mark, (dy, dx) in zip(marks, AROUND):
            meta = jnp.where(mark, turned[(lon + dx) % tiles_lon][dy], meta)
        out_ref[lon, :, len(AROUND)] = meta.astype(BF16).reshape(tiles_lat, capacity, LANES)
    copies[3].wait()
    for n, (dy, dx) in enumerate(AROUND):
        spans = {0: [(0, tiles_lat)], 1: [(0, tiles_lat - 1), (tiles_lat - 1, tiles_lat)]}
        spans[-1] = [(0, 1), (1, tiles_lat)]

        def copy_tiles(lon, n=n, dx=dx, dy=dy, spans=spans[dy]):
            source = lax.rem(lon + dx + tiles_lon, tiles_lon)
            for low, end in spans:
                first = (low + dy) % tiles_lat
                out_ref[lon, low:end, n] = values[source, first : first + end - low]

        if tiles_lon <= 8:
            for lon in range(tiles_lon):
                copy_tiles(lon)
        else:
            pl.loop(0, tiles_lon)(copy_tiles)


def packed(record_values, record_cell, record_instrument, block_counts, lon_cells):
    tiles_lon, tiles_lat, capacity, wide = record_values.shape
    anywhere = pl.BlockSpec(memory_space=pltpu.HBM)
    ints = pltpu.VMEM((tiles_lat * capacity, tiles_lon), jnp.int32)
    shape = (tiles_lon, tiles_lat, len(AROUND) + 1, capacity, wide)
    out = pl.pallas_call(
        functools.partial(pack_kernel, lon_cells=lon_cells),
        out_shape=jax.ShapeDtypeStruct(shape, BF16),
        in_specs=[anywhere] * 4,
        out_specs=pl.BlockSpec(memory_space=pltpu.VMEM),
        scratch_shapes=[
            pltpu.VMEM(record_values.shape, BF16),
            ints,
            ints,
            pltpu.VMEM((tiles_lat, tiles_lon), jnp.int32),
            pltpu.SemaphoreType.DMA((4,)),
        ],
        compiler_params=pltpu.CompilerParams(vmem_limit_bytes=56 * 2**20),
    )(
        record_values,
        record_cell.transpose(1, 2, 0).reshape(-1, tiles_lon),
        record_instrument.transpose(1, 2, 0).reshape(-1, tiles_lon),
        block_counts.T,
    )
    return out.reshape((-1,) + shape[2:])


def token_codes(part, lon_cells):
    top, high, left, wide = part
    count = tokens_of(part)
    place = lax.broadcasted_iota(jnp.int32, (padded(count), LANES), 0)
    code = place + (top * lon_cells + left) * LEV
    for row in range(1, high):
        step = (lon_cells - wide) * LEV
        code = code + jnp.where(place >= row * wide * LEV, step, 0)
    return jnp.where(place < count, code, -8).astype(F32)


def block_kernel(
    plan,
    scalars_ref,
    recv_ref,
    north_ref,
    south_ref,
    west_ref,
    east_ref,
    back_ref,
    first_ref,
    table_ref,
    lift_ref,
    gain_one_ref,
    attn_ref,
    mix_ref,
    gain_two_ref,
    up_ref,
    down_ref,
    out_ref,
):
    sources, _, capacity, _ = recv_ref.shape
    lat_cells, lon_cells, _, width = back_ref.shape
    chunk = min(CHUNK, sources)
    slots = chunk * capacity

    first, table, lift = first_ref[...], table_ref[...].astype(F32), lift_ref[...]
    table = below(*[table] * (LANES // INSTR)).astype(BF16)
    lane = lax.broadcasted_iota(jnp.int32, (16, LANES), 1)
    sub = lax.broadcasted_iota(jnp.int32, (16, LANES), 0)
    weigh = jnp.where(lane == ROWS + sub, float(lon_cells * LEV), 0.0)
    weigh = jnp.where(lane == COLS + sub, float(LEV), weigh).astype(BF16)
    codes = [below(*[token_codes(part, lon_cells) for part in parts]) for parts in plan]

    def scatter(begin):
        meta = recv_ref[pl.ds(begin, chunk), len(AROUND)].reshape(slots, LANES)
        records = below(
            *[
                recv_ref[pl.ds(begin, chunk), n].reshape(slots, LANES)
                for n in range(len(AROUND))
            ]
        )
        lane = lax.broadcasted_iota(jnp.int32, meta.shape, 1) // INSTR
        wide = meta.astype(F32)
        chosen = below(*[jnp.where(lane == n, wide, 0.0) for n in range(len(AROUND))]).astype(BF16)
        encoded = gelu(dot_nt(records, first) + dot(chosen, table)).astype(BF16)
        lifted = gelu(dot(encoded, lift))
        tokens = dot_nt(weigh, meta)
        sums = []
        for n in range(len(AROUND)):
            part = lifted[n * slots : (n + 1) * slots]
            part = with_ones(
                below(*[part[:, level * width : (level + 1) * width] for level in range(LEV)])
            )
            token = tokens[n : n + 1]
            token = jnp.concatenate([token + float(level) for level in range(LEV)], axis=1)
            if token.shape[1] == LANES:
                hot = codes[n] == token
            else:
                hot = codes[n][:, :1] == token
            sums.append(dot(jnp.where(hot, 1.0, 0.0).astype(BF16), part))
        return below(*sums)

    sums = scatter(0)
    if sources > chunk:
        sums = lax.fori_loop(
            1, sources // chunk, lambda step, total: total + scatter(step * chunk), sums
        )

    pieces, spans, start = [], [], 0
    for (dy, dx), parts in zip(AROUND, plan):
        for part in parts:
            top, high, left, wide = part
            count = tokens_of(part)
            if dx:
                ref = west_ref if dx < 0 else east_ref
                top = {-1: 0, 0: top + HLAT, 1: lat_cells + HLAT}[dy]
                left = 0
            elif dy:
                ref, top = (north_ref, 0) if dy < 0 else (south_ref, 0)
            else:
                ref = back_ref
            piece = ref[top : top + high, left : left + wide].reshape(count, width).astype(F32)
            full = padded(count)
            if full > count:
                piece = below(piece, jnp.zeros((full - count, width), F32))
            pieces.append(piece)
            spans.append((start, count, full))
            start += full
    share = 1.0 / (1.0 + sums[:, width : width + 1])
    latent = ((below(*pieces) + sums[:, :width]) * share).astype(BF16).astype(F32)
    normed = normalise(latent, gain_one_ref[...].astype(F32))

    def piece_of(tile, number):
        at = sum(len(parts) for parts in plan[:tile]) + number
        start, count, _ = spans[at]
        return normed[start : start + count]

    own = 4
    begin = spans[sum(len(parts) for parts in plan[:own])][0]
    groups = [padded(tokens_of(part)) for part in plan[own]]
    end = begin + sum(groups)
    windows = []
    for i, dy in enumerate((-1, 0, 1)):
        for j, dx in enumerate((-1, 0, 1)):
            window = [piece_of(own, 3 * i + j)]
            if dy:
                window.append(piece_of(3 * (dy + 1) + 1, j))
            if dx:
                window.append(piece_of(3 + dx + 1, i))
            if dy and dx:
                window.append(piece_of(3 * (dy + 1) + dx + 1, 0))
            windows.append(window)
    tokens = below(*[piece for window in windows for piece in window]).astype(BF16)
    weight = attn_ref[...]
    head = width // HEADS
    keys = dot(tokens, weight[:, width : 2 * width]).astype(BF16)
    values = with_ones(dot(tokens, weight[:, 2 * width :]))
    query = dot(normed[begin:end].astype(BF16), weight[:, :width]) * head ** (-0.5)

    head_of = lax.broadcasted_iota(jnp.int32, (1, width), 1) // head
    many = WLAT * WLON * LEV
    corner = HLAT * HLON * LEV
    key = lax.broadcasted_iota(jnp.int32, (1, many), 1)
    mixed, start = [], 0
    for w, rows in enumerate(groups):
        part = query[start : start + rows]
        stacked = below(*[jnp.where(head_of == h, part, 0.0) for h in range(HEADS)]).astype(BF16)
        scores = dot_nt(stacked, keys[w * many : (w + 1) * many])
        if w // 3 != 1:
            if w % 3 == 1:
                inside = key < 2 * corner
            else:
                inside = (key < corner) | ((key >= 2 * corner) & (key < 3 * corner))
            scores = jnp.where(inside | (scalars_ref[w // 3] == 0), scores, -1e30)
        largest = jnp.max(scores, axis=-1, keepdims=True)
        raised = jnp.exp(scores - largest).astype(BF16)
        product = dot(raised, values[w * many : (w + 1) * many])
        product = product[:, :width] * (1.0 / product[:, width : width + 1])
        total = jnp.zeros((rows, width), F32)
        for h in range(HEADS):
            total = jnp.where(head_of == h, product[h * rows : (h + 1) * rows], total)
        mixed.append(total)
        start += rows
    mixed = below(*mixed).astype(BF16)

    after = (latent[begin:end] + dot(mixed, mix_ref[...])).astype(BF16).astype(F32)
    normed_two = normalise(after, gain_two_ref[...].astype(F32)).astype(BF16)
    hidden = gelu(dot(normed_two, up_ref[...])).astype(BF16)
    result = after + dot_nt(hidden, down_ref[...])
    start = 0
    for part, rows in zip(plan[own], groups):
        top, high, left, wide = part
        piece = result[start : start + tokens_of(part)].astype(BF16)
        out_ref[top : top + high, left : left + wide] = piece.reshape(high, wide, LEV, width)
        start += rows


def local(
    record_values,
    record_cell,
    record_instrument,
    block_counts,
    background,
    input_weight,
    instrument_table,
    lift_weight,
    first_gain,
    attn_weight,
    mix_weight,
    second_gain,
    up_weight,
    down_weight,
):
    lat_cells, lon_cells, _, width = background.shape
    tiles_lat = record_values.shape[1]

    north = shifted(background[lat_cells - HLAT :], "lat", 1, wraps=False)
    south = shifted(background[:HLAT], "lat", -1, wraps=False)
    sent = packed(record_values, record_cell, record_instrument, block_counts, lon_cells)
    sent, north, south = lax.optimization_barrier((sent, north, south))
    received = lax.all_to_all(sent, ("lon", "lat"), split_axis=0, concat_axis=0, tiled=True)

    def columns(low, end):
        return jnp.concatenate(
            [north[:, low:end], background[:, low:end], south[:, low:end]], axis=0
        )

    west = shifted(columns(lon_cells - HLON, lon_cells), "lon", 1)
    east = shifted(columns(0, HLON), "lon", -1)

    lat = lax.axis_index("lat")
    scalars = jnp.stack([lat == 0, lat < 0, lat == tiles_lat - 1]).astype(jnp.int32)
    vmem = pl.BlockSpec(memory_space=pltpu.VMEM)
    return pl.pallas_call(
        functools.partial(block_kernel, rectangles(lat_cells, lon_cells)),
        out_shape=jax.ShapeDtypeStruct(background.shape, BF16),
        in_specs=[pl.BlockSpec(memory_space=pltpu.SMEM)] + [vmem] * 15,
        out_specs=vmem,
        compiler_params=pltpu.CompilerParams(vmem_limit_bytes=LIMIT),
    )(
        scalars,
        received,
        north,
        south,
        west,
        east,
        background,
        input_weight.T,
        instrument_table,
        lift_weight,
        first_gain.reshape(1, width),
        attn_weight,
        mix_weight,
        second_gain.reshape(1, width),
        up_weight,
        down_weight.T,
    )


def solution(mesh):
    placed = (
        P("lon", "lat", None, None),
        P("lon", "lat", None),
        P("lon", "lat", None),
        P("lon", "lat"),
        P("lat", "lon", None, None),
        P(),
        P(),
        P(),
        P(),
        P(),
        P(),
        P(),
        P(),
        P(),
    )
    return jax.shard_map(
        local, mesh=mesh, in_specs=placed, out_specs=P("lat", "lon", None, None), check_vma=False
    )
```

time: 43.1 us -> 35.4 us (0.82)
  waiting for transfers between devices: 14.7 us -> 5.61 us
  starting transfers between devices: 13.7 us -> 15.5 us
  local copies, waits for them, and re-layouts: 3.06 us -> 2.58 us
    all_to_all x1, waiting for transfers between devices: 7.27 us -> 2.57 us  [local(): lax.all_to_all(sent, ('lon', 'lat'), split_axis=0, concat_axis=0, tiled=T...]
    ppermute x4, waiting for transfers between devices: 7.45 us -> 3.04 us  [shifted(): return lax.ppermute(value, axis, pairs)]
    ppermute x4, starting transfers between devices: 6.36 us -> 9.6 us  [shifted(): return lax.ppermute(value, axis, pairs)]
    unnamed x24 -> x20, local copies, waits for them, and re-layouts: 2.89 us -> 1.34 us
    all_to_all x1, starting transfers between devices: 7.3 us -> 5.89 us  [local(): lax.all_to_all(sent, ('lon', 'lat'), split_axis=0, concat_axis=0, tiled=T...]
    slice x2 -> x3, local copies, waits for them, and re-layouts: 0.15 us -> 1.23 us  [the longest x1 1.07 us: local(): south = shifted(background[:HLAT], 'lat', -1, wraps=False)]
    pallas_call x2 -> x1, Pallas kernels: 9.36 us -> 9.18 us  [local(): pl.pallas_call(functools.partial(block_kernel, rectangles(lat_cells, lon_...]
  transfers between devices with their start and end apart: 5 -> 5, of which waited for: 4 -> 2; matrix products, arithmetic and copies ran while one was open for 1% -> 2% of each run, Pallas kernels for 0% -> 5%
where the time goes in v6:
time: 35.4 us; the launch traced here: 35.1 us
  starting transfers between devices  15.5 us (44%)
  Pallas kernels  10.8 us (31%)
  waiting for transfers between devices  5.61 us (16%)
  local copies, waits for them, and re-layouts  2.58 us (7%)
  other arithmetic  0.42 us (1%)
    ppermute x4, starting transfers between devices, shifted(): return lax.ppermute(value, axis, pairs)  9.6 us
    pallas_call x1, Pallas kernels, local(): pl.pallas_call(functools.partial(block_kernel, rectangles(lat_cells, lon_...  9.18 us
    all_to_all x1, starting transfers between devices, local(): lax.all_to_all(sent, ('lon', 'lat'), split_axis=0, concat_axis=0, tiled=T...  5.89 us
    ppermute x4, waiting for transfers between devices, shifted(): return lax.ppermute(value, axis, pairs)  3.04 us
    all_to_all x1, waiting for transfers between devices, local(): lax.all_to_all(sent, ('lon', 'lat'), split_axis=0, concat_axis=0, tiled=T...  2.57 us
    pallas_call x1, Pallas kernels, packed(): pl.pallas_call(functools.partial(pack_kernel, lon_cells=lon_cells), out_s...  1.64 us
    unnamed x20, local copies, waits for them, and re-layouts  1.34 us
    slice x1, local copies, waits for them, and re-layouts, local(): south = shifted(background[:HLAT], 'lat', -1, wraps=False)  1.07 us
  transfers between devices with their start and end apart: 5, of which 2 were waited for; matrix products, arithmetic and copies ran while one was open for 2% of the time, Pallas kernels for 5%

profile of v6, /device:TPU:0, one launch (start us, length us, event | category | flops | bytes accessed | tf_op | source)
XLA Modules:
  0.0 35.1 jit_solution(10423100270914533865)
XLA Ops:
  0.0 0.0 copy-start
  0.0 1.1 %fusion.1 = (bf16[3,24,2,192]{3,2,1,0:T(2,128)(2,1)S(1)}, bf16[3,24,2,192]{3,2,1,0:T(2,128)(2,1)S(1)}) fusion(bf16[12,24,2,192]{3,2,1,0:T(2,128)(2,1)} %back_ref.1), kind=kLoop, calls=%fused_computation.4 | loop fusion | bytes 221184 | tf_op jit(solution)/shard_map/slice | solution.py:358
  1.1 1.3 %collective-permute-start.1 = (bf16[3,24,2,192]{3,2,1,0:T(2,128)(2,1)S(1)}, bf16[3,24,2,192]{3,2,1,0:T(2,128)(2,1)S(1)}, u32[]{:S(2)}, u32[]{:S(2)}) collective-permute-start(bf16[3,24,2,192]{3,2,1,0:T(2,128)(2,1)S(1)} %get-tuple-element.13), channel_id=1, source_target_pairs={{1,0},{2,1},{3,2},{5,4},{6,5},{7,6},{9,8},{10,9},{11,10},{13,12},{... | collective-permute-start | bytes 165896 | tf_op jit(solution)/shard_map/ppermute | solution.py:34
  2.4 5.6 %collective-permute-start = (bf16[3,24,2,192]{3,2,1,0:T(2,128)(2,1)S(1)}, bf16[3,24,2,192]{3,2,1,0:T(2,128)(2,1)S(1)}, u32[]{:S(2)}, u32[]{:S(2)}) collective-permute-start(bf16[3,24,2,192]{3,2,1,0:T(2,128)(2,1)S(1)} %get-tuple-element.14), channel_id=1, source_target_pairs={{0,1},{1,2},{2,3},{4,5},{5,6},{6,7},{8,9},{9,10},{10,11},{12,13},{... | collective-permute-start | bytes 165896 | tf_op jit(solution)/shard_map/ppermute | solution.py:34
  7.9 0.0 copy-done
  8.0 0.1 fusion
  8.1 0.0 copy-start.7
  8.1 0.0 copy-start.8
  8.1 0.6 %copy-done.8 = bf16[192]{0:T(256)(128)(2,1)S(1)} copy-done((bf16[192]{0:T(256)(128)(2,1)S(1)}, bf16[192]{0:T(256)(128)(2,1)}, u32[]{:S(2)}) %copy-start.8) | copy-done | bytes 408
  8.7 0.0 copy-start.9
  8.7 0.6 %copy-done.9 = bf16[192]{0:T(256)(128)(2,1)S(1)} copy-done((bf16[192]{0:T(256)(128)(2,1)S(1)}, bf16[192]{0:T(256)(128)(2,1)}, u32[]{:S(2)}) %copy-start.9) | copy-done | bytes 408
  9.4 0.0 copy-start.4
  9.4 0.0 copy-start.6
  9.4 1.6 %shard_map.136 = bf16[8,4,10,2,128]{4,3,2,1,0:T(2,128)(2,1)} custom-call(bf16[8,4,2,128]{3,2,1,0:T(2,128)(2,1)} %values_ref.1, s32[8,8]{1,0:T(8,128)} %bitcast.16, s32[8,8]{1,0:T(8,128)} %bitcast.17, s32[4,8]{1,0:T(4,128)} %bitcast.18), custom_call_target="tpu_custom_call" | custom-call | tf_op jit(solution)/shard_map/pallas_call | solution.py:148
  11.1 0.0 collective-permute-done.1.south_ref
  11.1 0.0 collective-permute-done.north_ref
  11.1 0.0 copy-start.3
  11.1 0.0 copy-start.5
  11.1 5.9 %all-to-all-start = ((bf16[32,10,2,128]{3,2,1,0:T(2,128)(2,1)}), bf16[32,10,2,128]{3,2,1,0:T(2,128)(2,1)S(1)}, u32[]{:S(2)}, u32[]{:S(2)}) async-start(bf16[32,10,2,128]{3,2,1,0:T(2,128)(2,1)} %bitcast.15), calls=%async_computation | async-start | bytes 327680 | tf_op jit(solution)/shard_map/all_to_all | solution.py:361
  17.0 0.0 copy-start.1
  17.0 0.0 copy-start.2
  17.0 0.1 fusion.2
  17.1 0.2 pad_maximum_fusion
  17.3 0.3 collective-permute-start.2
  17.6 0.2 pad_maximum_fusion.1
  17.7 2.4 %collective-permute-start.3 = (bf16[18,6,2,192]{3,2,1,0:T(2,128)(2,1)S(1)}, bf16[18,6,2,192]{3,2,1,0:T(2,128)(2,1)S(1)}, u32[]{:S(2)}, u32[]{:S(2)}) collective-permute-start(bf16[18,6,2,192]{3,2,1,0:T(2,128)(2,1)S(1)} %pad_maximum_fusion.1), channel_id=1, source_target_pairs={{0,28},{4,0},{8,4},{12,8},{16,12},{20,16},{24,20},{28,24},{1,29},{... | collective-permute-start | bytes 248840 | tf_op jit(solution)/shard_map/ppermute | solution.py:34
  20.2 0.1 add_convert_fusion.scalars_ref
  20.3 3.0 %collective-permute-done.2.west_ref = bf16[18,6,2,192]{3,2,1,0:T(2,128)(2,1)S(1)} collective-permute-done((bf16[18,6,2,192]{3,2,1,0:T(2,128)(2,1)S(1)}, bf16[18,6,2,192]{3,2,1,0:T(2,128)(2,1)S(1)}, u32[]{:S(2)}, u32[]{:S(2)}) %collective-permute-start.2) | collective-permute-done | bytes 82976 | tf_op jit(solution)/shard_map/ppermute | solution.py:34
  23.3 0.0 collective-permute-done.3.east_ref
  23.3 2.6 %all-to-all-done.recv_ref = bf16[32,10,2,128]{3,2,1,0:T(2,128)(2,1)S(1)} async-done(((bf16[32,10,2,128]{3,2,1,0:T(2,128)(2,1)}), bf16[32,10,2,128]{3,2,1,0:T(2,128)(2,1)S(1)}, u32[]{:S(2)}, u32[]{:S(2)}) %all-to-all-start) | async-done | bytes 163872 | tf_op jit(solution)/shard_map/all_to_all | solution.py:361
  25.9 0.0 copy-done.7
  25.9 0.0 copy-done.4
  25.9 0.0 copy-done.6
  25.9 0.0 copy-done.3
  25.9 0.0 copy-done.5
  25.9 0.0 copy-done.1
  25.9 0.0 copy-done.2
  25.9 9.2 %shard_map.137 = bf16[12,24,2,192]{3,2,1,0:T(2,128)(2,1)} custom-call(s32[3]{0:T(128)S(1)} %add_convert_fusion.scalars_ref, bf16[32,10,2,128]{3,2,1,0:T(2,128)(2,1)S(1)} %all-to-all-done.recv_ref, bf16[3,24,2,192]{3,2,1,0:T(2,128)(2,1)S(1)} %collective-permute-done.north_ref, bf16[3,24,2,192]{3,2,1,0:T(2,128)(2,1)S(1)} %collective-permute-done.1.south_ref, ...), custom_call_target="tpu_custom_call" | custom-call | tf_op jit(solution)/shard_map/pallas_call | solution.py:374
  (2 shorter events, 0.0 us)
Async XLA Ops:
  0.0 7.9 %copy-start = (bf16[12,24,2,192]{3,2,1,0:T(2,128)(2,1)S(1)}, bf16[12,24,2,192]{3,2,1,0:T(2,128)(2,1)}, u32[]{:S(2)}) copy-start(bf16[12,24,2,192]{3,2,1,0:T(2,128)(2,1)} %back_ref.1) | copy-start | bytes 663556
  1.1 10.0 %collective-permute-start.1 = (bf16[3,24,2,192]{3,2,1,0:T(2,128)(2,1)S(1)}, bf16[3,24,2,192]{3,2,1,0:T(2,128)(2,1)S(1)}, u32[]{:S(2)}, u32[]{:S(2)}) collective-permute-start(bf16[3,24,2,192]{3,2,1,0:T(2,128)(2,1)S(1)} %get-tuple-element.13), channel_id=1, source_target_pairs={{1,0},{2,1},{3,2},{5,4},{6,5},{7,6},{9,8},{10,9},{11,10},{13,12},{... | collective-permute-start | bytes 165896 | tf_op jit(solution)/shard_map/ppermute | solution.py:34
  2.4 8.7 %collective-permute-start = (bf16[3,24,2,192]{3,2,1,0:T(2,128)(2,1)S(1)}, bf16[3,24,2,192]{3,2,1,0:T(2,128)(2,1)S(1)}, u32[]{:S(2)}, u32[]{:S(2)}) collective-permute-start(bf16[3,24,2,192]{3,2,1,0:T(2,128)(2,1)S(1)} %get-tuple-element.14), channel_id=1, source_target_pairs={{0,1},{1,2},{2,3},{4,5},{5,6},{6,7},{8,9},{9,10},{10,11},{12,13},{... | collective-permute-start | bytes 165896 | tf_op jit(solution)/shard_map/ppermute | solution.py:34
  8.1 17.8 %copy-start.7 = (bf16[8,192]{1,0:T(8,128)(2,1)S(1)}, bf16[8,192]{1,0:T(8,128)(2,1)}, u32[]{:S(2)}) copy-start(bf16[8,192]{1,0:T(8,128)(2,1)} %table_ref.1) | copy-start | bytes 9220
  8.1 0.7 %copy-start.8 = (bf16[192]{0:T(256)(128)(2,1)S(1)}, bf16[192]{0:T(256)(128)(2,1)}, u32[]{:S(2)}) copy-start(bf16[192]{0:T(256)(128)(2,1)} %param.22) | copy-start | bytes 1156
  8.7 0.7 %copy-start.9 = (bf16[192]{0:T(256)(128)(2,1)S(1)}, bf16[192]{0:T(256)(128)(2,1)}, u32[]{:S(2)}) copy-start(bf16[192]{0:T(256)(128)(2,1)} %param.25) | copy-start | bytes 1156
  9.4 16.5 %copy-start.4 = (bf16[192,384]{1,0:T(8,128)(2,1)S(1)}, bf16[192,384]{1,0:T(8,128)(2,1)}, u32[]{:S(2)}) copy-start(bf16[192,384]{1,0:T(8,128)(2,1)} %lift_ref.1) | copy-start | bytes 442372
  9.4 16.5 %copy-start.6 = (bf16[128,192]{0,1:T(8,128)(2,1)S(1)}, bf16[128,192]{0,1:T(8,128)(2,1)}, u32[]{:S(2)}) copy-start(bf16[128,192]{0,1:T(8,128)(2,1)} %param.19) | copy-start | bytes 147460
  11.1 14.8 %copy-start.3 = (bf16[192,576]{1,0:T(8,128)(2,1)S(1)}, bf16[192,576]{1,0:T(8,128)(2,1)}, u32[]{:S(2)}) copy-start(bf16[192,576]{1,0:T(8,128)(2,1)} %attn_ref.1) | copy-start | bytes 663556
  11.1 14.8 %copy-start.5 = (bf16[192,192]{1,0:T(8,128)(2,1)S(1)}, bf16[192,192]{1,0:T(8,128)(2,1)}, u32[]{:S(2)}) copy-start(bf16[192,192]{1,0:T(8,128)(2,1)} %mix_ref.1) | copy-start | bytes 221188
  11.1 14.8 %all-to-all-start = ((bf16[32,10,2,128]{3,2,1,0:T(2,128)(2,1)}), bf16[32,10,2,128]{3,2,1,0:T(2,128)(2,1)S(1)}, u32[]{:S(2)}, u32[]{:S(2)}) async-start(bf16[32,10,2,128]{3,2,1,0:T(2,128)(2,1)} %bitcast.15), calls=%async_computation | async-start | bytes 327680 | tf_op jit(solution)/shard_map/all_to_all | solution.py:361
  17.0 8.9 %copy-start.1 = (bf16[192,768]{1,0:T(8,128)(2,1)S(1)}, bf16[192,768]{1,0:T(8,128)(2,1)}, u32[]{:S(2)}) copy-start(bf16[192,768]{1,0:T(8,128)(2,1)} %up_ref.1) | copy-start | bytes 884740
  17.0 8.9 %copy-start.2 = (bf16[768,192]{0,1:T(8,128)(2,1)S(1)}, bf16[768,192]{0,1:T(8,128)(2,1)}, u32[]{:S(2)}) copy-start(bf16[768,192]{0,1:T(8,128)(2,1)} %param.27) | copy-start | bytes 884740
  17.3 6.0 %collective-permute-start.2 = (bf16[18,6,2,192]{3,2,1,0:T(2,128)(2,1)S(1)}, bf16[18,6,2,192]{3,2,1,0:T(2,128)(2,1)S(1)}, u32[]{:S(2)}, u32[]{:S(2)}) collective-permute-start(bf16[18,6,2,192]{3,2,1,0:T(2,128)(2,1)S(1)} %pad_maximum_fusion), channel_id=1, source_target_pairs={{0,4},{4,8},{8,12},{12,16},{16,20},{20,24},{24,28},{28,0},{1,5},{5... | collective-permute-start | bytes 248840 | tf_op jit(solution)/shard_map/ppermute | solution.py:34
  17.7 5.6 %collective-permute-start.3 = (bf16[18,6,2,192]{3,2,1,0:T(2,128)(2,1)S(1)}, bf16[18,6,2,192]{3,2,1,0:T(2,128)(2,1)S(1)}, u32[]{:S(2)}, u32[]{:S(2)}) collective-permute-start(bf16[18,6,2,192]{3,2,1,0:T(2,128)(2,1)S(1)} %pad_maximum_fusion.1), channel_id=1, source_target_pairs={{0,28},{4,0},{8,4},{12,8},{16,12},{20,16},{24,20},{28,24},{1,29},{... | collective-permute-start | bytes 248840 | tf_op jit(solution)/shard_map/ppermute | solution.py:34

commit v7 on v6

--- a/solution.py
+++ b/solution.py
@@ -82,14 +82,39 @@
 
 
 def pack_kernel(
-    values_ref, cell_ref, tag_ref, count_ref, out_ref, values, cells, tags, held, sem, *, lon_cells
+    values_ref,
+    cell_ref,
+    tag_ref,
+    count_ref,
+    back_ref,
+    out_ref,
+    up_ref,
+    down_ref,
+    left_ref,
+    right_ref,
+    values,
+    cells,
+    tags,
+    held,
+    sem,
 ):
     tiles_lon, tiles_lat, capacity, _ = values_ref.shape
+    lat_cells, lon_cells = back_ref.shape[:2]
+    strips = [
+        (back_ref.at[:HLAT], up_ref),
+        (back_ref.at[lat_cells - HLAT :], down_ref),
+        (back_ref.at[:, :HLON], left_ref),
+        (back_ref.at[:, lon_cells - HLON :], right_ref),
+    ]
     copies = [
         pltpu.make_async_copy(cell_ref, cells, sem.at[0]),
         pltpu.make_async_copy(tag_ref, tags, sem.at[1]),
         pltpu.make_async_copy(count_ref, held, sem.at[2]),
         pltpu.make_async_copy(values_ref, values, sem.at[3]),
+    ]
+    copies += [
+        pltpu.make_async_copy(source, strip, sem.at[4 + n])
+        for n, (source, strip) in enumerate(strips)
     ]
     for copy in copies:
         copy.start()
@@ -138,24 +163,29 @@
                 copy_tiles(lon)
         else:
             pl.loop(0, tiles_lon)(copy_tiles)
-
-
-def packed(record_values, record_cell, record_instrument, block_counts, lon_cells):
+    for copy in copies[4:]:
+        copy.wait()
+
+
+def packed(record_values, record_cell, record_instrument, block_counts, background):
     tiles_lon, tiles_lat, capacity, wide = record_values.shape
     anywhere = pl.BlockSpec(memory_space=pltpu.HBM)
     ints = pltpu.VMEM((tiles_lat * capacity, tiles_lon), jnp.int32)
     shape = (tiles_lon, tiles_lat, len(AROUND) + 1, capacity, wide)
-    out = pl.pallas_call(
-        functools.partial(pack_kernel, lon_cells=lon_cells),
-        out_shape=jax.ShapeDtypeStruct(shape, BF16),
-        in_specs=[anywhere] * 4,
-        out_specs=pl.BlockSpec(memory_space=pltpu.VMEM),
+    lat_cells, lon_cells, levels, width = background.shape
+    across = jax.ShapeDtypeStruct((HLAT, lon_cells, levels, width), BF16)
+    along = jax.ShapeDtypeStruct((lat_cells, HLON, levels, width), BF16)
+    out, *strips = pl.pallas_call(
+        pack_kernel,
+        out_shape=[jax.ShapeDtypeStruct(shape, BF16), across, across, along, along],
+        in_specs=[anywhere] * 5,
+        out_specs=[pl.BlockSpec(memory_space=pltpu.VMEM)] * 5,
         scratch_shapes=[
             pltpu.VMEM(record_values.shape, BF16),
             ints,
             ints,
             pltpu.VMEM((tiles_lat, tiles_lon), jnp.int32),
-            pltpu.SemaphoreType.DMA((4,)),
+            pltpu.SemaphoreType.DMA((8,)),
         ],
         compiler_params=pltpu.CompilerParams(vmem_limit_bytes=56 * 2**20),
     )(
@@ -163,8 +193,9 @@
         record_cell.transpose(1, 2, 0).reshape(-1, tiles_lon),
         record_instrument.transpose(1, 2, 0).reshape(-1, tiles_lon),
         block_counts.T,
+        background,
     )
-    return out.reshape((-1,) + shape[2:])
+    return out.reshape((-1,) + shape[2:]), *strips
 
 
 def token_codes(part, lon_cells):
@@ -178,33 +209,22 @@
     return jnp.where(place < count, code, -8).astype(F32)
 
 
-def block_kernel(
-    plan,
-    scalars_ref,
-    recv_ref,
-    north_ref,
-    south_ref,
-    west_ref,
-    east_ref,
-    back_ref,
-    first_ref,
-    table_ref,
-    lift_ref,
-    gain_one_ref,
-    attn_ref,
-    mix_ref,
-    gain_two_ref,
-    up_ref,
-    down_ref,
-    out_ref,
-):
+def column_entries(plan, columns):
+    own = [(4, 3 * i + j) for i in range(3) for j in columns]
+    around = [(tile, j) for tile in (1, 7) for j in columns]
+    for j in columns:
+        if j != 1:
+            around += [(3 + j, i) for i in range(3)] + [(j, 0), (6 + j, 0)]
+    return own + around
+
+
+def scattered(recv_ref, first_ref, table_ref, lift_ref, plan, lon_cells):
     sources, _, capacity, _ = recv_ref.shape
-    lat_cells, lon_cells, _, width = back_ref.shape
+    width = table_ref.shape[1]
     chunk = min(CHUNK, sources)
     slots = chunk * capacity
-
-    first, table, lift = first_ref[...], table_ref[...].astype(F32), lift_ref[...]
-    table = below(*[table] * (LANES // INSTR)).astype(BF16)
+    first, lift = first_ref[...], lift_ref[...]
+    table = below(*[table_ref[...].astype(F32)] * (LANES // INSTR)).astype(BF16)
     lane = lax.broadcasted_iota(jnp.int32, (16, LANES), 1)
     sub = lax.broadcasted_iota(jnp.int32, (16, LANES), 0)
     weigh = jnp.where(lane == ROWS + sub, float(lon_cells * LEV), 0.0)
@@ -238,80 +258,86 @@
             else:
                 hot = codes[n][:, :1] == token
             sums.append(dot(jnp.where(hot, 1.0, 0.0).astype(BF16), part))
-        return below(*sums)
+        return tuple(sums)
 
     sums = scatter(0)
     if sources > chunk:
         sums = lax.fori_loop(
-            1, sources // chunk, lambda step, total: total + scatter(step * chunk), sums
+            1,
+            sources // chunk,
+            lambda step, total: tuple(a + b for a, b in zip(total, scatter(step * chunk))),
+            sums,
         )
-
-    pieces, spans, start = [], [], 0
-    for (dy, dx), parts in zip(AROUND, plan):
-        for part in parts:
-            top, high, left, wide = part
-            count = tokens_of(part)
-            if dx:
-                ref = west_ref if dx < 0 else east_ref
-                top = {-1: 0, 0: top + HLAT, 1: lat_cells + HLAT}[dy]
-                left = 0
-            elif dy:
-                ref, top = (north_ref, 0) if dy < 0 else (south_ref, 0)
-            else:
-                ref = back_ref
-            piece = ref[top : top + high, left : left + wide].reshape(count, width).astype(F32)
-            full = padded(count)
-            if full > count:
-                piece = below(piece, jnp.zeros((full - count, width), F32))
-            pieces.append(piece)
-            spans.append((start, count, full))
-            start += full
+    return sums
+
+
+def worked(plan, columns, sums, borders, weights, scalars_ref, put):
+    back_ref, north_ref, south_ref, west_ref, east_ref = borders
+    gain_one_ref, attn_ref, mix_ref, gain_two_ref, up_ref, down_ref = weights
+    lat_cells, width = back_ref.shape[0], back_ref.shape[3]
+    pieces, spans, start = [], {}, 0
+    for tile, number in column_entries(plan, columns):
+        dy, dx = AROUND[tile]
+        part = plan[tile][number]
+        top, high, left, wide = part
+        count = tokens_of(part)
+        if dx:
+            ref = west_ref if dx < 0 else east_ref
+            top, left = {-1: 0, 0: top + HLAT, 1: lat_cells + HLAT}[dy], 0
+        elif dy:
+            ref, top = (north_ref, 0) if dy < 0 else (south_ref, 0)
+        else:
+            ref = back_ref
+        piece = ref[top : top + high, left : left + wide].reshape(count, width).astype(F32)
+        full = padded(count)
+        if full > count:
+            piece = below(piece, jnp.zeros((full - count, width), F32))
+        pieces.append(piece)
+        spans[tile, number] = (start, count)
+        start += full
     share = 1.0 / (1.0 + sums[:, width : width + 1])
     latent = ((below(*pieces) + sums[:, :width]) * share).astype(BF16).astype(F32)
     normed = normalise(latent, gain_one_ref[...].astype(F32))
 
     def piece_of(tile, number):
-        at = sum(len(parts) for parts in plan[:tile]) + number
-        start, count, _ = spans[at]
+        start, count = spans[tile, number]
         return normed[start : start + count]
 
-    own = 4
-    begin = spans[sum(len(parts) for parts in plan[:own])][0]
-    groups = [padded(tokens_of(part)) for part in plan[own]]
-    end = begin + sum(groups)
+    places = [(i, j) for i in range(3) for j in columns]
+    groups = [padded(tokens_of(plan[4][3 * i + j])) for i, j in places]
+    end = sum(groups)
     windows = []
-    for i, dy in enumerate((-1, 0, 1)):
-        for j, dx in enumerate((-1, 0, 1)):
-            window = [piece_of(own, 3 * i + j)]
-            if dy:
-                window.append(piece_of(3 * (dy + 1) + 1, j))
-            if dx:
-                window.append(piece_of(3 + dx + 1, i))
-            if dy and dx:
-                window.append(piece_of(3 * (dy + 1) + dx + 1, 0))
-            windows.append(window)
+    for i, j in places:
+        window = [piece_of(4, 3 * i + j)]
+        if i != 1:
+            window.append(piece_of(3 * i + 1, j))
+        if j != 1:
+            window.append(piece_of(3 + j, i))
+        if i != 1 and j != 1:
+            window.append(piece_of(3 * i + j, 0))
+        windows.append(window)
     tokens = below(*[piece for window in windows for piece in window]).astype(BF16)
     weight = attn_ref[...]
     head = width // HEADS
     keys = dot(tokens, weight[:, width : 2 * width]).astype(BF16)
     values = with_ones(dot(tokens, weight[:, 2 * width :]))
-    query = dot(normed[begin:end].astype(BF16), weight[:, :width]) * head ** (-0.5)
+    query = dot(normed[:end].astype(BF16), weight[:, :width]) * head ** (-0.5)
 
     head_of = lax.broadcasted_iota(jnp.int32, (1, width), 1) // head
     many = WLAT * WLON * LEV
     corner = HLAT * HLON * LEV
     key = lax.broadcasted_iota(jnp.int32, (1, many), 1)
     mixed, start = [], 0
-    for w, rows in enumerate(groups):
+    for w, ((i, j), rows) in enumerate(zip(places, groups)):
         part = query[start : start + rows]
         stacked = below(*[jnp.where(head_of == h, part, 0.0) for h in range(HEADS)]).astype(BF16)
         scores = dot_nt(stacked, keys[w * many : (w + 1) * many])
-        if w // 3 != 1:
-            if w % 3 == 1:
+        if i != 1:
+            if j == 1:
                 inside = key < 2 * corner
             else:
                 inside = (key < corner) | ((key >= 2 * corner) & (key < 3 * corner))
-            scores = jnp.where(inside | (scalars_ref[w // 3] == 0), scores, -1e30)
+            scores = jnp.where(inside | (scalars_ref[i] == 0), scores, -1e30)
         largest = jnp.max(scores, axis=-1, keepdims=True)
         raised = jnp.exp(scores - largest).astype(BF16)
         product = dot(raised, values[w * many : (w + 1) * many])
@@ -323,16 +349,78 @@
         start += rows
     mixed = below(*mixed).astype(BF16)
 
-    after = (latent[begin:end] + dot(mixed, mix_ref[...])).astype(BF16).astype(F32)
+    after = (latent[:end] + dot(mixed, mix_ref[...])).astype(BF16).astype(F32)
     normed_two = normalise(after, gain_two_ref[...].astype(F32)).astype(BF16)
     hidden = gelu(dot(normed_two, up_ref[...])).astype(BF16)
     result = after + dot_nt(hidden, down_ref[...])
     start = 0
-    for part, rows in zip(plan[own], groups):
-        top, high, left, wide = part
+    for (i, j), rows in zip(places, groups):
+        part = plan[4][3 * i + j]
         piece = result[start : start + tokens_of(part)].astype(BF16)
-        out_ref[top : top + high, left : left + wide] = piece.reshape(high, wide, LEV, width)
+        put(part, j, piece.reshape(part[1], part[3], LEV, width))
         start += rows
+
+
+def middle_kernel(
+    plan,
+    scalars_ref,
+    recv_ref,
+    north_ref,
+    south_ref,
+    back_ref,
+    first_ref,
+    table_ref,
+    lift_ref,
+    *refs,
+):
+    *weights, out_ref, rest_ref, held_ref, sem = refs
+    sums = scattered(recv_ref, first_ref, table_ref, lift_ref, plan, back_ref.shape[1])
+
+    def sum_of(tile, number):
+        start = sum(padded(tokens_of(part)) for part in plan[tile][:number])
+        return sums[tile][start : start + padded(tokens_of(plan[tile][number]))]
+
+    rest_ref[...] = below(*[sum_of(*entry) for entry in column_entries(plan, (0, 2))])
+    mine = below(*[sum_of(*entry) for entry in column_entries(plan, (1,))])
+    left, wide = plan[4][4][2:]
+
+    def put(part, _, piece):
+        held_ref[part[0] : part[0] + part[1]] = piece
+
+    borders = (back_ref, north_ref, south_ref, None, None)
+    worked(plan, (1,), mine, borders, weights, scalars_ref, put)
+    copy = pltpu.make_async_copy(held_ref, out_ref.at[:, left : left + wide], sem.at[0])
+    copy.start()
+    copy.wait()
+
+
+def side_kernel(
+    plan,
+    scalars_ref,
+    rest_ref,
+    north_ref,
+    south_ref,
+    west_ref,
+    east_ref,
+    back_ref,
+    *refs,
+):
+    *weights, _, out_ref, held_ref, sem = refs
+
+    def put(part, j, piece):
+        held_ref[j // 2, part[0] : part[0] + part[1]] = piece
+
+    borders = (back_ref, north_ref, south_ref, west_ref, east_ref)
+    worked(plan, (0, 2), rest_ref[...], borders, weights, scalars_ref, put)
+    copies = []
+    for n, number in enumerate((0, 2)):
+        left, wide = plan[4][number][2:]
+        copies.append(
+            pltpu.make_async_copy(held_ref.at[n], out_ref.at[:, left : left + wide], sem.at[n])
+        )
+        copies[n].start()
+    for copy in copies:
+        copy.wait()
 
 
 def local(
@@ -354,47 +442,75 @@
     lat_cells, lon_cells, _, width = background.shape
     tiles_lat = record_values.shape[1]
 
-    north = shifted(background[lat_cells - HLAT :], "lat", 1, wraps=False)
-    south = shifted(background[:HLAT], "lat", -1, wraps=False)
-    sent = packed(record_values, record_cell, record_instrument, block_counts, lon_cells)
-    sent, north, south = lax.optimization_barrier((sent, north, south))
+    sent, up, down, left, right = packed(
+        record_values, record_cell, record_instrument, block_counts, background
+    )
     received = lax.all_to_all(sent, ("lon", "lat"), split_axis=0, concat_axis=0, tiled=True)
-
-    def columns(low, end):
-        return jnp.concatenate(
-            [north[:, low:end], background[:, low:end], south[:, low:end]], axis=0
-        )
-
-    west = shifted(columns(lon_cells - HLON, lon_cells), "lon", 1)
-    east = shifted(columns(0, HLON), "lon", -1)
+    north = shifted(down, "lat", 1, wraps=False)
+    south = shifted(up, "lat", -1, wraps=False)
+    right = jnp.concatenate([north[:, lon_cells - HLON :], right, south[:, lon_cells - HLON :]], axis=0)
+    left = jnp.concatenate([north[:, :HLON], left, south[:, :HLON]], axis=0)
+    west = shifted(right, "lon", 1)
+    east = shifted(left, "lon", -1)
 
     lat = lax.axis_index("lat")
     scalars = jnp.stack([lat == 0, lat < 0, lat == tiles_lat - 1]).astype(jnp.int32)
-    vmem = pl.BlockSpec(memory_space=pltpu.VMEM)
-    return pl.pallas_call(
-        functools.partial(block_kernel, rectangles(lat_cells, lon_cells)),
-        out_shape=jax.ShapeDtypeStruct(background.shape, BF16),
-        in_specs=[pl.BlockSpec(memory_space=pltpu.SMEM)] + [vmem] * 15,
-        out_specs=vmem,
-        compiler_params=pltpu.CompilerParams(vmem_limit_bytes=LIMIT),
-    )(
-        scalars,
-        received,
-        north,
-        south,
-        west,
-        east,
-        background,
-        input_weight.T,
-        instrument_table,
-        lift_weight,
+    plan = rectangles(lat_cells, lon_cells)
+    rest = sum(
+        padded(tokens_of(plan[tile][number])) for tile, number in column_entries(plan, (0, 2))
+    )
+    weights = [
         first_gain.reshape(1, width),
         attn_weight,
         mix_weight,
         second_gain.reshape(1, width),
         up_weight,
         down_weight.T,
+    ]
+    smem = pl.BlockSpec(memory_space=pltpu.SMEM)
+    vmem = pl.BlockSpec(memory_space=pltpu.VMEM)
+    anywhere = pl.BlockSpec(memory_space=pl.ANY)
+    params = pltpu.CompilerParams(vmem_limit_bytes=LIMIT)
+    result = jax.ShapeDtypeStruct(background.shape, BF16)
+    middle, rest = pl.pallas_call(
+        functools.partial(middle_kernel, plan),
+        out_shape=[result, jax.ShapeDtypeStruct((rest, PAD), F32)],
+        in_specs=[smem] + [vmem] * (7 + len(weights)),
+        out_specs=[anywhere, vmem],
+        scratch_shapes=[
+            pltpu.VMEM((lat_cells, lon_cells - WLON, LEV, width), BF16),
+            pltpu.SemaphoreType.DMA((1,)),
+        ],
+        compiler_params=params,
+        cost_estimate=pl.CostEstimate(
+            flops=4 * 10**9, bytes_accessed=4 * 10**6, transcendentals=10**6
+        ),
+    )(
+        scalars,
+        received,
+        north,
+        south,
+        background,
+        input_weight.T,
+        instrument_table,
+        lift_weight,
+        *weights,
     )
+    return pl.pallas_call(
+        functools.partial(side_kernel, plan),
+        out_shape=result,
+        in_specs=[smem] + [vmem] * (6 + len(weights)) + [anywhere],
+        out_specs=anywhere,
+        scratch_shapes=[
+            pltpu.VMEM((2, lat_cells, HLON, LEV, width), BF16),
+            pltpu.SemaphoreType.DMA((2,)),
+        ],
+        input_output_aliases={7 + len(weights): 0},
+        compiler_params=params,
+        cost_estimate=pl.CostEstimate(
+            flops=3 * 10**9, bytes_accessed=4 * 10**6, transcendentals=10**6
+        ),
+    )(scalars, rest, north, south, west, east, background, *weights, middle)
 
 
 def solution(mesh):

time: 35.4 us -> 36.4 us (1.028)
  other arithmetic: 0.42 us -> 2.2 us
  Pallas kernels: 10.8 us -> 11.8 us
  local copies, waits for them, and re-layouts: 2.58 us -> 1.79 us
  waiting for transfers between devices: 5.61 us -> 5 us
  starting transfers between devices: 15.5 us -> 15 us
    all_to_all x1, waiting for transfers between devices: 2.57 us -> 0.01 us  [local(): lax.all_to_all(sent, ('lon', 'lat'), split_axis=0, concat_axis=0, tiled=T...]
    ppermute x4, waiting for transfers between devices: 3.04 us -> 5 us  [shifted(): return lax.ppermute(value, axis, pairs)]
    ppermute x4, starting transfers between devices: 9.6 us -> 7.71 us  [shifted(): return lax.ppermute(value, axis, pairs)]
    concatenate x2, other arithmetic: 0.35 us -> 2.13 us  [the longest x1 1.06 us: local(): left = jnp.concatenate([north[:, :HLON], left, south[:, :HLON]], axis=0)]
    all_to_all x1, starting transfers between devices: 5.89 us -> 7.32 us  [local(): lax.all_to_all(sent, ('lon', 'lat'), split_axis=0, concat_axis=0, tiled=T...]
    slice x3 -> x2, local copies, waits for them, and re-layouts: 1.23 us -> 0.05 us  [local(): left = jnp.concatenate([north[:, :HLON], left, south[:, :HLON]], axis=0)]
    pallas_call x2 -> x3, Pallas kernels: 10.8 us -> 11.8 us  [the longest x1 5.29 us: local(): pl.pallas_call(functools.partial(middle_kernel, plan), out_shape=[result,...]
    unnamed x20, local copies, waits for them, and re-layouts: 1.34 us -> 1.73 us
  transfers between devices with their start and end apart: 5 -> 5, of which waited for: 2 -> 2; matrix products, arithmetic and copies ran while one was open for 2% -> 6% of each run, Pallas kernels for 5% -> 15%
where the time goes in v7:
time: 36.4 us; the launch traced here: 36 us
  starting transfers between devices  15 us (41%)
  Pallas kernels  11.8 us (32%)
  waiting for transfers between devices  5 us (14%)
  other arithmetic  2.2 us (6%)
  local copies, waits for them, and re-layouts  1.79 us (5%)
    ppermute x4, starting transfers between devices, shifted(): return lax.ppermute(value, axis, pairs)  7.71 us
    all_to_all x1, starting transfers between devices, local(): lax.all_to_all(sent, ('lon', 'lat'), split_axis=0, concat_axis=0, tiled=T...  7.32 us
    pallas_call x1, Pallas kernels, local(): pl.pallas_call(functools.partial(middle_kernel, plan), out_shape=[result,...  5.29 us
    ppermute x4, waiting for transfers between devices, shifted(): return lax.ppermute(value, axis, pairs)  5 us
    pallas_call x1, Pallas kernels, local(): pl.pallas_call(functools.partial(side_kernel, plan), out_shape=result, in...  4.64 us
    pallas_call x1, Pallas kernels, packed(): pl.pallas_call(pack_kernel, out_shape=[jax.ShapeDtypeStruct(shape, BF16),...  1.93 us
    unnamed x20, local copies, waits for them, and re-layouts  1.73 us
    concatenate x1, other arithmetic, local(): left = jnp.concatenate([north[:, :HLON], left, south[:, :HLON]], axis=0)  1.06 us
  transfers between devices with their start and end apart: 5, of which 2 were waited for; matrix products, arithmetic and copies ran while one was open for 6% of the time, Pallas kernels for 15%

profile of v7, /device:TPU:0, one launch (start us, length us, event | category | flops | bytes accessed | tf_op | source)
XLA Modules:
  0.0 36.0 jit_solution(12430716333127371408)
XLA Ops:
  0.0 0.0 copy-start.8
  0.0 0.0 copy-start.9
  0.0 0.0 copy-start.3
  0.0 0.0 copy-start.4
  0.0 1.9 %shard_map.136 = (bf16[8,4,10,2,128]{4,3,2,1,0:T(2,128)(2,1)}, bf16[3,24,2,192]{3,2,1,0:T(2,128)(2,1)}, bf16[3,24,2,192]{3,2,1,0:T(2,128)(2,1)}, bf16[12,6,2,192]{3,2,1,0:T(2,128)(2,1)}, bf16[12,6,2,192]{3,2,1,0:T(2,128)(2,1)}) custom-call(bf16[8,4,2,128]{3,2,1,0:T(2,128)(2,1)} %values_ref.1, s32[8,8]{1,0:T(8,128)} %bitcast.17, s32[8,8]{1,0:T(8,128)} %bitcast.18, ...), custom_call_target="tpu_custom_call" | custom-call | tf_op jit(solution)/shard_map/pallas_call | solution.py:178
  1.9 0.0 copy-start.2
  2.0 7.3 %all-to-all-start = ((bf16[32,10,2,128]{3,2,1,0:T(2,128)(2,1)}), bf16[32,10,2,128]{3,2,1,0:T(2,128)(2,1)S(1)}, u32[]{:S(2)}, u32[]{:S(2)}) async-start(bf16[32,10,2,128]{3,2,1,0:T(2,128)(2,1)} %bitcast.16), calls=%async_computation | async-start | bytes 327680 | tf_op jit(solution)/shard_map/all_to_all | solution.py:448
  9.3 3.7 %collective-permute-start = (bf16[3,24,2,192]{3,2,1,0:T(2,128)(2,1)}, bf16[3,24,2,192]{3,2,1,0:T(2,128)(2,1)S(1)}, u32[]{:S(2)}, u32[]{:S(2)}) collective-permute-start(bf16[3,24,2,192]{3,2,1,0:T(2,128)(2,1)} %get-tuple-element.13), channel_id=1, source_target_pairs={{0,1},{1,2},{2,3},{4,5},{5,6},{6,7},{8,9},{9,10},{10,11},{12,13},{... | collective-permute-start | bytes 165896 | tf_op jit(solution)/shard_map/ppermute | solution.py:34
  13.0 1.3 %collective-permute-start.1 = (bf16[3,24,2,192]{3,2,1,0:T(2,128)(2,1)}, bf16[3,24,2,192]{3,2,1,0:T(2,128)(2,1)S(1)}, u32[]{:S(2)}, u32[]{:S(2)}) collective-permute-start(bf16[3,24,2,192]{3,2,1,0:T(2,128)(2,1)} %get-tuple-element.14), channel_id=1, source_target_pairs={{1,0},{2,1},{3,2},{5,4},{6,5},{7,6},{9,8},{10,9},{11,10},{13,12},{... | collective-permute-start | bytes 165896 | tf_op jit(solution)/shard_map/ppermute | solution.py:34
  14.3 0.1 add_convert_fusion.scalars_ref
  14.4 0.0 copy-done.8
  14.4 0.0 copy-done.9
  14.4 0.0 copy-start
  14.4 0.0 copy-start.1
  14.4 0.8 %collective-permute-done.north_ref = bf16[3,24,2,192]{3,2,1,0:T(2,128)(2,1)S(1)} collective-permute-done((bf16[3,24,2,192]{3,2,1,0:T(2,128)(2,1)}, bf16[3,24,2,192]{3,2,1,0:T(2,128)(2,1)S(1)}, u32[]{:S(2)}, u32[]{:S(2)}) %collective-permute-start) | collective-permute-done | bytes 55328 | tf_op jit(solution)/shard_map/ppermute | solution.py:34
  15.3 4.1 %collective-permute-done.1.south_ref = bf16[3,24,2,192]{3,2,1,0:T(2,128)(2,1)S(1)} collective-permute-done((bf16[3,24,2,192]{3,2,1,0:T(2,128)(2,1)}, bf16[3,24,2,192]{3,2,1,0:T(2,128)(2,1)S(1)}, u32[]{:S(2)}, u32[]{:S(2)}) %collective-permute-start.1) | collective-permute-done | bytes 55328 | tf_op jit(solution)/shard_map/ppermute | solution.py:34
  19.5 1.1 %pad_maximum_fusion = bf16[18,6,2,192]{3,2,1,0:T(2,128)(2,1)S(1)} fusion(bf16[3,6,2,192]{3,2,1,0:T(2,128)(2,1)S(1)} %get-tuple-element.22, bf16[12,6,2,192]{3,2,1,0:T(2,128)(2,1)} %get-tuple-element.16, bf16[3,6,2,192]{3,2,1,0:T(2,128)(2,1)S(1)} %get-tuple-element.20), kind=kLoop, calls=%fused_computation | loop fusion | flops 82944 | bytes 165888 | tf_op jit(solution)/shard_map/concatenate | solution.py:451
  20.5 0.1 collective-permute-start.2
  20.6 0.0 copy-start.7
  20.6 1.1 %pad_maximum_fusion.1 = bf16[18,6,2,192]{3,2,1,0:T(2,128)(2,1)S(1)} fusion(bf16[3,6,2,192]{3,2,1,0:T(2,128)(2,1)S(1)} %get-tuple-element.21, bf16[12,6,2,192]{3,2,1,0:T(2,128)(2,1)} %get-tuple-element.17, bf16[3,6,2,192]{3,2,1,0:T(2,128)(2,1)S(1)} %get-tuple-element.19), kind=kLoop, calls=%fused_computation.1 | loop fusion | flops 82944 | bytes 165888 | tf_op jit(solution)/shard_map/concatenate | solution.py:452
  21.7 2.7 %collective-permute-start.3 = (bf16[18,6,2,192]{3,2,1,0:T(2,128)(2,1)S(1)}, bf16[18,6,2,192]{3,2,1,0:T(2,128)(2,1)S(1)}, u32[]{:S(2)}, u32[]{:S(2)}) collective-permute-start(bf16[18,6,2,192]{3,2,1,0:T(2,128)(2,1)S(1)} %pad_maximum_fusion.1), channel_id=1, source_target_pairs={{0,28},{4,0},{8,4},{12,8},{16,12},{20,16},{24,20},{28,24},{1,29},{... | collective-permute-start | bytes 248840 | tf_op jit(solution)/shard_map/ppermute | solution.py:34
  24.3 0.0 all-to-all-done.recv_ref
  24.3 0.0 copy-done.3
  24.4 0.0 copy-done.4
  24.4 0.0 copy-done.2
  24.4 0.0 copy-done
  24.4 0.0 copy-done.1
  24.4 0.0 copy-done.7
  24.4 0.0 copy-start.5
  24.4 0.9 %copy-done.5 = bf16[192,192]{1,0:T(8,128)(2,1)S(1)} copy-done((bf16[192,192]{1,0:T(8,128)(2,1)S(1)}, bf16[192,192]{1,0:T(8,128)(2,1)}, u32[]{:S(2)}) %copy-start.5) | copy-done | bytes 73752
  25.3 0.0 copy-start.6
  25.3 0.8 %copy-done.6 = bf16[128,192]{0,1:T(8,128)(2,1)S(1)} copy-done((bf16[128,192]{0,1:T(8,128)(2,1)S(1)}, bf16[128,192]{0,1:T(8,128)(2,1)}, u32[]{:S(2)}) %copy-start.6) | copy-done | bytes 49176
  26.1 5.3 %shard_map.137 = (bf16[12,24,2,192]{3,2,1,0:T(2,128)(2,1)}, f32[928,256]{1,0:T(8,128)S(1)}) custom-call(s32[3]{0:T(128)S(1)} %add_convert_fusion.scalars_ref, bf16[32,10,2,128]{3,2,1,0:T(2,128)(2,1)S(1)} %all-to-all-done.recv_ref, bf16[3,24,2,192]{3,2,1,0:T(2,128)(2,1)S(1)} %collective-permute-done.north_ref, ...), custom_call_target="tpu_custom_call" | custom-call | flops 4000000000 | bytes 4000000 | tf_op jit(solution)/shard_map/pallas_call | solution.py:475
  31.4 0.0 collective-permute-done.2.west_ref
  31.4 0.0 collective-permute-done.3.east_ref
  31.4 4.6 %shard_map.138 = bf16[12,24,2,192]{3,2,1,0:T(2,128)(2,1)} custom-call(s32[3]{0:T(128)S(1)} %add_convert_fusion.scalars_ref, f32[928,256]{1,0:T(8,128)S(1)} %get-tuple-element.15.rest_ref, bf16[3,24,2,192]{3,2,1,0:T(2,128)(2,1)S(1)} %collective-permute-done.north_ref, ...), custom_call_target="tpu_custom_call", output_to_operand_aliasing={{}: (13, {})} | custom-call | flops 3000000000 | bytes 4000000 | tf_op jit(solution)/shard_map/pallas_call | solution.py:499
  (4 shorter events, 0.1 us)
Async XLA Ops:
  0.0 14.4 %copy-start.8 = (bf16[192]{0:T(256)(128)(2,1)S(1)}, bf16[192]{0:T(256)(128)(2,1)}, u32[]{:S(2)}) copy-start(bf16[192]{0:T(256)(128)(2,1)} %param.22) | copy-start | bytes 1156
  0.0 14.4 %copy-start.9 = (bf16[192]{0:T(256)(128)(2,1)S(1)}, bf16[192]{0:T(256)(128)(2,1)}, u32[]{:S(2)}) copy-start(bf16[192]{0:T(256)(128)(2,1)} %param.25) | copy-start | bytes 1156
  0.0 24.3 %copy-start.3 = (bf16[192,576]{1,0:T(8,128)(2,1)S(1)}, bf16[192,576]{1,0:T(8,128)(2,1)}, u32[]{:S(2)}) copy-start(bf16[192,576]{1,0:T(8,128)(2,1)} %refs_1_.3) | copy-start | bytes 663556
  0.0 24.3 %copy-start.4 = (bf16[192,384]{1,0:T(8,128)(2,1)S(1)}, bf16[192,384]{1,0:T(8,128)(2,1)}, u32[]{:S(2)}) copy-start(bf16[192,384]{1,0:T(8,128)(2,1)} %lift_ref.1) | copy-start | bytes 442372
  1.9 22.4 %copy-start.2 = (bf16[768,192]{0,1:T(8,128)(2,1)S(1)}, bf16[768,192]{0,1:T(8,128)(2,1)}, u32[]{:S(2)}) copy-start(bf16[768,192]{0,1:T(8,128)(2,1)} %param.27) | copy-start | bytes 884740
  2.0 22.4 %all-to-all-start = ((bf16[32,10,2,128]{3,2,1,0:T(2,128)(2,1)}), bf16[32,10,2,128]{3,2,1,0:T(2,128)(2,1)S(1)}, u32[]{:S(2)}, u32[]{:S(2)}) async-start(bf16[32,10,2,128]{3,2,1,0:T(2,128)(2,1)} %bitcast.16), calls=%async_computation | async-start | bytes 327680 | tf_op jit(solution)/shard_map/all_to_all | solution.py:448
  9.3 6.0 %collective-permute-start = (bf16[3,24,2,192]{3,2,1,0:T(2,128)(2,1)}, bf16[3,24,2,192]{3,2,1,0:T(2,128)(2,1)S(1)}, u32[]{:S(2)}, u32[]{:S(2)}) collective-permute-start(bf16[3,24,2,192]{3,2,1,0:T(2,128)(2,1)} %get-tuple-element.13), channel_id=1, source_target_pairs={{0,1},{1,2},{2,3},{4,5},{5,6},{6,7},{8,9},{9,10},{10,11},{12,13},{... | collective-permute-start | bytes 165896 | tf_op jit(solution)/shard_map/ppermute | solution.py:34
  13.0 6.5 %collective-permute-start.1 = (bf16[3,24,2,192]{3,2,1,0:T(2,128)(2,1)}, bf16[3,24,2,192]{3,2,1,0:T(2,128)(2,1)S(1)}, u32[]{:S(2)}, u32[]{:S(2)}) collective-permute-start(bf16[3,24,2,192]{3,2,1,0:T(2,128)(2,1)} %get-tuple-element.14), channel_id=1, source_target_pairs={{1,0},{2,1},{3,2},{5,4},{6,5},{7,6},{9,8},{10,9},{11,10},{13,12},{... | collective-permute-start | bytes 165896 | tf_op jit(solution)/shard_map/ppermute | solution.py:34
  14.4 10.0 %copy-start = (bf16[12,24,2,192]{3,2,1,0:T(2,128)(2,1)S(1)}, bf16[12,24,2,192]{3,2,1,0:T(2,128)(2,1)}, u32[]{:S(2)}) copy-start(bf16[12,24,2,192]{3,2,1,0:T(2,128)(2,1)} %back_ref.5) | copy-start | bytes 663556
  14.4 10.0 %copy-start.1 = (bf16[192,768]{1,0:T(8,128)(2,1)S(1)}, bf16[192,768]{1,0:T(8,128)(2,1)}, u32[]{:S(2)}) copy-start(bf16[192,768]{1,0:T(8,128)(2,1)} %refs_4_.3) | copy-start | bytes 884740
  20.5 10.9 %collective-permute-start.2 = (bf16[18,6,2,192]{3,2,1,0:T(2,128)(2,1)S(1)}, bf16[18,6,2,192]{3,2,1,0:T(2,128)(2,1)S(1)}, u32[]{:S(2)}, u32[]{:S(2)}) collective-permute-start(bf16[18,6,2,192]{3,2,1,0:T(2,128)(2,1)S(1)} %pad_maximum_fusion), channel_id=1, source_target_pairs={{0,4},{4,8},{8,12},{12,16},{16,20},{20,24},{24,28},{28,0},{1,5},{5... | collective-permute-start | bytes 248840 | tf_op jit(solution)/shard_map/ppermute | solution.py:34
  20.6 3.8 %copy-start.7 = (bf16[8,192]{1,0:T(8,128)(2,1)S(1)}, bf16[8,192]{1,0:T(8,128)(2,1)}, u32[]{:S(2)}) copy-start(bf16[8,192]{1,0:T(8,128)(2,1)} %table_ref.1) | copy-start | bytes 9220
  21.7 9.7 %collective-permute-start.3 = (bf16[18,6,2,192]{3,2,1,0:T(2,128)(2,1)S(1)}, bf16[18,6,2,192]{3,2,1,0:T(2,128)(2,1)S(1)}, u32[]{:S(2)}, u32[]{:S(2)}) collective-permute-start(bf16[18,6,2,192]{3,2,1,0:T(2,128)(2,1)S(1)} %pad_maximum_fusion.1), channel_id=1, source_target_pairs={{0,28},{4,0},{8,4},{12,8},{16,12},{20,16},{24,20},{28,24},{1,29},{... | collective-permute-start | bytes 248840 | tf_op jit(solution)/shard_map/ppermute | solution.py:34
  24.4 0.9 %copy-start.5 = (bf16[192,192]{1,0:T(8,128)(2,1)S(1)}, bf16[192,192]{1,0:T(8,128)(2,1)}, u32[]{:S(2)}) copy-start(bf16[192,192]{1,0:T(8,128)(2,1)} %refs_2_.3) | copy-start | bytes 221188
  25.3 0.8 %copy-start.6 = (bf16[128,192]{0,1:T(8,128)(2,1)S(1)}, bf16[128,192]{0,1:T(8,128)(2,1)}, u32[]{:S(2)}) copy-start(bf16[128,192]{0,1:T(8,128)(2,1)} %param.19) | copy-start | bytes 147460

commit v8 on v7

--- a/solution.py
+++ b/solution.py
@@ -54,7 +54,9 @@
 
 
 def gelu(x):
-    return jax.nn.gelu(x)
+    half = 0.5 * x
+    inner = x * (0.7978845608028654 + 0.035677408136300125 * (x * x))
+    return half + half * jnp.tanh(inner)
 
 
 def normalise(wide, gain):
@@ -87,24 +89,16 @@
     tag_ref,
     count_ref,
     back_ref,
-    out_ref,
-    up_ref,
-    down_ref,
-    left_ref,
-    right_ref,
-    values,
-    cells,
-    tags,
-    held,
-    sem,
+    *refs,
 ):
+    out_ref, up_ref, down_ref, left_ref, right_ref, values, cells, tags, held, sem = refs
     tiles_lon, tiles_lat, capacity, _ = values_ref.shape
     lat_cells, lon_cells = back_ref.shape[:2]
     strips = [
         (back_ref.at[:HLAT], up_ref),
         (back_ref.at[lat_cells - HLAT :], down_ref),
-        (back_ref.at[:, :HLON], left_ref),
-        (back_ref.at[:, lon_cells - HLON :], right_ref),
+        (back_ref.at[:, :HLON], left_ref.at[HLAT : HLAT + lat_cells]),
+        (back_ref.at[:, lon_cells - HLON :], right_ref.at[HLAT : HLAT + lat_cells]),
     ]
     copies = [
         pltpu.make_async_copy(cell_ref, cells, sem.at[0]),
@@ -174,7 +168,7 @@
     shape = (tiles_lon, tiles_lat, len(AROUND) + 1, capacity, wide)
     lat_cells, lon_cells, levels, width = background.shape
     across = jax.ShapeDtypeStruct((HLAT, lon_cells, levels, width), BF16)
-    along = jax.ShapeDtypeStruct((lat_cells, HLON, levels, width), BF16)
+    along = jax.ShapeDtypeStruct((lat_cells + WLAT, HLON, levels, width), BF16)
     out, *strips = pl.pallas_call(
         pack_kernel,
         out_shape=[jax.ShapeDtypeStruct(shape, BF16), across, across, along, along],
@@ -188,6 +182,9 @@
             pltpu.SemaphoreType.DMA((8,)),
         ],
         compiler_params=pltpu.CompilerParams(vmem_limit_bytes=56 * 2**20),
+        cost_estimate=pl.CostEstimate(
+            flops=20 * 10**9, bytes_accessed=10**6, transcendentals=0
+        ),
     )(
         record_values,
         record_cell.transpose(1, 2, 0).reshape(-1, tiles_lon),
@@ -209,13 +206,26 @@
     return jnp.where(place < count, code, -8).astype(F32)
 
 
-def column_entries(plan, columns):
-    own = [(4, 3 * i + j) for i in range(3) for j in columns]
-    around = [(tile, j) for tile in (1, 7) for j in columns]
-    for j in columns:
+def entries_of(windows):
+    entries = [(4, 3 * i + j) for i, j in windows]
+    for i, j in windows:
+        if i != 1:
+            entries.append((3 * i + 1, j))
         if j != 1:
-            around += [(3 + j, i) for i in range(3)] + [(j, 0), (6 + j, 0)]
-    return own + around
+            entries.append((3 + j, i))
+        if i != 1 and j != 1:
+            entries.append((3 * i + j, 0))
+    return entries
+
+
+def alternate(*chains):
+    chains, begun = list(chains), 1
+    while chains:
+        for chain in chains[:begun]:
+            if next(chain, None) is None:
+                chains.remove(chain)
+                begun -= 1
+        begun += 1
 
 
 def scattered(recv_ref, first_ref, table_ref, lift_ref, plan, lon_cells):
@@ -271,12 +281,12 @@
     return sums
 
 
-def worked(plan, columns, sums, borders, weights, scalars_ref, put):
+def worked(plan, places, sum_of, borders, weights, scalars_ref, put):
     back_ref, north_ref, south_ref, west_ref, east_ref = borders
     gain_one_ref, attn_ref, mix_ref, gain_two_ref, up_ref, down_ref = weights
     lat_cells, width = back_ref.shape[0], back_ref.shape[3]
     pieces, spans, start = [], {}, 0
-    for tile, number in column_entries(plan, columns):
+    for tile, number in entries_of(places):
         dy, dx = AROUND[tile]
         part = plan[tile][number]
         top, high, left, wide = part
@@ -295,15 +305,16 @@
         pieces.append(piece)
         spans[tile, number] = (start, count)
         start += full
+    sums = below(*[sum_of(*entry) for entry in entries_of(places)])
     share = 1.0 / (1.0 + sums[:, width : width + 1])
     latent = ((below(*pieces) + sums[:, :width]) * share).astype(BF16).astype(F32)
     normed = normalise(latent, gain_one_ref[...].astype(F32))
+    yield True
 
     def piece_of(tile, number):
         start, count = spans[tile, number]
         return normed[start : start + count]
 
-    places = [(i, j) for i in range(3) for j in columns]
     groups = [padded(tokens_of(plan[4][3 * i + j])) for i, j in places]
     end = sum(groups)
     windows = []
@@ -320,8 +331,9 @@
     weight = attn_ref[...]
     head = width // HEADS
     keys = dot(tokens, weight[:, width : 2 * width]).astype(BF16)
+    query = dot(normed[:end].astype(BF16), weight[:, :width]) * head ** (-0.5)
     values = with_ones(dot(tokens, weight[:, 2 * width :]))
-    query = dot(normed[:end].astype(BF16), weight[:, :width]) * head ** (-0.5)
+    yield True
 
     head_of = lax.broadcasted_iota(jnp.int32, (1, width), 1) // head
     many = WLAT * WLON * LEV
@@ -332,6 +344,7 @@
         part = query[start : start + rows]
         stacked = below(*[jnp.where(head_of == h, part, 0.0) for h in range(HEADS)]).astype(BF16)
         scores = dot_nt(stacked, keys[w * many : (w + 1) * many])
+        yield True
         if i != 1:
             if j == 1:
                 inside = key < 2 * corner
@@ -341,6 +354,7 @@
         largest = jnp.max(scores, axis=-1, keepdims=True)
         raised = jnp.exp(scores - largest).astype(BF16)
         product = dot(raised, values[w * many : (w + 1) * many])
+        yield True
         product = product[:, :width] * (1.0 / product[:, width : width + 1])
         total = jnp.zeros((rows, width), F32)
         for h in range(HEADS):
@@ -350,15 +364,26 @@
     mixed = below(*mixed).astype(BF16)
 
     after = (latent[:end] + dot(mixed, mix_ref[...])).astype(BF16).astype(F32)
+    yield True
     normed_two = normalise(after, gain_two_ref[...].astype(F32)).astype(BF16)
-    hidden = gelu(dot(normed_two, up_ref[...])).astype(BF16)
-    result = after + dot_nt(hidden, down_ref[...])
+    hidden = dot(normed_two, up_ref[...])
+    yield True
+    result = after + dot_nt(gelu(hidden).astype(BF16), down_ref[...])
+    yield True
     start = 0
     for (i, j), rows in zip(places, groups):
         part = plan[4][3 * i + j]
         piece = result[start : start + tokens_of(part)].astype(BF16)
         put(part, j, piece.reshape(part[1], part[3], LEV, width))
         start += rows
+
+
+MIDDLE = [[(0, 1), (2, 1)], [(1, 1)]]
+SIDES = [[(0, 0), (1, 0), (2, 0)], [(0, 2), (1, 2), (2, 2)]]
+
+
+def side_entries():
+    return [entry for places in SIDES for entry in entries_of(places)]
 
 
 def middle_kernel(
@@ -380,15 +405,16 @@
         start = sum(padded(tokens_of(part)) for part in plan[tile][:number])
         return sums[tile][start : start + padded(tokens_of(plan[tile][number]))]
 
-    rest_ref[...] = below(*[sum_of(*entry) for entry in column_entries(plan, (0, 2))])
-    mine = below(*[sum_of(*entry) for entry in column_entries(plan, (1,))])
+    rest_ref[...] = below(*[sum_of(*entry) for entry in side_entries()])
     left, wide = plan[4][4][2:]
 
     def put(part, _, piece):
         held_ref[part[0] : part[0] + part[1]] = piece
 
     borders = (back_ref, north_ref, south_ref, None, None)
-    worked(plan, (1,), mine, borders, weights, scalars_ref, put)
+    alternate(
+        *[worked(plan, places, sum_of, borders, weights, scalars_ref, put) for places in MIDDLE]
+    )
     copy = pltpu.make_async_copy(held_ref, out_ref.at[:, left : left + wide], sem.at[0])
     copy.start()
     copy.wait()
@@ -406,12 +432,23 @@
     *refs,
 ):
     *weights, _, out_ref, held_ref, sem = refs
+    spans, start = {}, 0
+    for tile, number in side_entries():
+        rows = padded(tokens_of(plan[tile][number]))
+        spans[tile, number] = (start, start + rows)
+        start += rows
+
+    def sum_of(tile, number):
+        start, end = spans[tile, number]
+        return rest_ref[start:end, :]
 
     def put(part, j, piece):
         held_ref[j // 2, part[0] : part[0] + part[1]] = piece
 
     borders = (back_ref, north_ref, south_ref, west_ref, east_ref)
-    worked(plan, (0, 2), rest_ref[...], borders, weights, scalars_ref, put)
+    alternate(
+        *[worked(plan, places, sum_of, borders, weights, scalars_ref, put) for places in SIDES]
+    )
     copies = []
     for n, number in enumerate((0, 2)):
         left, wide = plan[4][number][2:]
@@ -448,17 +485,17 @@
     received = lax.all_to_all(sent, ("lon", "lat"), split_axis=0, concat_axis=0, tiled=True)
     north = shifted(down, "lat", 1, wraps=False)
     south = shifted(up, "lat", -1, wraps=False)
-    right = jnp.concatenate([north[:, lon_cells - HLON :], right, south[:, lon_cells - HLON :]], axis=0)
-    left = jnp.concatenate([north[:, :HLON], left, south[:, :HLON]], axis=0)
+    right = right.at[:HLAT].set(north[:, lon_cells - HLON :])
+    right = right.at[HLAT + lat_cells :].set(south[:, lon_cells - HLON :])
+    left = left.at[:HLAT].set(north[:, :HLON])
+    left = left.at[HLAT + lat_cells :].set(south[:, :HLON])
     west = shifted(right, "lon", 1)
     east = shifted(left, "lon", -1)
 
     lat = lax.axis_index("lat")
     scalars = jnp.stack([lat == 0, lat < 0, lat == tiles_lat - 1]).astype(jnp.int32)
     plan = rectangles(lat_cells, lon_cells)
-    rest = sum(
-        padded(tokens_of(plan[tile][number])) for tile, number in column_entries(plan, (0, 2))
-    )
+    rest = sum(padded(tokens_of(plan[tile][number])) for tile, number in side_entries())
     weights = [
         first_gain.reshape(1, width),
         attn_weight,

time: 36.4 us -> 31.8 us (0.87)
  other arithmetic: 2.2 us -> 0.08 us
  starting transfers between devices: 15 us -> 13.1 us
  local copies, waits for them, and re-layouts: 1.79 us -> 1.35 us
    concatenate x2 -> x0, other arithmetic: 2.13 us -> none  [the longest x1 1.06 us: local(): left = jnp.concatenate([north[:, :HLON], left, south[:, :HLON]], axis=0)]
    ppermute x4, starting transfers between devices: 7.71 us -> 5.79 us  [shifted(): return lax.ppermute(value, axis, pairs)]
    unnamed x20, local copies, waits for them, and re-layouts: 1.73 us -> 0.04 us
    scatter x0 -> x2, local copies, waits for them, and re-layouts: none -> 1.3 us  [the longest x1 0.66 us: local(): left = left.at[:HLAT].set(north[:, :HLON])]
  transfers between devices with their start and end apart: 5 -> 5, of which waited for: 2 -> 3; matrix products, arithmetic and copies ran while one was open for 6% -> 4% of each run, Pallas kernels for 15% -> 16%
where the time goes in v8:
time: 31.8 us; the launch traced here: 31.6 us
  starting transfers between devices  13.1 us (41%)
  Pallas kernels  11.8 us (37%)
  waiting for transfers between devices  5.1 us (16%)
  local copies, waits for them, and re-layouts  1.35 us (4%)
    all_to_all x1, starting transfers between devices, local(): lax.all_to_all(sent, ('lon', 'lat'), split_axis=0, concat_axis=0, tiled=T...  7.32 us
    ppermute x4, starting transfers between devices, shifted(): return lax.ppermute(value, axis, pairs)  5.79 us
    ppermute x4, waiting for transfers between devices, shifted(): return lax.ppermute(value, axis, pairs)  5.1 us
    pallas_call x1, Pallas kernels, local(): pl.pallas_call(functools.partial(middle_kernel, plan), out_shape=[result,...  4.99 us
    pallas_call x1, Pallas kernels, local(): pl.pallas_call(functools.partial(side_kernel, plan), out_shape=result, in...  4.81 us
    pallas_call x1, Pallas kernels, packed(): pl.pallas_call(pack_kernel, out_shape=[jax.ShapeDtypeStruct(shape, BF16),...  1.97 us
    scatter x1, local copies, waits for them, and re-layouts, local(): left = left.at[:HLAT].set(north[:, :HLON])  0.66 us
    scatter x1, local copies, waits for them, and re-layouts, local(): left = left.at[HLAT + lat_cells:].set(south[:, :HLON])  0.64 us
  transfers between devices with their start and end apart: 5, of which 3 were waited for; matrix products, arithmetic and copies ran while one was open for 4% of the time, Pallas kernels for 16%

profile of v8, /device:TPU:0, one launch (start us, length us, event | category | flops | bytes accessed | tf_op | source)
XLA Modules:
  0.0 31.6 jit_solution(8938184550955150410)
XLA Ops:
  0.0 0.0 copy-start.8
  0.0 0.0 copy-start.9
  0.0 0.0 copy-start.1
  0.0 0.0 copy-start.2
  0.0 0.0 copy-start.3
  0.0 0.0 copy-start.5
  0.0 0.0 copy-start.6
  0.0 2.0 %shard_map.136 = (bf16[8,4,10,2,128]{4,3,2,1,0:T(2,128)(2,1)}, bf16[3,24,2,192]{3,2,1,0:T(2,128)(2,1)}, bf16[3,24,2,192]{3,2,1,0:T(2,128)(2,1)}, bf16[18,6,2,192]{3,2,1,0:T(2,128)(2,1)}, bf16[18,6,2,192]{3,2,1,0:T(2,128)(2,1)}) custom-call(bf16[8,4,2,128]{3,2,1,0:T(2,128)(2,1)} %values_ref.1, s32[8,8]{1,0:T(8,128)} %bitcast.17, s32[8,8]{1,0:T(8,128)} %bitcast.18, ...), custom_call_target="tpu_custom_call" | custom-call | flops 20000000000 | bytes 1000000 | tf_op jit(solution)/shard_map/pallas_call | solution.py:172
  2.0 0.0 copy-start
  2.0 7.3 %all-to-all-start = ((bf16[32,10,2,128]{3,2,1,0:T(2,128)(2,1)}), bf16[32,10,2,128]{3,2,1,0:T(2,128)(2,1)S(1)}, u32[]{:S(2)}, u32[]{:S(2)}) async-start(bf16[32,10,2,128]{3,2,1,0:T(2,128)(2,1)} %bitcast.16), calls=%async_computation | async-start | bytes 327680 | tf_op jit(solution)/shard_map/all_to_all | solution.py:485
  9.4 0.0 copy-start.4
  9.4 3.8 %collective-permute-start = (bf16[3,24,2,192]{3,2,1,0:T(2,128)(2,1)}, bf16[3,24,2,192]{3,2,1,0:T(2,128)(2,1)S(1)}, u32[]{:S(2)}, u32[]{:S(2)}) collective-permute-start(bf16[3,24,2,192]{3,2,1,0:T(2,128)(2,1)} %get-tuple-element.61), channel_id=1, source_target_pairs={{0,1},{1,2},{2,3},{4,5},{5,6},{6,7},{8,9},{9,10},{10,11},{12,13},{... | collective-permute-start | bytes 165896 | tf_op jit(solution)/shard_map/ppermute | solution.py:34
  13.2 1.3 %collective-permute-start.1 = (bf16[3,24,2,192]{3,2,1,0:T(2,128)(2,1)}, bf16[3,24,2,192]{3,2,1,0:T(2,128)(2,1)S(1)}, u32[]{:S(2)}, u32[]{:S(2)}) collective-permute-start(bf16[3,24,2,192]{3,2,1,0:T(2,128)(2,1)} %get-tuple-element.62), channel_id=1, source_target_pairs={{1,0},{2,1},{3,2},{5,4},{6,5},{7,6},{9,8},{10,9},{11,10},{13,12},{... | collective-permute-start | bytes 165896 | tf_op jit(solution)/shard_map/ppermute | solution.py:34
  14.5 0.1 add_convert_fusion.scalars_ref
  14.6 0.0 copy-done.8
  14.6 0.0 copy-done.9
  14.6 0.9 %collective-permute-done.north_ref = bf16[3,24,2,192]{3,2,1,0:T(2,128)(2,1)S(1)} collective-permute-done((bf16[3,24,2,192]{3,2,1,0:T(2,128)(2,1)}, bf16[3,24,2,192]{3,2,1,0:T(2,128)(2,1)S(1)}, u32[]{:S(2)}, u32[]{:S(2)}) %collective-permute-start) | collective-permute-done | bytes 55328 | tf_op jit(solution)/shard_map/ppermute | solution.py:34
  15.5 0.7 %slice_dynamic-update-slice_fusion.1 = (bf16[18,6,2,192]{3,2,1,0:T(2,128)(2,1)}, bf16[18,6,2,192]{3,2,1,0:T(2,128)(2,1)}) fusion(bf16[18,6,2,192]{3,2,1,0:T(2,128)(2,1)} %get-tuple-element.65, bf16[3,24,2,192]{3,2,1,0:T(2,128)(2,1)S(1)} %collective-permute-done.north_ref, bf16[18,6,2,192]{3,2,1,0:T(2,128)(2,1)} %get-tuple-element.64), kind=kLoop, calls=%fused_computation.1 | loop fusion | bytes 64512 | tf_op jit(solution)/shard_map/scatter | solution.py:490
  16.1 3.5 %collective-permute-done.1.south_ref = bf16[3,24,2,192]{3,2,1,0:T(2,128)(2,1)S(1)} collective-permute-done((bf16[3,24,2,192]{3,2,1,0:T(2,128)(2,1)}, bf16[3,24,2,192]{3,2,1,0:T(2,128)(2,1)S(1)}, u32[]{:S(2)}, u32[]{:S(2)}) %collective-permute-start.1) | collective-permute-done | bytes 55328 | tf_op jit(solution)/shard_map/ppermute | solution.py:34
  19.6 0.6 %slice_dynamic-update-slice_fusion = (bf16[18,6,2,192]{3,2,1,0:T(2,128)(2,1)}, bf16[18,6,2,192]{3,2,1,0:T(2,128)(2,1)}) fusion(bf16[18,6,2,192]{3,2,1,0:T(2,128)(2,1)} %get-tuple-element.69, bf16[3,24,2,192]{3,2,1,0:T(2,128)(2,1)S(1)} %collective-permute-done.1.south_ref, bf16[18,6,2,192]{3,2,1,0:T(2,128)(2,1)} %get-tuple-element.70), kind=kLoop, calls=%fused_computation | loop fusion | bytes 64512 | tf_op jit(solution)/shard_map/scatter | solution.py:491
  20.3 0.0 copy-start.7
  20.3 0.7 %collective-permute-start.3 = (bf16[18,6,2,192]{3,2,1,0:T(2,128)(2,1)}, bf16[18,6,2,192]{3,2,1,0:T(2,128)(2,1)S(1)}, u32[]{:S(2)}, u32[]{:S(2)}) collective-permute-start(bf16[18,6,2,192]{3,2,1,0:T(2,128)(2,1)} %get-tuple-element.67), channel_id=1, source_target_pairs={{0,28},{4,0},{8,4},{12,8},{16,12},{20,16},{24,20},{28,24},{1,29},{... | collective-permute-start | bytes 248840 | tf_op jit(solution)/shard_map/ppermute | solution.py:34
  21.0 0.0 collective-permute-start.2
  21.0 0.0 all-to-all-done.recv_ref
  21.0 0.0 copy-done.1
  21.0 0.0 copy-done.2
  21.0 0.0 copy-done.3
  21.0 0.0 copy-done.5
  21.0 0.0 copy-done.6
  21.0 0.0 copy-done
  21.0 0.0 copy-done.4
  21.0 0.0 copy-done.7
  21.1 5.0 %shard_map.137 = (bf16[12,24,2,192]{3,2,1,0:T(2,128)(2,1)}, f32[928,256]{1,0:T(8,128)S(1)}) custom-call(s32[3]{0:T(128)S(1)} %add_convert_fusion.scalars_ref, bf16[32,10,2,128]{3,2,1,0:T(2,128)(2,1)S(1)} %all-to-all-done.recv_ref, bf16[3,24,2,192]{3,2,1,0:T(2,128)(2,1)S(1)} %collective-permute-done.north_ref, ...), custom_call_target="tpu_custom_call" | custom-call | flops 4000000000 | bytes 4000000 | tf_op jit(solution)/shard_map/pallas_call | solution.py:512
  26.1 0.0 collective-permute-done.3.east_ref
  26.1 0.7 %collective-permute-done.2.west_ref = bf16[18,6,2,192]{3,2,1,0:T(2,128)(2,1)S(1)} collective-permute-done((bf16[18,6,2,192]{3,2,1,0:T(2,128)(2,1)}, bf16[18,6,2,192]{3,2,1,0:T(2,128)(2,1)S(1)}, u32[]{:S(2)}, u32[]{:S(2)}) %collective-permute-start.2) | collective-permute-done | bytes 82976 | tf_op jit(solution)/shard_map/ppermute | solution.py:34
  26.8 4.8 %shard_map.138 = bf16[12,24,2,192]{3,2,1,0:T(2,128)(2,1)} custom-call(s32[3]{0:T(128)S(1)} %add_convert_fusion.scalars_ref, f32[928,256]{1,0:T(8,128)S(1)} %get-tuple-element.63.rest_ref, bf16[3,24,2,192]{3,2,1,0:T(2,128)(2,1)S(1)} %collective-permute-done.north_ref, ...), custom_call_target="tpu_custom_call", output_to_operand_aliasing={{}: (13, {})} | custom-call | flops 3000000000 | bytes 4000000 | tf_op jit(solution)/shard_map/pallas_call | solution.py:536
  (2 shorter events, 0.0 us)
Async XLA Ops:
  0.0 14.6 %copy-start.8 = (bf16[192]{0:T(256)(128)(2,1)S(1)}, bf16[192]{0:T(256)(128)(2,1)}, u32[]{:S(2)}) copy-start(bf16[192]{0:T(256)(128)(2,1)} %param.30) | copy-start | bytes 1156
  0.0 14.6 %copy-start.9 = (bf16[192]{0:T(256)(128)(2,1)S(1)}, bf16[192]{0:T(256)(128)(2,1)}, u32[]{:S(2)}) copy-start(bf16[192]{0:T(256)(128)(2,1)} %param.33) | copy-start | bytes 1156
  0.0 21.0 %copy-start.1 = (bf16[192,768]{1,0:T(8,128)(2,1)S(1)}, bf16[192,768]{1,0:T(8,128)(2,1)}, u32[]{:S(2)}) copy-start(bf16[192,768]{1,0:T(8,128)(2,1)} %refs_4_.3) | copy-start | bytes 884740
  0.0 21.0 %copy-start.2 = (bf16[768,192]{0,1:T(8,128)(2,1)S(1)}, bf16[768,192]{0,1:T(8,128)(2,1)}, u32[]{:S(2)}) copy-start(bf16[768,192]{0,1:T(8,128)(2,1)} %param.35) | copy-start | bytes 884740
  0.0 21.0 %copy-start.3 = (bf16[192,576]{1,0:T(8,128)(2,1)S(1)}, bf16[192,576]{1,0:T(8,128)(2,1)}, u32[]{:S(2)}) copy-start(bf16[192,576]{1,0:T(8,128)(2,1)} %refs_1_.3) | copy-start | bytes 663556
  0.0 21.0 %copy-start.5 = (bf16[192,192]{1,0:T(8,128)(2,1)S(1)}, bf16[192,192]{1,0:T(8,128)(2,1)}, u32[]{:S(2)}) copy-start(bf16[192,192]{1,0:T(8,128)(2,1)} %refs_2_.3) | copy-start | bytes 221188
  0.0 21.0 %copy-start.6 = (bf16[128,192]{0,1:T(8,128)(2,1)S(1)}, bf16[128,192]{0,1:T(8,128)(2,1)}, u32[]{:S(2)}) copy-start(bf16[128,192]{0,1:T(8,128)(2,1)} %param.27) | copy-start | bytes 147460
  2.0 19.0 %copy-start = (bf16[12,24,2,192]{3,2,1,0:T(2,128)(2,1)S(1)}, bf16[12,24,2,192]{3,2,1,0:T(2,128)(2,1)}, u32[]{:S(2)}) copy-start(bf16[12,24,2,192]{3,2,1,0:T(2,128)(2,1)} %back_ref.5) | copy-start | bytes 663556
  2.0 18.9 %all-to-all-start = ((bf16[32,10,2,128]{3,2,1,0:T(2,128)(2,1)}), bf16[32,10,2,128]{3,2,1,0:T(2,128)(2,1)S(1)}, u32[]{:S(2)}, u32[]{:S(2)}) async-start(bf16[32,10,2,128]{3,2,1,0:T(2,128)(2,1)} %bitcast.16), calls=%async_computation | async-start | bytes 327680 | tf_op jit(solution)/shard_map/all_to_all | solution.py:485
  9.4 11.7 %copy-start.4 = (bf16[192,384]{1,0:T(8,128)(2,1)S(1)}, bf16[192,384]{1,0:T(8,128)(2,1)}, u32[]{:S(2)}) copy-start(bf16[192,384]{1,0:T(8,128)(2,1)} %lift_ref.1) | copy-start | bytes 442372
  9.4 6.1 %collective-permute-start = (bf16[3,24,2,192]{3,2,1,0:T(2,128)(2,1)}, bf16[3,24,2,192]{3,2,1,0:T(2,128)(2,1)S(1)}, u32[]{:S(2)}, u32[]{:S(2)}) collective-permute-start(bf16[3,24,2,192]{3,2,1,0:T(2,128)(2,1)} %get-tuple-element.61), channel_id=1, source_target_pairs={{0,1},{1,2},{2,3},{4,5},{5,6},{6,7},{8,9},{9,10},{10,11},{12,13},{... | collective-permute-start | bytes 165896 | tf_op jit(solution)/shard_map/ppermute | solution.py:34
  13.2 6.5 %collective-permute-start.1 = (bf16[3,24,2,192]{3,2,1,0:T(2,128)(2,1)}, bf16[3,24,2,192]{3,2,1,0:T(2,128)(2,1)S(1)}, u32[]{:S(2)}, u32[]{:S(2)}) collective-permute-start(bf16[3,24,2,192]{3,2,1,0:T(2,128)(2,1)} %get-tuple-element.62), channel_id=1, source_target_pairs={{1,0},{2,1},{3,2},{5,4},{6,5},{7,6},{9,8},{10,9},{11,10},{13,12},{... | collective-permute-start | bytes 165896 | tf_op jit(solution)/shard_map/ppermute | solution.py:34
  20.3 0.8 %copy-start.7 = (bf16[8,192]{1,0:T(8,128)(2,1)S(1)}, bf16[8,192]{1,0:T(8,128)(2,1)}, u32[]{:S(2)}) copy-start(bf16[8,192]{1,0:T(8,128)(2,1)} %table_ref.1) | copy-start | bytes 9220
  20.3 5.8 %collective-permute-start.3 = (bf16[18,6,2,192]{3,2,1,0:T(2,128)(2,1)}, bf16[18,6,2,192]{3,2,1,0:T(2,128)(2,1)S(1)}, u32[]{:S(2)}, u32[]{:S(2)}) collective-permute-start(bf16[18,6,2,192]{3,2,1,0:T(2,128)(2,1)} %get-tuple-element.67), channel_id=1, source_target_pairs={{0,28},{4,0},{8,4},{12,8},{16,12},{20,16},{24,20},{28,24},{1,29},{... | collective-permute-start | bytes 248840 | tf_op jit(solution)/shard_map/ppermute | solution.py:34
  21.0 5.8 %collective-permute-start.2 = (bf16[18,6,2,192]{3,2,1,0:T(2,128)(2,1)}, bf16[18,6,2,192]{3,2,1,0:T(2,128)(2,1)S(1)}, u32[]{:S(2)}, u32[]{:S(2)}) collective-permute-start(bf16[18,6,2,192]{3,2,1,0:T(2,128)(2,1)} %get-tuple-element.68), channel_id=1, source_target_pairs={{0,4},{4,8},{8,12},{12,16},{16,20},{20,24},{24,28},{28,0},{1,5},{5... | collective-permute-start | bytes 248840 | tf_op jit(solution)/shard_map/ppermute | solution.py:34

commit v9 on v8

--- a/solution.py
+++ b/solution.py
@@ -26,12 +26,18 @@
 COLS = ROWS + len(AROUND)
 
 
-def shifted(value, axis, steps, wraps=True):
+def swapped(up, down, axis, wraps):
     count = lax.axis_size(axis)
-    pairs = [(source, (source + steps) % count) for source in range(count)]
-    if not wraps:
-        pairs = [pair for pair in pairs if pair[1] == pair[0] + steps]
-    return lax.ppermute(value, axis, pairs)
+    even = lax.axis_index(axis) % 2 == 0
+    got = []
+    for first, mine in ((0, jnp.where(even, down, up)), (1, jnp.where(even, up, down))):
+        pairs = []
+        for low in range(first, count, 2):
+            high = (low + 1) % count
+            if high > low or wraps:
+                pairs += [(low, high), (high, low)]
+        got.append(lax.ppermute(mine, axis, pairs))
+    return jnp.where(even, got[1], got[0]), jnp.where(even, got[0], got[1])
 
 
 def rectangles(lat_cells, lon_cells):
@@ -91,14 +97,12 @@
     back_ref,
     *refs,
 ):
-    out_ref, up_ref, down_ref, left_ref, right_ref, values, cells, tags, held, sem = refs
+    out_ref, up_ref, down_ref, values, cells, tags, held, sem = refs
     tiles_lon, tiles_lat, capacity, _ = values_ref.shape
     lat_cells, lon_cells = back_ref.shape[:2]
     strips = [
         (back_ref.at[:HLAT], up_ref),
         (back_ref.at[lat_cells - HLAT :], down_ref),
-        (back_ref.at[:, :HLON], left_ref.at[HLAT : HLAT + lat_cells]),
-        (back_ref.at[:, lon_cells - HLON :], right_ref.at[HLAT : HLAT + lat_cells]),
     ]
     copies = [
         pltpu.make_async_copy(cell_ref, cells, sem.at[0]),
@@ -168,18 +172,17 @@
     shape = (tiles_lon, tiles_lat, len(AROUND) + 1, capacity, wide)
     lat_cells, lon_cells, levels, width = background.shape
     across = jax.ShapeDtypeStruct((HLAT, lon_cells, levels, width), BF16)
-    along = jax.ShapeDtypeStruct((lat_cells + WLAT, HLON, levels, width), BF16)
     out, *strips = pl.pallas_call(
         pack_kernel,
-        out_shape=[jax.ShapeDtypeStruct(shape, BF16), across, across, along, along],
+        out_shape=[jax.ShapeDtypeStruct(shape, BF16), across, across],
         in_specs=[anywhere] * 5,
-        out_specs=[pl.BlockSpec(memory_space=pltpu.VMEM)] * 5,
+        out_specs=[pl.BlockSpec(memory_space=pltpu.VMEM)] * 3,
         scratch_shapes=[
             pltpu.VMEM(record_values.shape, BF16),
             ints,
             ints,
             pltpu.VMEM((tiles_lat, tiles_lon), jnp.int32),
-            pltpu.SemaphoreType.DMA((8,)),
+            pltpu.SemaphoreType.DMA((6,)),
         ],
         compiler_params=pltpu.CompilerParams(vmem_limit_bytes=56 * 2**20),
         cost_estimate=pl.CostEstimate(
@@ -479,18 +482,18 @@
     lat_cells, lon_cells, _, width = background.shape
     tiles_lat = record_values.shape[1]
 
-    sent, up, down, left, right = packed(
+    sent, up, down = packed(
         record_values, record_cell, record_instrument, block_counts, background
     )
     received = lax.all_to_all(sent, ("lon", "lat"), split_axis=0, concat_axis=0, tiled=True)
-    north = shifted(down, "lat", 1, wraps=False)
-    south = shifted(up, "lat", -1, wraps=False)
-    right = right.at[:HLAT].set(north[:, lon_cells - HLON :])
-    right = right.at[HLAT + lat_cells :].set(south[:, lon_cells - HLON :])
-    left = left.at[:HLAT].set(north[:, :HLON])
-    left = left.at[HLAT + lat_cells :].set(south[:, :HLON])
-    west = shifted(right, "lon", 1)
-    east = shifted(left, "lon", -1)
+    north, south = swapped(up, down, "lat", wraps=False)
+
+    later, _ = lax.optimization_barrier((background, up))
+
+    def columns(low, end):
+        return jnp.concatenate([north[:, low:end], later[:, low:end], south[:, low:end]], axis=0)
+
+    west, east = swapped(columns(0, HLON), columns(lon_cells - HLON, lon_cells), "lon", wraps=True)
 
     lat = lax.axis_index("lat")
     scalars = jnp.stack([lat == 0, lat < 0, lat == tiles_lat - 1]).astype(jnp.int32)

time: 31.8 us -> 32.9 us (1.035)
  waiting for transfers between devices: 5.1 us -> 6.07 us
  starting transfers between devices: 13.1 us -> 12.3 us
  other arithmetic: 0.08 us -> 0.66 us
    unnamed x20 -> x24, local copies, waits for them, and re-layouts: 0.04 us -> 1.35 us
    scatter x2 -> x0, local copies, waits for them, and re-layouts: 1.3 us -> none  [the longest x1 0.66 us: local(): left = left.at[:HLAT].set(north[:, :HLON])]
    ppermute x4, waiting for transfers between devices: 5.1 us -> 6.07 us  [swapped(): got.append(lax.ppermute(mine, axis, pairs))]
    ppermute x4, starting transfers between devices: 5.79 us -> 5.02 us  [swapped(): got.append(lax.ppermute(mine, axis, pairs))]
    select_n x0 -> x4, other arithmetic: none -> 0.58 us  [the longest x2 0.39 us: swapped(): jnp.where(even, down, up)]
  transfers between devices with their start and end apart: 5 -> 5, of which waited for: 3 -> 2; matrix products, arithmetic and copies ran while one was open for 4% -> 3% of each run, Pallas kernels for 16% -> 0%
where the time goes in v9:
time: 32.9 us; the launch traced here: 32.5 us
  starting transfers between devices  12.3 us (37%)
  Pallas kernels  11.6 us (35%)
  waiting for transfers between devices  6.07 us (18%)
  local copies, waits for them, and re-layouts  1.52 us (5%)
  other arithmetic  0.66 us (2%)
    all_to_all x1, starting transfers between devices, local(): lax.all_to_all(sent, ('lon', 'lat'), split_axis=0, concat_axis=0, tiled=T...  7.3 us
    ppermute x4, waiting for transfers between devices, swapped(): got.append(lax.ppermute(mine, axis, pairs))  6.07 us
    pallas_call x1, Pallas kernels, local(): pl.pallas_call(functools.partial(middle_kernel, plan), out_shape=[result,...  5.04 us
    ppermute x4, starting transfers between devices, swapped(): got.append(lax.ppermute(mine, axis, pairs))  5.02 us
    pallas_call x1, Pallas kernels, local(): pl.pallas_call(functools.partial(side_kernel, plan), out_shape=result, in...  4.85 us
    pallas_call x1, Pallas kernels, packed(): pl.pallas_call(pack_kernel, out_shape=[jax.ShapeDtypeStruct(shape, BF16),...  1.74 us
    unnamed x24, local copies, waits for them, and re-layouts  1.35 us
  transfers between devices with their start and end apart: 5, of which 2 were waited for; matrix products, arithmetic and copies ran while one was open for 3% of the time, Pallas kernels for 0%

profile of v9, /device:TPU:0, one launch (start us, length us, event | category | flops | bytes accessed | tf_op | source)
XLA Modules:
  0.0 32.5 jit_solution(14339111773579357959)
XLA Ops:
  0.0 1.7 %shard_map.136 = (bf16[8,4,10,2,128]{4,3,2,1,0:T(2,128)(2,1)}, bf16[3,24,2,192]{3,2,1,0:T(2,128)(2,1)}, bf16[3,24,2,192]{3,2,1,0:T(2,128)(2,1)}) custom-call(bf16[8,4,2,128]{3,2,1,0:T(2,128)(2,1)} %values_ref.1, s32[8,8]{1,0:T(8,128)} %bitcast.37, s32[8,8]{1,0:T(8,128)} %bitcast.38, s32[4,8]{1,0:T(4,128)} %bitcast.39, bf16[12,24,2,192]{3,2,1,0:T(2,128)(2,1)} %back_ref.5), custom_call_target="tpu_custom_call" | custom-call | flops 20000000000 | bytes 1000000 | tf_op jit(solution)/shard_map/pallas_call | solution.py:175
  1.7 0.0 copy-start.8
  1.8 0.0 copy-start.9
  1.8 0.0 copy-start
  1.8 7.3 %all-to-all-start = ((bf16[32,10,2,128]{3,2,1,0:T(2,128)(2,1)}), bf16[32,10,2,128]{3,2,1,0:T(2,128)(2,1)S(1)}, u32[]{:S(2)}, u32[]{:S(2)}) async-start(bf16[32,10,2,128]{3,2,1,0:T(2,128)(2,1)} %bitcast.30), calls=%async_computation | async-start | bytes 327680 | tf_op jit(solution)/shard_map/all_to_all | solution.py:488
  9.1 0.0 copy-done.8
  9.1 0.0 copy-done.9
  9.1 1.8 %collective-permute-start.1 = (bf16[3,24,2,192]{3,2,1,0:T(2,128)(2,1)S(1)}, bf16[3,24,2,192]{3,2,1,0:T(2,128)(2,1)S(1)}, u32[]{:S(2)}, u32[]{:S(2)}) collective-permute-start(bf16[3,24,2,192]{3,2,1,0:T(2,128)(2,1)S(1)} %bitcast.34), channel_id=1, source_target_pairs={{0,1},{1,0},{2,3},{3,2},{4,5},{5,4},{6,7},{7,6},{8,9},{9,8},{10,11... | collective-permute-start | bytes 165896 | tf_op jit(solution)/shard_map/ppermute | solution.py:39
  11.0 0.7 %collective-permute-start = (bf16[3,24,2,192]{3,2,1,0:T(2,128)(2,1)S(1)}, bf16[3,24,2,192]{3,2,1,0:T(2,128)(2,1)S(1)}, u32[]{:S(2)}, u32[]{:S(2)}) collective-permute-start(bf16[3,24,2,192]{3,2,1,0:T(2,128)(2,1)S(1)} %bitcast.32), channel_id=1, source_target_pairs={{1,2},{2,1},{5,6},{6,5},{9,10},{10,9},{13,14},{14,13},{17,18},{18,... | collective-permute-start | bytes 165896 | tf_op jit(solution)/shard_map/ppermute | solution.py:39
  11.6 0.0 copy-done
  11.7 0.1 fusion
  11.8 0.0 copy-start.10
  11.8 0.6 %copy-done.10 = bf16[192]{0:T(256)(128)(2,1)S(1)} copy-done((bf16[192]{0:T(256)(128)(2,1)S(1)}, bf16[192]{0:T(256)(128)(2,1)}, u32[]{:S(2)}) %copy-start.10) | copy-done | bytes 408
  12.4 0.0 copy-start.11
  12.5 0.6 %copy-done.11 = bf16[192]{0:T(256)(128)(2,1)S(1)} copy-done((bf16[192]{0:T(256)(128)(2,1)S(1)}, bf16[192]{0:T(256)(128)(2,1)}, u32[]{:S(2)}) %copy-start.11) | copy-done | bytes 408
  13.1 2.9 %collective-permute-done.1 = bf16[3,24,2,192]{3,2,1,0:T(2,128)(2,1)S(1)} collective-permute-done((bf16[3,24,2,192]{3,2,1,0:T(2,128)(2,1)S(1)}, bf16[3,24,2,192]{3,2,1,0:T(2,128)(2,1)S(1)}, u32[]{:S(2)}, u32[]{:S(2)}) %collective-permute-start.1) | collective-permute-done | bytes 55328 | tf_op jit(solution)/shard_map/ppermute | solution.py:39
  16.0 0.0 collective-permute-done
  16.0 0.0 copy-start.4
  16.0 0.0 copy-start.5
  16.0 0.1 fusion.1
  16.1 0.0 copy-start.2
  16.1 0.0 copy-start.3
  16.1 0.4 %broadcast_select_fusion.2 = (bf16[18,6,2,192]{3,2,1,0:T(2,128)(2,1)S(1)}, bf16[18,6,2,192]{3,2,1,0:T(2,128)(2,1)S(1)}) fusion(pred[]{:T(512)S(6)} %eq.18, bf16[3,6,2,192]{3,2,1,0:T(2,128)(2,1)S(1)} %get-tuple-element.31, bf16[12,6,2,192]{3,2,1,0:T(2,128)(2,1)S(1)} %get-tuple-element.18, bf16[3,6,2,192]{3,2,1,0:T(2,128)(2,1)S(1)} %get-tuple-element.28, ...), kind=kLoop, calls=%fused_computation.2 | loop fusion | flops 248832 | bytes 331777 | tf_op jit(solution)/shard_map/jit(_where)/select_n | solution.py:33
  16.5 0.0 copy-start.1
  16.5 0.1 collective-permute-start.3
  16.5 2.5 %collective-permute-start.2 = (bf16[18,6,2,192]{3,2,1,0:T(2,128)(2,1)S(1)}, bf16[18,6,2,192]{3,2,1,0:T(2,128)(2,1)S(1)}, u32[]{:S(2)}, u32[]{:S(2)}) collective-permute-start(bf16[18,6,2,192]{3,2,1,0:T(2,128)(2,1)S(1)} %get-tuple-element.22), channel_id=1, source_target_pairs={{4,8},{8,4},{12,16},{16,12},{20,24},{24,20},{28,0},{0,28},{5,9},{9... | collective-permute-start | bytes 248840 | tf_op jit(solution)/shard_map/ppermute | solution.py:39
  19.0 0.1 add_convert_fusion.scalars_ref
  19.1 0.0 copy-start.6
  19.1 0.0 copy-start.7
  19.1 0.0 collective-permute-done.3
  19.1 3.2 %collective-permute-done.2 = bf16[18,6,2,192]{3,2,1,0:T(2,128)(2,1)S(1)} collective-permute-done((bf16[18,6,2,192]{3,2,1,0:T(2,128)(2,1)S(1)}, bf16[18,6,2,192]{3,2,1,0:T(2,128)(2,1)S(1)}, u32[]{:S(2)}, u32[]{:S(2)}) %collective-permute-start.2) | collective-permute-done | bytes 82976 | tf_op jit(solution)/shard_map/ppermute | solution.py:39
  22.3 0.2 broadcast_select_fusion
  22.5 0.0 all-to-all-done.recv_ref
  22.5 0.0 copy-done.4
  22.5 0.0 copy-done.5
  22.5 0.0 copy-done.2
  22.5 0.0 copy-done.3
  22.5 0.0 copy-done.1
  22.5 0.0 copy-done.6
  22.6 0.0 copy-done.7
  22.6 5.0 %shard_map.137 = (bf16[12,24,2,192]{3,2,1,0:T(2,128)(2,1)}, f32[928,256]{1,0:T(8,128)S(1)}) custom-call(s32[3]{0:T(128)S(1)} %add_convert_fusion.scalars_ref, bf16[32,10,2,128]{3,2,1,0:T(2,128)(2,1)S(1)} %all-to-all-done.recv_ref, bf16[3,24,2,192]{3,2,1,0:T(2,128)(2,1)S(1)} %bitcast.25, bf16[3,24,2,192]{3,2,1,0:T(2,128)(2,1)S(1)} %bitcast.22, ...), custom_call_target="tpu_custom_call" | custom-call | flops 4000000000 | bytes 4000000 | tf_op jit(solution)/shard_map/pallas_call | solution.py:515
  27.6 4.9 %shard_map.138 = bf16[12,24,2,192]{3,2,1,0:T(2,128)(2,1)} custom-call(s32[3]{0:T(128)S(1)} %add_convert_fusion.scalars_ref, f32[928,256]{1,0:T(8,128)S(1)} %get-tuple-element.14.rest_ref, bf16[3,24,2,192]{3,2,1,0:T(2,128)(2,1)S(1)} %bitcast.26, bf16[3,24,2,192]{3,2,1,0:T(2,128)(2,1)S(1)} %bitcast.23, ...), custom_call_target="tpu_custom_call", output_to_operand_aliasing={{}: (13, {})} | custom-call | flops 3000000000 | bytes 4000000 | tf_op jit(solution)/shard_map/pallas_call | solution.py:539
  (4 shorter events, 0.0 us)
Async XLA Ops:
  1.7 7.4 %copy-start.8 = (bf16[3,24,2,192]{3,2,1,0:T(2,128)(2,1)S(1)}, bf16[3,24,2,192]{3,2,1,0:T(2,128)(2,1)}, u32[]{:S(2)}) copy-start(bf16[3,24,2,192]{3,2,1,0:T(2,128)(2,1)} %get-tuple-element.12) | copy-start | bytes 165892
  1.8 7.4 %copy-start.9 = (bf16[3,24,2,192]{3,2,1,0:T(2,128)(2,1)S(1)}, bf16[3,24,2,192]{3,2,1,0:T(2,128)(2,1)}, u32[]{:S(2)}) copy-start(bf16[3,24,2,192]{3,2,1,0:T(2,128)(2,1)} %get-tuple-element.13) | copy-start | bytes 165892
  1.8 9.9 %copy-start = (bf16[12,24,2,192]{3,2,1,0:T(2,128)(2,1)S(1)}, bf16[12,24,2,192]{3,2,1,0:T(2,128)(2,1)}, u32[]{:S(2)}) copy-start(bf16[12,24,2,192]{3,2,1,0:T(2,128)(2,1)} %back_ref.5) | copy-start | bytes 663556
  1.8 20.7 %all-to-all-start = ((bf16[32,10,2,128]{3,2,1,0:T(2,128)(2,1)}), bf16[32,10,2,128]{3,2,1,0:T(2,128)(2,1)S(1)}, u32[]{:S(2)}, u32[]{:S(2)}) async-start(bf16[32,10,2,128]{3,2,1,0:T(2,128)(2,1)} %bitcast.30), calls=%async_computation | async-start | bytes 327680 | tf_op jit(solution)/shard_map/all_to_all | solution.py:488
  9.1 6.8 %collective-permute-start.1 = (bf16[3,24,2,192]{3,2,1,0:T(2,128)(2,1)S(1)}, bf16[3,24,2,192]{3,2,1,0:T(2,128)(2,1)S(1)}, u32[]{:S(2)}, u32[]{:S(2)}) collective-permute-start(bf16[3,24,2,192]{3,2,1,0:T(2,128)(2,1)S(1)} %bitcast.34), channel_id=1, source_target_pairs={{0,1},{1,0},{2,3},{3,2},{4,5},{5,4},{6,7},{7,6},{8,9},{9,8},{10,11... | collective-permute-start | bytes 165896 | tf_op jit(solution)/shard_map/ppermute | solution.py:39
  11.0 5.0 %collective-permute-start = (bf16[3,24,2,192]{3,2,1,0:T(2,128)(2,1)S(1)}, bf16[3,24,2,192]{3,2,1,0:T(2,128)(2,1)S(1)}, u32[]{:S(2)}, u32[]{:S(2)}) collective-permute-start(bf16[3,24,2,192]{3,2,1,0:T(2,128)(2,1)S(1)} %bitcast.32), channel_id=1, source_target_pairs={{1,2},{2,1},{5,6},{6,5},{9,10},{10,9},{13,14},{14,13},{17,18},{18,... | collective-permute-start | bytes 165896 | tf_op jit(solution)/shard_map/ppermute | solution.py:39
  11.8 0.7 %copy-start.10 = (bf16[192]{0:T(256)(128)(2,1)S(1)}, bf16[192]{0:T(256)(128)(2,1)}, u32[]{:S(2)}) copy-start(bf16[192]{0:T(256)(128)(2,1)} %param.22) | copy-start | bytes 1156
  12.4 0.7 %copy-start.11 = (bf16[192]{0:T(256)(128)(2,1)S(1)}, bf16[192]{0:T(256)(128)(2,1)}, u32[]{:S(2)}) copy-start(bf16[192]{0:T(256)(128)(2,1)} %param.25) | copy-start | bytes 1156
  16.0 6.5 %copy-start.4 = (bf16[192,384]{1,0:T(8,128)(2,1)S(1)}, bf16[192,384]{1,0:T(8,128)(2,1)}, u32[]{:S(2)}) copy-start(bf16[192,384]{1,0:T(8,128)(2,1)} %lift_ref.1) | copy-start | bytes 442372
  16.0 6.5 %copy-start.5 = (bf16[192,192]{1,0:T(8,128)(2,1)S(1)}, bf16[192,192]{1,0:T(8,128)(2,1)}, u32[]{:S(2)}) copy-start(bf16[192,192]{1,0:T(8,128)(2,1)} %refs_2_.3) | copy-start | bytes 221188
  16.1 6.5 %copy-start.2 = (bf16[768,192]{0,1:T(8,128)(2,1)S(1)}, bf16[768,192]{0,1:T(8,128)(2,1)}, u32[]{:S(2)}) copy-start(bf16[768,192]{0,1:T(8,128)(2,1)} %param.27) | copy-start | bytes 884740
  16.1 6.5 %copy-start.3 = (bf16[192,576]{1,0:T(8,128)(2,1)S(1)}, bf16[192,576]{1,0:T(8,128)(2,1)}, u32[]{:S(2)}) copy-start(bf16[192,576]{1,0:T(8,128)(2,1)} %refs_1_.3) | copy-start | bytes 663556
  16.5 6.1 %copy-start.1 = (bf16[192,768]{1,0:T(8,128)(2,1)S(1)}, bf16[192,768]{1,0:T(8,128)(2,1)}, u32[]{:S(2)}) copy-start(bf16[192,768]{1,0:T(8,128)(2,1)} %refs_4_.3) | copy-start | bytes 884740
  16.5 2.6 %collective-permute-start.3 = (bf16[18,6,2,192]{3,2,1,0:T(2,128)(2,1)S(1)}, bf16[18,6,2,192]{3,2,1,0:T(2,128)(2,1)S(1)}, u32[]{:S(2)}, u32[]{:S(2)}) collective-permute-start(bf16[18,6,2,192]{3,2,1,0:T(2,128)(2,1)S(1)} %get-tuple-element.21), channel_id=1, source_target_pairs={{0,4},{4,0},{8,12},{12,8},{16,20},{20,16},{24,28},{28,24},{1,5},{5... | collective-permute-start | bytes 248840 | tf_op jit(solution)/shard_map/ppermute | solution.py:39
  16.5 5.8 %collective-permute-start.2 = (bf16[18,6,2,192]{3,2,1,0:T(2,128)(2,1)S(1)}, bf16[18,6,2,192]{3,2,1,0:T(2,128)(2,1)S(1)}, u32[]{:S(2)}, u32[]{:S(2)}) collective-permute-start(bf16[18,6,2,192]{3,2,1,0:T(2,128)(2,1)S(1)} %get-tuple-element.22), channel_id=1, source_target_pairs={{4,8},{8,4},{12,16},{16,12},{20,24},{24,20},{28,0},{0,28},{5,9},{9... | collective-permute-start | bytes 248840 | tf_op jit(solution)/shard_map/ppermute | solution.py:39
  19.1 3.5 %copy-start.6 = (bf16[128,192]{0,1:T(8,128)(2,1)S(1)}, bf16[128,192]{0,1:T(8,128)(2,1)}, u32[]{:S(2)}) copy-start(bf16[128,192]{0,1:T(8,128)(2,1)} %param.19) | copy-start | bytes 147460
  19.1 3.5 %copy-start.7 = (bf16[8,192]{1,0:T(8,128)(2,1)S(1)}, bf16[8,192]{1,0:T(8,128)(2,1)}, u32[]{:S(2)}) copy-start(bf16[8,192]{1,0:T(8,128)(2,1)} %table_ref.1) | copy-start | bytes 9220

commit v10 on v9

--- a/solution.py
+++ b/solution.py
@@ -37,6 +37,11 @@
             if high > low or wraps:
                 pairs += [(low, high), (high, low)]
         got.append(lax.ppermute(mine, axis, pairs))
+    return got
+
+
+def before_and_after(got, axis):
+    even = lax.axis_index(axis) % 2 == 0
     return jnp.where(even, got[1], got[0]), jnp.where(even, got[0], got[1])
 
 
@@ -486,14 +491,14 @@
         record_values, record_cell, record_instrument, block_counts, background
     )
     received = lax.all_to_all(sent, ("lon", "lat"), split_axis=0, concat_axis=0, tiled=True)
-    north, south = swapped(up, down, "lat", wraps=False)
+    north, south = before_and_after(swapped(up, down, "lat", wraps=False), "lat")
 
     later, _ = lax.optimization_barrier((background, up))
 
     def columns(low, end):
         return jnp.concatenate([north[:, low:end], later[:, low:end], south[:, low:end]], axis=0)
 
-    west, east = swapped(columns(0, HLON), columns(lon_cells - HLON, lon_cells), "lon", wraps=True)
+    got = swapped(columns(0, HLON), columns(lon_cells - HLON, lon_cells), "lon", wraps=True)
 
     lat = lax.axis_index("lat")
     scalars = jnp.stack([lat == 0, lat < 0, lat == tiles_lat - 1]).astype(jnp.int32)
@@ -536,6 +541,8 @@
         lift_weight,
         *weights,
     )
+    rest, *got = lax.optimization_barrier((rest, *got))
+    west, east = before_and_after(got, "lon")
     return pl.pallas_call(
         functools.partial(side_kernel, plan),
         out_shape=result,

time: 32.9 us -> 28.8 us (0.88)
  waiting for transfers between devices: 6.07 us -> 2.76 us
  starting transfers between devices: 12.3 us -> 11.5 us
    ppermute x4, waiting for transfers between devices: 6.07 us -> 2.76 us  [swapped(): got.append(lax.ppermute(mine, axis, pairs))]
    ppermute x4, starting transfers between devices: 5.02 us -> 4.15 us  [swapped(): got.append(lax.ppermute(mine, axis, pairs))]
    select_n x2 -> x3, other arithmetic: 0.19 us -> 0.57 us  [the longest x1 0.37 us: swapped(): jnp.where(even, up, down)]
    select_n x2 -> x1, other arithmetic: 0.39 us -> 0.02 us  [swapped(): jnp.where(even, down, up)]
  transfers between devices with their start and end apart: 5 -> 5, of which waited for: 2 -> 1; matrix products, arithmetic and copies ran while one was open for 3% -> 2% of each run, Pallas kernels for 0% -> 18%
where the time goes in v10:
time: 28.8 us; the launch traced here: 28.3 us
  Pallas kernels  11.6 us (40%)
  starting transfers between devices  11.5 us (40%)
  waiting for transfers between devices  2.76 us (10%)
  local copies, waits for them, and re-layouts  1.54 us (5%)
  other arithmetic  0.66 us (2%)
    all_to_all x1, starting transfers between devices, local(): lax.all_to_all(sent, ('lon', 'lat'), split_axis=0, concat_axis=0, tiled=T...  7.3 us
    pallas_call x1, Pallas kernels, local(): pl.pallas_call(functools.partial(middle_kernel, plan), out_shape=[result,...  5.02 us
    pallas_call x1, Pallas kernels, local(): pl.pallas_call(functools.partial(side_kernel, plan), out_shape=result, in...  4.83 us
    ppermute x4, starting transfers between devices, swapped(): got.append(lax.ppermute(mine, axis, pairs))  4.15 us
    ppermute x4, waiting for transfers between devices, swapped(): got.append(lax.ppermute(mine, axis, pairs))  2.76 us
    pallas_call x1, Pallas kernels, packed(): pl.pallas_call(pack_kernel, out_shape=[jax.ShapeDtypeStruct(shape, BF16),...  1.74 us
    unnamed x24, local copies, waits for them, and re-layouts  1.36 us
  transfers between devices with their start and end apart: 5, of which 1 were waited for; matrix products, arithmetic and copies ran while one was open for 2% of the time, Pallas kernels for 18%

profile of v10, /device:TPU:0, one launch (start us, length us, event | category | flops | bytes accessed | tf_op | source)
XLA Modules:
  0.0 28.3 jit_solution(15961569044641689619)
XLA Ops:
  0.0 1.7 %shard_map.136 = (bf16[8,4,10,2,128]{4,3,2,1,0:T(2,128)(2,1)}, bf16[3,24,2,192]{3,2,1,0:T(2,128)(2,1)}, bf16[3,24,2,192]{3,2,1,0:T(2,128)(2,1)}) custom-call(bf16[8,4,2,128]{3,2,1,0:T(2,128)(2,1)} %values_ref.1, s32[8,8]{1,0:T(8,128)} %bitcast.37, s32[8,8]{1,0:T(8,128)} %bitcast.38, s32[4,8]{1,0:T(4,128)} %bitcast.39, bf16[12,24,2,192]{3,2,1,0:T(2,128)(2,1)} %back_ref.5), custom_call_target="tpu_custom_call" | custom-call | flops 20000000000 | bytes 1000000 | tf_op jit(solution)/shard_map/pallas_call | solution.py:180
  1.7 0.0 copy-start.8
  1.8 0.0 copy-start.9
  1.8 0.0 copy-start
  1.8 7.3 %all-to-all-start = ((bf16[32,10,2,128]{3,2,1,0:T(2,128)(2,1)}), bf16[32,10,2,128]{3,2,1,0:T(2,128)(2,1)S(1)}, u32[]{:S(2)}, u32[]{:S(2)}) async-start(bf16[32,10,2,128]{3,2,1,0:T(2,128)(2,1)} %bitcast.30), calls=%async_computation | async-start | bytes 327680 | tf_op jit(solution)/shard_map/all_to_all | solution.py:493
  9.1 0.0 copy-done.8
  9.1 0.0 copy-done.9
  9.1 1.8 %collective-permute-start.1 = (bf16[3,24,2,192]{3,2,1,0:T(2,128)(2,1)S(1)}, bf16[3,24,2,192]{3,2,1,0:T(2,128)(2,1)S(1)}, u32[]{:S(2)}, u32[]{:S(2)}) collective-permute-start(bf16[3,24,2,192]{3,2,1,0:T(2,128)(2,1)S(1)} %bitcast.34), channel_id=1, source_target_pairs={{0,1},{1,0},{2,3},{3,2},{4,5},{5,4},{6,7},{7,6},{8,9},{9,8},{10,11... | collective-permute-start | bytes 165896 | tf_op jit(solution)/shard_map/ppermute | solution.py:39
  11.0 0.7 %collective-permute-start = (bf16[3,24,2,192]{3,2,1,0:T(2,128)(2,1)S(1)}, bf16[3,24,2,192]{3,2,1,0:T(2,128)(2,1)S(1)}, u32[]{:S(2)}, u32[]{:S(2)}) collective-permute-start(bf16[3,24,2,192]{3,2,1,0:T(2,128)(2,1)S(1)} %bitcast.32), channel_id=1, source_target_pairs={{1,2},{2,1},{5,6},{6,5},{9,10},{10,9},{13,14},{14,13},{17,18},{18,... | collective-permute-start | bytes 165896 | tf_op jit(solution)/shard_map/ppermute | solution.py:39
  11.7 0.0 copy-done
  11.7 0.0 copy-start.4
  11.7 0.0 copy-start.5
  11.7 0.0 copy-start.6
  11.7 0.1 fusion
  11.8 0.1 add_convert_fusion.scalars_ref
  11.9 0.0 copy-start.10
  11.9 0.7 %copy-done.10 = bf16[192]{0:T(256)(128)(2,1)S(1)} copy-done((bf16[192]{0:T(256)(128)(2,1)S(1)}, bf16[192]{0:T(256)(128)(2,1)}, u32[]{:S(2)}) %copy-start.10) | copy-done | bytes 408
  12.5 0.0 copy-start.11
  12.6 0.6 %copy-done.11 = bf16[192]{0:T(256)(128)(2,1)S(1)} copy-done((bf16[192]{0:T(256)(128)(2,1)S(1)}, bf16[192]{0:T(256)(128)(2,1)}, u32[]{:S(2)}) %copy-start.11) | copy-done | bytes 408
  13.2 2.7 %collective-permute-done.1 = bf16[3,24,2,192]{3,2,1,0:T(2,128)(2,1)S(1)} collective-permute-done((bf16[3,24,2,192]{3,2,1,0:T(2,128)(2,1)S(1)}, bf16[3,24,2,192]{3,2,1,0:T(2,128)(2,1)S(1)}, u32[]{:S(2)}, u32[]{:S(2)}) %collective-permute-start.1) | collective-permute-done | bytes 55328 | tf_op jit(solution)/shard_map/ppermute | solution.py:39
  16.0 0.0 collective-permute-done
  16.0 0.0 copy-start.3
  16.0 0.0 copy-start.1
  16.0 0.0 copy-start.2
  16.0 0.1 fusion.1
  16.1 0.4 %broadcast_select_fusion.2 = (bf16[18,6,2,192]{3,2,1,0:T(2,128)(2,1)S(1)}, bf16[18,6,2,192]{3,2,1,0:T(2,128)(2,1)S(1)}) fusion(pred[]{:T(512)S(6)} %eq.22, bf16[3,6,2,192]{3,2,1,0:T(2,128)(2,1)S(1)} %get-tuple-element.37, bf16[12,6,2,192]{3,2,1,0:T(2,128)(2,1)S(1)} %get-tuple-element.24, bf16[3,6,2,192]{3,2,1,0:T(2,128)(2,1)S(1)} %get-tuple-element.34, ...), kind=kLoop, calls=%fused_computation.2 | loop fusion | flops 248832 | bytes 331777 | tf_op jit(solution)/shard_map/jit(_where)/select_n | solution.py:33
  16.5 0.0 copy-start.7
  16.5 1.2 %collective-permute-start.3 = (bf16[18,6,2,192]{3,2,1,0:T(2,128)(2,1)S(1)}, bf16[18,6,2,192]{3,2,1,0:T(2,128)(2,1)S(1)}, u32[]{:S(2)}, u32[]{:S(2)}) collective-permute-start(bf16[18,6,2,192]{3,2,1,0:T(2,128)(2,1)S(1)} %get-tuple-element.27), channel_id=1, source_target_pairs={{4,8},{8,4},{12,16},{16,12},{20,24},{24,20},{28,0},{0,28},{5,9},{9... | collective-permute-start | bytes 248840 | tf_op jit(solution)/shard_map/ppermute | solution.py:39
  17.7 0.4 %collective-permute-start.2 = (bf16[18,6,2,192]{3,2,1,0:T(2,128)(2,1)S(1)}, bf16[18,6,2,192]{3,2,1,0:T(2,128)(2,1)S(1)}, u32[]{:S(2)}, u32[]{:S(2)}) collective-permute-start(bf16[18,6,2,192]{3,2,1,0:T(2,128)(2,1)S(1)} %get-tuple-element.28), channel_id=1, source_target_pairs={{0,4},{4,0},{8,12},{12,8},{16,20},{20,16},{24,28},{28,24},{1,5},{5... | collective-permute-start | bytes 248840 | tf_op jit(solution)/shard_map/ppermute | solution.py:39
  18.1 0.0 all-to-all-done.recv_ref
  18.1 0.0 copy-done.4
  18.1 0.0 copy-done.5
  18.1 0.0 copy-done.6
  18.1 0.0 copy-done.3
  18.2 0.0 copy-done.1
  18.2 0.0 copy-done.2
  18.2 0.0 copy-done.7
  18.2 5.0 %shard_map.137 = (bf16[12,24,2,192]{3,2,1,0:T(2,128)(2,1)}, f32[928,256]{1,0:T(8,128)S(1)}) custom-call(s32[3]{0:T(128)S(1)} %add_convert_fusion.scalars_ref, bf16[32,10,2,128]{3,2,1,0:T(2,128)(2,1)S(1)} %all-to-all-done.recv_ref, bf16[3,24,2,192]{3,2,1,0:T(2,128)(2,1)S(1)} %bitcast.25, bf16[3,24,2,192]{3,2,1,0:T(2,128)(2,1)S(1)} %bitcast.22, ...), custom_call_target="tpu_custom_call" | custom-call | flops 4000000000 | bytes 4000000 | tf_op jit(solution)/shard_map/pallas_call | solution.py:520
  23.2 0.0 collective-permute-done.3
  23.2 0.0 collective-permute-done.2
  23.2 0.2 broadcast_select_fusion
  23.4 4.8 %shard_map.138 = bf16[12,24,2,192]{3,2,1,0:T(2,128)(2,1)} custom-call(s32[3]{0:T(128)S(1)} %add_convert_fusion.scalars_ref, f32[928,256]{1,0:T(8,128)S(1)} %get-tuple-element.19.rest_ref, bf16[3,24,2,192]{3,2,1,0:T(2,128)(2,1)S(1)} %bitcast.26, bf16[3,24,2,192]{3,2,1,0:T(2,128)(2,1)S(1)} %bitcast.23, ...), custom_call_target="tpu_custom_call", output_to_operand_aliasing={{}: (13, {})} | custom-call | flops 3000000000 | bytes 4000000 | tf_op jit(solution)/shard_map/pallas_call | solution.py:546
  (4 shorter events, 0.0 us)
Async XLA Ops:
  1.7 7.4 %copy-start.8 = (bf16[3,24,2,192]{3,2,1,0:T(2,128)(2,1)S(1)}, bf16[3,24,2,192]{3,2,1,0:T(2,128)(2,1)}, u32[]{:S(2)}) copy-start(bf16[3,24,2,192]{3,2,1,0:T(2,128)(2,1)} %get-tuple-element.15) | copy-start | bytes 165892
  1.8 7.4 %copy-start.9 = (bf16[3,24,2,192]{3,2,1,0:T(2,128)(2,1)S(1)}, bf16[3,24,2,192]{3,2,1,0:T(2,128)(2,1)}, u32[]{:S(2)}) copy-start(bf16[3,24,2,192]{3,2,1,0:T(2,128)(2,1)} %get-tuple-element.16) | copy-start | bytes 165892
  1.8 9.9 %copy-start = (bf16[12,24,2,192]{3,2,1,0:T(2,128)(2,1)S(1)}, bf16[12,24,2,192]{3,2,1,0:T(2,128)(2,1)}, u32[]{:S(2)}) copy-start(bf16[12,24,2,192]{3,2,1,0:T(2,128)(2,1)} %back_ref.5) | copy-start | bytes 663556
  1.8 16.4 %all-to-all-start = ((bf16[32,10,2,128]{3,2,1,0:T(2,128)(2,1)}), bf16[32,10,2,128]{3,2,1,0:T(2,128)(2,1)S(1)}, u32[]{:S(2)}, u32[]{:S(2)}) async-start(bf16[32,10,2,128]{3,2,1,0:T(2,128)(2,1)} %bitcast.30), calls=%async_computation | async-start | bytes 327680 | tf_op jit(solution)/shard_map/all_to_all | solution.py:493
  9.1 6.8 %collective-permute-start.1 = (bf16[3,24,2,192]{3,2,1,0:T(2,128)(2,1)S(1)}, bf16[3,24,2,192]{3,2,1,0:T(2,128)(2,1)S(1)}, u32[]{:S(2)}, u32[]{:S(2)}) collective-permute-start(bf16[3,24,2,192]{3,2,1,0:T(2,128)(2,1)S(1)} %bitcast.34), channel_id=1, source_target_pairs={{0,1},{1,0},{2,3},{3,2},{4,5},{5,4},{6,7},{7,6},{8,9},{9,8},{10,11... | collective-permute-start | bytes 165896 | tf_op jit(solution)/shard_map/ppermute | solution.py:39
  11.0 5.0 %collective-permute-start = (bf16[3,24,2,192]{3,2,1,0:T(2,128)(2,1)S(1)}, bf16[3,24,2,192]{3,2,1,0:T(2,128)(2,1)S(1)}, u32[]{:S(2)}, u32[]{:S(2)}) collective-permute-start(bf16[3,24,2,192]{3,2,1,0:T(2,128)(2,1)S(1)} %bitcast.32), channel_id=1, source_target_pairs={{1,2},{2,1},{5,6},{6,5},{9,10},{10,9},{13,14},{14,13},{17,18},{18,... | collective-permute-start | bytes 165896 | tf_op jit(solution)/shard_map/ppermute | solution.py:39
  11.7 6.5 %copy-start.4 = (bf16[192,384]{1,0:T(8,128)(2,1)S(1)}, bf16[192,384]{1,0:T(8,128)(2,1)}, u32[]{:S(2)}) copy-start(bf16[192,384]{1,0:T(8,128)(2,1)} %lift_ref.1) | copy-start | bytes 442372
  11.7 6.5 %copy-start.5 = (bf16[192,192]{1,0:T(8,128)(2,1)S(1)}, bf16[192,192]{1,0:T(8,128)(2,1)}, u32[]{:S(2)}) copy-start(bf16[192,192]{1,0:T(8,128)(2,1)} %refs_2_.3) | copy-start | bytes 221188
  11.7 6.5 %copy-start.6 = (bf16[128,192]{0,1:T(8,128)(2,1)S(1)}, bf16[128,192]{0,1:T(8,128)(2,1)}, u32[]{:S(2)}) copy-start(bf16[128,192]{0,1:T(8,128)(2,1)} %param.19) | copy-start | bytes 147460
  11.9 0.7 %copy-start.10 = (bf16[192]{0:T(256)(128)(2,1)S(1)}, bf16[192]{0:T(256)(128)(2,1)}, u32[]{:S(2)}) copy-start(bf16[192]{0:T(256)(128)(2,1)} %param.22) | copy-start | bytes 1156
  12.5 0.7 %copy-start.11 = (bf16[192]{0:T(256)(128)(2,1)S(1)}, bf16[192]{0:T(256)(128)(2,1)}, u32[]{:S(2)}) copy-start(bf16[192]{0:T(256)(128)(2,1)} %param.25) | copy-start | bytes 1156
  16.0 2.2 %copy-start.3 = (bf16[192,576]{1,0:T(8,128)(2,1)S(1)}, bf16[192,576]{1,0:T(8,128)(2,1)}, u32[]{:S(2)}) copy-start(bf16[192,576]{1,0:T(8,128)(2,1)} %refs_1_.3) | copy-start | bytes 663556
  16.0 2.2 %copy-start.1 = (bf16[192,768]{1,0:T(8,128)(2,1)S(1)}, bf16[192,768]{1,0:T(8,128)(2,1)}, u32[]{:S(2)}) copy-start(bf16[192,768]{1,0:T(8,128)(2,1)} %refs_4_.3) | copy-start | bytes 884740
  16.0 2.2 %copy-start.2 = (bf16[768,192]{0,1:T(8,128)(2,1)S(1)}, bf16[768,192]{0,1:T(8,128)(2,1)}, u32[]{:S(2)}) copy-start(bf16[768,192]{0,1:T(8,128)(2,1)} %param.27) | copy-start | bytes 884740
  16.5 1.7 %copy-start.7 = (bf16[8,192]{1,0:T(8,128)(2,1)S(1)}, bf16[8,192]{1,0:T(8,128)(2,1)}, u32[]{:S(2)}) copy-start(bf16[8,192]{1,0:T(8,128)(2,1)} %table_ref.1) | copy-start | bytes 9220
  16.5 6.8 %collective-permute-start.3 = (bf16[18,6,2,192]{3,2,1,0:T(2,128)(2,1)S(1)}, bf16[18,6,2,192]{3,2,1,0:T(2,128)(2,1)S(1)}, u32[]{:S(2)}, u32[]{:S(2)}) collective-permute-start(bf16[18,6,2,192]{3,2,1,0:T(2,128)(2,1)S(1)} %get-tuple-element.27), channel_id=1, source_target_pairs={{4,8},{8,4},{12,16},{16,12},{20,24},{24,20},{28,0},{0,28},{5,9},{9... | collective-permute-start | bytes 248840 | tf_op jit(solution)/shard_map/ppermute | solution.py:39
  17.7 5.5 %collective-permute-start.2 = (bf16[18,6,2,192]{3,2,1,0:T(2,128)(2,1)S(1)}, bf16[18,6,2,192]{3,2,1,0:T(2,128)(2,1)S(1)}, u32[]{:S(2)}, u32[]{:S(2)}) collective-permute-start(bf16[18,6,2,192]{3,2,1,0:T(2,128)(2,1)S(1)} %get-tuple-element.28), channel_id=1, source_target_pairs={{0,4},{4,0},{8,12},{12,8},{16,20},{20,16},{24,28},{28,24},{1,5},{5... | collective-permute-start | bytes 248840 | tf_op jit(solution)/shard_map/ppermute | solution.py:39

commit v11 on v9

--- a/solution.py
+++ b/solution.py
@@ -26,17 +26,22 @@
 COLS = ROWS + len(AROUND)
 
 
-def swapped(up, down, axis, wraps):
+def swap_pairs(axis, first, wraps):
     count = lax.axis_size(axis)
+    pairs = []
+    for low in range(first, count, 2):
+        high = (low + 1) % count
+        if high > low or wraps:
+            pairs += [(low, high), (high, low)]
+    return pairs
+
+
+def swapped(mine, axis, wraps):
+    return [lax.ppermute(one, axis, swap_pairs(axis, n, wraps)) for n, one in enumerate(mine)]
+
+
+def in_order(got, axis):
     even = lax.axis_index(axis) % 2 == 0
-    got = []
-    for first, mine in ((0, jnp.where(even, down, up)), (1, jnp.where(even, up, down))):
-        pairs = []
-        for low in range(first, count, 2):
-            high = (low + 1) % count
-            if high > low or wraps:
-                pairs += [(low, high), (high, low)]
-        got.append(lax.ppermute(mine, axis, pairs))
     return jnp.where(even, got[1], got[0]), jnp.where(even, got[0], got[1])
 
 
@@ -463,6 +468,42 @@
         copy.wait()
 
 
+def join_kernel(even_ref, one_ref, two_ref, back_ref, north_ref, south_ref, first_ref, second_ref):
+    lat_cells, lon_cells = back_ref.shape[:2]
+
+    def strips(before, after):
+        north_ref[...] = before[...]
+        south_ref[...] = after[...]
+
+    def sides(left, right):
+        for ref, low in ((left, 0), (right, lon_cells - HLON)):
+            ref[:HLAT] = north_ref[:, low : low + HLON]
+            ref[HLAT : HLAT + lat_cells] = back_ref[:, low : low + HLON]
+            ref[HLAT + lat_cells :] = south_ref[:, low : low + HLON]
+
+    pl.when(even_ref[0] == 1)(lambda: strips(two_ref, one_ref))
+    pl.when(even_ref[0] == 0)(lambda: strips(one_ref, two_ref))
+    pl.when(even_ref[1] == 1)(lambda: sides(second_ref, first_ref))
+    pl.when(even_ref[1] == 0)(lambda: sides(first_ref, second_ref))
+
+
+def joined(even, got, background):
+    lat_cells, lon_cells, levels, width = background.shape
+    across = jax.ShapeDtypeStruct((HLAT, lon_cells, levels, width), BF16)
+    along = jax.ShapeDtypeStruct((lat_cells + WLAT, HLON, levels, width), BF16)
+    vmem = pl.BlockSpec(memory_space=pltpu.VMEM)
+    return pl.pallas_call(
+        join_kernel,
+        out_shape=[across, across, along, along],
+        in_specs=[pl.BlockSpec(memory_space=pltpu.SMEM), vmem, vmem, vmem],
+        out_specs=[vmem] * 4,
+        compiler_params=pltpu.CompilerParams(vmem_limit_bytes=LIMIT),
+        cost_estimate=pl.CostEstimate(
+            flops=20 * 10**9, bytes_accessed=10**6, transcendentals=0
+        ),
+    )(even, *got, background)
+
+
 def local(
     record_values,
     record_cell,
@@ -486,14 +527,12 @@
         record_values, record_cell, record_instrument, block_counts, background
     )
     received = lax.all_to_all(sent, ("lon", "lat"), split_axis=0, concat_axis=0, tiled=True)
-    north, south = swapped(up, down, "lat", wraps=False)
-
+    even = [lax.axis_index(axis) % 2 == 0 for axis in ("lat", "lon")]
+    mine = (jnp.where(even[0], down, up), jnp.where(even[0], up, down))
+    got = swapped(mine, "lat", wraps=False)
     later, _ = lax.optimization_barrier((background, up))
-
-    def columns(low, end):
-        return jnp.concatenate([north[:, low:end], later[:, low:end], south[:, low:end]], axis=0)
-
-    west, east = swapped(columns(0, HLON), columns(lon_cells - HLON, lon_cells), "lon", wraps=True)
+    north, south, *mine = joined(jnp.stack(even).astype(jnp.int32), got, later)
+    got = swapped(mine, "lon", wraps=True)
 
     lat = lax.axis_index("lat")
     scalars = jnp.stack([lat == 0, lat < 0, lat == tiles_lat - 1]).astype(jnp.int32)
@@ -536,6 +575,8 @@
         lift_weight,
         *weights,
     )
+    rest, *got = lax.optimization_barrier((rest, *got))
+    west, east = in_order(got, "lon")
     return pl.pallas_call(
         functools.partial(side_kernel, plan),
         out_shape=result,

time: 32.9 us -> 31 us (0.942)
  waiting for transfers between devices: 6.07 us -> 1.5 us
  starting transfers between devices: 12.3 us -> 15.1 us
  Pallas kernels: 11.6 us -> 12.3 us
    ppermute x4, waiting for transfers between devices: 6.07 us -> 1.5 us  [swapped(): lax.ppermute(one, axis, swap_pairs(axis, n, wraps))]
    ppermute x4, starting transfers between devices: 5.02 us -> 7.78 us  [swapped(): lax.ppermute(one, axis, swap_pairs(axis, n, wraps))]
    pallas_call x0 -> x1, Pallas kernels: none -> 0.69 us  [joined(): pl.pallas_call(join_kernel, out_shape=[across, across, along, along], in_...]
    select_n x4 -> x2, other arithmetic: 0.58 us -> 0.2 us  [the longest x1 0.18 us: in_order(): return (jnp.where(even, got[1], got[0]), jnp.where(even, got[0], got[1]))]
  transfers between devices with their start and end apart: 5 -> 5, of which waited for: 2 -> 1; matrix products, arithmetic and copies ran while one was open for 3% -> 1% of each run, Pallas kernels for 0% -> 19%
where the time goes in v11:
time: 31 us; the launch traced here: 30.7 us
  starting transfers between devices  15.1 us (49%)
  Pallas kernels  12.3 us (40%)
  waiting for transfers between devices  1.5 us (5%)
  local copies, waits for them, and re-layouts  1.29 us (4%)
  other arithmetic  0.35 us (1%)
    ppermute x4, starting transfers between devices, swapped(): lax.ppermute(one, axis, swap_pairs(axis, n, wraps))  7.78 us
    all_to_all x1, starting transfers between devices, local(): lax.all_to_all(sent, ('lon', 'lat'), split_axis=0, concat_axis=0, tiled=T...  7.3 us
    pallas_call x1, Pallas kernels, local(): pl.pallas_call(functools.partial(middle_kernel, plan), out_shape=[result,...  5.03 us
    pallas_call x1, Pallas kernels, local(): pl.pallas_call(functools.partial(side_kernel, plan), out_shape=result, in...  4.84 us
    pallas_call x1, Pallas kernels, packed(): pl.pallas_call(pack_kernel, out_shape=[jax.ShapeDtypeStruct(shape, BF16),...  1.73 us
    ppermute x4, waiting for transfers between devices, swapped(): lax.ppermute(one, axis, swap_pairs(axis, n, wraps))  1.5 us
    unnamed x24, local copies, waits for them, and re-layouts  1.28 us
    pallas_call x1, Pallas kernels, joined(): pl.pallas_call(join_kernel, out_shape=[across, across, along, along], in_...  0.69 us
  transfers between devices with their start and end apart: 5, of which 1 were waited for; matrix products, arithmetic and copies ran while one was open for 1% of the time, Pallas kernels for 19%

profile of v11, /device:TPU:0, one launch (start us, length us, event | category | flops | bytes accessed | tf_op | source)
XLA Modules:
  0.0 30.7 jit_solution(6159855809177414635)
XLA Ops:
  0.0 1.7 %shard_map.136 = (bf16[8,4,10,2,128]{4,3,2,1,0:T(2,128)(2,1)}, bf16[3,24,2,192]{3,2,1,0:T(2,128)(2,1)}, bf16[3,24,2,192]{3,2,1,0:T(2,128)(2,1)}) custom-call(bf16[8,4,2,128]{3,2,1,0:T(2,128)(2,1)} %values_ref.1, s32[8,8]{1,0:T(8,128)} %bitcast.27, s32[8,8]{1,0:T(8,128)} %bitcast.28, s32[4,8]{1,0:T(4,128)} %bitcast.29, bf16[12,24,2,192]{3,2,1,0:T(2,128)(2,1)} %back_ref.6), custom_call_target="tpu_custom_call" | custom-call | flops 20000000000 | bytes 1000000 | tf_op jit(solution)/shard_map/pallas_call | solution.py:180
  1.7 0.0 copy-start.8
  1.8 0.0 copy-start.9
  1.8 0.0 copy-start
  1.8 7.3 %all-to-all-start = ((bf16[32,10,2,128]{3,2,1,0:T(2,128)(2,1)}), bf16[32,10,2,128]{3,2,1,0:T(2,128)(2,1)S(1)}, u32[]{:S(2)}, u32[]{:S(2)}) async-start(bf16[32,10,2,128]{3,2,1,0:T(2,128)(2,1)} %bitcast.22), calls=%async_computation | async-start | bytes 327680 | tf_op jit(solution)/shard_map/all_to_all | solution.py:529
  9.1 0.0 copy-done.8
  9.1 0.0 copy-done.9
  9.1 0.7 %collective-permute-start.1 = (bf16[3,24,2,192]{3,2,1,0:T(2,128)(2,1)S(1)}, bf16[3,24,2,192]{3,2,1,0:T(2,128)(2,1)S(1)}, u32[]{:S(2)}, u32[]{:S(2)}) collective-permute-start(bf16[3,24,2,192]{3,2,1,0:T(2,128)(2,1)S(1)} %bitcast.24), channel_id=1, source_target_pairs={{1,2},{2,1},{5,6},{6,5},{9,10},{10,9},{13,14},{14,13},{17,18},{18,... | collective-permute-start | bytes 165896 | tf_op jit(solution)/shard_map/ppermute | solution.py:40
  9.8 4.5 %collective-permute-start = (bf16[3,24,2,192]{3,2,1,0:T(2,128)(2,1)S(1)}, bf16[3,24,2,192]{3,2,1,0:T(2,128)(2,1)S(1)}, u32[]{:S(2)}, u32[]{:S(2)}) collective-permute-start(bf16[3,24,2,192]{3,2,1,0:T(2,128)(2,1)S(1)} %bitcast.23), channel_id=1, source_target_pairs={{0,1},{1,0},{2,3},{3,2},{4,5},{5,4},{6,7},{7,6},{8,9},{9,8},{10,11... | collective-permute-start | bytes 165896 | tf_op jit(solution)/shard_map/ppermute | solution.py:40
  14.4 0.1 add_convert_fusion.1.even_ref
  14.4 0.0 copy-start.10
  14.4 0.1 add_convert_fusion.scalars_ref
  14.5 0.6 %copy-done.10 = bf16[192]{0:T(256)(128)(2,1)S(1)} copy-done((bf16[192]{0:T(256)(128)(2,1)S(1)}, bf16[192]{0:T(256)(128)(2,1)}, u32[]{:S(2)}) %copy-start.10) | copy-done | bytes 408
  15.1 0.0 copy-start.11
  15.1 0.6 %copy-done.11 = bf16[192]{0:T(256)(128)(2,1)S(1)} copy-done((bf16[192]{0:T(256)(128)(2,1)S(1)}, bf16[192]{0:T(256)(128)(2,1)}, u32[]{:S(2)}) %copy-start.11) | copy-done | bytes 408
  15.8 0.0 copy-start.1
  15.8 0.0 copy-start.2
  15.8 0.0 copy-start.3
  15.8 0.0 copy-start.4
  15.8 0.0 copy-start.5
  15.8 0.0 copy-start.6
  15.8 0.0 collective-permute-done.1.two_ref
  15.8 1.5 %collective-permute-done.one_ref = bf16[3,24,2,192]{3,2,1,0:T(2,128)(2,1)S(1)} collective-permute-done((bf16[3,24,2,192]{3,2,1,0:T(2,128)(2,1)S(1)}, bf16[3,24,2,192]{3,2,1,0:T(2,128)(2,1)S(1)}, u32[]{:S(2)}, u32[]{:S(2)}) %collective-permute-start) | collective-permute-done | bytes 55328 | tf_op jit(solution)/shard_map/ppermute | solution.py:40
  17.3 0.0 copy-done
  17.3 0.7 %shard_map.137 = (bf16[3,24,2,192]{3,2,1,0:T(2,128)(2,1)S(1)}, bf16[3,24,2,192]{3,2,1,0:T(2,128)(2,1)S(1)}, bf16[18,6,2,192]{3,2,1,0:T(2,128)(2,1)S(1)}, bf16[18,6,2,192]{3,2,1,0:T(2,128)(2,1)S(1)}) custom-call(s32[2]{0:T(128)S(1)} %add_convert_fusion.1.even_ref, bf16[3,24,2,192]{3,2,1,0:T(2,128)(2,1)S(1)} %collective-permute-done.one_ref, ...), custom_call_target="tpu_custom_call" | custom-call | flops 20000000000 | bytes 1000000 | tf_op jit(solution)/shard_map/pallas_call | solution.py:495
  18.0 0.1 collective-permute-start.2
  18.1 0.0 copy-start.7
  18.1 2.5 %collective-permute-start.3 = (bf16[18,6,2,192]{3,2,1,0:T(2,128)(2,1)S(1)}, bf16[18,6,2,192]{3,2,1,0:T(2,128)(2,1)S(1)}, u32[]{:S(2)}, u32[]{:S(2)}) collective-permute-start(bf16[18,6,2,192]{3,2,1,0:T(2,128)(2,1)S(1)} %get-tuple-element.26), channel_id=1, source_target_pairs={{4,8},{8,4},{12,16},{16,12},{20,24},{24,20},{28,0},{0,28},{5,9},{9... | collective-permute-start | bytes 248840 | tf_op jit(solution)/shard_map/ppermute | solution.py:40
  20.6 0.0 all-to-all-done.recv_ref
  20.6 0.0 copy-done.1
  20.6 0.0 copy-done.2
  20.6 0.0 copy-done.3
  20.6 0.0 copy-done.4
  20.6 0.0 copy-done.5
  20.6 0.0 copy-done.6
  20.6 0.0 copy-done.7
  20.6 5.0 %shard_map.138 = (bf16[12,24,2,192]{3,2,1,0:T(2,128)(2,1)}, f32[928,256]{1,0:T(8,128)S(1)}) custom-call(s32[3]{0:T(128)S(1)} %add_convert_fusion.scalars_ref, bf16[32,10,2,128]{3,2,1,0:T(2,128)(2,1)S(1)} %all-to-all-done.recv_ref, bf16[3,24,2,192]{3,2,1,0:T(2,128)(2,1)S(1)} %get-tuple-element.22.north_ref, ...), custom_call_target="tpu_custom_call" | custom-call | flops 4000000000 | bytes 4000000 | tf_op jit(solution)/shard_map/pallas_call | solution.py:554
  25.7 0.0 collective-permute-done.2
  25.7 0.0 collective-permute-done.3
  25.7 0.2 broadcast_select_fusion
  25.9 4.8 %shard_map.139 = bf16[12,24,2,192]{3,2,1,0:T(2,128)(2,1)} custom-call(s32[3]{0:T(128)S(1)} %add_convert_fusion.scalars_ref, f32[928,256]{1,0:T(8,128)S(1)} %get-tuple-element.27.rest_ref, bf16[3,24,2,192]{3,2,1,0:T(2,128)(2,1)S(1)} %get-tuple-element.22.north_ref, ...), custom_call_target="tpu_custom_call", output_to_operand_aliasing={{}: (13, {})} | custom-call | flops 3000000000 | bytes 4000000 | tf_op jit(solution)/shard_map/pallas_call | solution.py:580
  (3 shorter events, 0.0 us)
Async XLA Ops:
  1.7 7.4 %copy-start.8 = (bf16[3,24,2,192]{3,2,1,0:T(2,128)(2,1)S(1)}, bf16[3,24,2,192]{3,2,1,0:T(2,128)(2,1)}, u32[]{:S(2)}) copy-start(bf16[3,24,2,192]{3,2,1,0:T(2,128)(2,1)} %get-tuple-element.20) | copy-start | bytes 165892
  1.8 7.4 %copy-start.9 = (bf16[3,24,2,192]{3,2,1,0:T(2,128)(2,1)S(1)}, bf16[3,24,2,192]{3,2,1,0:T(2,128)(2,1)}, u32[]{:S(2)}) copy-start(bf16[3,24,2,192]{3,2,1,0:T(2,128)(2,1)} %get-tuple-element.19) | copy-start | bytes 165892
  1.8 15.5 %copy-start = (bf16[12,24,2,192]{3,2,1,0:T(2,128)(2,1)S(1)}, bf16[12,24,2,192]{3,2,1,0:T(2,128)(2,1)}, u32[]{:S(2)}) copy-start(bf16[12,24,2,192]{3,2,1,0:T(2,128)(2,1)} %back_ref.6) | copy-start | bytes 663556
  1.8 18.8 %all-to-all-start = ((bf16[32,10,2,128]{3,2,1,0:T(2,128)(2,1)}), bf16[32,10,2,128]{3,2,1,0:T(2,128)(2,1)S(1)}, u32[]{:S(2)}, u32[]{:S(2)}) async-start(bf16[32,10,2,128]{3,2,1,0:T(2,128)(2,1)} %bitcast.22), calls=%async_computation | async-start | bytes 327680 | tf_op jit(solution)/shard_map/all_to_all | solution.py:529
  9.1 6.7 %collective-permute-start.1 = (bf16[3,24,2,192]{3,2,1,0:T(2,128)(2,1)S(1)}, bf16[3,24,2,192]{3,2,1,0:T(2,128)(2,1)S(1)}, u32[]{:S(2)}, u32[]{:S(2)}) collective-permute-start(bf16[3,24,2,192]{3,2,1,0:T(2,128)(2,1)S(1)} %bitcast.24), channel_id=1, source_target_pairs={{1,2},{2,1},{5,6},{6,5},{9,10},{10,9},{13,14},{14,13},{17,18},{18,... | collective-permute-start | bytes 165896 | tf_op jit(solution)/shard_map/ppermute | solution.py:40
  9.8 7.5 %collective-permute-start = (bf16[3,24,2,192]{3,2,1,0:T(2,128)(2,1)S(1)}, bf16[3,24,2,192]{3,2,1,0:T(2,128)(2,1)S(1)}, u32[]{:S(2)}, u32[]{:S(2)}) collective-permute-start(bf16[3,24,2,192]{3,2,1,0:T(2,128)(2,1)S(1)} %bitcast.23), channel_id=1, source_target_pairs={{0,1},{1,0},{2,3},{3,2},{4,5},{5,4},{6,7},{7,6},{8,9},{9,8},{10,11... | collective-permute-start | bytes 165896 | tf_op jit(solution)/shard_map/ppermute | solution.py:40
  14.4 0.7 %copy-start.10 = (bf16[192]{0:T(256)(128)(2,1)S(1)}, bf16[192]{0:T(256)(128)(2,1)}, u32[]{:S(2)}) copy-start(bf16[192]{0:T(256)(128)(2,1)} %param.22) | copy-start | bytes 1156
  15.1 0.7 %copy-start.11 = (bf16[192]{0:T(256)(128)(2,1)S(1)}, bf16[192]{0:T(256)(128)(2,1)}, u32[]{:S(2)}) copy-start(bf16[192]{0:T(256)(128)(2,1)} %param.25) | copy-start | bytes 1156
  15.8 4.8 %copy-start.1 = (bf16[192,768]{1,0:T(8,128)(2,1)S(1)}, bf16[192,768]{1,0:T(8,128)(2,1)}, u32[]{:S(2)}) copy-start(bf16[192,768]{1,0:T(8,128)(2,1)} %refs_4_.3) | copy-start | bytes 884740
  15.8 4.8 %copy-start.2 = (bf16[768,192]{0,1:T(8,128)(2,1)S(1)}, bf16[768,192]{0,1:T(8,128)(2,1)}, u32[]{:S(2)}) copy-start(bf16[768,192]{0,1:T(8,128)(2,1)} %param.27) | copy-start | bytes 884740
  15.8 4.8 %copy-start.3 = (bf16[192,576]{1,0:T(8,128)(2,1)S(1)}, bf16[192,576]{1,0:T(8,128)(2,1)}, u32[]{:S(2)}) copy-start(bf16[192,576]{1,0:T(8,128)(2,1)} %refs_1_.3) | copy-start | bytes 663556
  15.8 4.8 %copy-start.4 = (bf16[192,384]{1,0:T(8,128)(2,1)S(1)}, bf16[192,384]{1,0:T(8,128)(2,1)}, u32[]{:S(2)}) copy-start(bf16[192,384]{1,0:T(8,128)(2,1)} %lift_ref.1) | copy-start | bytes 442372
  15.8 4.8 %copy-start.5 = (bf16[192,192]{1,0:T(8,128)(2,1)S(1)}, bf16[192,192]{1,0:T(8,128)(2,1)}, u32[]{:S(2)}) copy-start(bf16[192,192]{1,0:T(8,128)(2,1)} %refs_2_.3) | copy-start | bytes 221188
  15.8 4.8 %copy-start.6 = (bf16[128,192]{0,1:T(8,128)(2,1)S(1)}, bf16[128,192]{0,1:T(8,128)(2,1)}, u32[]{:S(2)}) copy-start(bf16[128,192]{0,1:T(8,128)(2,1)} %param.19) | copy-start | bytes 147460
  18.0 7.7 %collective-permute-start.2 = (bf16[18,6,2,192]{3,2,1,0:T(2,128)(2,1)S(1)}, bf16[18,6,2,192]{3,2,1,0:T(2,128)(2,1)S(1)}, u32[]{:S(2)}, u32[]{:S(2)}) collective-permute-start(bf16[18,6,2,192]{3,2,1,0:T(2,128)(2,1)S(1)} %get-tuple-element.25), channel_id=1, source_target_pairs={{0,4},{4,0},{8,12},{12,8},{16,20},{20,16},{24,28},{28,24},{1,5},{5... | collective-permute-start | bytes 248840 | tf_op jit(solution)/shard_map/ppermute | solution.py:40
  18.1 2.6 %copy-start.7 = (bf16[8,192]{1,0:T(8,128)(2,1)S(1)}, bf16[8,192]{1,0:T(8,128)(2,1)}, u32[]{:S(2)}) copy-start(bf16[8,192]{1,0:T(8,128)(2,1)} %table_ref.1) | copy-start | bytes 9220
  18.1 7.6 %collective-permute-start.3 = (bf16[18,6,2,192]{3,2,1,0:T(2,128)(2,1)S(1)}, bf16[18,6,2,192]{3,2,1,0:T(2,128)(2,1)S(1)}, u32[]{:S(2)}, u32[]{:S(2)}) collective-permute-start(bf16[18,6,2,192]{3,2,1,0:T(2,128)(2,1)S(1)} %get-tuple-element.26), channel_id=1, source_target_pairs={{4,8},{8,4},{12,16},{16,12},{20,24},{24,20},{28,0},{0,28},{5,9},{9... | collective-permute-start | bytes 248840 | tf_op jit(solution)/shard_map/ppermute | solution.py:40

commit v12 on v10

--- a/solution.py
+++ b/solution.py
@@ -83,6 +83,10 @@
 
 def dot_nt(a, b):
     return lax.dot_general(a, b, (((1,), (1,)), ((), ())), preferred_element_type=F32)
+
+
+def about_one_over(x):
+    return pl.reciprocal(x, approx=True)
 
 
 def with_ones(tensor):
@@ -260,7 +264,7 @@
         lane = lax.broadcasted_iota(jnp.int32, meta.shape, 1) // INSTR
         wide = meta.astype(F32)
         chosen = below(*[jnp.where(lane == n, wide, 0.0) for n in range(len(AROUND))]).astype(BF16)
-        encoded = gelu(dot_nt(records, first) + dot(chosen, table)).astype(BF16)
+        encoded = gelu(dot(records, first) + dot(chosen, table)).astype(BF16)
         lifted = gelu(dot(encoded, lift))
         tokens = dot_nt(weigh, meta)
         sums = []
@@ -289,7 +293,7 @@
     return sums
 
 
-def worked(plan, places, sum_of, borders, weights, scalars_ref, put):
+def worked(plan, places, sum_of, borders, weights, scalars_ref, put, done):
     back_ref, north_ref, south_ref, west_ref, east_ref = borders
     gain_one_ref, attn_ref, mix_ref, gain_two_ref, up_ref, down_ref = weights
     lat_cells, width = back_ref.shape[0], back_ref.shape[3]
@@ -314,7 +318,9 @@
         spans[tile, number] = (start, count)
         start += full
     sums = below(*[sum_of(*entry) for entry in entries_of(places)])
-    share = 1.0 / (1.0 + sums[:, width : width + 1])
+    tally = 1.0 + sums[:, width : width + 1]
+    share = about_one_over(tally)
+    share = share * (2.0 - tally * share)
     latent = ((below(*pieces) + sums[:, :width]) * share).astype(BF16).astype(F32)
     normed = normalise(latent, gain_one_ref[...].astype(F32))
     yield True
@@ -363,7 +369,7 @@
         raised = jnp.exp(scores - largest).astype(BF16)
         product = dot(raised, values[w * many : (w + 1) * many])
         yield True
-        product = product[:, :width] * (1.0 / product[:, width : width + 1])
+        product = product[:, :width] * about_one_over(product[:, width : width + 1])
         total = jnp.zeros((rows, width), F32)
         for h in range(HEADS):
             total = jnp.where(head_of == h, product[h * rows : (h + 1) * rows], total)
@@ -376,7 +382,7 @@
     normed_two = normalise(after, gain_two_ref[...].astype(F32)).astype(BF16)
     hidden = dot(normed_two, up_ref[...])
     yield True
-    result = after + dot_nt(gelu(hidden).astype(BF16), down_ref[...])
+    result = after + dot(gelu(hidden).astype(BF16), down_ref[...])
     yield True
     start = 0
     for (i, j), rows in zip(places, groups):
@@ -384,6 +390,7 @@
         piece = result[start : start + tokens_of(part)].astype(BF16)
         put(part, j, piece.reshape(part[1], part[3], LEV, width))
         start += rows
+    done(places)
 
 
 MIDDLE = [[(0, 1), (2, 1)], [(1, 1)]]
@@ -419,13 +426,29 @@
     def put(part, _, piece):
         held_ref[part[0] : part[0] + part[1]] = piece
 
+    copies = []
+
+    def done(places):
+        for i, _ in places:
+            top, high = plan[4][3 * i + 1][:2]
+            copies.append(
+                pltpu.make_async_copy(
+                    held_ref.at[top : top + high],
+                    out_ref.at[top : top + high, left : left + wide],
+                    sem.at[i],
+                )
+            )
+            copies[-1].start()
+
     borders = (back_ref, north_ref, south_ref, None, None)
     alternate(
-        *[worked(plan, places, sum_of, borders, weights, scalars_ref, put) for places in MIDDLE]
-    )
-    copy = pltpu.make_async_copy(held_ref, out_ref.at[:, left : left + wide], sem.at[0])
-    copy.start()
-    copy.wait()
+        *[
+            worked(plan, places, sum_of, borders, weights, scalars_ref, put, done)
+            for places in MIDDLE
+        ]
+    )
+    for copy in copies:
+        copy.wait()
 
 
 def side_kernel(
@@ -453,17 +476,25 @@
     def put(part, j, piece):
         held_ref[j // 2, part[0] : part[0] + part[1]] = piece
 
+    copies = []
+
+    def done(places):
+        j = places[0][1]
+        left, wide = plan[4][j][2:]
+        copies.append(
+            pltpu.make_async_copy(
+                held_ref.at[j // 2], out_ref.at[:, left : left + wide], sem.at[j // 2]
+            )
+        )
+        copies[-1].start()
+
     borders = (back_ref, north_ref, south_ref, west_ref, east_ref)
     alternate(
-        *[worked(plan, places, sum_of, borders, weights, scalars_ref, put) for places in SIDES]
-    )
-    copies = []
-    for n, number in enumerate((0, 2)):
-        left, wide = plan[4][number][2:]
-        copies.append(
-            pltpu.make_async_copy(held_ref.at[n], out_ref.at[:, left : left + wide], sem.at[n])
-        )
-        copies[n].start()
+        *[
+            worked(plan, places, sum_of, borders, weights, scalars_ref, put, done)
+            for places in SIDES
+        ]
+    )
     for copy in copies:
         copy.wait()
 
@@ -493,7 +524,9 @@
     received = lax.all_to_all(sent, ("lon", "lat"), split_axis=0, concat_axis=0, tiled=True)
     north, south = before_and_after(swapped(up, down, "lat", wraps=False), "lat")
 
-    later, _ = lax.optimization_barrier((background, up))
+    later, input_weight, down_weight, _ = lax.optimization_barrier(
+        (background, input_weight, down_weight, up)
+    )
 
     def columns(low, end):
         return jnp.concatenate([north[:, low:end], later[:, low:end], south[:, low:end]], axis=0)
@@ -510,7 +543,7 @@
         mix_weight,
         second_gain.reshape(1, width),
         up_weight,
-        down_weight.T,
+        down_weight,
     ]
     smem = pl.BlockSpec(memory_space=pltpu.SMEM)
     vmem = pl.BlockSpec(memory_space=pltpu.VMEM)
@@ -524,7 +557,7 @@
         out_specs=[anywhere, vmem],
         scratch_shapes=[
             pltpu.VMEM((lat_cells, lon_cells - WLON, LEV, width), BF16),
-            pltpu.SemaphoreType.DMA((1,)),
+            pltpu.SemaphoreType.DMA((3,)),
         ],
         compiler_params=params,
         cost_estimate=pl.CostEstimate(
@@ -536,7 +569,7 @@
         north,
         south,
         background,
-        input_weight.T,
+        input_weight,
         instrument_table,
         lift_weight,
         *weights,

time: 28.8 us -> 28.9 us (level)
  local copies, waits for them, and re-layouts: 1.54 us -> 1.16 us
  waiting for transfers between devices: 2.76 us -> 3.1 us
    unnamed x24, local copies, waits for them, and re-layouts: 1.36 us -> 0.71 us
    ppermute x4, waiting for transfers between devices: 2.76 us -> 3.1 us  [swapped(): got.append(lax.ppermute(mine, axis, pairs))]
  transfers between devices with their start and end apart: 5 -> 5, of which waited for: 1 -> 1; matrix products, arithmetic and copies ran while one was open for 2% -> 3% of each run, Pallas kernels for 18% -> 18%
where the time goes in v12:
time: 28.9 us; the launch traced here: 28.4 us
  Pallas kernels  11.7 us (40%)
  starting transfers between devices  11.5 us (40%)
  waiting for transfers between devices  3.1 us (11%)
  local copies, waits for them, and re-layouts  1.16 us (4%)
  other arithmetic  0.66 us (2%)
    all_to_all x1, starting transfers between devices, local(): lax.all_to_all(sent, ('lon', 'lat'), split_axis=0, concat_axis=0, tiled=T...  7.3 us
    pallas_call x1, Pallas kernels, local(): pl.pallas_call(functools.partial(middle_kernel, plan), out_shape=[result,...  5.14 us
    pallas_call x1, Pallas kernels, local(): pl.pallas_call(functools.partial(side_kernel, plan), out_shape=result, in...  4.82 us
    ppermute x4, starting transfers between devices, swapped(): got.append(lax.ppermute(mine, axis, pairs))  4.15 us
    ppermute x4, waiting for transfers between devices, swapped(): got.append(lax.ppermute(mine, axis, pairs))  3.1 us
    pallas_call x1, Pallas kernels, packed(): pl.pallas_call(pack_kernel, out_shape=[jax.ShapeDtypeStruct(shape, BF16),...  1.74 us
    unnamed x24, local copies, waits for them, and re-layouts  0.71 us
  transfers between devices with their start and end apart: 5, of which 1 were waited for; matrix products, arithmetic and copies ran while one was open for 3% of the time, Pallas kernels for 18%

profile of v12, /device:TPU:0, one launch (start us, length us, event | category | flops | bytes accessed | tf_op | source)
XLA Modules:
  0.0 28.4 jit_solution(5251640616158226982)
XLA Ops:
  0.0 1.7 %shard_map.136 = (bf16[8,4,10,2,128]{4,3,2,1,0:T(2,128)(2,1)}, bf16[3,24,2,192]{3,2,1,0:T(2,128)(2,1)}, bf16[3,24,2,192]{3,2,1,0:T(2,128)(2,1)}) custom-call(bf16[8,4,2,128]{3,2,1,0:T(2,128)(2,1)} %values_ref.1, s32[8,8]{1,0:T(8,128)} %bitcast.32, s32[8,8]{1,0:T(8,128)} %bitcast.33, s32[4,8]{1,0:T(4,128)} %bitcast.34, bf16[12,24,2,192]{3,2,1,0:T(2,128)(2,1)} %back_ref.5), custom_call_target="tpu_custom_call" | custom-call | flops 20000000000 | bytes 1000000 | tf_op jit(solution)/shard_map/pallas_call | solution.py:184
  1.7 0.0 copy-start.7
  1.8 0.0 copy-start.8
  1.8 0.0 copy-start
  1.8 0.0 copy-start.10
  1.8 7.3 %all-to-all-start = ((bf16[32,10,2,128]{3,2,1,0:T(2,128)(2,1)}), bf16[32,10,2,128]{3,2,1,0:T(2,128)(2,1)S(1)}, u32[]{:S(2)}, u32[]{:S(2)}) async-start(bf16[32,10,2,128]{3,2,1,0:T(2,128)(2,1)} %bitcast.25), calls=%async_computation | async-start | bytes 327680 | tf_op jit(solution)/shard_map/all_to_all | solution.py:524
  9.1 0.0 copy-done.7
  9.1 0.0 copy-done.8
  9.2 0.0 copy-start.6
  9.2 1.8 %collective-permute-start.1 = (bf16[3,24,2,192]{3,2,1,0:T(2,128)(2,1)S(1)}, bf16[3,24,2,192]{3,2,1,0:T(2,128)(2,1)S(1)}, u32[]{:S(2)}, u32[]{:S(2)}) collective-permute-start(bf16[3,24,2,192]{3,2,1,0:T(2,128)(2,1)S(1)} %bitcast.29), channel_id=1, source_target_pairs={{0,1},{1,0},{2,3},{3,2},{4,5},{5,4},{6,7},{7,6},{8,9},{9,8},{10,11... | collective-permute-start | bytes 165896 | tf_op jit(solution)/shard_map/ppermute | solution.py:39
  11.0 0.7 %collective-permute-start = (bf16[3,24,2,192]{3,2,1,0:T(2,128)(2,1)S(1)}, bf16[3,24,2,192]{3,2,1,0:T(2,128)(2,1)S(1)}, u32[]{:S(2)}, u32[]{:S(2)}) collective-permute-start(bf16[3,24,2,192]{3,2,1,0:T(2,128)(2,1)S(1)} %bitcast.27), channel_id=1, source_target_pairs={{1,2},{2,1},{5,6},{6,5},{9,10},{10,9},{13,14},{14,13},{17,18},{18,... | collective-permute-start | bytes 165896 | tf_op jit(solution)/shard_map/ppermute | solution.py:39
  11.7 0.0 copy-done
  11.7 0.0 copy-start.9
  11.7 0.1 fusion
  11.8 0.1 add_convert_fusion.scalars_ref
  11.9 0.0 copy-done.10
  11.9 0.0 copy-start.11
  11.9 0.6 %copy-done.11 = bf16[192]{0:T(256)(128)(2,1)S(1)} copy-done((bf16[192]{0:T(256)(128)(2,1)S(1)}, bf16[192]{0:T(256)(128)(2,1)}, u32[]{:S(2)}) %copy-start.11) | copy-done | bytes 408
  12.6 0.0 copy-done.9
  12.6 0.1 copy.16.first_ref
  12.7 0.0 copy-done.6
  12.7 0.0 copy-start.3
  12.7 0.0 copy-start.4
  12.7 0.2 copy.17.refs_5_
  12.9 3.1 %collective-permute-done.1 = bf16[3,24,2,192]{3,2,1,0:T(2,128)(2,1)S(1)} collective-permute-done((bf16[3,24,2,192]{3,2,1,0:T(2,128)(2,1)S(1)}, bf16[3,24,2,192]{3,2,1,0:T(2,128)(2,1)S(1)}, u32[]{:S(2)}, u32[]{:S(2)}) %collective-permute-start.1) | collective-permute-done | bytes 55328 | tf_op jit(solution)/shard_map/ppermute | solution.py:39
  16.0 0.0 collective-permute-done
  16.0 0.0 copy-start.1
  16.0 0.1 fusion.1
  16.1 0.0 copy-start.2
  16.1 0.0 copy-start.5
  16.1 0.4 %broadcast_select_fusion.2 = (bf16[18,6,2,192]{3,2,1,0:T(2,128)(2,1)S(1)}, bf16[18,6,2,192]{3,2,1,0:T(2,128)(2,1)S(1)}) fusion(pred[]{:T(512)S(6)} %eq.22, bf16[3,6,2,192]{3,2,1,0:T(2,128)(2,1)S(1)} %get-tuple-element.41, bf16[12,6,2,192]{3,2,1,0:T(2,128)(2,1)S(1)} %get-tuple-element.28, bf16[3,6,2,192]{3,2,1,0:T(2,128)(2,1)S(1)} %get-tuple-element.38, ...), kind=kLoop, calls=%fused_computation.2 | loop fusion | flops 248832 | bytes 331777 | tf_op jit(solution)/shard_map/jit(_where)/select_n | solution.py:33
  16.5 1.2 %collective-permute-start.3 = (bf16[18,6,2,192]{3,2,1,0:T(2,128)(2,1)S(1)}, bf16[18,6,2,192]{3,2,1,0:T(2,128)(2,1)S(1)}, u32[]{:S(2)}, u32[]{:S(2)}) collective-permute-start(bf16[18,6,2,192]{3,2,1,0:T(2,128)(2,1)S(1)} %get-tuple-element.31), channel_id=1, source_target_pairs={{4,8},{8,4},{12,16},{16,12},{20,24},{24,20},{28,0},{0,28},{5,9},{9... | collective-permute-start | bytes 248840 | tf_op jit(solution)/shard_map/ppermute | solution.py:39
  17.7 0.4 %collective-permute-start.2 = (bf16[18,6,2,192]{3,2,1,0:T(2,128)(2,1)S(1)}, bf16[18,6,2,192]{3,2,1,0:T(2,128)(2,1)S(1)}, u32[]{:S(2)}, u32[]{:S(2)}) collective-permute-start(bf16[18,6,2,192]{3,2,1,0:T(2,128)(2,1)S(1)} %get-tuple-element.32), channel_id=1, source_target_pairs={{0,4},{4,0},{8,12},{12,8},{16,20},{20,16},{24,28},{28,24},{1,5},{5... | collective-permute-start | bytes 248840 | tf_op jit(solution)/shard_map/ppermute | solution.py:39
  18.1 0.0 all-to-all-done.recv_ref
  18.1 0.0 copy-done.3
  18.1 0.0 copy-done.4
  18.1 0.0 copy-done.1
  18.2 0.0 copy-done.2
  18.2 0.0 copy-done.5
  18.2 5.1 %shard_map.137 = (bf16[12,24,2,192]{3,2,1,0:T(2,128)(2,1)}, f32[928,256]{1,0:T(8,128)S(1)}) custom-call(s32[3]{0:T(128)S(1)} %add_convert_fusion.scalars_ref, bf16[32,10,2,128]{3,2,1,0:T(2,128)(2,1)S(1)} %all-to-all-done.recv_ref, bf16[3,24,2,192]{3,2,1,0:T(2,128)(2,1)S(1)} %bitcast.23, bf16[3,24,2,192]{3,2,1,0:T(2,128)(2,1)S(1)} %bitcast.20, ...), custom_call_target="tpu_custom_call" | custom-call | flops 4000000000 | bytes 4000000 | tf_op jit(solution)/shard_map/pallas_call | solution.py:553
  23.3 0.0 collective-permute-done.3
  23.3 0.0 collective-permute-done.2
  23.3 0.2 broadcast_select_fusion
  23.5 4.8 %shard_map.138 = bf16[12,24,2,192]{3,2,1,0:T(2,128)(2,1)} custom-call(s32[3]{0:T(128)S(1)} %add_convert_fusion.scalars_ref, f32[928,256]{1,0:T(8,128)S(1)} %get-tuple-element.23.rest_ref, bf16[3,24,2,192]{3,2,1,0:T(2,128)(2,1)S(1)} %bitcast.24, bf16[3,24,2,192]{3,2,1,0:T(2,128)(2,1)S(1)} %bitcast.21, ...), custom_call_target="tpu_custom_call", output_to_operand_aliasing={{}: (13, {})} | custom-call | flops 3000000000 | bytes 4000000 | tf_op jit(solution)/shard_map/pallas_call | solution.py:579
  (4 shorter events, 0.0 us)
Async XLA Ops:
  1.7 7.4 %copy-start.7 = (bf16[3,24,2,192]{3,2,1,0:T(2,128)(2,1)S(1)}, bf16[3,24,2,192]{3,2,1,0:T(2,128)(2,1)}, u32[]{:S(2)}) copy-start(bf16[3,24,2,192]{3,2,1,0:T(2,128)(2,1)} %get-tuple-element.17) | copy-start | bytes 165892
  1.8 7.4 %copy-start.8 = (bf16[3,24,2,192]{3,2,1,0:T(2,128)(2,1)S(1)}, bf16[3,24,2,192]{3,2,1,0:T(2,128)(2,1)}, u32[]{:S(2)}) copy-start(bf16[3,24,2,192]{3,2,1,0:T(2,128)(2,1)} %get-tuple-element.18) | copy-start | bytes 165892
  1.8 9.9 %copy-start = (bf16[12,24,2,192]{3,2,1,0:T(2,128)(2,1)S(1)}, bf16[12,24,2,192]{3,2,1,0:T(2,128)(2,1)}, u32[]{:S(2)}) copy-start(bf16[12,24,2,192]{3,2,1,0:T(2,128)(2,1)} %back_ref.5) | copy-start | bytes 663556
  1.8 10.1 %copy-start.10 = (bf16[192]{0:T(256)(128)(2,1)S(1)}, bf16[192]{0:T(256)(128)(2,1)}, u32[]{:S(2)}) copy-start(bf16[192]{0:T(256)(128)(2,1)} %param.22) | copy-start | bytes 1156
  1.8 16.3 %all-to-all-start = ((bf16[32,10,2,128]{3,2,1,0:T(2,128)(2,1)}), bf16[32,10,2,128]{3,2,1,0:T(2,128)(2,1)S(1)}, u32[]{:S(2)}, u32[]{:S(2)}) async-start(bf16[32,10,2,128]{3,2,1,0:T(2,128)(2,1)} %bitcast.25), calls=%async_computation | async-start | bytes 327680 | tf_op jit(solution)/shard_map/all_to_all | solution.py:524
  9.2 3.5 %copy-start.6 = (bf16[768,192]{0,1:T(8,128)(2,1)S(1)}, bf16[768,192]{0,1:T(8,128)(2,1)}, u32[]{:S(2)}) copy-start(bf16[768,192]{0,1:T(8,128)(2,1)} %param.27) | copy-start | bytes 884740
  9.2 6.8 %collective-permute-start.1 = (bf16[3,24,2,192]{3,2,1,0:T(2,128)(2,1)S(1)}, bf16[3,24,2,192]{3,2,1,0:T(2,128)(2,1)S(1)}, u32[]{:S(2)}, u32[]{:S(2)}) collective-permute-start(bf16[3,24,2,192]{3,2,1,0:T(2,128)(2,1)S(1)} %bitcast.29), channel_id=1, source_target_pairs={{0,1},{1,0},{2,3},{3,2},{4,5},{5,4},{6,7},{7,6},{8,9},{9,8},{10,11... | collective-permute-start | bytes 165896 | tf_op jit(solution)/shard_map/ppermute | solution.py:39
  11.0 5.0 %collective-permute-start = (bf16[3,24,2,192]{3,2,1,0:T(2,128)(2,1)S(1)}, bf16[3,24,2,192]{3,2,1,0:T(2,128)(2,1)S(1)}, u32[]{:S(2)}, u32[]{:S(2)}) collective-permute-start(bf16[3,24,2,192]{3,2,1,0:T(2,128)(2,1)S(1)} %bitcast.27), channel_id=1, source_target_pairs={{1,2},{2,1},{5,6},{6,5},{9,10},{10,9},{13,14},{14,13},{17,18},{18,... | collective-permute-start | bytes 165896 | tf_op jit(solution)/shard_map/ppermute | solution.py:39
  11.7 0.9 %copy-start.9 = (bf16[128,192]{0,1:T(8,128)(2,1)S(1)}, bf16[128,192]{0,1:T(8,128)(2,1)}, u32[]{:S(2)}) copy-start(bf16[128,192]{0,1:T(8,128)(2,1)} %param.19) | copy-start | bytes 147460
  11.9 0.7 %copy-start.11 = (bf16[192]{0:T(256)(128)(2,1)S(1)}, bf16[192]{0:T(256)(128)(2,1)}, u32[]{:S(2)}) copy-start(bf16[192]{0:T(256)(128)(2,1)} %param.25) | copy-start | bytes 1156
  12.7 5.5 %copy-start.3 = (bf16[192,384]{1,0:T(8,128)(2,1)S(1)}, bf16[192,384]{1,0:T(8,128)(2,1)}, u32[]{:S(2)}) copy-start(bf16[192,384]{1,0:T(8,128)(2,1)} %lift_ref.1) | copy-start | bytes 442372
  12.7 5.5 %copy-start.4 = (bf16[192,192]{1,0:T(8,128)(2,1)S(1)}, bf16[192,192]{1,0:T(8,128)(2,1)}, u32[]{:S(2)}) copy-start(bf16[192,192]{1,0:T(8,128)(2,1)} %refs_2_.3) | copy-start | bytes 221188
  16.0 2.2 %copy-start.1 = (bf16[192,768]{1,0:T(8,128)(2,1)S(1)}, bf16[192,768]{1,0:T(8,128)(2,1)}, u32[]{:S(2)}) copy-start(bf16[192,768]{1,0:T(8,128)(2,1)} %refs_4_.3) | copy-start | bytes 884740
  16.1 2.1 %copy-start.2 = (bf16[192,576]{1,0:T(8,128)(2,1)S(1)}, bf16[192,576]{1,0:T(8,128)(2,1)}, u32[]{:S(2)}) copy-start(bf16[192,576]{1,0:T(8,128)(2,1)} %refs_1_.3) | copy-start | bytes 663556
  16.1 2.1 %copy-start.5 = (bf16[8,192]{1,0:T(8,128)(2,1)S(1)}, bf16[8,192]{1,0:T(8,128)(2,1)}, u32[]{:S(2)}) copy-start(bf16[8,192]{1,0:T(8,128)(2,1)} %table_ref.1) | copy-start | bytes 9220
  16.5 6.9 %collective-permute-start.3 = (bf16[18,6,2,192]{3,2,1,0:T(2,128)(2,1)S(1)}, bf16[18,6,2,192]{3,2,1,0:T(2,128)(2,1)S(1)}, u32[]{:S(2)}, u32[]{:S(2)}) collective-permute-start(bf16[18,6,2,192]{3,2,1,0:T(2,128)(2,1)S(1)} %get-tuple-element.31), channel_id=1, source_target_pairs={{4,8},{8,4},{12,16},{16,12},{20,24},{24,20},{28,0},{0,28},{5,9},{9... | collective-permute-start | bytes 248840 | tf_op jit(solution)/shard_map/ppermute | solution.py:39
  17.7 5.6 %collective-permute-start.2 = (bf16[18,6,2,192]{3,2,1,0:T(2,128)(2,1)S(1)}, bf16[18,6,2,192]{3,2,1,0:T(2,128)(2,1)S(1)}, u32[]{:S(2)}, u32[]{:S(2)}) collective-permute-start(bf16[18,6,2,192]{3,2,1,0:T(2,128)(2,1)S(1)} %get-tuple-element.32), channel_id=1, source_target_pairs={{0,4},{4,0},{8,12},{12,8},{16,20},{20,16},{24,28},{28,24},{1,5},{5... | collective-permute-start | bytes 248840 | tf_op jit(solution)/shard_map/ppermute | solution.py:39

commit v13 on v12

--- a/solution.py
+++ b/solution.py
@@ -70,10 +70,18 @@
     return half + half * jnp.tanh(inner)
 
 
-def normalise(wide, gain):
-    average = jnp.mean(wide, axis=-1, keepdims=True)
-    centred = wide - average
-    spread = jnp.mean(centred * centred, axis=-1, keepdims=True)
+def row_sums(tensor):
+    width = tensor.shape[1]
+    return dot(tensor, jnp.ones((width, PAD), BF16))[:, :width]
+
+
+def normalise(tensor, gain):
+    scale = 1.0 / tensor.shape[1]
+    centred = tensor - row_sums(tensor.astype(BF16)) * scale
+    square = centred * centred
+    high = square.astype(BF16)
+    low = (square - high.astype(F32)).astype(BF16)
+    spread = (row_sums(high) + row_sums(low)) * scale
     return centred * lax.rsqrt(spread + 1e-05) * gain
 
 
@@ -346,13 +354,14 @@
     head = width // HEADS
     keys = dot(tokens, weight[:, width : 2 * width]).astype(BF16)
     query = dot(normed[:end].astype(BF16), weight[:, :width]) * head ** (-0.5)
-    values = with_ones(dot(tokens, weight[:, 2 * width :]))
+    values = dot(tokens, weight[:, 2 * width :]).astype(BF16)
     yield True
 
     head_of = lax.broadcasted_iota(jnp.int32, (1, width), 1) // head
     many = WLAT * WLON * LEV
     corner = HLAT * HLON * LEV
     key = lax.broadcasted_iota(jnp.int32, (1, many), 1)
+    ones = jnp.ones((many, width), BF16)
     mixed, start = [], 0
     for w, ((i, j), rows) in enumerate(zip(places, groups)):
         part = query[start : start + rows]
@@ -368,11 +377,14 @@
         largest = jnp.max(scores, axis=-1, keepdims=True)
         raised = jnp.exp(scores - largest).astype(BF16)
         product = dot(raised, values[w * many : (w + 1) * many])
+        weight_sums = dot(raised, ones)
         yield True
-        product = product[:, :width] * about_one_over(product[:, width : width + 1])
-        total = jnp.zeros((rows, width), F32)
-        for h in range(HEADS):
-            total = jnp.where(head_of == h, product[h * rows : (h + 1) * rows], total)
+        total, divisor = product[:rows], weight_sums[:rows]
+        for h in range(1, HEADS):
+            own = head_of == h
+            total = jnp.where(own, product[h * rows : (h + 1) * rows], total)
+            divisor = jnp.where(own, weight_sums[h * rows : (h + 1) * rows], divisor)
+        total = total * about_one_over(divisor)
         mixed.append(total)
         start += rows
     mixed = below(*mixed).astype(BF16)

time: 28.9 us -> 29.2 us (1.010)
  Pallas kernels: 11.7 us -> 12.1 us
where the time goes in v13:
time: 29.2 us; the launch traced here: 28.7 us
  Pallas kernels  12.1 us (41%)
  starting transfers between devices  11.5 us (39%)
  waiting for transfers between devices  3.1 us (11%)
  local copies, waits for them, and re-layouts  1.16 us (4%)
  other arithmetic  0.66 us (2%)
    all_to_all x1, starting transfers between devices, local(): lax.all_to_all(sent, ('lon', 'lat'), split_axis=0, concat_axis=0, tiled=T...  7.3 us
    pallas_call x1, Pallas kernels, local(): pl.pallas_call(functools.partial(middle_kernel, plan), out_shape=[result,...  5.26 us
    pallas_call x1, Pallas kernels, local(): pl.pallas_call(functools.partial(side_kernel, plan), out_shape=result, in...  5.09 us
    ppermute x4, starting transfers between devices, swapped(): got.append(lax.ppermute(mine, axis, pairs))  4.15 us
    ppermute x4, waiting for transfers between devices, swapped(): got.append(lax.ppermute(mine, axis, pairs))  3.1 us
    pallas_call x1, Pallas kernels, packed(): pl.pallas_call(pack_kernel, out_shape=[jax.ShapeDtypeStruct(shape, BF16),...  1.74 us
    unnamed x24, local copies, waits for them, and re-layouts  0.71 us
  transfers between devices with their start and end apart: 5, of which 1 were waited for; matrix products, arithmetic and copies ran while one was open for 3% of the time, Pallas kernels for 18%

profile of v13, /device:TPU:0, one launch (start us, length us, event | category | flops | bytes accessed | tf_op | source)
XLA Modules:
  0.0 28.7 jit_solution(2673926456336423085)
XLA Ops:
  0.0 1.7 %shard_map.136 = (bf16[8,4,10,2,128]{4,3,2,1,0:T(2,128)(2,1)}, bf16[3,24,2,192]{3,2,1,0:T(2,128)(2,1)}, bf16[3,24,2,192]{3,2,1,0:T(2,128)(2,1)}) custom-call(bf16[8,4,2,128]{3,2,1,0:T(2,128)(2,1)} %values_ref.1, s32[8,8]{1,0:T(8,128)} %bitcast.32, s32[8,8]{1,0:T(8,128)} %bitcast.33, s32[4,8]{1,0:T(4,128)} %bitcast.34, bf16[12,24,2,192]{3,2,1,0:T(2,128)(2,1)} %back_ref.5), custom_call_target="tpu_custom_call" | custom-call | flops 20000000000 | bytes 1000000 | tf_op jit(solution)/shard_map/pallas_call | solution.py:192
  1.7 0.0 copy-start.7
  1.8 0.0 copy-start.8
  1.8 0.0 copy-start
  1.8 0.0 copy-start.10
  1.8 7.3 %all-to-all-start = ((bf16[32,10,2,128]{3,2,1,0:T(2,128)(2,1)}), bf16[32,10,2,128]{3,2,1,0:T(2,128)(2,1)S(1)}, u32[]{:S(2)}, u32[]{:S(2)}) async-start(bf16[32,10,2,128]{3,2,1,0:T(2,128)(2,1)} %bitcast.25), calls=%async_computation | async-start | bytes 327680 | tf_op jit(solution)/shard_map/all_to_all | solution.py:536
  9.1 0.0 copy-done.7
  9.1 0.0 copy-done.8
  9.2 0.0 copy-start.6
  9.2 1.8 %collective-permute-start.1 = (bf16[3,24,2,192]{3,2,1,0:T(2,128)(2,1)S(1)}, bf16[3,24,2,192]{3,2,1,0:T(2,128)(2,1)S(1)}, u32[]{:S(2)}, u32[]{:S(2)}) collective-permute-start(bf16[3,24,2,192]{3,2,1,0:T(2,128)(2,1)S(1)} %bitcast.29), channel_id=1, source_target_pairs={{0,1},{1,0},{2,3},{3,2},{4,5},{5,4},{6,7},{7,6},{8,9},{9,8},{10,11... | collective-permute-start | bytes 165896 | tf_op jit(solution)/shard_map/ppermute | solution.py:39
  11.0 0.7 %collective-permute-start = (bf16[3,24,2,192]{3,2,1,0:T(2,128)(2,1)S(1)}, bf16[3,24,2,192]{3,2,1,0:T(2,128)(2,1)S(1)}, u32[]{:S(2)}, u32[]{:S(2)}) collective-permute-start(bf16[3,24,2,192]{3,2,1,0:T(2,128)(2,1)S(1)} %bitcast.27), channel_id=1, source_target_pairs={{1,2},{2,1},{5,6},{6,5},{9,10},{10,9},{13,14},{14,13},{17,18},{18,... | collective-permute-start | bytes 165896 | tf_op jit(solution)/shard_map/ppermute | solution.py:39
  11.7 0.0 copy-done
  11.7 0.0 copy-start.9
  11.7 0.1 fusion
  11.8 0.1 add_convert_fusion.scalars_ref
  11.9 0.0 copy-done.10
  11.9 0.0 copy-start.11
  11.9 0.6 %copy-done.11 = bf16[192]{0:T(256)(128)(2,1)S(1)} copy-done((bf16[192]{0:T(256)(128)(2,1)S(1)}, bf16[192]{0:T(256)(128)(2,1)}, u32[]{:S(2)}) %copy-start.11) | copy-done | bytes 408
  12.6 0.0 copy-done.9
  12.6 0.1 copy.16.first_ref
  12.7 0.0 copy-done.6
  12.7 0.0 copy-start.3
  12.7 0.0 copy-start.4
  12.7 0.2 copy.17.refs_5_
  12.9 3.1 %collective-permute-done.1 = bf16[3,24,2,192]{3,2,1,0:T(2,128)(2,1)S(1)} collective-permute-done((bf16[3,24,2,192]{3,2,1,0:T(2,128)(2,1)S(1)}, bf16[3,24,2,192]{3,2,1,0:T(2,128)(2,1)S(1)}, u32[]{:S(2)}, u32[]{:S(2)}) %collective-permute-start.1) | collective-permute-done | bytes 55328 | tf_op jit(solution)/shard_map/ppermute | solution.py:39
  16.0 0.0 collective-permute-done
  16.0 0.0 copy-start.1
  16.0 0.1 fusion.1
  16.1 0.0 copy-start.2
  16.1 0.0 copy-start.5
  16.1 0.4 %broadcast_select_fusion.2 = (bf16[18,6,2,192]{3,2,1,0:T(2,128)(2,1)S(1)}, bf16[18,6,2,192]{3,2,1,0:T(2,128)(2,1)S(1)}) fusion(pred[]{:T(512)S(6)} %eq.22, bf16[3,6,2,192]{3,2,1,0:T(2,128)(2,1)S(1)} %get-tuple-element.41, bf16[12,6,2,192]{3,2,1,0:T(2,128)(2,1)S(1)} %get-tuple-element.28, bf16[3,6,2,192]{3,2,1,0:T(2,128)(2,1)S(1)} %get-tuple-element.38, ...), kind=kLoop, calls=%fused_computation.2 | loop fusion | flops 248832 | bytes 331777 | tf_op jit(solution)/shard_map/jit(_where)/select_n | solution.py:33
  16.5 1.2 %collective-permute-start.3 = (bf16[18,6,2,192]{3,2,1,0:T(2,128)(2,1)S(1)}, bf16[18,6,2,192]{3,2,1,0:T(2,128)(2,1)S(1)}, u32[]{:S(2)}, u32[]{:S(2)}) collective-permute-start(bf16[18,6,2,192]{3,2,1,0:T(2,128)(2,1)S(1)} %get-tuple-element.31), channel_id=1, source_target_pairs={{4,8},{8,4},{12,16},{16,12},{20,24},{24,20},{28,0},{0,28},{5,9},{9... | collective-permute-start | bytes 248840 | tf_op jit(solution)/shard_map/ppermute | solution.py:39
  17.7 0.4 %collective-permute-start.2 = (bf16[18,6,2,192]{3,2,1,0:T(2,128)(2,1)S(1)}, bf16[18,6,2,192]{3,2,1,0:T(2,128)(2,1)S(1)}, u32[]{:S(2)}, u32[]{:S(2)}) collective-permute-start(bf16[18,6,2,192]{3,2,1,0:T(2,128)(2,1)S(1)} %get-tuple-element.32), channel_id=1, source_target_pairs={{0,4},{4,0},{8,12},{12,8},{16,20},{20,16},{24,28},{28,24},{1,5},{5... | collective-permute-start | bytes 248840 | tf_op jit(solution)/shard_map/ppermute | solution.py:39
  18.1 0.0 all-to-all-done.recv_ref
  18.1 0.0 copy-done.3
  18.1 0.0 copy-done.4
  18.1 0.0 copy-done.1
  18.2 0.0 copy-done.2
  18.2 0.0 copy-done.5
  18.2 5.3 %shard_map.137 = (bf16[12,24,2,192]{3,2,1,0:T(2,128)(2,1)}, f32[928,256]{1,0:T(8,128)S(1)}) custom-call(s32[3]{0:T(128)S(1)} %add_convert_fusion.scalars_ref, bf16[32,10,2,128]{3,2,1,0:T(2,128)(2,1)S(1)} %all-to-all-done.recv_ref, bf16[3,24,2,192]{3,2,1,0:T(2,128)(2,1)S(1)} %bitcast.23, bf16[3,24,2,192]{3,2,1,0:T(2,128)(2,1)S(1)} %bitcast.20, ...), custom_call_target="tpu_custom_call" | custom-call | flops 4000000000 | bytes 4000000 | tf_op jit(solution)/shard_map/pallas_call | solution.py:565
  23.4 0.0 collective-permute-done.3
  23.5 0.0 collective-permute-done.2
  23.5 0.2 broadcast_select_fusion
  23.7 5.1 %shard_map.138 = bf16[12,24,2,192]{3,2,1,0:T(2,128)(2,1)} custom-call(s32[3]{0:T(128)S(1)} %add_convert_fusion.scalars_ref, f32[928,256]{1,0:T(8,128)S(1)} %get-tuple-element.23.rest_ref, bf16[3,24,2,192]{3,2,1,0:T(2,128)(2,1)S(1)} %bitcast.24, bf16[3,24,2,192]{3,2,1,0:T(2,128)(2,1)S(1)} %bitcast.21, ...), custom_call_target="tpu_custom_call", output_to_operand_aliasing={{}: (13, {})} | custom-call | flops 3000000000 | bytes 4000000 | tf_op jit(solution)/shard_map/pallas_call | solution.py:591
  (4 shorter events, 0.0 us)
Async XLA Ops:
  1.7 7.4 %copy-start.7 = (bf16[3,24,2,192]{3,2,1,0:T(2,128)(2,1)S(1)}, bf16[3,24,2,192]{3,2,1,0:T(2,128)(2,1)}, u32[]{:S(2)}) copy-start(bf16[3,24,2,192]{3,2,1,0:T(2,128)(2,1)} %get-tuple-element.17) | copy-start | bytes 165892
  1.8 7.4 %copy-start.8 = (bf16[3,24,2,192]{3,2,1,0:T(2,128)(2,1)S(1)}, bf16[3,24,2,192]{3,2,1,0:T(2,128)(2,1)}, u32[]{:S(2)}) copy-start(bf16[3,24,2,192]{3,2,1,0:T(2,128)(2,1)} %get-tuple-element.18) | copy-start | bytes 165892
  1.8 9.9 %copy-start = (bf16[12,24,2,192]{3,2,1,0:T(2,128)(2,1)S(1)}, bf16[12,24,2,192]{3,2,1,0:T(2,128)(2,1)}, u32[]{:S(2)}) copy-start(bf16[12,24,2,192]{3,2,1,0:T(2,128)(2,1)} %back_ref.5) | copy-start | bytes 663556
  1.8 10.1 %copy-start.10 = (bf16[192]{0:T(256)(128)(2,1)S(1)}, bf16[192]{0:T(256)(128)(2,1)}, u32[]{:S(2)}) copy-start(bf16[192]{0:T(256)(128)(2,1)} %param.22) | copy-start | bytes 1156
  1.8 16.3 %all-to-all-start = ((bf16[32,10,2,128]{3,2,1,0:T(2,128)(2,1)}), bf16[32,10,2,128]{3,2,1,0:T(2,128)(2,1)S(1)}, u32[]{:S(2)}, u32[]{:S(2)}) async-start(bf16[32,10,2,128]{3,2,1,0:T(2,128)(2,1)} %bitcast.25), calls=%async_computation | async-start | bytes 327680 | tf_op jit(solution)/shard_map/all_to_all | solution.py:536
  9.2 3.5 %copy-start.6 = (bf16[768,192]{0,1:T(8,128)(2,1)S(1)}, bf16[768,192]{0,1:T(8,128)(2,1)}, u32[]{:S(2)}) copy-start(bf16[768,192]{0,1:T(8,128)(2,1)} %param.27) | copy-start | bytes 884740
  9.2 6.8 %collective-permute-start.1 = (bf16[3,24,2,192]{3,2,1,0:T(2,128)(2,1)S(1)}, bf16[3,24,2,192]{3,2,1,0:T(2,128)(2,1)S(1)}, u32[]{:S(2)}, u32[]{:S(2)}) collective-permute-start(bf16[3,24,2,192]{3,2,1,0:T(2,128)(2,1)S(1)} %bitcast.29), channel_id=1, source_target_pairs={{0,1},{1,0},{2,3},{3,2},{4,5},{5,4},{6,7},{7,6},{8,9},{9,8},{10,11... | collective-permute-start | bytes 165896 | tf_op jit(solution)/shard_map/ppermute | solution.py:39
  11.0 5.0 %collective-permute-start = (bf16[3,24,2,192]{3,2,1,0:T(2,128)(2,1)S(1)}, bf16[3,24,2,192]{3,2,1,0:T(2,128)(2,1)S(1)}, u32[]{:S(2)}, u32[]{:S(2)}) collective-permute-start(bf16[3,24,2,192]{3,2,1,0:T(2,128)(2,1)S(1)} %bitcast.27), channel_id=1, source_target_pairs={{1,2},{2,1},{5,6},{6,5},{9,10},{10,9},{13,14},{14,13},{17,18},{18,... | collective-permute-start | bytes 165896 | tf_op jit(solution)/shard_map/ppermute | solution.py:39
  11.7 0.9 %copy-start.9 = (bf16[128,192]{0,1:T(8,128)(2,1)S(1)}, bf16[128,192]{0,1:T(8,128)(2,1)}, u32[]{:S(2)}) copy-start(bf16[128,192]{0,1:T(8,128)(2,1)} %param.19) | copy-start | bytes 147460
  11.9 0.7 %copy-start.11 = (bf16[192]{0:T(256)(128)(2,1)S(1)}, bf16[192]{0:T(256)(128)(2,1)}, u32[]{:S(2)}) copy-start(bf16[192]{0:T(256)(128)(2,1)} %param.25) | copy-start | bytes 1156
  12.7 5.5 %copy-start.3 = (bf16[192,384]{1,0:T(8,128)(2,1)S(1)}, bf16[192,384]{1,0:T(8,128)(2,1)}, u32[]{:S(2)}) copy-start(bf16[192,384]{1,0:T(8,128)(2,1)} %lift_ref.1) | copy-start | bytes 442372
  12.7 5.5 %copy-start.4 = (bf16[192,192]{1,0:T(8,128)(2,1)S(1)}, bf16[192,192]{1,0:T(8,128)(2,1)}, u32[]{:S(2)}) copy-start(bf16[192,192]{1,0:T(8,128)(2,1)} %refs_2_.3) | copy-start | bytes 221188
  16.0 2.2 %copy-start.1 = (bf16[192,768]{1,0:T(8,128)(2,1)S(1)}, bf16[192,768]{1,0:T(8,128)(2,1)}, u32[]{:S(2)}) copy-start(bf16[192,768]{1,0:T(8,128)(2,1)} %refs_4_.3) | copy-start | bytes 884740
  16.1 2.1 %copy-start.2 = (bf16[192,576]{1,0:T(8,128)(2,1)S(1)}, bf16[192,576]{1,0:T(8,128)(2,1)}, u32[]{:S(2)}) copy-start(bf16[192,576]{1,0:T(8,128)(2,1)} %refs_1_.3) | copy-start | bytes 663556
  16.1 2.1 %copy-start.5 = (bf16[8,192]{1,0:T(8,128)(2,1)S(1)}, bf16[8,192]{1,0:T(8,128)(2,1)}, u32[]{:S(2)}) copy-start(bf16[8,192]{1,0:T(8,128)(2,1)} %table_ref.1) | copy-start | bytes 9220
  16.5 7.0 %collective-permute-start.3 = (bf16[18,6,2,192]{3,2,1,0:T(2,128)(2,1)S(1)}, bf16[18,6,2,192]{3,2,1,0:T(2,128)(2,1)S(1)}, u32[]{:S(2)}, u32[]{:S(2)}) collective-permute-start(bf16[18,6,2,192]{3,2,1,0:T(2,128)(2,1)S(1)} %get-tuple-element.31), channel_id=1, source_target_pairs={{4,8},{8,4},{12,16},{16,12},{20,24},{24,20},{28,0},{0,28},{5,9},{9... | collective-permute-start | bytes 248840 | tf_op jit(solution)/shard_map/ppermute | solution.py:39
  17.7 5.8 %collective-permute-start.2 = (bf16[18,6,2,192]{3,2,1,0:T(2,128)(2,1)S(1)}, bf16[18,6,2,192]{3,2,1,0:T(2,128)(2,1)S(1)}, u32[]{:S(2)}, u32[]{:S(2)}) collective-permute-start(bf16[18,6,2,192]{3,2,1,0:T(2,128)(2,1)S(1)} %get-tuple-element.32), channel_id=1, source_target_pairs={{0,4},{4,0},{8,12},{12,8},{16,20},{20,16},{24,28},{28,24},{1,5},{5... | collective-permute-start | bytes 248840 | tf_op jit(solution)/shard_map/ppermute | solution.py:39

commit v14 on v12

v14 whole, which is shorter than its diff:
```python
import functools

import jax
import jax.numpy as jnp
from jax import lax
from jax.experimental import pallas as pl
from jax.experimental.pallas import tpu as pltpu
from jax.sharding import PartitionSpec as P

HEADS = 6
INSTR = 8
LEV = 2
WLAT = 6
WLON = 12
HLAT = WLAT // 2
HLON = WLON // 2
LANES = 128
PAD = 256
CHUNK = 32
LIMIT = 40 * 2**20
BF16 = jnp.bfloat16
F32 = jnp.float32

AROUND = (-1, 0, 1)
ROWS = INSTR * len(AROUND)
COLS = ROWS + len(AROUND)


def swapped(first, second, axis, wraps):
    count = lax.axis_size(axis)
    got = []
    for begin, mine in enumerate((first, second)):
        pairs = []
        for low in range(begin, count, 2):
            high = (low + 1) % count
            if high > low or wraps:
                pairs += [(low, high), (high, low)]
        got.append(lax.ppermute(mine, axis, pairs))
    return got


def rectangles(lat_cells, lon_cells):
    lat = {-1: [(lat_cells - HLAT, HLAT)], 1: [(0, HLAT)]}
    lat[0] = [(0, HLAT), (HLAT, lat_cells - WLAT), (lat_cells - HLAT, HLAT)]
    lon = [(0, HLON), (HLON, lon_cells - WLON), (lon_cells - HLON, HLON)]
    return [[(top, high, left, wide) for top, high in lat[dy] for left, wide in lon] for dy in AROUND]


def tokens_of(part):
    return part[1] * part[3] * LEV


def padded(count):
    return -(-count // 8) * 8


def gelu(x):
    half = 0.5 * x
    inner = x * (0.7978845608028654 + 0.035677408136300125 * (x * x))
    return half + half * jnp.tanh(inner)


def normalise(wide, gain):
    average = jnp.mean(wide, axis=-1, keepdims=True)
    centred = wide - average
    spread = jnp.mean(centred * centred, axis=-1, keepdims=True)
    return centred * lax.rsqrt(spread + 1e-05) * gain


def dot(a, b):
    return jnp.dot(a, b, preferred_element_type=F32)


def dot_nt(a, b):
    return lax.dot_general(a, b, (((1,), (1,)), ((), ())), preferred_element_type=F32)


def about_one_over(x):
    return pl.reciprocal(x, approx=True)


def with_ones(tensor):
    ones = jnp.ones((tensor.shape[0], PAD - tensor.shape[1]), F32)
    return jnp.concatenate([tensor, ones], axis=1).astype(BF16)


def below(*pieces):
    return jnp.concatenate(pieces, axis=0) if len(pieces) > 1 else pieces[0]


def pack_kernel(
    values_ref,
    cell_ref,
    tag_ref,
    count_ref,
    back_ref,
    *refs,
):
    out_ref, up_ref, down_ref, values, cells, tags, held, sem = refs
    tiles_lon, tiles_lat, capacity, _ = values_ref.shape
    lat_cells, lon_cells = back_ref.shape[:2]
    strips = [
        (back_ref.at[:HLAT], up_ref),
        (back_ref.at[lat_cells - HLAT :], down_ref),
    ]
    copies = [
        pltpu.make_async_copy(cell_ref, cells, sem.at[0]),
        pltpu.make_async_copy(tag_ref, tags, sem.at[1]),
        pltpu.make_async_copy(count_ref, held, sem.at[2]),
        pltpu.make_async_copy(values_ref, values, sem.at[3]),
    ]
    copies += [
        pltpu.make_async_copy(source, strip, sem.at[4 + n])
        for n, (source, strip) in enumerate(strips)
    ]
    for copy in copies:
        copy.start()
    for copy in copies[:3]:
        copy.wait()
    counts = below(*[held[tile : tile + 1, :] for tile in range(tiles_lat) for _ in range(capacity)])
    cell = cells[...]
    slot = lax.broadcasted_iota(jnp.int32, cell.shape, 0) % capacity
    row = cell // lon_cells
    fields = [jnp.where(slot < counts, row, 255), cell - row * lon_cells, tags[...]]
    rows, columns, kinds = (field.astype(F32) for field in fields)
    lane = lax.broadcasted_iota(jnp.int32, (cell.shape[0], LANES), 1)
    kind_of = (lane % INSTR).astype(F32)
    marks = [
        ((lane < ROWS) & (lane // INSTR == n)) | (lane == ROWS + n) | (lane == COLS + n)
        for n in range(len(AROUND))
    ]
    turned = []
    for lon in range(tiles_lon):
        meta = jnp.where(kind_of == kinds[:, lon : lon + 1], 1.0, 0.0)
        meta = jnp.where(lane >= ROWS, rows[:, lon : lon + 1], meta)
        meta = jnp.where(lane >= COLS, columns[:, lon : lon + 1], meta)
        turns = {0: meta}
        for dy in (-1, 1):
            by = dy * capacity % meta.shape[0]
            turns[dy] = below(meta[by:], meta[:by])
        turned.append(turns)
    for lon in range(tiles_lon):
        meta = jnp.zeros(lane.shape, F32)
        for mark, dy in zip(marks, AROUND):
            meta = jnp.where(mark, turned[lon][dy], meta)
        out_ref[lon, :, len(AROUND)] = meta.astype(BF16).reshape(tiles_lat, capacity, LANES)
    copies[3].wait()
    for n, dy in enumerate(AROUND):
        spans = {0: [(0, tiles_lat)], 1: [(0, tiles_lat - 1), (tiles_lat - 1, tiles_lat)]}
        spans[-1] = [(0, 1), (1, tiles_lat)]

        for low, end in spans[dy]:
            first = (low + dy) % tiles_lat
            out_ref[:, low:end, n] = values[:, first : first + end - low]
    for copy in copies[4:]:
        copy.wait()


def packed(record_values, record_cell, record_instrument, block_counts, background):
    tiles_lon, tiles_lat, capacity, wide = record_values.shape
    anywhere = pl.BlockSpec(memory_space=pltpu.HBM)
    ints = pltpu.VMEM((tiles_lat * capacity, tiles_lon), jnp.int32)
    shape = (tiles_lon, tiles_lat, len(AROUND) + 1, capacity, wide)
    lat_cells, lon_cells, levels, width = background.shape
    across = jax.ShapeDtypeStruct((HLAT, lon_cells, levels, width), BF16)
    out, *strips = pl.pallas_call(
        pack_kernel,
        out_shape=[jax.ShapeDtypeStruct(shape, BF16), across, across],
        in_specs=[anywhere] * 5,
        out_specs=[pl.BlockSpec(memory_space=pltpu.VMEM)] * 3,
        scratch_shapes=[
            pltpu.VMEM(record_values.shape, BF16),
            ints,
            ints,
            pltpu.VMEM((tiles_lat, tiles_lon), jnp.int32),
            pltpu.SemaphoreType.DMA((6,)),
        ],
        compiler_params=pltpu.CompilerParams(vmem_limit_bytes=56 * 2**20),
        cost_estimate=pl.CostEstimate(
            flops=20 * 10**9, bytes_accessed=10**6, transcendentals=0
        ),
    )(
        record_values,
        record_cell.transpose(1, 2, 0).reshape(-1, tiles_lon),
        record_instrument.transpose(1, 2, 0).reshape(-1, tiles_lon),
        block_counts.T,
        background,
    )
    return out.reshape((-1,) + shape[2:]), *strips


def token_codes(part, lon_cells):
    top, high, left, wide = part
    count = tokens_of(part)
    place = lax.broadcasted_iota(jnp.int32, (padded(count), LANES), 0)
    code = place + (top * lon_cells + left) * LEV
    for row in range(1, high):
        step = (lon_cells - wide) * LEV
        code = code + jnp.where(place >= row * wide * LEV, step, 0)
    return jnp.where(place < count, code, -8).astype(F32)


def alternate(*chains):
    chains, begun = list(chains), 1
    while chains:
        for chain in chains[:begun]:
            if next(chain, None) is None:
                chains.remove(chain)
                begun -= 1
        begun += 1


def scattered(recv_ref, first_ref, table_ref, lift_ref, plan, lon_cells):
    sources, _, capacity, _ = recv_ref.shape
    width = table_ref.shape[1]
    chunk = min(CHUNK, sources)
    slots = chunk * capacity
    first, lift = first_ref[...], lift_ref[...]
    table = below(*[table_ref[...].astype(F32)] * (LANES // INSTR)).astype(BF16)
    lane = lax.broadcasted_iota(jnp.int32, (16, LANES), 1)
    sub = lax.broadcasted_iota(jnp.int32, (16, LANES), 0)
    weigh = jnp.where(lane == ROWS + sub, float(lon_cells * LEV), 0.0)
    weigh = jnp.where(lane == COLS + sub, float(LEV), weigh).astype(BF16)
    codes = [below(*[token_codes(part, lon_cells) for part in parts]) for parts in plan]

    def scatter(begin):
        meta = recv_ref[pl.ds(begin, chunk), len(AROUND)].reshape(slots, LANES)
        records = below(
            *[
                recv_ref[pl.ds(begin, chunk), n].reshape(slots, LANES)
                for n in range(len(AROUND))
            ]
        )
        lane = lax.broadcasted_iota(jnp.int32, meta.shape, 1) // INSTR
        wide = meta.astype(F32)
        chosen = below(*[jnp.where(lane == n, wide, 0.0) for n in range(len(AROUND))]).astype(BF16)
        encoded = gelu(dot(records, first) + dot(chosen, table)).astype(BF16)
        lifted = gelu(dot(encoded, lift))
        tokens = dot_nt(weigh, meta)
        sums = []
        for n in range(len(AROUND)):
            part = lifted[n * slots : (n + 1) * slots]
            part = with_ones(
                below(*[part[:, level * width : (level + 1) * width] for level in range(LEV)])
            )
            token = tokens[n : n + 1]
            token = jnp.concatenate([token + float(level) for level in range(LEV)], axis=1)
            if token.shape[1] == LANES:
                hot = codes[n] == token
            else:
                hot = codes[n][:, :1] == token
            sums.append(dot(jnp.where(hot, 1.0, 0.0).astype(BF16), part))
        return tuple(sums)

    sums = scatter(0)
    if sources > chunk:
        sums = lax.fori_loop(
            1,
            sources // chunk,
            lambda step, total: tuple(a + b for a, b in zip(total, scatter(step * chunk))),
            sums,
        )
    return sums


def spans_of(plan):
    spans, start = {}, 0
    for tile in (1, 0, 2):
        for number, part in enumerate(plan[tile]):
            spans[tile, number] = (start, tokens_of(part))
            start += padded(tokens_of(part))
    return spans, start


def norm_kernel(
    plan,
    even_ref,
    recv_ref,
    one_ref,
    two_ref,
    back_ref,
    first_ref,
    table_ref,
    lift_ref,
    gain_ref,
    latent_ref,
    normed_ref,
    mine_ref,
    other_ref,
    north_ref,
    south_ref,
):
    def sort(before, after):
        north_ref[...] = before[...]
        south_ref[...] = after[...]

    pl.when(even_ref[0] == 1)(lambda: sort(two_ref, one_ref))
    pl.when(even_ref[0] == 0)(lambda: sort(one_ref, two_ref))
    sums = scattered(recv_ref, first_ref, table_ref, lift_ref, plan, back_ref.shape[1])
    width = back_ref.shape[3]
    spans, _ = spans_of(plan)
    normed = {}
    for tile, ref in ((1, back_ref), (0, north_ref), (2, south_ref)):
        pieces = []
        for top, high, left, wide in plan[tile]:
            top = top if tile == 1 else 0
            count = high * wide * LEV
            piece = ref[top : top + high, left : left + wide].reshape(count, width).astype(F32)
            if padded(count) > count:
                piece = below(piece, jnp.zeros((padded(count) - count, width), F32))
            pieces.append(piece)
        total = sums[tile]
        tally = 1.0 + total[:, width : width + 1]
        share = about_one_over(tally)
        share = share * (2.0 - tally * share)
        latent = ((below(*pieces) + total[:, :width]) * share).astype(BF16)
        if tile == 1:
            latent_ref[...] = latent
        normed[tile] = normalise(latent.astype(F32), gain_ref[...].astype(F32))
    normed = below(*[normed[tile] for tile in (1, 0, 2)])
    normed_ref[...] = normed.astype(BF16)

    half = HLAT * HLON * LEV

    def piece_of(tile, number, at=0):
        start = spans[tile, number][0] + at
        return normed[start : start + half]

    def strip(j):
        pairs = [
            (piece_of(1, j), piece_of(1, 3 + j)),
            (piece_of(1, 6 + j), piece_of(1, 3 + j, half)),
            (piece_of(0, j), piece_of(2, j)),
        ]
        return below(*[jnp.concatenate(pair, axis=1) for pair in pairs]).astype(BF16)

    left, right = strip(0), strip(2)

    def store(first, second):
        mine_ref[...] = first
        other_ref[...] = second

    pl.when(even_ref[1] == 1)(lambda: store(right, left))
    pl.when(even_ref[1] == 0)(lambda: store(left, right))


def worked(plan, places, token_pieces, own_normed, latent, weights, scalars_ref, put, done):
    attn_ref, mix_ref, gain_ref, up_ref, down_ref = weights
    width = mix_ref.shape[0]
    head = width // HEADS
    many = WLAT * WLON * LEV
    corner = HLAT * HLON * LEV
    groups = [padded(tokens_of(plan[1][3 * i + j])) for i, j in places]
    tokens = below(*[piece for i, j in places for piece in token_pieces(i, j)]).astype(BF16)
    weight = attn_ref[...]
    keys = dot(tokens, weight[:, width : 2 * width])
    query = dot(own_normed.astype(BF16), weight[:, :width]) * head ** (-0.5)
    query = jnp.concatenate([query, jnp.ones((query.shape[0], PAD - width), F32)], axis=1)
    values = with_ones(dot(tokens, weight[:, 2 * width :]))
    yield True

    lane = lax.broadcasted_iota(jnp.int32, (1, PAD), 1)
    key = lax.broadcasted_iota(jnp.int32, (many, PAD - width), 0)
    spare = lax.broadcasted_iota(jnp.int32, (many, PAD - width), 1)
    mixed, start = [], 0
    for w, ((i, j), rows) in enumerate(zip(places, groups)):
        part = query[start : start + rows]
        stacked = below(
            *[jnp.where((lane // head == h) | (lane >= width), part, 0.0) for h in range(HEADS)]
        ).astype(BF16)
        bias = jnp.zeros((many, PAD - width), F32)
        if i != 1:
            if j == 1:
                inside = key < 2 * corner
            else:
                inside = (key < corner) | ((key >= 2 * corner) & (key < 3 * corner))
            bias = jnp.where(inside | (spare > 0), 0.0, -3e38) * scalars_ref[i].astype(F32)
        here = jnp.concatenate([keys[w * many : (w + 1) * many], bias], axis=1).astype(BF16)
        scores = dot_nt(stacked, here)
        yield True
        largest = jnp.max(scores, axis=-1, keepdims=True)
        raised = jnp.exp(scores - largest).astype(BF16)
        product = dot(raised, values[w * many : (w + 1) * many])
        yield True
        product = product[:, :width] * about_one_over(product[:, width : width + 1])
        total = product[:rows]
        for h in range(1, HEADS):
            own = lane[:, :width] // head == h
            total = jnp.where(own, product[h * rows : (h + 1) * rows], total)
        mixed.append(total)
        start += rows
    mixed = below(*mixed).astype(BF16)

    after = (latent + dot(mixed, mix_ref[...])).astype(BF16).astype(F32)
    yield True
    normed_two = normalise(after, gain_ref[...].astype(F32)).astype(BF16)
    hidden = dot(normed_two, up_ref[...])
    yield True
    result = after + dot(gelu(hidden).astype(BF16), down_ref[...])
    yield True
    start = 0
    for (i, j), rows in zip(places, groups):
        part = plan[1][3 * i + j]
        piece = result[start : start + tokens_of(part)].astype(BF16)
        put(part, j, piece.reshape(part[1], part[3], LEV, width))
        start += rows
    done(places)


MIDDLE = [[(0, 1), (2, 1)], [(1, 1)]]
SIDES = [[(0, 0), (1, 0), (2, 0)], [(0, 2), (1, 2), (2, 2)]]


def chains_of(plan, groups, latent_ref, normed_ref, far, weights, scalars_ref, put, done):
    spans, _ = spans_of(plan)

    def rows_of(ref, tile, number, full=False):
        start, count = spans[tile, number]
        stop = start + (padded(count) if full else count)
        low = start // 16 * 16
        high = min(-(-stop // 16) * 16, ref.shape[0])
        return ref[low:high, :].astype(F32)[start - low : stop - low]

    def token_pieces(i, j):
        pieces = [rows_of(normed_ref, 1, 3 * i + j)]
        if i != 1:
            pieces.append(rows_of(normed_ref, i, j))
        if j != 1:
            north, first, south, second, far_north, far_south = far[j]
            pieces += {0: [north, far_north], 1: [first, second], 2: [south, far_south]}[i]
        return pieces

    chains = []
    for places in groups:
        own = [(1, 3 * i + j) for i, j in places]
        own_normed = below(*[rows_of(normed_ref, *entry, True) for entry in own])
        latent = below(*[rows_of(latent_ref, *entry, True) for entry in own])
        chains.append(
            worked(
                plan, places, token_pieces, own_normed, latent, weights, scalars_ref, put, done
            )
        )
    return chains


def middle_kernel(plan, scalars_ref, latent_ref, normed_ref, *refs):
    *weights, out_ref, held_ref, sem = refs
    left, wide = plan[1][4][2:]

    def put(part, _, piece):
        held_ref[part[0] : part[0] + part[1]] = piece

    copies = []

    def done(places):
        for i, _ in places:
            top, high = plan[1][3 * i + 1][:2]
            copies.append(
                pltpu.make_async_copy(
                    held_ref.at[top : top + high],
                    out_ref.at[top : top + high, left : left + wide],
                    sem.at[i],
                )
            )
            copies[-1].start()

    alternate(
        *chains_of(plan, MIDDLE, latent_ref, normed_ref, {}, weights, scalars_ref, put, done)
    )
    for copy in copies:
        copy.wait()


def side_kernel(plan, scalars_ref, latent_ref, normed_ref, one_ref, two_ref, *refs):
    *weights, _, out_ref, held_ref, west_ref, east_ref, sem = refs

    def sort(before, after):
        west_ref[...] = before[...]
        east_ref[...] = after[...]

    pl.when(scalars_ref[3] == 1)(lambda: sort(two_ref, one_ref))
    pl.when(scalars_ref[3] == 0)(lambda: sort(one_ref, two_ref))
    far = {}
    width = normed_ref.shape[1]
    half = HLAT * HLON * LEV
    for j, ref in ((0, west_ref), (2, east_ref)):
        value = ref[...].astype(F32)
        rows = [value[at : at + half] for at in range(0, 3 * half, half)]
        far[j] = [part[:, at : at + width] for part in rows for at in (0, width)]

    def put(part, j, piece):
        held_ref[j // 2, part[0] : part[0] + part[1]] = piece

    copies = []

    def done(places):
        j = places[0][1]
        left, wide = plan[1][j][2:]
        copies.append(
            pltpu.make_async_copy(
                held_ref.at[j // 2], out_ref.at[:, left : left + wide], sem.at[j // 2]
            )
        )
        copies[-1].start()

    alternate(
        *chains_of(plan, SIDES, latent_ref, normed_ref, far, weights, scalars_ref, put, done)
    )
    for copy in copies:
        copy.wait()


def local(
    record_values,
    record_cell,
    record_instrument,
    block_counts,
    background,
    input_weight,
    instrument_table,
    lift_weight,
    first_gain,
    attn_weight,
    mix_weight,
    second_gain,
    up_weight,
    down_weight,
):
    lat_cells, lon_cells, _, width = background.shape
    tiles_lat = record_values.shape[1]

    sent, up, down = packed(
        record_values, record_cell, record_instrument, block_counts, background
    )
    received = lax.all_to_all(sent, ("lon", "lat"), split_axis=0, concat_axis=0, tiled=True)
    even = [lax.axis_index(axis) % 2 == 0 for axis in ("lat", "lon")]
    got = swapped(jnp.where(even[0], down, up), jnp.where(even[0], up, down), "lat", wraps=False)
    input_weight, down_weight, _ = lax.optimization_barrier((input_weight, down_weight, up))

    plan = rectangles(lat_cells, lon_cells)
    _, rows = spans_of(plan)
    own = sum(padded(tokens_of(part)) for part in plan[1])
    half = HLAT * HLON * LEV
    smem = pl.BlockSpec(memory_space=pltpu.SMEM)
    vmem = pl.BlockSpec(memory_space=pltpu.VMEM)
    anywhere = pl.BlockSpec(memory_space=pl.ANY)
    params = pltpu.CompilerParams(vmem_limit_bytes=LIMIT)
    border = pltpu.VMEM((HLAT, lon_cells, LEV, width), BF16)
    strip = jax.ShapeDtypeStruct((3 * half, 2 * width), BF16)
    latent, normed, first, second = pl.pallas_call(
        functools.partial(norm_kernel, plan),
        out_shape=[
            jax.ShapeDtypeStruct((own, width), BF16),
            jax.ShapeDtypeStruct((rows, width), BF16),
            strip,
            strip,
        ],
        in_specs=[smem] + [vmem] * 8,
        out_specs=[vmem] * 4,
        scratch_shapes=[border, border],
        compiler_params=params,
        cost_estimate=pl.CostEstimate(
            flops=10**9, bytes_accessed=2 * 10**6, transcendentals=10**6
        ),
    )(
        jnp.stack(even).astype(jnp.int32),
        received,
        *got,
        background,
        input_weight,
        instrument_table,
        lift_weight,
        first_gain.reshape(1, width),
    )
    got = swapped(first, second, "lon", wraps=True)

    lat = lax.axis_index("lat")
    scalars = jnp.stack([lat == 0, lat < 0, lat == tiles_lat - 1, even[1]]).astype(jnp.int32)
    weights = [attn_weight, mix_weight, second_gain.reshape(1, width), up_weight, down_weight]
    result = jax.ShapeDtypeStruct(background.shape, BF16)
    middle = pl.pallas_call(
        functools.partial(middle_kernel, plan),
        out_shape=result,
        in_specs=[smem] + [vmem] * (2 + len(weights)),
        out_specs=anywhere,
        scratch_shapes=[
            pltpu.VMEM((lat_cells, lon_cells - WLON, LEV, width), BF16),
            pltpu.SemaphoreType.DMA((3,)),
        ],
        compiler_params=params,
        cost_estimate=pl.CostEstimate(
            flops=4 * 10**9, bytes_accessed=4 * 10**6, transcendentals=10**6
        ),
    )(scalars, latent, normed, *weights)
    return pl.pallas_call(
        functools.partial(side_kernel, plan),
        out_shape=result,
        in_specs=[smem] + [vmem] * (4 + len(weights)) + [anywhere],
        out_specs=anywhere,
        scratch_shapes=[
            pltpu.VMEM((2, lat_cells, HLON, LEV, width), BF16),
            pltpu.VMEM(strip.shape, BF16),
            pltpu.VMEM(strip.shape, BF16),
            pltpu.SemaphoreType.DMA((2,)),
        ],
        input_output_aliases={5 + len(weights): 0},
        compiler_params=params,
        cost_estimate=pl.CostEstimate(
            flops=3 * 10**9, bytes_accessed=4 * 10**6, transcendentals=10**6
        ),
    )(scalars, latent, normed, *got, *weights, middle)


def solution(mesh):
    placed = (
        P("lon", "lat", None, None),
        P("lon", "lat", None),
        P("lon", "lat", None),
        P("lon", "lat"),
        P("lat", "lon", None, None),
        P(),
        P(),
        P(),
        P(),
        P(),
        P(),
        P(),
        P(),
        P(),
    )
    return jax.shard_map(
        local, mesh=mesh, in_specs=placed, out_specs=P("lat", "lon", None, None), check_vma=False
    )
```

time: 28.9 us -> 30.1 us (1.042)
  starting transfers between devices: 11.5 us -> 15.2 us
  waiting for transfers between devices: 3.1 us -> 0.57 us
  local copies, waits for them, and re-layouts: 1.16 us -> 1.75 us
  other arithmetic: 0.66 us -> 0.17 us
    ppermute x4, starting transfers between devices: 4.15 us -> 7.91 us  [swapped(): got.append(lax.ppermute(mine, axis, pairs))]
    ppermute x4, waiting for transfers between devices: 3.1 us -> 0.57 us  [swapped(): got.append(lax.ppermute(mine, axis, pairs))]
    pallas_call x1 -> x2, Pallas kernels: 5.14 us -> 6.22 us  [the longest x1 3.78 us: local(): pl.pallas_call(functools.partial(middle_kernel, plan), out_shape=result,...]
    pallas_call x1, Pallas kernels: 4.82 us -> 3.96 us  [local(): pl.pallas_call(functools.partial(side_kernel, plan), out_shape=result, in...]
    unnamed x24, local copies, waits for them, and re-layouts: 0.71 us -> 1.47 us
    select_n x4 -> x1, other arithmetic: 0.58 us -> 0.02 us  [local(): jnp.where(even[0], up, down)]
  transfers between devices with their start and end apart: 5 -> 5, of which waited for: 1 -> 1; matrix products, arithmetic and copies ran while one was open for 3% -> 2% of each run, Pallas kernels for 18% -> 13%
where the time goes in v14:
time: 30.1 us; the launch traced here: 29.8 us
  starting transfers between devices  15.2 us (50%)
  Pallas kernels  11.9 us (40%)
  local copies, waits for them, and re-layouts  1.75 us (6%)
  waiting for transfers between devices  0.57 us (2%)
    ppermute x4, starting transfers between devices, swapped(): got.append(lax.ppermute(mine, axis, pairs))  7.91 us
    all_to_all x1, starting transfers between devices, local(): lax.all_to_all(sent, ('lon', 'lat'), split_axis=0, concat_axis=0, tiled=T...  7.3 us
    pallas_call x1, Pallas kernels, local(): pl.pallas_call(functools.partial(side_kernel, plan), out_shape=result, in...  3.96 us
    pallas_call x1, Pallas kernels, local(): pl.pallas_call(functools.partial(middle_kernel, plan), out_shape=result,...  3.78 us
    pallas_call x1, Pallas kernels, local(): pl.pallas_call(functools.partial(norm_kernel, plan), out_shape=[jax.Shape...  2.44 us
    pallas_call x1, Pallas kernels, packed(): pl.pallas_call(pack_kernel, out_shape=[jax.ShapeDtypeStruct(shape, BF16),...  1.69 us
    unnamed x24, local copies, waits for them, and re-layouts  1.47 us
  transfers between devices with their start and end apart: 5, of which 1 were waited for; matrix products, arithmetic and copies ran while one was open for 2% of the time, Pallas kernels for 13%

profile of v14, /device:TPU:0, one launch (start us, length us, event | category | flops | bytes accessed | tf_op | source)
XLA Modules:
  0.0 29.8 jit_solution(12998690802433899599)
XLA Ops:
  0.0 1.7 %shard_map.136 = (bf16[8,4,4,2,128]{4,3,2,1,0:T(2,128)(2,1)}, bf16[3,24,2,192]{3,2,1,0:T(2,128)(2,1)}, bf16[3,24,2,192]{3,2,1,0:T(2,128)(2,1)}) custom-call(bf16[8,4,2,128]{3,2,1,0:T(2,128)(2,1)} %values_ref.1, s32[8,8]{1,0:T(8,128)} %bitcast.22, s32[8,8]{1,0:T(8,128)} %bitcast.23, s32[4,8]{1,0:T(4,128)} %bitcast.24, bf16[12,24,2,192]{3,2,1,0:T(2,128)(2,1)} %back_ref.3), custom_call_target="tpu_custom_call" | custom-call | flops 20000000000 | bytes 1000000 | tf_op jit(solution)/shard_map/pallas_call | solution.py:166
  1.7 0.0 copy-start.7
  1.7 0.0 copy-start.8
  1.7 0.0 copy-start.6
  1.7 7.3 %all-to-all-start = ((bf16[32,4,2,128]{3,2,1,0:T(2,128)(2,1)}), bf16[32,4,2,128]{3,2,1,0:T(2,128)(2,1)S(1)}, u32[]{:S(2)}, u32[]{:S(2)}) async-start(bf16[32,4,2,128]{3,2,1,0:T(2,128)(2,1)} %bitcast.21), calls=%async_computation | async-start | bytes 131072 | tf_op jit(solution)/shard_map/all_to_all | solution.py:535
  9.1 0.0 copy-done.7
  9.1 0.0 copy-done.8
  9.1 0.0 copy-start.9
  9.1 0.8 %collective-permute-start.1 = (bf16[3,24,2,192]{3,2,1,0:T(2,128)(2,1)S(1)}, bf16[3,24,2,192]{3,2,1,0:T(2,128)(2,1)S(1)}, u32[]{:S(2)}, u32[]{:S(2)}) collective-permute-start(bf16[3,24,2,192]{3,2,1,0:T(2,128)(2,1)S(1)} %bitcast.18), channel_id=1, source_target_pairs={{1,2},{2,1},{5,6},{6,5},{9,10},{10,9},{13,14},{14,13},{17,18},{18,... | collective-permute-start | bytes 165896 | tf_op jit(solution)/shard_map/ppermute | solution.py:38
  9.9 4.5 %collective-permute-start = (bf16[3,24,2,192]{3,2,1,0:T(2,128)(2,1)S(1)}, bf16[3,24,2,192]{3,2,1,0:T(2,128)(2,1)S(1)}, u32[]{:S(2)}, u32[]{:S(2)}) collective-permute-start(bf16[3,24,2,192]{3,2,1,0:T(2,128)(2,1)S(1)} %bitcast.17), channel_id=1, source_target_pairs={{0,1},{1,0},{2,3},{3,2},{4,5},{5,4},{6,7},{7,6},{8,9},{9,8},{10,11... | collective-permute-start | bytes 165896 | tf_op jit(solution)/shard_map/ppermute | solution.py:38
  14.5 0.1 add_convert_fusion.1.even_ref
  14.5 0.0 copy-start.10
  14.5 0.1 add_convert_fusion.scalars_ref
  14.6 0.6 %copy-done.10 = bf16[192]{0:T(256)(128)(2,1)S(1)} copy-done((bf16[192]{0:T(256)(128)(2,1)S(1)}, bf16[192]{0:T(256)(128)(2,1)}, u32[]{:S(2)}) %copy-start.10) | copy-done | bytes 408
  15.2 0.0 copy-start.11
  15.2 0.6 %copy-done.11 = bf16[192]{0:T(256)(128)(2,1)S(1)} copy-done((bf16[192]{0:T(256)(128)(2,1)S(1)}, bf16[192]{0:T(256)(128)(2,1)}, u32[]{:S(2)}) %copy-start.11) | copy-done | bytes 408
  15.9 0.0 copy-done.9
  15.9 0.1 copy.16.first_ref
  16.0 0.0 copy-done.6
  16.0 0.0 copy-start
  16.0 0.0 copy-start.3
  16.0 0.0 copy-start.5
  16.0 0.2 copy.18.refs_4_
  16.2 0.0 copy-start.1
  16.2 0.0 copy-start.2
  16.2 0.0 copy-start.4
  16.2 0.0 collective-permute-done.1.two_ref
  16.2 0.6 %collective-permute-done.one_ref = bf16[3,24,2,192]{3,2,1,0:T(2,128)(2,1)S(1)} collective-permute-done((bf16[3,24,2,192]{3,2,1,0:T(2,128)(2,1)S(1)}, bf16[3,24,2,192]{3,2,1,0:T(2,128)(2,1)S(1)}, u32[]{:S(2)}, u32[]{:S(2)}) %collective-permute-start) | collective-permute-done | bytes 55328 | tf_op jit(solution)/shard_map/ppermute | solution.py:38
  16.8 0.0 all-to-all-done.recv_ref
  16.8 0.1 copy-done
  16.9 0.0 copy-done.3
  17.0 0.0 copy-done.5
  17.0 2.4 %shard_map.137 = (bf16[592,192]{1,0:T(8,128)(2,1)S(1)}, bf16[896,192]{1,0:T(8,128)(2,1)S(1)}, bf16[108,384]{1,0:T(8,128)(2,1)S(1)}, bf16[108,384]{1,0:T(8,128)(2,1)S(1)}) custom-call(s32[2]{0:T(128)S(1)} %add_convert_fusion.1.even_ref, bf16[32,4,2,128]{3,2,1,0:T(2,128)(2,1)S(1)} %all-to-all-done.recv_ref, ...), custom_call_target="tpu_custom_call" | custom-call | flops 1000000000 | bytes 2000000 | tf_op jit(solution)/shard_map/pallas_call | solution.py:550
  19.4 0.1 collective-permute-start.2
  19.5 2.5 %collective-permute-start.3 = (bf16[108,384]{1,0:T(8,128)(2,1)S(1)}, bf16[108,384]{1,0:T(8,128)(2,1)S(1)}, u32[]{:S(2)}, u32[]{:S(2)}) collective-permute-start(bf16[108,384]{1,0:T(8,128)(2,1)S(1)} %get-tuple-element.21), channel_id=1, source_target_pairs={{4,8},{8,4},{12,16},{16,12},{20,24},{24,20},{28,0},{0,28},{5,9},{9... | collective-permute-start | bytes 248840 | tf_op jit(solution)/shard_map/ppermute | solution.py:38
  22.0 0.0 copy-done.1
  22.0 0.0 copy-done.2
  22.0 0.0 copy-done.4
  22.0 3.8 %shard_map.138.refs_5_ = bf16[12,24,2,192]{3,2,1,0:T(2,128)(2,1)} custom-call(s32[4]{0:T(128)S(1)} %add_convert_fusion.scalars_ref, bf16[592,192]{1,0:T(8,128)(2,1)S(1)} %get-tuple-element.18.latent_ref, bf16[896,192]{1,0:T(8,128)(2,1)S(1)} %get-tuple-element.19.normed_ref, bf16[192,576]{1,0:T(8,128)(2,1)S(1)} %copy-done.2, bf16[192,192]{1,0:T(8,128)(2,1)S(1)} %copy-done.4, ...), custom_call_target="tpu_custom_call" | custom-call | flops 4000000000 | bytes 4000000 | tf_op jit(solution)/shard_map/pallas_call | solution.py:581
  25.8 0.0 collective-permute-done.2.one_ref
  25.8 0.0 collective-permute-done.3.two_ref
  25.8 4.0 %shard_map.139 = bf16[12,24,2,192]{3,2,1,0:T(2,128)(2,1)} custom-call(s32[4]{0:T(128)S(1)} %add_convert_fusion.scalars_ref, bf16[592,192]{1,0:T(8,128)(2,1)S(1)} %get-tuple-element.18.latent_ref, bf16[896,192]{1,0:T(8,128)(2,1)S(1)} %get-tuple-element.19.normed_ref, ...), custom_call_target="tpu_custom_call", output_to_operand_aliasing={{}: (10, {})} | custom-call | flops 3000000000 | bytes 4000000 | tf_op jit(solution)/shard_map/pallas_call | solution.py:595
  (3 shorter events, 0.0 us)
Async XLA Ops:
  1.7 7.4 %copy-start.7 = (bf16[3,24,2,192]{3,2,1,0:T(2,128)(2,1)S(1)}, bf16[3,24,2,192]{3,2,1,0:T(2,128)(2,1)}, u32[]{:S(2)}) copy-start(bf16[3,24,2,192]{3,2,1,0:T(2,128)(2,1)} %get-tuple-element.16) | copy-start | bytes 165892
  1.7 7.4 %copy-start.8 = (bf16[3,24,2,192]{3,2,1,0:T(2,128)(2,1)S(1)}, bf16[3,24,2,192]{3,2,1,0:T(2,128)(2,1)}, u32[]{:S(2)}) copy-start(bf16[3,24,2,192]{3,2,1,0:T(2,128)(2,1)} %get-tuple-element.15) | copy-start | bytes 165892
  1.7 14.3 %copy-start.6 = (bf16[768,192]{0,1:T(8,128)(2,1)S(1)}, bf16[768,192]{0,1:T(8,128)(2,1)}, u32[]{:S(2)}) copy-start(bf16[768,192]{0,1:T(8,128)(2,1)} %param.27) | copy-start | bytes 884740
  1.7 15.1 %all-to-all-start = ((bf16[32,4,2,128]{3,2,1,0:T(2,128)(2,1)}), bf16[32,4,2,128]{3,2,1,0:T(2,128)(2,1)S(1)}, u32[]{:S(2)}, u32[]{:S(2)}) async-start(bf16[32,4,2,128]{3,2,1,0:T(2,128)(2,1)} %bitcast.21), calls=%async_computation | async-start | bytes 131072 | tf_op jit(solution)/shard_map/all_to_all | solution.py:535
  9.1 6.8 %copy-start.9 = (bf16[128,192]{0,1:T(8,128)(2,1)S(1)}, bf16[128,192]{0,1:T(8,128)(2,1)}, u32[]{:S(2)}) copy-start(bf16[128,192]{0,1:T(8,128)(2,1)} %param.19) | copy-start | bytes 147460
  9.1 7.1 %collective-permute-start.1 = (bf16[3,24,2,192]{3,2,1,0:T(2,128)(2,1)S(1)}, bf16[3,24,2,192]{3,2,1,0:T(2,128)(2,1)S(1)}, u32[]{:S(2)}, u32[]{:S(2)}) collective-permute-start(bf16[3,24,2,192]{3,2,1,0:T(2,128)(2,1)S(1)} %bitcast.18), channel_id=1, source_target_pairs={{1,2},{2,1},{5,6},{6,5},{9,10},{10,9},{13,14},{14,13},{17,18},{18,... | collective-permute-start | bytes 165896 | tf_op jit(solution)/shard_map/ppermute | solution.py:38
  9.9 6.9 %collective-permute-start = (bf16[3,24,2,192]{3,2,1,0:T(2,128)(2,1)S(1)}, bf16[3,24,2,192]{3,2,1,0:T(2,128)(2,1)S(1)}, u32[]{:S(2)}, u32[]{:S(2)}) collective-permute-start(bf16[3,24,2,192]{3,2,1,0:T(2,128)(2,1)S(1)} %bitcast.17), channel_id=1, source_target_pairs={{0,1},{1,0},{2,3},{3,2},{4,5},{5,4},{6,7},{7,6},{8,9},{9,8},{10,11... | collective-permute-start | bytes 165896 | tf_op jit(solution)/shard_map/ppermute | solution.py:38
  14.5 0.7 %copy-start.10 = (bf16[192]{0:T(256)(128)(2,1)S(1)}, bf16[192]{0:T(256)(128)(2,1)}, u32[]{:S(2)}) copy-start(bf16[192]{0:T(256)(128)(2,1)} %param.25) | copy-start | bytes 1156
  15.2 0.7 %copy-start.11 = (bf16[192]{0:T(256)(128)(2,1)S(1)}, bf16[192]{0:T(256)(128)(2,1)}, u32[]{:S(2)}) copy-start(bf16[192]{0:T(256)(128)(2,1)} %param.22) | copy-start | bytes 1156
  16.0 1.0 %copy-start = (bf16[12,24,2,192]{3,2,1,0:T(2,128)(2,1)S(1)}, bf16[12,24,2,192]{3,2,1,0:T(2,128)(2,1)}, u32[]{:S(2)}) copy-start(bf16[12,24,2,192]{3,2,1,0:T(2,128)(2,1)} %back_ref.3) | copy-start | bytes 663556
  16.0 1.0 %copy-start.3 = (bf16[192,384]{1,0:T(8,128)(2,1)S(1)}, bf16[192,384]{1,0:T(8,128)(2,1)}, u32[]{:S(2)}) copy-start(bf16[192,384]{1,0:T(8,128)(2,1)} %lift_ref.1) | copy-start | bytes 442372
  16.0 1.0 %copy-start.5 = (bf16[8,192]{1,0:T(8,128)(2,1)S(1)}, bf16[8,192]{1,0:T(8,128)(2,1)}, u32[]{:S(2)}) copy-start(bf16[8,192]{1,0:T(8,128)(2,1)} %table_ref.1) | copy-start | bytes 9220
  16.2 5.8 %copy-start.1 = (bf16[192,768]{1,0:T(8,128)(2,1)S(1)}, bf16[192,768]{1,0:T(8,128)(2,1)}, u32[]{:S(2)}) copy-start(bf16[192,768]{1,0:T(8,128)(2,1)} %refs_3_.3) | copy-start | bytes 884740
  16.2 5.8 %copy-start.2 = (bf16[192,576]{1,0:T(8,128)(2,1)S(1)}, bf16[192,576]{1,0:T(8,128)(2,1)}, u32[]{:S(2)}) copy-start(bf16[192,576]{1,0:T(8,128)(2,1)} %refs_0_.3) | copy-start | bytes 663556
  16.2 5.8 %copy-start.4 = (bf16[192,192]{1,0:T(8,128)(2,1)S(1)}, bf16[192,192]{1,0:T(8,128)(2,1)}, u32[]{:S(2)}) copy-start(bf16[192,192]{1,0:T(8,128)(2,1)} %refs_1_.3) | copy-start | bytes 221188
  19.4 6.4 %collective-permute-start.2 = (bf16[108,384]{1,0:T(8,128)(2,1)S(1)}, bf16[108,384]{1,0:T(8,128)(2,1)S(1)}, u32[]{:S(2)}, u32[]{:S(2)}) collective-permute-start(bf16[108,384]{1,0:T(8,128)(2,1)S(1)} %get-tuple-element.20), channel_id=1, source_target_pairs={{0,4},{4,0},{8,12},{12,8},{16,20},{20,16},{24,28},{28,24},{1,5},{5... | collective-permute-start | bytes 248840 | tf_op jit(solution)/shard_map/ppermute | solution.py:38
  19.5 6.3 %collective-permute-start.3 = (bf16[108,384]{1,0:T(8,128)(2,1)S(1)}, bf16[108,384]{1,0:T(8,128)(2,1)S(1)}, u32[]{:S(2)}, u32[]{:S(2)}) collective-permute-start(bf16[108,384]{1,0:T(8,128)(2,1)S(1)} %get-tuple-element.21), channel_id=1, source_target_pairs={{4,8},{8,4},{12,16},{16,12},{20,24},{24,20},{28,0},{0,28},{5,9},{9... | collective-permute-start | bytes 248840 | tf_op jit(solution)/shard_map/ppermute | solution.py:38

commit v15 on v12

--- a/solution.py
+++ b/solution.py
@@ -344,35 +344,45 @@
     tokens = below(*[piece for window in windows for piece in window]).astype(BF16)
     weight = attn_ref[...]
     head = width // HEADS
-    keys = dot(tokens, weight[:, width : 2 * width]).astype(BF16)
+    keys = dot(tokens, weight[:, width : 2 * width])
     query = dot(normed[:end].astype(BF16), weight[:, :width]) * head ** (-0.5)
+    query = jnp.concatenate([query, jnp.ones((end, PAD - width), F32)], axis=1)
     values = with_ones(dot(tokens, weight[:, 2 * width :]))
     yield True
 
-    head_of = lax.broadcasted_iota(jnp.int32, (1, width), 1) // head
+    lane = lax.broadcasted_iota(jnp.int32, (1, PAD), 1)
     many = WLAT * WLON * LEV
     corner = HLAT * HLON * LEV
-    key = lax.broadcasted_iota(jnp.int32, (1, many), 1)
+    key = lax.broadcasted_iota(jnp.int32, (many, PAD - width), 0)
+    spare = lax.broadcasted_iota(jnp.int32, (many, PAD - width), 1)
+    unused = lax.broadcasted_iota(jnp.int32, (PAD - many, PAD), 1)
+    unused = jnp.where(unused == width, -3e38, 0.0).astype(BF16)
     mixed, start = [], 0
     for w, ((i, j), rows) in enumerate(zip(places, groups)):
         part = query[start : start + rows]
-        stacked = below(*[jnp.where(head_of == h, part, 0.0) for h in range(HEADS)]).astype(BF16)
-        scores = dot_nt(stacked, keys[w * many : (w + 1) * many])
-        yield True
+        stacked = below(
+            *[jnp.where((lane // head == h) | (lane >= width), part, 0.0) for h in range(HEADS)]
+        ).astype(BF16)
+        bias = jnp.zeros((many, PAD - width), F32)
         if i != 1:
             if j == 1:
                 inside = key < 2 * corner
             else:
                 inside = (key < corner) | ((key >= 2 * corner) & (key < 3 * corner))
-            scores = jnp.where(inside | (scalars_ref[i] == 0), scores, -1e30)
+            bias = jnp.where(inside | (spare > 0), 0.0, -3e38) * scalars_ref[i].astype(F32)
+        here = jnp.concatenate([keys[w * many : (w + 1) * many], bias], axis=1).astype(BF16)
+        scores = dot_nt(stacked, below(here, unused))
+        yield True
         largest = jnp.max(scores, axis=-1, keepdims=True)
-        raised = jnp.exp(scores - largest).astype(BF16)
-        product = dot(raised, values[w * many : (w + 1) * many])
+        raised = jnp.exp((scores - largest).astype(BF16))
+        here = below(values[w * many : (w + 1) * many], jnp.zeros((PAD - many, PAD), BF16))
+        product = dot(raised, here)
         yield True
         product = product[:, :width] * about_one_over(product[:, width : width + 1])
-        total = jnp.zeros((rows, width), F32)
-        for h in range(HEADS):
-            total = jnp.where(head_of == h, product[h * rows : (h + 1) * rows], total)
+        total = product[:rows]
+        for h in range(1, HEADS):
+            own = lane[:, :width] // head == h
+            total = jnp.where(own, product[h * rows : (h + 1) * rows], total)
         mixed.append(total)
         start += rows
     mixed = below(*mixed).astype(BF16)
@@ -382,7 +392,7 @@
     normed_two = normalise(after, gain_two_ref[...].astype(F32)).astype(BF16)
     hidden = dot(normed_two, up_ref[...])
     yield True
-    result = after + dot(gelu(hidden).astype(BF16), down_ref[...])
+    result = after + dot(gelu(hidden.astype(BF16)), down_ref[...])
     yield True
     start = 0
     for (i, j), rows in zip(places, groups):

time: 28.9 us -> 28.7 us (level)
  no operation moved by 1% of the time
where the time goes in v15:
time: 28.7 us; the launch traced here: 28.2 us
  Pallas kernels  11.5 us (40%)
  starting transfers between devices  11.5 us (40%)
  waiting for transfers between devices  3.1 us (11%)
  local copies, waits for them, and re-layouts  1.16 us (4%)
  other arithmetic  0.66 us (2%)
    all_to_all x1, starting transfers between devices, local(): lax.all_to_all(sent, ('lon', 'lat'), split_axis=0, concat_axis=0, tiled=T...  7.3 us
    pallas_call x1, Pallas kernels, local(): pl.pallas_call(functools.partial(middle_kernel, plan), out_shape=[result,...  5.05 us
    pallas_call x1, Pallas kernels, local(): pl.pallas_call(functools.partial(side_kernel, plan), out_shape=result, in...  4.75 us
    ppermute x4, starting transfers between devices, swapped(): got.append(lax.ppermute(mine, axis, pairs))  4.15 us
    ppermute x4, waiting for transfers between devices, swapped(): got.append(lax.ppermute(mine, axis, pairs))  3.1 us
    pallas_call x1, Pallas kernels, packed(): pl.pallas_call(pack_kernel, out_shape=[jax.ShapeDtypeStruct(shape, BF16),...  1.74 us
    unnamed x24, local copies, waits for them, and re-layouts  0.71 us
  transfers between devices with their start and end apart: 5, of which 1 were waited for; matrix products, arithmetic and copies ran while one was open for 3% of the time, Pallas kernels for 18%

profile of v15, /device:TPU:0, one launch (start us, length us, event | category | flops | bytes accessed | tf_op | source)
XLA Modules:
  0.0 28.2 jit_solution(4358209902544040437)
XLA Ops:
  0.0 1.7 %shard_map.136 = (bf16[8,4,10,2,128]{4,3,2,1,0:T(2,128)(2,1)}, bf16[3,24,2,192]{3,2,1,0:T(2,128)(2,1)}, bf16[3,24,2,192]{3,2,1,0:T(2,128)(2,1)}) custom-call(bf16[8,4,2,128]{3,2,1,0:T(2,128)(2,1)} %values_ref.1, s32[8,8]{1,0:T(8,128)} %bitcast.32, s32[8,8]{1,0:T(8,128)} %bitcast.33, s32[4,8]{1,0:T(4,128)} %bitcast.34, bf16[12,24,2,192]{3,2,1,0:T(2,128)(2,1)} %back_ref.5), custom_call_target="tpu_custom_call" | custom-call | flops 20000000000 | bytes 1000000 | tf_op jit(solution)/shard_map/pallas_call | solution.py:184
  1.7 0.0 copy-start.7
  1.8 0.0 copy-start.8
  1.8 0.0 copy-start
  1.8 0.0 copy-start.10
  1.8 7.3 %all-to-all-start = ((bf16[32,10,2,128]{3,2,1,0:T(2,128)(2,1)}), bf16[32,10,2,128]{3,2,1,0:T(2,128)(2,1)S(1)}, u32[]{:S(2)}, u32[]{:S(2)}) async-start(bf16[32,10,2,128]{3,2,1,0:T(2,128)(2,1)} %bitcast.25), calls=%async_computation | async-start | bytes 327680 | tf_op jit(solution)/shard_map/all_to_all | solution.py:534
  9.1 0.0 copy-done.7
  9.1 0.0 copy-done.8
  9.2 0.0 copy-start.6
  9.2 1.8 %collective-permute-start.1 = (bf16[3,24,2,192]{3,2,1,0:T(2,128)(2,1)S(1)}, bf16[3,24,2,192]{3,2,1,0:T(2,128)(2,1)S(1)}, u32[]{:S(2)}, u32[]{:S(2)}) collective-permute-start(bf16[3,24,2,192]{3,2,1,0:T(2,128)(2,1)S(1)} %bitcast.29), channel_id=1, source_target_pairs={{0,1},{1,0},{2,3},{3,2},{4,5},{5,4},{6,7},{7,6},{8,9},{9,8},{10,11... | collective-permute-start | bytes 165896 | tf_op jit(solution)/shard_map/ppermute | solution.py:39
  11.0 0.7 %collective-permute-start = (bf16[3,24,2,192]{3,2,1,0:T(2,128)(2,1)S(1)}, bf16[3,24,2,192]{3,2,1,0:T(2,128)(2,1)S(1)}, u32[]{:S(2)}, u32[]{:S(2)}) collective-permute-start(bf16[3,24,2,192]{3,2,1,0:T(2,128)(2,1)S(1)} %bitcast.27), channel_id=1, source_target_pairs={{1,2},{2,1},{5,6},{6,5},{9,10},{10,9},{13,14},{14,13},{17,18},{18,... | collective-permute-start | bytes 165896 | tf_op jit(solution)/shard_map/ppermute | solution.py:39
  11.7 0.0 copy-done
  11.7 0.0 copy-start.9
  11.7 0.1 fusion
  11.8 0.1 add_convert_fusion.scalars_ref
  11.9 0.0 copy-done.10
  11.9 0.0 copy-start.11
  11.9 0.6 %copy-done.11 = bf16[192]{0:T(256)(128)(2,1)S(1)} copy-done((bf16[192]{0:T(256)(128)(2,1)S(1)}, bf16[192]{0:T(256)(128)(2,1)}, u32[]{:S(2)}) %copy-start.11) | copy-done | bytes 408
  12.6 0.0 copy-done.9
  12.6 0.1 copy.16.first_ref
  12.7 0.0 copy-done.6
  12.7 0.0 copy-start.3
  12.7 0.0 copy-start.4
  12.7 0.2 copy.17.refs_5_
  12.9 3.1 %collective-permute-done.1 = bf16[3,24,2,192]{3,2,1,0:T(2,128)(2,1)S(1)} collective-permute-done((bf16[3,24,2,192]{3,2,1,0:T(2,128)(2,1)S(1)}, bf16[3,24,2,192]{3,2,1,0:T(2,128)(2,1)S(1)}, u32[]{:S(2)}, u32[]{:S(2)}) %collective-permute-start.1) | collective-permute-done | bytes 55328 | tf_op jit(solution)/shard_map/ppermute | solution.py:39
  16.0 0.0 collective-permute-done
  16.0 0.0 copy-start.1
  16.0 0.1 fusion.1
  16.1 0.0 copy-start.2
  16.1 0.0 copy-start.5
  16.1 0.4 %broadcast_select_fusion.2 = (bf16[18,6,2,192]{3,2,1,0:T(2,128)(2,1)S(1)}, bf16[18,6,2,192]{3,2,1,0:T(2,128)(2,1)S(1)}) fusion(pred[]{:T(512)S(6)} %eq.22, bf16[3,6,2,192]{3,2,1,0:T(2,128)(2,1)S(1)} %get-tuple-element.41, bf16[12,6,2,192]{3,2,1,0:T(2,128)(2,1)S(1)} %get-tuple-element.28, bf16[3,6,2,192]{3,2,1,0:T(2,128)(2,1)S(1)} %get-tuple-element.38, ...), kind=kLoop, calls=%fused_computation.2 | loop fusion | flops 248832 | bytes 331777 | tf_op jit(solution)/shard_map/jit(_where)/select_n | solution.py:33
  16.5 1.2 %collective-permute-start.3 = (bf16[18,6,2,192]{3,2,1,0:T(2,128)(2,1)S(1)}, bf16[18,6,2,192]{3,2,1,0:T(2,128)(2,1)S(1)}, u32[]{:S(2)}, u32[]{:S(2)}) collective-permute-start(bf16[18,6,2,192]{3,2,1,0:T(2,128)(2,1)S(1)} %get-tuple-element.31), channel_id=1, source_target_pairs={{4,8},{8,4},{12,16},{16,12},{20,24},{24,20},{28,0},{0,28},{5,9},{9... | collective-permute-start | bytes 248840 | tf_op jit(solution)/shard_map/ppermute | solution.py:39
  17.7 0.4 %collective-permute-start.2 = (bf16[18,6,2,192]{3,2,1,0:T(2,128)(2,1)S(1)}, bf16[18,6,2,192]{3,2,1,0:T(2,128)(2,1)S(1)}, u32[]{:S(2)}, u32[]{:S(2)}) collective-permute-start(bf16[18,6,2,192]{3,2,1,0:T(2,128)(2,1)S(1)} %get-tuple-element.32), channel_id=1, source_target_pairs={{0,4},{4,0},{8,12},{12,8},{16,20},{20,16},{24,28},{28,24},{1,5},{5... | collective-permute-start | bytes 248840 | tf_op jit(solution)/shard_map/ppermute | solution.py:39
  18.1 0.0 all-to-all-done.recv_ref
  18.1 0.0 copy-done.3
  18.1 0.0 copy-done.4
  18.1 0.0 copy-done.1
  18.2 0.0 copy-done.2
  18.2 0.0 copy-done.5
  18.2 5.0 %shard_map.137 = (bf16[12,24,2,192]{3,2,1,0:T(2,128)(2,1)}, f32[928,256]{1,0:T(8,128)S(1)}) custom-call(s32[3]{0:T(128)S(1)} %add_convert_fusion.scalars_ref, bf16[32,10,2,128]{3,2,1,0:T(2,128)(2,1)S(1)} %all-to-all-done.recv_ref, bf16[3,24,2,192]{3,2,1,0:T(2,128)(2,1)S(1)} %bitcast.23, bf16[3,24,2,192]{3,2,1,0:T(2,128)(2,1)S(1)} %bitcast.20, ...), custom_call_target="tpu_custom_call" | custom-call | flops 4000000000 | bytes 4000000 | tf_op jit(solution)/shard_map/pallas_call | solution.py:563
  23.2 0.0 collective-permute-done.3
  23.2 0.0 collective-permute-done.2
  23.3 0.2 broadcast_select_fusion
  23.4 4.8 %shard_map.138 = bf16[12,24,2,192]{3,2,1,0:T(2,128)(2,1)} custom-call(s32[3]{0:T(128)S(1)} %add_convert_fusion.scalars_ref, f32[928,256]{1,0:T(8,128)S(1)} %get-tuple-element.23.rest_ref, bf16[3,24,2,192]{3,2,1,0:T(2,128)(2,1)S(1)} %bitcast.24, bf16[3,24,2,192]{3,2,1,0:T(2,128)(2,1)S(1)} %bitcast.21, ...), custom_call_target="tpu_custom_call", output_to_operand_aliasing={{}: (13, {})} | custom-call | flops 3000000000 | bytes 4000000 | tf_op jit(solution)/shard_map/pallas_call | solution.py:589
  (4 shorter events, 0.0 us)
Async XLA Ops:
  1.7 7.4 %copy-start.7 = (bf16[3,24,2,192]{3,2,1,0:T(2,128)(2,1)S(1)}, bf16[3,24,2,192]{3,2,1,0:T(2,128)(2,1)}, u32[]{:S(2)}) copy-start(bf16[3,24,2,192]{3,2,1,0:T(2,128)(2,1)} %get-tuple-element.17) | copy-start | bytes 165892
  1.8 7.4 %copy-start.8 = (bf16[3,24,2,192]{3,2,1,0:T(2,128)(2,1)S(1)}, bf16[3,24,2,192]{3,2,1,0:T(2,128)(2,1)}, u32[]{:S(2)}) copy-start(bf16[3,24,2,192]{3,2,1,0:T(2,128)(2,1)} %get-tuple-element.18) | copy-start | bytes 165892
  1.8 9.9 %copy-start = (bf16[12,24,2,192]{3,2,1,0:T(2,128)(2,1)S(1)}, bf16[12,24,2,192]{3,2,1,0:T(2,128)(2,1)}, u32[]{:S(2)}) copy-start(bf16[12,24,2,192]{3,2,1,0:T(2,128)(2,1)} %back_ref.5) | copy-start | bytes 663556
  1.8 10.1 %copy-start.10 = (bf16[192]{0:T(256)(128)(2,1)S(1)}, bf16[192]{0:T(256)(128)(2,1)}, u32[]{:S(2)}) copy-start(bf16[192]{0:T(256)(128)(2,1)} %param.22) | copy-start | bytes 1156
  1.8 16.3 %all-to-all-start = ((bf16[32,10,2,128]{3,2,1,0:T(2,128)(2,1)}), bf16[32,10,2,128]{3,2,1,0:T(2,128)(2,1)S(1)}, u32[]{:S(2)}, u32[]{:S(2)}) async-start(bf16[32,10,2,128]{3,2,1,0:T(2,128)(2,1)} %bitcast.25), calls=%async_computation | async-start | bytes 327680 | tf_op jit(solution)/shard_map/all_to_all | solution.py:534
  9.2 3.5 %copy-start.6 = (bf16[768,192]{0,1:T(8,128)(2,1)S(1)}, bf16[768,192]{0,1:T(8,128)(2,1)}, u32[]{:S(2)}) copy-start(bf16[768,192]{0,1:T(8,128)(2,1)} %param.27) | copy-start | bytes 884740
  9.2 6.8 %collective-permute-start.1 = (bf16[3,24,2,192]{3,2,1,0:T(2,128)(2,1)S(1)}, bf16[3,24,2,192]{3,2,1,0:T(2,128)(2,1)S(1)}, u32[]{:S(2)}, u32[]{:S(2)}) collective-permute-start(bf16[3,24,2,192]{3,2,1,0:T(2,128)(2,1)S(1)} %bitcast.29), channel_id=1, source_target_pairs={{0,1},{1,0},{2,3},{3,2},{4,5},{5,4},{6,7},{7,6},{8,9},{9,8},{10,11... | collective-permute-start | bytes 165896 | tf_op jit(solution)/shard_map/ppermute | solution.py:39
  11.0 5.0 %collective-permute-start = (bf16[3,24,2,192]{3,2,1,0:T(2,128)(2,1)S(1)}, bf16[3,24,2,192]{3,2,1,0:T(2,128)(2,1)S(1)}, u32[]{:S(2)}, u32[]{:S(2)}) collective-permute-start(bf16[3,24,2,192]{3,2,1,0:T(2,128)(2,1)S(1)} %bitcast.27), channel_id=1, source_target_pairs={{1,2},{2,1},{5,6},{6,5},{9,10},{10,9},{13,14},{14,13},{17,18},{18,... | collective-permute-start | bytes 165896 | tf_op jit(solution)/shard_map/ppermute | solution.py:39
  11.7 0.9 %copy-start.9 = (bf16[128,192]{0,1:T(8,128)(2,1)S(1)}, bf16[128,192]{0,1:T(8,128)(2,1)}, u32[]{:S(2)}) copy-start(bf16[128,192]{0,1:T(8,128)(2,1)} %param.19) | copy-start | bytes 147460
  11.9 0.7 %copy-start.11 = (bf16[192]{0:T(256)(128)(2,1)S(1)}, bf16[192]{0:T(256)(128)(2,1)}, u32[]{:S(2)}) copy-start(bf16[192]{0:T(256)(128)(2,1)} %param.25) | copy-start | bytes 1156
  12.7 5.5 %copy-start.3 = (bf16[192,384]{1,0:T(8,128)(2,1)S(1)}, bf16[192,384]{1,0:T(8,128)(2,1)}, u32[]{:S(2)}) copy-start(bf16[192,384]{1,0:T(8,128)(2,1)} %lift_ref.1) | copy-start | bytes 442372
  12.7 5.5 %copy-start.4 = (bf16[192,192]{1,0:T(8,128)(2,1)S(1)}, bf16[192,192]{1,0:T(8,128)(2,1)}, u32[]{:S(2)}) copy-start(bf16[192,192]{1,0:T(8,128)(2,1)} %refs_2_.3) | copy-start | bytes 221188
  16.0 2.2 %copy-start.1 = (bf16[192,768]{1,0:T(8,128)(2,1)S(1)}, bf16[192,768]{1,0:T(8,128)(2,1)}, u32[]{:S(2)}) copy-start(bf16[192,768]{1,0:T(8,128)(2,1)} %refs_4_.3) | copy-start | bytes 884740
  16.1 2.1 %copy-start.2 = (bf16[192,576]{1,0:T(8,128)(2,1)S(1)}, bf16[192,576]{1,0:T(8,128)(2,1)}, u32[]{:S(2)}) copy-start(bf16[192,576]{1,0:T(8,128)(2,1)} %refs_1_.3) | copy-start | bytes 663556
  16.1 2.1 %copy-start.5 = (bf16[8,192]{1,0:T(8,128)(2,1)S(1)}, bf16[8,192]{1,0:T(8,128)(2,1)}, u32[]{:S(2)}) copy-start(bf16[8,192]{1,0:T(8,128)(2,1)} %table_ref.1) | copy-start | bytes 9220
  16.5 6.8 %collective-permute-start.3 = (bf16[18,6,2,192]{3,2,1,0:T(2,128)(2,1)S(1)}, bf16[18,6,2,192]{3,2,1,0:T(2,128)(2,1)S(1)}, u32[]{:S(2)}, u32[]{:S(2)}) collective-permute-start(bf16[18,6,2,192]{3,2,1,0:T(2,128)(2,1)S(1)} %get-tuple-element.31), channel_id=1, source_target_pairs={{4,8},{8,4},{12,16},{16,12},{20,24},{24,20},{28,0},{0,28},{5,9},{9... | collective-permute-start | bytes 248840 | tf_op jit(solution)/shard_map/ppermute | solution.py:39
  17.7 5.5 %collective-permute-start.2 = (bf16[18,6,2,192]{3,2,1,0:T(2,128)(2,1)S(1)}, bf16[18,6,2,192]{3,2,1,0:T(2,128)(2,1)S(1)}, u32[]{:S(2)}, u32[]{:S(2)}) collective-permute-start(bf16[18,6,2,192]{3,2,1,0:T(2,128)(2,1)S(1)} %get-tuple-element.32), channel_id=1, source_target_pairs={{0,4},{4,0},{8,12},{12,8},{16,20},{20,16},{24,28},{28,24},{1,5},{5... | collective-permute-start | bytes 248840 | tf_op jit(solution)/shard_map/ppermute | solution.py:39

commit v16 on v15

--- a/solution.py
+++ b/solution.py
@@ -230,16 +230,6 @@
     return entries
 
 
-def alternate(*chains):
-    chains, begun = list(chains), 1
-    while chains:
-        for chain in chains[:begun]:
-            if next(chain, None) is None:
-                chains.remove(chain)
-                begun -= 1
-        begun += 1
-
-
 def scattered(recv_ref, first_ref, table_ref, lift_ref, plan, lon_cells):
     sources, _, capacity, _ = recv_ref.shape
     width = table_ref.shape[1]
@@ -267,19 +257,23 @@
         encoded = gelu(dot(records, first) + dot(chosen, table)).astype(BF16)
         lifted = gelu(dot(encoded, lift))
         tokens = dot_nt(weigh, meta)
-        sums = []
+        hots, parts = [], []
         for n in range(len(AROUND)):
-            part = lifted[n * slots : (n + 1) * slots]
-            part = with_ones(
-                below(*[part[:, level * width : (level + 1) * width] for level in range(LEV)])
-            )
             token = tokens[n : n + 1]
             token = jnp.concatenate([token + float(level) for level in range(LEV)], axis=1)
             if token.shape[1] == LANES:
                 hot = codes[n] == token
             else:
                 hot = codes[n][:, :1] == token
-            sums.append(dot(jnp.where(hot, 1.0, 0.0).astype(BF16), part))
+            hots.append(jnp.where(hot, 1.0, 0.0).astype(BF16))
+        for n in range(len(AROUND)):
+            part = lifted[n * slots : (n + 1) * slots]
+            parts.append(
+                with_ones(
+                    below(*[part[:, level * width : (level + 1) * width] for level in range(LEV)])
+                )
+            )
+        sums = [dot(hot, part) for hot, part in zip(hots, parts)]
         return tuple(sums)
 
     sums = scatter(0)
@@ -293,7 +287,7 @@
     return sums
 
 
-def worked(plan, places, sum_of, borders, weights, scalars_ref, put, done):
+def worked(plan, places, sum_of, borders, weights, scalars_ref, put):
     back_ref, north_ref, south_ref, west_ref, east_ref = borders
     gain_one_ref, attn_ref, mix_ref, gain_two_ref, up_ref, down_ref = weights
     lat_cells, width = back_ref.shape[0], back_ref.shape[3]
@@ -323,7 +317,6 @@
     share = share * (2.0 - tally * share)
     latent = ((below(*pieces) + sums[:, :width]) * share).astype(BF16).astype(F32)
     normed = normalise(latent, gain_one_ref[...].astype(F32))
-    yield True
 
     def piece_of(tile, number):
         start, count = spans[tile, number]
@@ -348,7 +341,6 @@
     query = dot(normed[:end].astype(BF16), weight[:, :width]) * head ** (-0.5)
     query = jnp.concatenate([query, jnp.ones((end, PAD - width), F32)], axis=1)
     values = with_ones(dot(tokens, weight[:, 2 * width :]))
-    yield True
 
     lane = lax.broadcasted_iota(jnp.int32, (1, PAD), 1)
     many = WLAT * WLON * LEV
@@ -357,12 +349,9 @@
     spare = lax.broadcasted_iota(jnp.int32, (many, PAD - width), 1)
     unused = lax.broadcasted_iota(jnp.int32, (PAD - many, PAD), 1)
     unused = jnp.where(unused == width, -3e38, 0.0).astype(BF16)
-    mixed, start = [], 0
-    for w, ((i, j), rows) in enumerate(zip(places, groups)):
-        part = query[start : start + rows]
-        stacked = below(
-            *[jnp.where((lane // head == h) | (lane >= width), part, 0.0) for h in range(HEADS)]
-        ).astype(BF16)
+    nothing = jnp.zeros((PAD - many, PAD), BF16)
+
+    def keys_of(w, i, j):
         bias = jnp.zeros((many, PAD - width), F32)
         if i != 1:
             if j == 1:
@@ -370,45 +359,50 @@
             else:
                 inside = (key < corner) | ((key >= 2 * corner) & (key < 3 * corner))
             bias = jnp.where(inside | (spare > 0), 0.0, -3e38) * scalars_ref[i].astype(F32)
-        here = jnp.concatenate([keys[w * many : (w + 1) * many], bias], axis=1).astype(BF16)
-        scores = dot_nt(stacked, below(here, unused))
-        yield True
-        largest = jnp.max(scores, axis=-1, keepdims=True)
-        raised = jnp.exp((scores - largest).astype(BF16))
-        here = below(values[w * many : (w + 1) * many], jnp.zeros((PAD - many, PAD), BF16))
-        product = dot(raised, here)
-        yield True
-        product = product[:, :width] * about_one_over(product[:, width : width + 1])
+        here = jnp.concatenate([keys[w * many : (w + 1) * many], bias], axis=1)
+        return below(here.astype(BF16), unused)
+
+    begins = [sum(groups[:w]) for w in range(len(groups))]
+    parts = [query[begin : begin + rows] for begin, rows in zip(begins, groups)]
+    stacks = [
+        below(
+            *[jnp.where((lane // head == h) | (lane >= width), part, 0.0) for h in range(HEADS)]
+        ).astype(BF16)
+        for part in parts
+    ]
+    held = [keys_of(w, i, j) for w, (i, j) in enumerate(places)]
+    scores = [dot_nt(stack, here) for stack, here in zip(stacks, held)]
+    largest = [jnp.max(score, axis=-1, keepdims=True) for score in scores]
+    raised = [jnp.exp((score - most).astype(BF16)) for score, most in zip(scores, largest)]
+    held = [below(values[w * many : (w + 1) * many], nothing) for w in range(len(places))]
+    products = [dot(one, here) for one, here in zip(raised, held)]
+    shares = [about_one_over(product[:, width : width + 1]) for product in products]
+    products = [product[:, :width] * share for product, share in zip(products, shares)]
+    mixed = []
+    for product, rows in zip(products, groups):
         total = product[:rows]
         for h in range(1, HEADS):
             own = lane[:, :width] // head == h
             total = jnp.where(own, product[h * rows : (h + 1) * rows], total)
         mixed.append(total)
-        start += rows
     mixed = below(*mixed).astype(BF16)
 
     after = (latent[:end] + dot(mixed, mix_ref[...])).astype(BF16).astype(F32)
-    yield True
     normed_two = normalise(after, gain_two_ref[...].astype(F32)).astype(BF16)
-    hidden = dot(normed_two, up_ref[...])
-    yield True
-    result = after + dot(gelu(hidden.astype(BF16)), down_ref[...])
-    yield True
-    start = 0
-    for (i, j), rows in zip(places, groups):
+    hidden = gelu(dot(normed_two, up_ref[...]).astype(BF16))
+    result = after + dot(hidden, down_ref[...])
+    for begin, (i, j) in zip(begins, places):
         part = plan[4][3 * i + j]
-        piece = result[start : start + tokens_of(part)].astype(BF16)
+        piece = result[begin : begin + tokens_of(part)].astype(BF16)
         put(part, j, piece.reshape(part[1], part[3], LEV, width))
-        start += rows
-    done(places)
-
-
-MIDDLE = [[(0, 1), (2, 1)], [(1, 1)]]
-SIDES = [[(0, 0), (1, 0), (2, 0)], [(0, 2), (1, 2), (2, 2)]]
+
+
+MIDDLE = [(0, 1), (1, 1), (2, 1)]
+SIDES = [(0, 0), (0, 2), (2, 0), (2, 2), (1, 0), (1, 2)]
 
 
 def side_entries():
-    return [entry for places in SIDES for entry in entries_of(places)]
+    return entries_of(SIDES)
 
 
 def middle_kernel(
@@ -423,7 +417,7 @@
     lift_ref,
     *refs,
 ):
-    *weights, out_ref, rest_ref, held_ref, sem = refs
+    *weights, out_ref, rest_ref = refs
     sums = scattered(recv_ref, first_ref, table_ref, lift_ref, plan, back_ref.shape[1])
 
     def sum_of(tile, number):
@@ -431,34 +425,12 @@
         return sums[tile][start : start + padded(tokens_of(plan[tile][number]))]
 
     rest_ref[...] = below(*[sum_of(*entry) for entry in side_entries()])
-    left, wide = plan[4][4][2:]
 
     def put(part, _, piece):
-        held_ref[part[0] : part[0] + part[1]] = piece
-
-    copies = []
-
-    def done(places):
-        for i, _ in places:
-            top, high = plan[4][3 * i + 1][:2]
-            copies.append(
-                pltpu.make_async_copy(
-                    held_ref.at[top : top + high],
-                    out_ref.at[top : top + high, left : left + wide],
-                    sem.at[i],
-                )
-            )
-            copies[-1].start()
+        out_ref[part[0] : part[0] + part[1]] = piece
 
     borders = (back_ref, north_ref, south_ref, None, None)
-    alternate(
-        *[
-            worked(plan, places, sum_of, borders, weights, scalars_ref, put, done)
-            for places in MIDDLE
-        ]
-    )
-    for copy in copies:
-        copy.wait()
+    worked(plan, MIDDLE, sum_of, borders, weights, scalars_ref, put)
 
 
 def side_kernel(
@@ -472,7 +444,10 @@
     back_ref,
     *refs,
 ):
-    *weights, _, out_ref, held_ref, sem = refs
+    *weights, middle_ref, out_ref, held_ref, sem = refs
+    left, wide = plan[4][4][2:]
+    copies = [pltpu.make_async_copy(middle_ref, out_ref.at[:, left : left + wide], sem.at[2])]
+    copies[0].start()
     spans, start = {}, 0
     for tile, number in side_entries():
         rows = padded(tokens_of(plan[tile][number]))
@@ -486,25 +461,14 @@
     def put(part, j, piece):
         held_ref[j // 2, part[0] : part[0] + part[1]] = piece
 
-    copies = []
-
-    def done(places):
-        j = places[0][1]
-        left, wide = plan[4][j][2:]
+    borders = (back_ref, north_ref, south_ref, west_ref, east_ref)
+    worked(plan, SIDES, sum_of, borders, weights, scalars_ref, put)
+    for n, number in enumerate((0, 2)):
+        left, wide = plan[4][number][2:]
         copies.append(
-            pltpu.make_async_copy(
-                held_ref.at[j // 2], out_ref.at[:, left : left + wide], sem.at[j // 2]
-            )
+            pltpu.make_async_copy(held_ref.at[n], out_ref.at[:, left : left + wide], sem.at[n])
         )
         copies[-1].start()
-
-    borders = (back_ref, north_ref, south_ref, west_ref, east_ref)
-    alternate(
-        *[
-            worked(plan, places, sum_of, borders, weights, scalars_ref, put, done)
-            for places in SIDES
-        ]
-    )
     for copy in copies:
         copy.wait()
 
@@ -562,13 +526,12 @@
     result = jax.ShapeDtypeStruct(background.shape, BF16)
     middle, rest = pl.pallas_call(
         functools.partial(middle_kernel, plan),
-        out_shape=[result, jax.ShapeDtypeStruct((rest, PAD), F32)],
+        out_shape=[
+            jax.ShapeDtypeStruct((lat_cells, lon_cells - WLON, LEV, width), BF16),
+            jax.ShapeDtypeStruct((rest, PAD), F32),
+        ],
         in_specs=[smem] + [vmem] * (7 + len(weights)),
-        out_specs=[anywhere, vmem],
-        scratch_shapes=[
-            pltpu.VMEM((lat_cells, lon_cells - WLON, LEV, width), BF16),
-            pltpu.SemaphoreType.DMA((3,)),
-        ],
+        out_specs=[vmem, vmem],
         compiler_params=params,
         cost_estimate=pl.CostEstimate(
             flops=4 * 10**9, bytes_accessed=4 * 10**6, transcendentals=10**6
@@ -589,13 +552,12 @@
     return pl.pallas_call(
         functools.partial(side_kernel, plan),
         out_shape=result,
-        in_specs=[smem] + [vmem] * (6 + len(weights)) + [anywhere],
+        in_specs=[smem] + [vmem] * (7 + len(weights)),
         out_specs=anywhere,
         scratch_shapes=[
             pltpu.VMEM((2, lat_cells, HLON, LEV, width), BF16),
-            pltpu.SemaphoreType.DMA((2,)),
+            pltpu.SemaphoreType.DMA((3,)),
         ],
-        input_output_aliases={7 + len(weights): 0},
         compiler_params=params,
         cost_estimate=pl.CostEstimate(
             flops=3 * 10**9, bytes_accessed=4 * 10**6, transcendentals=10**6

time: 28.7 us -> 27.7 us (0.965); the launches traced: 28.2 us -> 27.5 us
  Pallas kernels: 11.5 us -> 10.1 us
  waiting for transfers between devices: 3.1 us -> 3.89 us
    pallas_call x1, Pallas kernels: 5.05 us -> 3.82 us  [local(): pl.pallas_call(functools.partial(middle_kernel, plan), out_shape=[jax.Sha...]
    ppermute x4, waiting for transfers between devices: 3.1 us -> 3.88 us  [swapped(): got.append(lax.ppermute(mine, axis, pairs))]
  transfers between devices with their start and end apart: 5 -> 5, of which waited for: 1 -> 2; matrix products, arithmetic and copies ran while one was open for 3% -> 3% of each run, Pallas kernels for 18% -> 14%
where the time goes in v16:
time: 27.7 us; the launch traced here: 27.5 us
  starting transfers between devices  11.5 us (42%)
  Pallas kernels  10.1 us (36%)
  waiting for transfers between devices  3.89 us (14%)
  local copies, waits for them, and re-layouts  1.16 us (4%)
  other arithmetic  0.66 us (2%)
    all_to_all x1, starting transfers between devices, local(): lax.all_to_all(sent, ('lon', 'lat'), split_axis=0, concat_axis=0, tiled=T...  7.3 us
    pallas_call x1, Pallas kernels, local(): pl.pallas_call(functools.partial(side_kernel, plan), out_shape=result, in...  4.51 us
    ppermute x4, starting transfers between devices, swapped(): got.append(lax.ppermute(mine, axis, pairs))  4.15 us
    ppermute x4, waiting for transfers between devices, swapped(): got.append(lax.ppermute(mine, axis, pairs))  3.88 us
    pallas_call x1, Pallas kernels, local(): pl.pallas_call(functools.partial(middle_kernel, plan), out_shape=[jax.Sha...  3.82 us
    pallas_call x1, Pallas kernels, packed(): pl.pallas_call(pack_kernel, out_shape=[jax.ShapeDtypeStruct(shape, BF16),...  1.74 us
    unnamed x24, local copies, waits for them, and re-layouts  0.71 us
  transfers between devices with their start and end apart: 5, of which 2 were waited for; matrix products, arithmetic and copies ran while one was open for 3% of the time, Pallas kernels for 14%

profile of v16, /device:TPU:0, one launch (start us, length us, event | category | flops | bytes accessed | tf_op | source)
XLA Modules:
  0.0 27.5 jit_solution(8460453544203010440)
XLA Ops:
  0.0 1.7 %shard_map.136 = (bf16[8,4,10,2,128]{4,3,2,1,0:T(2,128)(2,1)}, bf16[3,24,2,192]{3,2,1,0:T(2,128)(2,1)}, bf16[3,24,2,192]{3,2,1,0:T(2,128)(2,1)}) custom-call(bf16[8,4,2,128]{3,2,1,0:T(2,128)(2,1)} %values_ref.1, s32[8,8]{1,0:T(8,128)} %bitcast.32, s32[8,8]{1,0:T(8,128)} %bitcast.33, s32[4,8]{1,0:T(4,128)} %bitcast.34, bf16[12,24,2,192]{3,2,1,0:T(2,128)(2,1)} %back_ref.5), custom_call_target="tpu_custom_call" | custom-call | flops 20000000000 | bytes 1000000 | tf_op jit(solution)/shard_map/pallas_call | solution.py:184
  1.7 0.0 copy-start.7
  1.8 0.0 copy-start.8
  1.8 0.0 copy-start
  1.8 0.0 copy-start.10
  1.8 7.3 %all-to-all-start = ((bf16[32,10,2,128]{3,2,1,0:T(2,128)(2,1)}), bf16[32,10,2,128]{3,2,1,0:T(2,128)(2,1)S(1)}, u32[]{:S(2)}, u32[]{:S(2)}) async-start(bf16[32,10,2,128]{3,2,1,0:T(2,128)(2,1)} %bitcast.25), calls=%async_computation | async-start | bytes 327680 | tf_op jit(solution)/shard_map/all_to_all | solution.py:498
  9.1 0.0 copy-done.7
  9.1 0.0 copy-done.8
  9.2 0.0 copy-start.6
  9.2 1.8 %collective-permute-start.1 = (bf16[3,24,2,192]{3,2,1,0:T(2,128)(2,1)S(1)}, bf16[3,24,2,192]{3,2,1,0:T(2,128)(2,1)S(1)}, u32[]{:S(2)}, u32[]{:S(2)}) collective-permute-start(bf16[3,24,2,192]{3,2,1,0:T(2,128)(2,1)S(1)} %bitcast.29), channel_id=1, source_target_pairs={{0,1},{1,0},{2,3},{3,2},{4,5},{5,4},{6,7},{7,6},{8,9},{9,8},{10,11... | collective-permute-start | bytes 165896 | tf_op jit(solution)/shard_map/ppermute | solution.py:39
  11.0 0.7 %collective-permute-start = (bf16[3,24,2,192]{3,2,1,0:T(2,128)(2,1)S(1)}, bf16[3,24,2,192]{3,2,1,0:T(2,128)(2,1)S(1)}, u32[]{:S(2)}, u32[]{:S(2)}) collective-permute-start(bf16[3,24,2,192]{3,2,1,0:T(2,128)(2,1)S(1)} %bitcast.27), channel_id=1, source_target_pairs={{1,2},{2,1},{5,6},{6,5},{9,10},{10,9},{13,14},{14,13},{17,18},{18,... | collective-permute-start | bytes 165896 | tf_op jit(solution)/shard_map/ppermute | solution.py:39
  11.7 0.0 copy-done
  11.7 0.0 copy-start.9
  11.7 0.1 fusion
  11.8 0.1 add_convert_fusion.scalars_ref
  11.9 0.0 copy-done.10
  11.9 0.0 copy-start.11
  11.9 0.6 %copy-done.11 = bf16[192]{0:T(256)(128)(2,1)S(1)} copy-done((bf16[192]{0:T(256)(128)(2,1)S(1)}, bf16[192]{0:T(256)(128)(2,1)}, u32[]{:S(2)}) %copy-start.11) | copy-done | bytes 408
  12.6 0.0 copy-done.9
  12.6 0.1 copy.15.first_ref
  12.7 0.0 copy-done.6
  12.7 0.0 copy-start.3
  12.7 0.0 copy-start.4
  12.7 0.2 copy.16.refs_5_
  12.9 3.1 %collective-permute-done.1 = bf16[3,24,2,192]{3,2,1,0:T(2,128)(2,1)S(1)} collective-permute-done((bf16[3,24,2,192]{3,2,1,0:T(2,128)(2,1)S(1)}, bf16[3,24,2,192]{3,2,1,0:T(2,128)(2,1)S(1)}, u32[]{:S(2)}, u32[]{:S(2)}) %collective-permute-start.1) | collective-permute-done | bytes 55328 | tf_op jit(solution)/shard_map/ppermute | solution.py:39
  16.0 0.0 collective-permute-done
  16.0 0.0 copy-start.1
  16.0 0.1 fusion.1
  16.1 0.0 copy-start.2
  16.1 0.0 copy-start.5
  16.1 0.4 %broadcast_select_fusion.2 = (bf16[18,6,2,192]{3,2,1,0:T(2,128)(2,1)S(1)}, bf16[18,6,2,192]{3,2,1,0:T(2,128)(2,1)S(1)}) fusion(pred[]{:T(512)S(6)} %eq.22, bf16[3,6,2,192]{3,2,1,0:T(2,128)(2,1)S(1)} %get-tuple-element.41, bf16[12,6,2,192]{3,2,1,0:T(2,128)(2,1)S(1)} %get-tuple-element.28, bf16[3,6,2,192]{3,2,1,0:T(2,128)(2,1)S(1)} %get-tuple-element.38, ...), kind=kLoop, calls=%fused_computation.2 | loop fusion | flops 248832 | bytes 331777 | tf_op jit(solution)/shard_map/jit(_where)/select_n | solution.py:33
  16.5 1.2 %collective-permute-start.3 = (bf16[18,6,2,192]{3,2,1,0:T(2,128)(2,1)S(1)}, bf16[18,6,2,192]{3,2,1,0:T(2,128)(2,1)S(1)}, u32[]{:S(2)}, u32[]{:S(2)}) collective-permute-start(bf16[18,6,2,192]{3,2,1,0:T(2,128)(2,1)S(1)} %get-tuple-element.31), channel_id=1, source_target_pairs={{4,8},{8,4},{12,16},{16,12},{20,24},{24,20},{28,0},{0,28},{5,9},{9... | collective-permute-start | bytes 248840 | tf_op jit(solution)/shard_map/ppermute | solution.py:39
  17.7 0.4 %collective-permute-start.2 = (bf16[18,6,2,192]{3,2,1,0:T(2,128)(2,1)S(1)}, bf16[18,6,2,192]{3,2,1,0:T(2,128)(2,1)S(1)}, u32[]{:S(2)}, u32[]{:S(2)}) collective-permute-start(bf16[18,6,2,192]{3,2,1,0:T(2,128)(2,1)S(1)} %get-tuple-element.32), channel_id=1, source_target_pairs={{0,4},{4,0},{8,12},{12,8},{16,20},{20,16},{24,28},{28,24},{1,5},{5... | collective-permute-start | bytes 248840 | tf_op jit(solution)/shard_map/ppermute | solution.py:39
  18.1 0.0 all-to-all-done.recv_ref
  18.1 0.0 copy-done.3
  18.1 0.0 copy-done.4
  18.1 0.0 copy-done.1
  18.2 0.0 copy-done.2
  18.2 0.0 copy-done.5
  18.2 3.8 %shard_map.137 = (bf16[12,12,2,192]{3,2,1,0:T(2,128)(2,1)S(1)}, f32[928,256]{1,0:T(8,128)S(1)}) custom-call(s32[3]{0:T(128)S(1)} %add_convert_fusion.scalars_ref, bf16[32,10,2,128]{3,2,1,0:T(2,128)(2,1)S(1)} %all-to-all-done.recv_ref, bf16[3,24,2,192]{3,2,1,0:T(2,128)(2,1)S(1)} %bitcast.23, bf16[3,24,2,192]{3,2,1,0:T(2,128)(2,1)S(1)} %bitcast.20, ...), custom_call_target="tpu_custom_call" | custom-call | flops 4000000000 | bytes 4000000 | tf_op jit(solution)/shard_map/pallas_call | solution.py:527
  22.0 0.8 %collective-permute-done.3 = bf16[18,6,2,192]{3,2,1,0:T(2,128)(2,1)S(1)} collective-permute-done((bf16[18,6,2,192]{3,2,1,0:T(2,128)(2,1)S(1)}, bf16[18,6,2,192]{3,2,1,0:T(2,128)(2,1)S(1)}, u32[]{:S(2)}, u32[]{:S(2)}) %collective-permute-start.3) | collective-permute-done | bytes 82976 | tf_op jit(solution)/shard_map/ppermute | solution.py:39
  22.8 0.0 collective-permute-done.2
  22.8 0.2 broadcast_select_fusion
  23.0 4.5 %shard_map.138 = bf16[12,24,2,192]{3,2,1,0:T(2,128)(2,1)} custom-call(s32[3]{0:T(128)S(1)} %add_convert_fusion.scalars_ref, f32[928,256]{1,0:T(8,128)S(1)} %get-tuple-element.23.rest_ref, bf16[3,24,2,192]{3,2,1,0:T(2,128)(2,1)S(1)} %bitcast.24, bf16[3,24,2,192]{3,2,1,0:T(2,128)(2,1)S(1)} %bitcast.21, bf16[18,6,2,192]{3,2,1,0:T(2,128)(2,1)S(1)} %get-tuple-element.30.west_ref, ...), custom_call_target="tpu_custom_call" | custom-call | flops 3000000000 | bytes 4000000 | tf_op jit(solution)/shard_map/pallas_call | solution.py:552
  (4 shorter events, 0.0 us)
Async XLA Ops:
  1.7 7.4 %copy-start.7 = (bf16[3,24,2,192]{3,2,1,0:T(2,128)(2,1)S(1)}, bf16[3,24,2,192]{3,2,1,0:T(2,128)(2,1)}, u32[]{:S(2)}) copy-start(bf16[3,24,2,192]{3,2,1,0:T(2,128)(2,1)} %get-tuple-element.17) | copy-start | bytes 165892
  1.8 7.4 %copy-start.8 = (bf16[3,24,2,192]{3,2,1,0:T(2,128)(2,1)S(1)}, bf16[3,24,2,192]{3,2,1,0:T(2,128)(2,1)}, u32[]{:S(2)}) copy-start(bf16[3,24,2,192]{3,2,1,0:T(2,128)(2,1)} %get-tuple-element.18) | copy-start | bytes 165892
  1.8 9.9 %copy-start = (bf16[12,24,2,192]{3,2,1,0:T(2,128)(2,1)S(1)}, bf16[12,24,2,192]{3,2,1,0:T(2,128)(2,1)}, u32[]{:S(2)}) copy-start(bf16[12,24,2,192]{3,2,1,0:T(2,128)(2,1)} %back_ref.5) | copy-start | bytes 663556
  1.8 10.1 %copy-start.10 = (bf16[192]{0:T(256)(128)(2,1)S(1)}, bf16[192]{0:T(256)(128)(2,1)}, u32[]{:S(2)}) copy-start(bf16[192]{0:T(256)(128)(2,1)} %param.22) | copy-start | bytes 1156
  1.8 16.3 %all-to-all-start = ((bf16[32,10,2,128]{3,2,1,0:T(2,128)(2,1)}), bf16[32,10,2,128]{3,2,1,0:T(2,128)(2,1)S(1)}, u32[]{:S(2)}, u32[]{:S(2)}) async-start(bf16[32,10,2,128]{3,2,1,0:T(2,128)(2,1)} %bitcast.25), calls=%async_computation | async-start | bytes 327680 | tf_op jit(solution)/shard_map/all_to_all | solution.py:498
  9.2 3.5 %copy-start.6 = (bf16[768,192]{0,1:T(8,128)(2,1)S(1)}, bf16[768,192]{0,1:T(8,128)(2,1)}, u32[]{:S(2)}) copy-start(bf16[768,192]{0,1:T(8,128)(2,1)} %param.27) | copy-start | bytes 884740
  9.2 6.8 %collective-permute-start.1 = (bf16[3,24,2,192]{3,2,1,0:T(2,128)(2,1)S(1)}, bf16[3,24,2,192]{3,2,1,0:T(2,128)(2,1)S(1)}, u32[]{:S(2)}, u32[]{:S(2)}) collective-permute-start(bf16[3,24,2,192]{3,2,1,0:T(2,128)(2,1)S(1)} %bitcast.29), channel_id=1, source_target_pairs={{0,1},{1,0},{2,3},{3,2},{4,5},{5,4},{6,7},{7,6},{8,9},{9,8},{10,11... | collective-permute-start | bytes 165896 | tf_op jit(solution)/shard_map/ppermute | solution.py:39
  11.0 5.0 %collective-permute-start = (bf16[3,24,2,192]{3,2,1,0:T(2,128)(2,1)S(1)}, bf16[3,24,2,192]{3,2,1,0:T(2,128)(2,1)S(1)}, u32[]{:S(2)}, u32[]{:S(2)}) collective-permute-start(bf16[3,24,2,192]{3,2,1,0:T(2,128)(2,1)S(1)} %bitcast.27), channel_id=1, source_target_pairs={{1,2},{2,1},{5,6},{6,5},{9,10},{10,9},{13,14},{14,13},{17,18},{18,... | collective-permute-start | bytes 165896 | tf_op jit(solution)/shard_map/ppermute | solution.py:39
  11.7 0.9 %copy-start.9 = (bf16[128,192]{0,1:T(8,128)(2,1)S(1)}, bf16[128,192]{0,1:T(8,128)(2,1)}, u32[]{:S(2)}) copy-start(bf16[128,192]{0,1:T(8,128)(2,1)} %param.19) | copy-start | bytes 147460
  11.9 0.7 %copy-start.11 = (bf16[192]{0:T(256)(128)(2,1)S(1)}, bf16[192]{0:T(256)(128)(2,1)}, u32[]{:S(2)}) copy-start(bf16[192]{0:T(256)(128)(2,1)} %param.25) | copy-start | bytes 1156
  12.7 5.5 %copy-start.3 = (bf16[192,384]{1,0:T(8,128)(2,1)S(1)}, bf16[192,384]{1,0:T(8,128)(2,1)}, u32[]{:S(2)}) copy-start(bf16[192,384]{1,0:T(8,128)(2,1)} %lift_ref.1) | copy-start | bytes 442372
  12.7 5.5 %copy-start.4 = (bf16[192,192]{1,0:T(8,128)(2,1)S(1)}, bf16[192,192]{1,0:T(8,128)(2,1)}, u32[]{:S(2)}) copy-start(bf16[192,192]{1,0:T(8,128)(2,1)} %refs_2_.3) | copy-start | bytes 221188
  16.0 2.2 %copy-start.1 = (bf16[192,768]{1,0:T(8,128)(2,1)S(1)}, bf16[192,768]{1,0:T(8,128)(2,1)}, u32[]{:S(2)}) copy-start(bf16[192,768]{1,0:T(8,128)(2,1)} %refs_4_.3) | copy-start | bytes 884740
  16.1 2.1 %copy-start.2 = (bf16[192,576]{1,0:T(8,128)(2,1)S(1)}, bf16[192,576]{1,0:T(8,128)(2,1)}, u32[]{:S(2)}) copy-start(bf16[192,576]{1,0:T(8,128)(2,1)} %refs_1_.3) | copy-start | bytes 663556
  16.1 2.1 %copy-start.5 = (bf16[8,192]{1,0:T(8,128)(2,1)S(1)}, bf16[8,192]{1,0:T(8,128)(2,1)}, u32[]{:S(2)}) copy-start(bf16[8,192]{1,0:T(8,128)(2,1)} %table_ref.1) | copy-start | bytes 9220
  16.5 6.3 %collective-permute-start.3 = (bf16[18,6,2,192]{3,2,1,0:T(2,128)(2,1)S(1)}, bf16[18,6,2,192]{3,2,1,0:T(2,128)(2,1)S(1)}, u32[]{:S(2)}, u32[]{:S(2)}) collective-permute-start(bf16[18,6,2,192]{3,2,1,0:T(2,128)(2,1)S(1)} %get-tuple-element.31), channel_id=1, source_target_pairs={{4,8},{8,4},{12,16},{16,12},{20,24},{24,20},{28,0},{0,28},{5,9},{9... | collective-permute-start | bytes 248840 | tf_op jit(solution)/shard_map/ppermute | solution.py:39
  17.7 5.1 %collective-permute-start.2 = (bf16[18,6,2,192]{3,2,1,0:T(2,128)(2,1)S(1)}, bf16[18,6,2,192]{3,2,1,0:T(2,128)(2,1)S(1)}, u32[]{:S(2)}, u32[]{:S(2)}) collective-permute-start(bf16[18,6,2,192]{3,2,1,0:T(2,128)(2,1)S(1)} %get-tuple-element.32), channel_id=1, source_target_pairs={{0,4},{4,0},{8,12},{12,8},{16,20},{20,16},{24,28},{28,24},{1,5},{5... | collective-permute-start | bytes 248840 | tf_op jit(solution)/shard_map/ppermute | solution.py:39

commit v17 on v16

--- a/solution.py
+++ b/solution.py
@@ -26,13 +26,12 @@
 COLS = ROWS + len(AROUND)
 
 
-def swapped(up, down, axis, wraps):
+def swapped(first, second, axis, wraps):
     count = lax.axis_size(axis)
-    even = lax.axis_index(axis) % 2 == 0
     got = []
-    for first, mine in ((0, jnp.where(even, down, up)), (1, jnp.where(even, up, down))):
+    for begin, mine in enumerate((first, second)):
         pairs = []
-        for low in range(first, count, 2):
+        for low in range(begin, count, 2):
             high = (low + 1) % count
             if high > low or wraps:
                 pairs += [(low, high), (high, low)]
@@ -40,7 +39,7 @@
     return got
 
 
-def before_and_after(got, axis):
+def in_order(got, axis):
     even = lax.axis_index(axis) % 2 == 0
     return jnp.where(even, got[1], got[0]), jnp.where(even, got[0], got[1])
 
@@ -473,6 +472,42 @@
         copy.wait()
 
 
+def join_kernel(even_ref, one_ref, two_ref, back_ref, north_ref, south_ref, first_ref, second_ref):
+    lat_cells, lon_cells = back_ref.shape[:2]
+
+    def strips(before, after):
+        north_ref[...] = before[...]
+        south_ref[...] = after[...]
+
+    def sides(left, right):
+        for ref, low in ((left, 0), (right, lon_cells - HLON)):
+            ref[:HLAT] = north_ref[:, low : low + HLON]
+            ref[HLAT : HLAT + lat_cells] = back_ref[:, low : low + HLON]
+            ref[HLAT + lat_cells :] = south_ref[:, low : low + HLON]
+
+    pl.when(even_ref[0] == 1)(lambda: strips(two_ref, one_ref))
+    pl.when(even_ref[0] == 0)(lambda: strips(one_ref, two_ref))
+    pl.when(even_ref[1] == 1)(lambda: sides(second_ref, first_ref))
+    pl.when(even_ref[1] == 0)(lambda: sides(first_ref, second_ref))
+
+
+def joined(even, got, background):
+    lat_cells, lon_cells, levels, width = background.shape
+    across = jax.ShapeDtypeStruct((HLAT, lon_cells, levels, width), BF16)
+    along = jax.ShapeDtypeStruct((lat_cells + WLAT, HLON, levels, width), BF16)
+    vmem = pl.BlockSpec(memory_space=pltpu.VMEM)
+    return pl.pallas_call(
+        join_kernel,
+        out_shape=[across, across, along, along],
+        in_specs=[pl.BlockSpec(memory_space=pltpu.SMEM), vmem, vmem, vmem],
+        out_specs=[vmem] * 4,
+        compiler_params=pltpu.CompilerParams(vmem_limit_bytes=LIMIT),
+        cost_estimate=pl.CostEstimate(
+            flops=10**12, bytes_accessed=10**6, transcendentals=0
+        ),
+    )(even, *got, background)
+
+
 def local(
     record_values,
     record_cell,
@@ -495,17 +530,14 @@
     sent, up, down = packed(
         record_values, record_cell, record_instrument, block_counts, background
     )
+    even = [lax.axis_index(axis) % 2 == 0 for axis in ("lat", "lon")]
+    got = swapped(jnp.where(even[0], down, up), jnp.where(even[0], up, down), "lat", wraps=False)
     received = lax.all_to_all(sent, ("lon", "lat"), split_axis=0, concat_axis=0, tiled=True)
-    north, south = before_and_after(swapped(up, down, "lat", wraps=False), "lat")
-
     later, input_weight, down_weight, _ = lax.optimization_barrier(
         (background, input_weight, down_weight, up)
     )
-
-    def columns(low, end):
-        return jnp.concatenate([north[:, low:end], later[:, low:end], south[:, low:end]], axis=0)
-
-    got = swapped(columns(0, HLON), columns(lon_cells - HLON, lon_cells), "lon", wraps=True)
+    north, south, *mine = joined(jnp.stack(even).astype(jnp.int32), got, later)
+    got = swapped(*mine, "lon", wraps=True)
 
     lat = lax.axis_index("lat")
     scalars = jnp.stack([lat == 0, lat < 0, lat == tiles_lat - 1]).astype(jnp.int32)
@@ -548,7 +580,7 @@
         *weights,
     )
     rest, *got = lax.optimization_barrier((rest, *got))
-    west, east = before_and_after(got, "lon")
+    west, east = in_order(got, "lon")
     return pl.pallas_call(
         functools.partial(side_kernel, plan),
         out_shape=result,

time: 27.7 us -> 30 us (1.083)
  starting transfers between devices: 11.5 us -> 15.3 us
  waiting for transfers between devices: 3.89 us -> 1.12 us
  Pallas kernels: 10.1 us -> 11.1 us
  local copies, waits for them, and re-layouts: 1.16 us -> 1.56 us
  other arithmetic: 0.66 us -> 0.35 us
    ppermute x4, starting transfers between devices: 4.15 us -> 7.84 us  [swapped(): got.append(lax.ppermute(mine, axis, pairs))]
    ppermute x4, waiting for transfers between devices: 3.88 us -> 1.12 us  [swapped(): got.append(lax.ppermute(mine, axis, pairs))]
    pallas_call x0 -> x1, Pallas kernels: none -> 0.69 us  [joined(): pl.pallas_call(join_kernel, out_shape=[across, across, along, along], in_...]
    unnamed x24, local copies, waits for them, and re-layouts: 0.71 us -> 1.28 us
    select_n x4 -> x2, other arithmetic: 0.58 us -> 0.2 us  [the longest x1 0.18 us: in_order(): return (jnp.where(even, got[1], got[0]), jnp.where(even, got[0], got[1]))]
    pallas_call x1, Pallas kernels: 3.82 us -> 4.2 us  [local(): pl.pallas_call(functools.partial(middle_kernel, plan), out_shape=[jax.Sha...]
  transfers between devices with their start and end apart: 5 -> 5, of which waited for: 2 -> 1; matrix products, arithmetic and copies ran while one was open for 3% -> 2% of each run, Pallas kernels for 14% -> 16%
where the time goes in v17:
time: 30 us; the launch traced here: 29.7 us
  starting transfers between devices  15.3 us (51%)
  Pallas kernels  11.1 us (37%)
  local copies, waits for them, and re-layouts  1.56 us (5%)
  waiting for transfers between devices  1.12 us (4%)
  other arithmetic  0.35 us (1%)
    ppermute x4, starting transfers between devices, swapped(): got.append(lax.ppermute(mine, axis, pairs))  7.84 us
    all_to_all x1, starting transfers between devices, local(): lax.all_to_all(sent, ('lon', 'lat'), split_axis=0, concat_axis=0, tiled=T...  7.42 us
    pallas_call x1, Pallas kernels, local(): pl.pallas_call(functools.partial(side_kernel, plan), out_shape=result, in...  4.5 us
    pallas_call x1, Pallas kernels, local(): pl.pallas_call(functools.partial(middle_kernel, plan), out_shape=[jax.Sha...  4.2 us
    pallas_call x1, Pallas kernels, packed(): pl.pallas_call(pack_kernel, out_shape=[jax.ShapeDtypeStruct(shape, BF16),...  1.74 us
    unnamed x24, local copies, waits for them, and re-layouts  1.28 us
    ppermute x4, waiting for transfers between devices, swapped(): got.append(lax.ppermute(mine, axis, pairs))  1.12 us
    pallas_call x1, Pallas kernels, joined(): pl.pallas_call(join_kernel, out_shape=[across, across, along, along], in_...  0.69 us
  transfers between devices with their start and end apart: 5, of which 1 were waited for; matrix products, arithmetic and copies ran while one was open for 2% of the time, Pallas kernels for 16%

profile of v17, /device:TPU:0, one launch (start us, length us, event | category | flops | bytes accessed | tf_op | source)
XLA Modules:
  0.0 29.7 jit_solution(12092559163111365657)
XLA Ops:
  0.0 1.7 %shard_map.136 = (bf16[8,4,10,2,128]{4,3,2,1,0:T(2,128)(2,1)}, bf16[3,24,2,192]{3,2,1,0:T(2,128)(2,1)}, bf16[3,24,2,192]{3,2,1,0:T(2,128)(2,1)}) custom-call(bf16[8,4,2,128]{3,2,1,0:T(2,128)(2,1)} %values_ref.1, s32[8,8]{1,0:T(8,128)} %bitcast.22, s32[8,8]{1,0:T(8,128)} %bitcast.23, s32[4,8]{1,0:T(4,128)} %bitcast.24, bf16[12,24,2,192]{3,2,1,0:T(2,128)(2,1)} %back_ref.6), custom_call_target="tpu_custom_call" | custom-call | flops 20000000000 | bytes 1000000 | tf_op jit(solution)/shard_map/pallas_call | solution.py:183
  1.8 0.0 copy-start.7
  1.8 0.0 copy-start.8
  1.8 7.4 %all-to-all-start = ((bf16[32,10,2,128]{3,2,1,0:T(2,128)(2,1)}), bf16[32,10,2,128]{3,2,1,0:T(2,128)(2,1)}, u32[]{:S(2)}, u32[]{:S(2)}) async-start(bf16[32,10,2,128]{3,2,1,0:T(2,128)(2,1)} %bitcast.17), calls=%async_computation | async-start | bytes 327680 | tf_op jit(solution)/shard_map/all_to_all | solution.py:535
  9.2 0.0 copy-start.6
  9.2 0.0 copy-done.7
  9.2 0.0 copy-done.8
  9.3 0.0 copy-start.9
  9.3 0.8 %collective-permute-start.1 = (bf16[3,24,2,192]{3,2,1,0:T(2,128)(2,1)S(1)}, bf16[3,24,2,192]{3,2,1,0:T(2,128)(2,1)S(1)}, u32[]{:S(2)}, u32[]{:S(2)}) collective-permute-start(bf16[3,24,2,192]{3,2,1,0:T(2,128)(2,1)S(1)} %bitcast.19), channel_id=1, source_target_pairs={{1,2},{2,1},{5,6},{6,5},{9,10},{10,9},{13,14},{14,13},{17,18},{18,... | collective-permute-start | bytes 165896 | tf_op jit(solution)/shard_map/ppermute | solution.py:38
  10.1 4.5 %collective-permute-start = (bf16[3,24,2,192]{3,2,1,0:T(2,128)(2,1)S(1)}, bf16[3,24,2,192]{3,2,1,0:T(2,128)(2,1)S(1)}, u32[]{:S(2)}, u32[]{:S(2)}) collective-permute-start(bf16[3,24,2,192]{3,2,1,0:T(2,128)(2,1)S(1)} %bitcast.18), channel_id=1, source_target_pairs={{0,1},{1,0},{2,3},{3,2},{4,5},{5,4},{6,7},{7,6},{8,9},{9,8},{10,11... | collective-permute-start | bytes 165896 | tf_op jit(solution)/shard_map/ppermute | solution.py:38
  14.6 0.1 add_convert_fusion.1.even_ref
  14.6 0.0 copy-start.10
  14.6 0.1 add_convert_fusion.scalars_ref
  14.7 0.6 %copy-done.10 = bf16[192]{0:T(256)(128)(2,1)S(1)} copy-done((bf16[192]{0:T(256)(128)(2,1)S(1)}, bf16[192]{0:T(256)(128)(2,1)}, u32[]{:S(2)}) %copy-start.10) | copy-done | bytes 408
  15.3 0.0 copy-start.11
  15.3 0.6 %copy-done.11 = bf16[192]{0:T(256)(128)(2,1)S(1)} copy-done((bf16[192]{0:T(256)(128)(2,1)S(1)}, bf16[192]{0:T(256)(128)(2,1)}, u32[]{:S(2)}) %copy-start.11) | copy-done | bytes 408
  16.0 0.0 copy-done.9
  16.0 0.1 copy.15.first_ref
  16.1 0.0 copy-done.6
  16.1 0.0 copy-start
  16.1 0.2 copy.16.refs_5_
  16.3 0.0 collective-permute-done.1.two_ref
  16.3 1.1 %collective-permute-done.one_ref = bf16[3,24,2,192]{3,2,1,0:T(2,128)(2,1)S(1)} collective-permute-done((bf16[3,24,2,192]{3,2,1,0:T(2,128)(2,1)S(1)}, bf16[3,24,2,192]{3,2,1,0:T(2,128)(2,1)S(1)}, u32[]{:S(2)}, u32[]{:S(2)}) %collective-permute-start) | collective-permute-done | bytes 55328 | tf_op jit(solution)/shard_map/ppermute | solution.py:38
  17.4 0.0 copy-done
  17.4 0.0 copy-start.1
  17.4 0.0 copy-start.2
  17.4 0.0 copy-start.3
  17.4 0.0 copy-start.4
  17.4 0.7 %shard_map.137 = (bf16[3,24,2,192]{3,2,1,0:T(2,128)(2,1)S(1)}, bf16[3,24,2,192]{3,2,1,0:T(2,128)(2,1)S(1)}, bf16[18,6,2,192]{3,2,1,0:T(2,128)(2,1)S(1)}, bf16[18,6,2,192]{3,2,1,0:T(2,128)(2,1)S(1)}) custom-call(s32[2]{0:T(128)S(1)} %add_convert_fusion.1.even_ref, bf16[3,24,2,192]{3,2,1,0:T(2,128)(2,1)S(1)} %collective-permute-done.one_ref, ...), custom_call_target="tpu_custom_call" | custom-call | flops 999999995904 | bytes 1000000 | tf_op jit(solution)/shard_map/pallas_call | solution.py:499
  18.1 0.0 copy-start.5
  18.1 0.1 collective-permute-start.2
  18.2 2.5 %collective-permute-start.3 = (bf16[18,6,2,192]{3,2,1,0:T(2,128)(2,1)S(1)}, bf16[18,6,2,192]{3,2,1,0:T(2,128)(2,1)S(1)}, u32[]{:S(2)}, u32[]{:S(2)}) collective-permute-start(bf16[18,6,2,192]{3,2,1,0:T(2,128)(2,1)S(1)} %get-tuple-element.30), channel_id=1, source_target_pairs={{4,8},{8,4},{12,16},{16,12},{20,24},{24,20},{28,0},{0,28},{5,9},{9... | collective-permute-start | bytes 248840 | tf_op jit(solution)/shard_map/ppermute | solution.py:38
  20.7 0.0 all-to-all-done.recv_ref
  20.7 0.0 copy-done.1
  20.7 0.0 copy-done.2
  20.7 0.0 copy-done.3
  20.7 0.0 copy-done.4
  20.7 0.0 copy-done.5
  20.7 4.2 %shard_map.138 = (bf16[12,12,2,192]{3,2,1,0:T(2,128)(2,1)S(1)}, f32[928,256]{1,0:T(8,128)S(1)}) custom-call(s32[3]{0:T(128)S(1)} %add_convert_fusion.scalars_ref, bf16[32,10,2,128]{3,2,1,0:T(2,128)(2,1)} %all-to-all-done.recv_ref, bf16[3,24,2,192]{3,2,1,0:T(2,128)(2,1)S(1)} %get-tuple-element.24.north_ref, ...), custom_call_target="tpu_custom_call" | custom-call | flops 4000000000 | bytes 4000000 | tf_op jit(solution)/shard_map/pallas_call | solution.py:559
  25.0 0.0 collective-permute-done.2
  25.0 0.0 collective-permute-done.3
  25.0 0.2 broadcast_select_fusion
  25.2 4.5 %shard_map.139 = bf16[12,24,2,192]{3,2,1,0:T(2,128)(2,1)} custom-call(s32[3]{0:T(128)S(1)} %add_convert_fusion.scalars_ref, f32[928,256]{1,0:T(8,128)S(1)} %get-tuple-element.31.rest_ref, bf16[3,24,2,192]{3,2,1,0:T(2,128)(2,1)S(1)} %get-tuple-element.24.north_ref, bf16[3,24,2,192]{3,2,1,0:T(2,128)(2,1)S(1)} %get-tuple-element.25.south_ref, ...), custom_call_target="tpu_custom_call" | custom-call | flops 3000000000 | bytes 4000000 | tf_op jit(solution)/shard_map/pallas_call | solution.py:584
  (3 shorter events, 0.0 us)
Async XLA Ops:
  1.8 7.5 %copy-start.7 = (bf16[3,24,2,192]{3,2,1,0:T(2,128)(2,1)S(1)}, bf16[3,24,2,192]{3,2,1,0:T(2,128)(2,1)}, u32[]{:S(2)}) copy-start(bf16[3,24,2,192]{3,2,1,0:T(2,128)(2,1)} %get-tuple-element.22) | copy-start | bytes 165892
  1.8 7.5 %copy-start.8 = (bf16[3,24,2,192]{3,2,1,0:T(2,128)(2,1)S(1)}, bf16[3,24,2,192]{3,2,1,0:T(2,128)(2,1)}, u32[]{:S(2)}) copy-start(bf16[3,24,2,192]{3,2,1,0:T(2,128)(2,1)} %get-tuple-element.21) | copy-start | bytes 165892
  1.8 18.9 %all-to-all-start = ((bf16[32,10,2,128]{3,2,1,0:T(2,128)(2,1)}), bf16[32,10,2,128]{3,2,1,0:T(2,128)(2,1)}, u32[]{:S(2)}, u32[]{:S(2)}) async-start(bf16[32,10,2,128]{3,2,1,0:T(2,128)(2,1)} %bitcast.17), calls=%async_computation | async-start | bytes 327680 | tf_op jit(solution)/shard_map/all_to_all | solution.py:535
  9.2 6.9 %copy-start.6 = (bf16[768,192]{0,1:T(8,128)(2,1)S(1)}, bf16[768,192]{0,1:T(8,128)(2,1)}, u32[]{:S(2)}) copy-start(bf16[768,192]{0,1:T(8,128)(2,1)} %param.27) | copy-start | bytes 884740
  9.3 6.7 %copy-start.9 = (bf16[128,192]{0,1:T(8,128)(2,1)S(1)}, bf16[128,192]{0,1:T(8,128)(2,1)}, u32[]{:S(2)}) copy-start(bf16[128,192]{0,1:T(8,128)(2,1)} %param.19) | copy-start | bytes 147460
  9.3 7.0 %collective-permute-start.1 = (bf16[3,24,2,192]{3,2,1,0:T(2,128)(2,1)S(1)}, bf16[3,24,2,192]{3,2,1,0:T(2,128)(2,1)S(1)}, u32[]{:S(2)}, u32[]{:S(2)}) collective-permute-start(bf16[3,24,2,192]{3,2,1,0:T(2,128)(2,1)S(1)} %bitcast.19), channel_id=1, source_target_pairs={{1,2},{2,1},{5,6},{6,5},{9,10},{10,9},{13,14},{14,13},{17,18},{18,... | collective-permute-start | bytes 165896 | tf_op jit(solution)/shard_map/ppermute | solution.py:38
  10.1 7.3 %collective-permute-start = (bf16[3,24,2,192]{3,2,1,0:T(2,128)(2,1)S(1)}, bf16[3,24,2,192]{3,2,1,0:T(2,128)(2,1)S(1)}, u32[]{:S(2)}, u32[]{:S(2)}) collective-permute-start(bf16[3,24,2,192]{3,2,1,0:T(2,128)(2,1)S(1)} %bitcast.18), channel_id=1, source_target_pairs={{0,1},{1,0},{2,3},{3,2},{4,5},{5,4},{6,7},{7,6},{8,9},{9,8},{10,11... | collective-permute-start | bytes 165896 | tf_op jit(solution)/shard_map/ppermute | solution.py:38
  14.6 0.7 %copy-start.10 = (bf16[192]{0:T(256)(128)(2,1)S(1)}, bf16[192]{0:T(256)(128)(2,1)}, u32[]{:S(2)}) copy-start(bf16[192]{0:T(256)(128)(2,1)} %param.22) | copy-start | bytes 1156
  15.3 0.7 %copy-start.11 = (bf16[192]{0:T(256)(128)(2,1)S(1)}, bf16[192]{0:T(256)(128)(2,1)}, u32[]{:S(2)}) copy-start(bf16[192]{0:T(256)(128)(2,1)} %param.25) | copy-start | bytes 1156
  16.1 1.3 %copy-start = (bf16[12,24,2,192]{3,2,1,0:T(2,128)(2,1)S(1)}, bf16[12,24,2,192]{3,2,1,0:T(2,128)(2,1)}, u32[]{:S(2)}) copy-start(bf16[12,24,2,192]{3,2,1,0:T(2,128)(2,1)} %back_ref.6) | copy-start | bytes 663556
  17.4 3.3 %copy-start.1 = (bf16[192,768]{1,0:T(8,128)(2,1)S(1)}, bf16[192,768]{1,0:T(8,128)(2,1)}, u32[]{:S(2)}) copy-start(bf16[192,768]{1,0:T(8,128)(2,1)} %refs_4_.3) | copy-start | bytes 884740
  17.4 3.3 %copy-start.2 = (bf16[192,576]{1,0:T(8,128)(2,1)S(1)}, bf16[192,576]{1,0:T(8,128)(2,1)}, u32[]{:S(2)}) copy-start(bf16[192,576]{1,0:T(8,128)(2,1)} %refs_1_.3) | copy-start | bytes 663556
  17.4 3.3 %copy-start.3 = (bf16[192,384]{1,0:T(8,128)(2,1)S(1)}, bf16[192,384]{1,0:T(8,128)(2,1)}, u32[]{:S(2)}) copy-start(bf16[192,384]{1,0:T(8,128)(2,1)} %lift_ref.1) | copy-start | bytes 442372
  17.4 3.3 %copy-start.4 = (bf16[192,192]{1,0:T(8,128)(2,1)S(1)}, bf16[192,192]{1,0:T(8,128)(2,1)}, u32[]{:S(2)}) copy-start(bf16[192,192]{1,0:T(8,128)(2,1)} %refs_2_.3) | copy-start | bytes 221188
  18.1 2.6 %copy-start.5 = (bf16[8,192]{1,0:T(8,128)(2,1)S(1)}, bf16[8,192]{1,0:T(8,128)(2,1)}, u32[]{:S(2)}) copy-start(bf16[8,192]{1,0:T(8,128)(2,1)} %table_ref.1) | copy-start | bytes 9220
  18.1 6.8 %collective-permute-start.2 = (bf16[18,6,2,192]{3,2,1,0:T(2,128)(2,1)S(1)}, bf16[18,6,2,192]{3,2,1,0:T(2,128)(2,1)S(1)}, u32[]{:S(2)}, u32[]{:S(2)}) collective-permute-start(bf16[18,6,2,192]{3,2,1,0:T(2,128)(2,1)S(1)} %get-tuple-element.29), channel_id=1, source_target_pairs={{0,4},{4,0},{8,12},{12,8},{16,20},{20,16},{24,28},{28,24},{1,5},{5... | collective-permute-start | bytes 248840 | tf_op jit(solution)/shard_map/ppermute | solution.py:38
  18.2 6.8 %collective-permute-start.3 = (bf16[18,6,2,192]{3,2,1,0:T(2,128)(2,1)S(1)}, bf16[18,6,2,192]{3,2,1,0:T(2,128)(2,1)S(1)}, u32[]{:S(2)}, u32[]{:S(2)}) collective-permute-start(bf16[18,6,2,192]{3,2,1,0:T(2,128)(2,1)S(1)} %get-tuple-element.30), channel_id=1, source_target_pairs={{4,8},{8,4},{12,16},{16,12},{20,24},{24,20},{28,0},{0,28},{5,9},{9... | collective-permute-start | bytes 248840 | tf_op jit(solution)/shard_map/ppermute | solution.py:38

commit v18 on v16

--- a/solution.py
+++ b/solution.py
@@ -218,25 +218,22 @@
     return jnp.where(place < count, code, -8).astype(F32)
 
 
-def entries_of(windows):
-    entries = [(4, 3 * i + j) for i, j in windows]
-    for i, j in windows:
-        if i != 1:
-            entries.append((3 * i + 1, j))
-        if j != 1:
-            entries.append((3 + j, i))
-        if i != 1 and j != 1:
-            entries.append((3 * i + j, 0))
-    return entries
-
-
-def scattered(recv_ref, first_ref, table_ref, lift_ref, plan, lon_cells):
+def near_entries(windows):
+    own = [(4, 3 * i + j) for i, j in windows]
+    return own + [(3 * i + 1, j) for i, j in windows if i != 1]
+
+
+def far_entries(windows):
+    beside = [(3 + j, i) for i, j in windows if j != 1]
+    return beside + [(3 * i + j, 0) for i, j in windows if i != 1 and j != 1]
+
+
+def scattered(recv_ref, first_ref, lift_ref, plan, lon_cells):
     sources, _, capacity, _ = recv_ref.shape
-    width = table_ref.shape[1]
+    width = first_ref.shape[1]
     chunk = min(CHUNK, sources)
     slots = chunk * capacity
     first, lift = first_ref[...], lift_ref[...]
-    table = below(*[table_ref[...].astype(F32)] * (LANES // INSTR)).astype(BF16)
     lane = lax.broadcasted_iota(jnp.int32, (16, LANES), 1)
     sub = lax.broadcasted_iota(jnp.int32, (16, LANES), 0)
     weigh = jnp.where(lane == ROWS + sub, float(lon_cells * LEV), 0.0)
@@ -254,7 +251,8 @@
         lane = lax.broadcasted_iota(jnp.int32, meta.shape, 1) // INSTR
         wide = meta.astype(F32)
         chosen = below(*[jnp.where(lane == n, wide, 0.0) for n in range(len(AROUND))]).astype(BF16)
-        encoded = gelu(dot(records, first) + dot(chosen, table)).astype(BF16)
+        both = jnp.concatenate([records, chosen], axis=1)
+        encoded = gelu(dot(both, first)).astype(BF16)
         lifted = gelu(dot(encoded, lift))
         tokens = dot_nt(weigh, meta)
         hots, parts = [], []
@@ -287,43 +285,76 @@
     return sums
 
 
-def worked(plan, places, sum_of, borders, weights, scalars_ref, put):
-    back_ref, north_ref, south_ref, west_ref, east_ref = borders
-    gain_one_ref, attn_ref, mix_ref, gain_two_ref, up_ref, down_ref = weights
-    lat_cells, width = back_ref.shape[0], back_ref.shape[3]
+def prepare_kernel(plan, back_ref, first_ref, table_ref, attn_ref, rows_ref, both_ref, parts_ref):
+    width = back_ref.shape[3]
+    pieces = []
+    for top, high, left, wide in plan[4]:
+        count = high * wide * LEV
+        piece = back_ref[top : top + high, left : left + wide].reshape(count, width).astype(F32)
+        if padded(count) > count:
+            piece = below(piece, jnp.zeros((padded(count) - count, width), F32))
+        pieces.append(piece)
+    rows_ref[...] = below(*pieces)
+    table = below(*[table_ref[...].astype(F32)] * (LANES // INSTR)).astype(BF16)
+    both_ref[:LANES, :] = first_ref[...]
+    both_ref[LANES:, :] = table
+    for n in range(3):
+        parts_ref[n] = attn_ref[:, n * width : (n + 1) * width]
+
+
+def prepared(plan, background, input_weight, instrument_table, attn_weight):
+    width = background.shape[3]
+    rows = sum(padded(tokens_of(part)) for part in plan[4])
+    vmem = pl.BlockSpec(memory_space=pltpu.VMEM)
+    return pl.pallas_call(
+        functools.partial(prepare_kernel, plan),
+        out_shape=[
+            jax.ShapeDtypeStruct((rows, width), F32),
+            jax.ShapeDtypeStruct((2 * LANES, width), BF16),
+            jax.ShapeDtypeStruct((3, width, width), BF16),
+        ],
+        in_specs=[vmem] * 4,
+        out_specs=[vmem] * 3,
+        compiler_params=pltpu.CompilerParams(vmem_limit_bytes=LIMIT),
+        cost_estimate=pl.CostEstimate(flops=10**9, bytes_accessed=10**6, transcendentals=0),
+    )(background, input_weight, instrument_table, attn_weight)
+
+
+def normed_of(plan, entries, sums, borders, gain):
+    rows_ref, north_ref, south_ref, west_ref, east_ref, lat_cells = borders
+    width = gain.shape[1]
     pieces, spans, start = [], {}, 0
-    for tile, number in entries_of(places):
+    for tile, number in entries:
         dy, dx = AROUND[tile]
-        part = plan[tile][number]
-        top, high, left, wide = part
-        count = tokens_of(part)
-        if dx:
-            ref = west_ref if dx < 0 else east_ref
-            top, left = {-1: 0, 0: top + HLAT, 1: lat_cells + HLAT}[dy], 0
-        elif dy:
-            ref, top = (north_ref, 0) if dy < 0 else (south_ref, 0)
+        top, high, left, wide = plan[tile][number]
+        count = high * wide * LEV
+        full = padded(count)
+        if tile == 4:
+            begin = sum(padded(tokens_of(part)) for part in plan[4][:number])
+            piece = rows_ref[begin : begin + full, :]
         else:
-            ref = back_ref
-        piece = ref[top : top + high, left : left + wide].reshape(count, width).astype(F32)
-        full = padded(count)
-        if full > count:
-            piece = below(piece, jnp.zeros((full - count, width), F32))
+            if dx:
+                ref = west_ref if dx < 0 else east_ref
+                top, left = {-1: 0, 0: top + HLAT, 1: lat_cells + HLAT}[dy], 0
+            else:
+                ref, top = (north_ref, 0) if dy < 0 else (south_ref, 0)
+            piece = ref[top : top + high, left : left + wide].reshape(count, width).astype(F32)
+            if full > count:
+                piece = below(piece, jnp.zeros((full - count, width), F32))
         pieces.append(piece)
         spans[tile, number] = (start, count)
         start += full
-    sums = below(*[sum_of(*entry) for entry in entries_of(places)])
     tally = 1.0 + sums[:, width : width + 1]
     share = about_one_over(tally)
     share = share * (2.0 - tally * share)
     latent = ((below(*pieces) + sums[:, :width]) * share).astype(BF16).astype(F32)
-    normed = normalise(latent, gain_one_ref[...].astype(F32))
-
-    def piece_of(tile, number):
-        start, count = spans[tile, number]
-        return normed[start : start + count]
-
+    return latent, normalise(latent, gain), spans
+
+
+def worked(plan, places, piece_of, own_normed, latent, weights, scalars_ref, put):
+    parts_ref, mix_ref, gain_ref, up_ref, down_ref = weights
+    width = mix_ref.shape[0]
     groups = [padded(tokens_of(plan[4][3 * i + j])) for i, j in places]
-    end = sum(groups)
     windows = []
     for i, j in places:
         window = [piece_of(4, 3 * i + j)]
@@ -335,12 +366,11 @@
             window.append(piece_of(3 * i + j, 0))
         windows.append(window)
     tokens = below(*[piece for window in windows for piece in window]).astype(BF16)
-    weight = attn_ref[...]
     head = width // HEADS
-    keys = dot(tokens, weight[:, width : 2 * width])
-    query = dot(normed[:end].astype(BF16), weight[:, :width]) * head ** (-0.5)
-    query = jnp.concatenate([query, jnp.ones((end, PAD - width), F32)], axis=1)
-    values = with_ones(dot(tokens, weight[:, 2 * width :]))
+    query = dot(own_normed.astype(BF16), parts_ref[0]) * head ** (-0.5)
+    query = jnp.concatenate([query, jnp.ones((query.shape[0], PAD - width), F32)], axis=1)
+    keys = dot(tokens, parts_ref[1])
+    values = with_ones(dot(tokens, parts_ref[2]))
 
     lane = lax.broadcasted_iota(jnp.int32, (1, PAD), 1)
     many = WLAT * WLON * LEV
@@ -387,8 +417,8 @@
         mixed.append(total)
     mixed = below(*mixed).astype(BF16)
 
-    after = (latent[:end] + dot(mixed, mix_ref[...])).astype(BF16).astype(F32)
-    normed_two = normalise(after, gain_two_ref[...].astype(F32)).astype(BF16)
+    after = (latent + dot(mixed, mix_ref[...])).astype(BF16).astype(F32)
+    normed_two = normalise(after, gain_ref[...].astype(F32)).astype(BF16)
     hidden = gelu(dot(normed_two, up_ref[...]).astype(BF16))
     result = after + dot(hidden, down_ref[...])
     for begin, (i, j) in zip(begins, places):
@@ -401,68 +431,93 @@
 SIDES = [(0, 0), (0, 2), (2, 0), (2, 2), (1, 0), (1, 2)]
 
 
-def side_entries():
-    return entries_of(SIDES)
+def own_rows(plan, places):
+    return sum(padded(tokens_of(plan[4][3 * i + j])) for i, j in places)
 
 
 def middle_kernel(
     plan,
+    lat_cells,
+    lon_cells,
     scalars_ref,
     recv_ref,
     north_ref,
     south_ref,
-    back_ref,
-    first_ref,
-    table_ref,
+    rows_ref,
+    both_ref,
     lift_ref,
+    gain_one_ref,
     *refs,
 ):
-    *weights, out_ref, rest_ref = refs
-    sums = scattered(recv_ref, first_ref, table_ref, lift_ref, plan, back_ref.shape[1])
-
-    def sum_of(tile, number):
-        start = sum(padded(tokens_of(part)) for part in plan[tile][:number])
-        return sums[tile][start : start + padded(tokens_of(plan[tile][number]))]
-
-    rest_ref[...] = below(*[sum_of(*entry) for entry in side_entries()])
+    *weights, out_ref, rest_ref, latent_ref, normed_ref = refs
+    sums = scattered(recv_ref, both_ref, lift_ref, plan, lon_cells)
+
+    def sums_of(entries):
+        pieces = []
+        for tile, number in entries:
+            start = sum(padded(tokens_of(part)) for part in plan[tile][:number])
+            pieces.append(sums[tile][start : start + padded(tokens_of(plan[tile][number]))])
+        return below(*pieces)
+
+    borders = (rows_ref, north_ref, south_ref, None, None, lat_cells)
+    gain = gain_one_ref[...].astype(F32)
+    entries = near_entries(MIDDLE)
+    latent, normed, spans = normed_of(plan, entries, sums_of(entries), borders, gain)
+
+    def piece_of(tile, number):
+        start, count = spans[tile, number]
+        return normed[start : start + count]
 
     def put(part, _, piece):
         out_ref[part[0] : part[0] + part[1]] = piece
 
-    borders = (back_ref, north_ref, south_ref, None, None)
-    worked(plan, MIDDLE, sum_of, borders, weights, scalars_ref, put)
+    end = own_rows(plan, MIDDLE)
+    worked(plan, MIDDLE, piece_of, normed[:end], latent[:end], weights, scalars_ref, put)
+    rest_ref[...] = sums_of(far_entries(SIDES))
+    entries = near_entries(SIDES)
+    latent, normed, _ = normed_of(plan, entries, sums_of(entries), borders, gain)
+    latent_ref[...] = latent[: latent_ref.shape[0]]
+    normed_ref[...] = normed
 
 
 def side_kernel(
     plan,
+    lat_cells,
     scalars_ref,
     rest_ref,
-    north_ref,
-    south_ref,
+    latent_ref,
+    normed_ref,
     west_ref,
     east_ref,
-    back_ref,
+    gain_one_ref,
     *refs,
 ):
     *weights, middle_ref, out_ref, held_ref, sem = refs
     left, wide = plan[4][4][2:]
     copies = [pltpu.make_async_copy(middle_ref, out_ref.at[:, left : left + wide], sem.at[2])]
     copies[0].start()
-    spans, start = {}, 0
-    for tile, number in side_entries():
-        rows = padded(tokens_of(plan[tile][number]))
-        spans[tile, number] = (start, start + rows)
-        start += rows
-
-    def sum_of(tile, number):
-        start, end = spans[tile, number]
-        return rest_ref[start:end, :]
+    near, start = {}, 0
+    for tile, number in near_entries(SIDES):
+        near[tile, number] = start
+        start += padded(tokens_of(plan[tile][number]))
+    borders = (None, None, None, west_ref, east_ref, lat_cells)
+    gain = gain_one_ref[...].astype(F32)
+    _, far, spans = normed_of(plan, far_entries(SIDES), rest_ref[...], borders, gain)
+
+    def piece_of(tile, number):
+        if (tile, number) in spans:
+            start, count = spans[tile, number]
+            return far[start : start + count]
+        start = near[tile, number]
+        return normed_ref[start : start + tokens_of(plan[tile][number]), :]
 
     def put(part, j, piece):
         held_ref[j // 2, part[0] : part[0] + part[1]] = piece
 
-    borders = (back_ref, north_ref, south_ref, west_ref, east_ref)
-    worked(plan, SIDES, sum_of, borders, weights, scalars_ref, put)
+    end = own_rows(plan, SIDES)
+    worked(
+        plan, SIDES, piece_of, normed_ref[:end, :], latent_ref[...], weights, scalars_ref, put
+    )
     for n, number in enumerate((0, 2)):
         left, wide = plan[4][number][2:]
         copies.append(
@@ -498,8 +553,8 @@
     received = lax.all_to_all(sent, ("lon", "lat"), split_axis=0, concat_axis=0, tiled=True)
     north, south = before_and_after(swapped(up, down, "lat", wraps=False), "lat")
 
-    later, input_weight, down_weight, _ = lax.optimization_barrier(
-        (background, input_weight, down_weight, up)
+    later, input_weight, instrument_table, attn_weight, down_weight, _ = lax.optimization_barrier(
+        (background, input_weight, instrument_table, attn_weight, down_weight, up)
     )
 
     def columns(low, end):
@@ -507,51 +562,40 @@
 
     got = swapped(columns(0, HLON), columns(lon_cells - HLON, lon_cells), "lon", wraps=True)
 
+    plan = rectangles(lat_cells, lon_cells)
+    rows, both, parts = prepared(plan, later, input_weight, instrument_table, attn_weight)
     lat = lax.axis_index("lat")
     scalars = jnp.stack([lat == 0, lat < 0, lat == tiles_lat - 1]).astype(jnp.int32)
-    plan = rectangles(lat_cells, lon_cells)
-    rest = sum(padded(tokens_of(plan[tile][number])) for tile, number in side_entries())
-    weights = [
-        first_gain.reshape(1, width),
-        attn_weight,
-        mix_weight,
-        second_gain.reshape(1, width),
-        up_weight,
-        down_weight,
-    ]
+
+    def rows_in(entries):
+        return sum(padded(tokens_of(plan[tile][number])) for tile, number in entries)
+
+    gain_one = first_gain.reshape(1, width)
+    weights = [parts, mix_weight, second_gain.reshape(1, width), up_weight, down_weight]
     smem = pl.BlockSpec(memory_space=pltpu.SMEM)
     vmem = pl.BlockSpec(memory_space=pltpu.VMEM)
     anywhere = pl.BlockSpec(memory_space=pl.ANY)
     params = pltpu.CompilerParams(vmem_limit_bytes=LIMIT)
-    result = jax.ShapeDtypeStruct(background.shape, BF16)
-    middle, rest = pl.pallas_call(
-        functools.partial(middle_kernel, plan),
+    middle, rest, latent, normed = pl.pallas_call(
+        functools.partial(middle_kernel, plan, lat_cells, lon_cells),
         out_shape=[
             jax.ShapeDtypeStruct((lat_cells, lon_cells - WLON, LEV, width), BF16),
-            jax.ShapeDtypeStruct((rest, PAD), F32),
+            jax.ShapeDtypeStruct((rows_in(far_entries(SIDES)), PAD), F32),
+            jax.ShapeDtypeStruct((own_rows(plan, SIDES), width), F32),
+            jax.ShapeDtypeStruct((rows_in(near_entries(SIDES)), width), F32),
         ],
         in_specs=[smem] + [vmem] * (7 + len(weights)),
-        out_specs=[vmem, vmem],
+        out_specs=[vmem] * 4,
         compiler_params=params,
         cost_estimate=pl.CostEstimate(
             flops=4 * 10**9, bytes_accessed=4 * 10**6, transcendentals=10**6
         ),
-    )(
-        scalars,
-        received,
-        north,
-        south,
-        background,
-        input_weight,
-        instrument_table,
-        lift_weight,
-        *weights,
-    )
+    )(scalars, received, north, south, rows, both, lift_weight, gain_one, *weights)
     rest, *got = lax.optimization_barrier((rest, *got))
     west, east = before_and_after(got, "lon")
     return pl.pallas_call(
-        functools.partial(side_kernel, plan),
-        out_shape=result,
+        functools.partial(side_kernel, plan, lat_cells),
+        out_shape=jax.ShapeDtypeStruct(background.shape, BF16),
         in_specs=[smem] + [vmem] * (7 + len(weights)),
         out_specs=anywhere,
         scratch_shapes=[
@@ -562,7 +606,7 @@
         cost_estimate=pl.CostEstimate(
             flops=3 * 10**9, bytes_accessed=4 * 10**6, transcendentals=10**6
         ),
-    )(scalars, rest, north, south, west, east, background, *weights, middle)
+    )(scalars, rest, latent, normed, west, east, gain_one, *weights, middle)
 
 
 def solution(mesh):

time: 27.7 us -> 27.8 us (level)
  the two profiles are of different devices: /device:TPU:0 before, /device:TPU:8 now
where the time goes in v18:
time: 27.8 us; the launch traced here: 27.4 us
  starting transfers between devices  13.6 us (49%)
  Pallas kernels  9.84 us (35%)
  local copies, waits for them, and re-layouts  3.07 us (11%)
  other arithmetic  0.66 us (2%)
  between operations  0.28 us (1%)
    ppermute x4, starting transfers between devices, swapped(): got.append(lax.ppermute(mine, axis, pairs))  7.52 us
    all_to_all x1, starting transfers between devices, local(): lax.all_to_all(sent, ('lon', 'lat'), split_axis=0, concat_axis=0, tiled=T...  6.05 us
    pallas_call x1, Pallas kernels, local(): pl.pallas_call(functools.partial(side_kernel, plan, lat_cells), out_shape...  3.97 us
    pallas_call x1, Pallas kernels, local(): pl.pallas_call(functools.partial(middle_kernel, plan, lat_cells, lon_cell...  3.95 us
    unnamed x24, local copies, waits for them, and re-layouts  2.62 us
    pallas_call x1, Pallas kernels, packed(): pl.pallas_call(pack_kernel, out_shape=[jax.ShapeDtypeStruct(shape, BF16),...  1.75 us
  transfers between devices with their start and end apart: 5, of which 0 were waited for; matrix products, arithmetic and copies ran while one was open for 3% of the time, Pallas kernels for 15%

profile of v18, /device:TPU:8, one launch (start us, length us, event | category | flops | bytes accessed | tf_op | source)
XLA Modules:
  0.0 27.4 jit_solution(7801310716430435938)
XLA Ops:
  0.0 1.8 %shard_map.136 = (bf16[8,4,10,2,128]{4,3,2,1,0:T(2,128)(2,1)}, bf16[3,24,2,192]{3,2,1,0:T(2,128)(2,1)}, bf16[3,24,2,192]{3,2,1,0:T(2,128)(2,1)}) custom-call(bf16[8,4,2,128]{3,2,1,0:T(2,128)(2,1)} %values_ref.1, s32[8,8]{1,0:T(8,128)} %bitcast.30, s32[8,8]{1,0:T(8,128)} %bitcast.31, s32[4,8]{1,0:T(4,128)} %bitcast.32, bf16[12,24,2,192]{3,2,1,0:T(2,128)(2,1)} %back_ref.2), custom_call_target="tpu_custom_call" | custom-call | flops 20000000000 | bytes 1000000 | tf_op jit(solution)/shard_map/pallas_call | solution.py:184
  1.8 0.0 copy-start.7
  1.8 0.0 copy-start.8
  1.8 6.0 %all-to-all-start = ((bf16[32,10,2,128]{3,2,1,0:T(2,128)(2,1)}), bf16[32,10,2,128]{3,2,1,0:T(2,128)(2,1)S(1)}, u32[]{:S(2)}, u32[]{:S(2)}) async-start(bf16[32,10,2,128]{3,2,1,0:T(2,128)(2,1)} %bitcast.23), calls=%async_computation | async-start | bytes 327680 | tf_op jit(solution)/shard_map/all_to_all | solution.py:553
  7.8 0.0 copy-start.6
  7.9 0.0 copy-done.7
  7.9 0.0 copy-done.8
  7.9 0.0 copy-start.9
  7.9 0.3 %collective-permute-start.1 = (bf16[3,24,2,192]{3,2,1,0:T(2,128)(2,1)S(1)}, bf16[3,24,2,192]{3,2,1,0:T(2,128)(2,1)S(1)}, u32[]{:S(2)}, u32[]{:S(2)}) collective-permute-start(bf16[3,24,2,192]{3,2,1,0:T(2,128)(2,1)S(1)} %bitcast.27), channel_id=1, source_target_pairs={{0,1},{1,0},{2,3},{3,2},{4,5},{5,4},{6,7},{7,6},{8,9},{9,8},{10,11... | collective-permute-start | bytes 165896 | tf_op jit(solution)/shard_map/ppermute | solution.py:39
  8.2 4.6 %collective-permute-start = (bf16[3,24,2,192]{3,2,1,0:T(2,128)(2,1)S(1)}, bf16[3,24,2,192]{3,2,1,0:T(2,128)(2,1)S(1)}, u32[]{:S(2)}, u32[]{:S(2)}) collective-permute-start(bf16[3,24,2,192]{3,2,1,0:T(2,128)(2,1)S(1)} %bitcast.25), channel_id=1, source_target_pairs={{1,2},{2,1},{5,6},{6,5},{9,10},{10,9},{13,14},{14,13},{17,18},{18,... | collective-permute-start | bytes 165896 | tf_op jit(solution)/shard_map/ppermute | solution.py:39
  12.9 0.0 copy-done.9
  12.9 0.0 copy-start.10
  12.9 0.1 copy.15.first_ref
  13.0 0.5 %copy-done.10 = bf16[192]{0:T(256)(128)(2,1)S(1)} copy-done((bf16[192]{0:T(256)(128)(2,1)S(1)}, bf16[192]{0:T(256)(128)(2,1)}, u32[]{:S(2)}) %copy-start.10) | copy-done | bytes 408
  13.6 0.0 copy-start.11
  13.6 0.6 %copy-done.11 = bf16[192]{0:T(256)(128)(2,1)S(1)} copy-done((bf16[192]{0:T(256)(128)(2,1)S(1)}, bf16[192]{0:T(256)(128)(2,1)}, u32[]{:S(2)}) %copy-start.11) | copy-done | bytes 408
  14.2 0.0 copy-done.6
  14.2 0.0 copy-start
  14.2 0.2 copy.16.refs_4_
  14.4 0.0 copy-start.2
  14.4 0.8 %copy-done = bf16[12,24,2,192]{3,2,1,0:T(2,128)(2,1)S(1)} copy-done((bf16[12,24,2,192]{3,2,1,0:T(2,128)(2,1)S(1)}, bf16[12,24,2,192]{3,2,1,0:T(2,128)(2,1)}, u32[]{:S(2)}) %copy-start) | copy-done | bytes 221208
  15.2 0.1 fusion
  15.3 0.0 copy-start.5
  15.3 0.1 add_convert_fusion.scalars_ref
  15.4 0.0 copy-done.2
  15.4 0.6 %copy-done.5 = bf16[8,192]{1,0:T(8,128)(2,1)S(1)} copy-done((bf16[8,192]{1,0:T(8,128)(2,1)S(1)}, bf16[8,192]{1,0:T(8,128)(2,1)}, u32[]{:S(2)}) %copy-start.5) | copy-done | bytes 3096
  16.0 0.2 shard_map.137
  16.2 0.0 collective-permute-done.1
  16.2 0.0 collective-permute-done
  16.2 0.0 copy-start.1
  16.2 0.1 fusion.1
  16.3 0.0 copy-start.3
  16.3 0.0 copy-start.4
  16.3 0.4 %broadcast_select_fusion.2 = (bf16[18,6,2,192]{3,2,1,0:T(2,128)(2,1)S(1)}, bf16[18,6,2,192]{3,2,1,0:T(2,128)(2,1)S(1)}) fusion(pred[]{:T(512)S(6)} %eq.22, bf16[3,6,2,192]{3,2,1,0:T(2,128)(2,1)S(1)} %get-tuple-element.55, bf16[12,6,2,192]{3,2,1,0:T(2,128)(2,1)S(1)} %get-tuple-element.42, bf16[3,6,2,192]{3,2,1,0:T(2,128)(2,1)S(1)} %get-tuple-element.52, ...), kind=kLoop, calls=%fused_computation.2 | loop fusion | flops 248832 | bytes 331777 | tf_op jit(solution)/shard_map/jit(_where)/select_n | solution.py:33
  16.7 0.1 collective-permute-start.2
  16.8 2.5 %collective-permute-start.3 = (bf16[18,6,2,192]{3,2,1,0:T(2,128)(2,1)S(1)}, bf16[18,6,2,192]{3,2,1,0:T(2,128)(2,1)S(1)}, u32[]{:S(2)}, u32[]{:S(2)}) collective-permute-start(bf16[18,6,2,192]{3,2,1,0:T(2,128)(2,1)S(1)} %get-tuple-element.45), channel_id=1, source_target_pairs={{4,8},{8,4},{12,16},{16,12},{20,24},{24,20},{28,0},{0,28},{5,9},{9... | collective-permute-start | bytes 248840 | tf_op jit(solution)/shard_map/ppermute | solution.py:39
  19.3 0.0 all-to-all-done.recv_ref
  19.3 0.0 copy-done.1
  19.3 0.0 copy-done.3
  19.3 0.0 copy-done.4
  19.3 3.9 %shard_map.138 = (bf16[12,12,2,192]{3,2,1,0:T(2,128)(2,1)S(1)}, f32[464,256]{1,0:T(8,128)S(1)}, f32[304,192]{1,0:T(8,128)S(1)}, f32[464,192]{1,0:T(8,128)S(1)}) custom-call(s32[3]{0:T(128)S(1)} %add_convert_fusion.scalars_ref, bf16[32,10,2,128]{3,2,1,0:T(2,128)(2,1)S(1)} %all-to-all-done.recv_ref, bf16[3,24,2,192]{3,2,1,0:T(2,128)(2,1)S(1)} %bitcast.22, ...), custom_call_target="tpu_custom_call" | custom-call | flops 4000000000 | bytes 4000000 | tf_op jit(solution)/shard_map/pallas_call | solution.py:579
  23.3 0.0 collective-permute-done.2
  23.3 0.0 collective-permute-done.3
  23.3 0.2 broadcast_select_fusion
  23.5 4.0 %shard_map.139 = bf16[12,24,2,192]{3,2,1,0:T(2,128)(2,1)} custom-call(s32[3]{0:T(128)S(1)} %add_convert_fusion.scalars_ref, f32[464,256]{1,0:T(8,128)S(1)} %get-tuple-element.35.rest_ref, f32[304,192]{1,0:T(8,128)S(1)} %get-tuple-element.36.latent_ref, f32[464,192]{1,0:T(8,128)S(1)} %get-tuple-element.37.normed_ref, ...), custom_call_target="tpu_custom_call" | custom-call | flops 3000000000 | bytes 4000000 | tf_op jit(solution)/shard_map/pallas_call | solution.py:596
  (4 shorter events, 0.0 us)
Async XLA Ops:
  1.8 6.1 %copy-start.7 = (bf16[3,24,2,192]{3,2,1,0:T(2,128)(2,1)S(1)}, bf16[3,24,2,192]{3,2,1,0:T(2,128)(2,1)}, u32[]{:S(2)}) copy-start(bf16[3,24,2,192]{3,2,1,0:T(2,128)(2,1)} %get-tuple-element.24) | copy-start | bytes 165892
  1.8 6.1 %copy-start.8 = (bf16[3,24,2,192]{3,2,1,0:T(2,128)(2,1)S(1)}, bf16[3,24,2,192]{3,2,1,0:T(2,128)(2,1)}, u32[]{:S(2)}) copy-start(bf16[3,24,2,192]{3,2,1,0:T(2,128)(2,1)} %get-tuple-element.25) | copy-start | bytes 165892
  1.8 17.5 %all-to-all-start = ((bf16[32,10,2,128]{3,2,1,0:T(2,128)(2,1)}), bf16[32,10,2,128]{3,2,1,0:T(2,128)(2,1)S(1)}, u32[]{:S(2)}, u32[]{:S(2)}) async-start(bf16[32,10,2,128]{3,2,1,0:T(2,128)(2,1)} %bitcast.23), calls=%async_computation | async-start | bytes 327680 | tf_op jit(solution)/shard_map/all_to_all | solution.py:553
  7.8 6.4 %copy-start.6 = (bf16[768,192]{0,1:T(8,128)(2,1)S(1)}, bf16[768,192]{0,1:T(8,128)(2,1)}, u32[]{:S(2)}) copy-start(bf16[768,192]{0,1:T(8,128)(2,1)} %param.27) | copy-start | bytes 884740
  7.9 5.0 %copy-start.9 = (bf16[128,192]{0,1:T(8,128)(2,1)S(1)}, bf16[128,192]{0,1:T(8,128)(2,1)}, u32[]{:S(2)}) copy-start(bf16[128,192]{0,1:T(8,128)(2,1)} %param.19) | copy-start | bytes 147460
  7.9 8.2 %collective-permute-start.1 = (bf16[3,24,2,192]{3,2,1,0:T(2,128)(2,1)S(1)}, bf16[3,24,2,192]{3,2,1,0:T(2,128)(2,1)S(1)}, u32[]{:S(2)}, u32[]{:S(2)}) collective-permute-start(bf16[3,24,2,192]{3,2,1,0:T(2,128)(2,1)S(1)} %bitcast.27), channel_id=1, source_target_pairs={{0,1},{1,0},{2,3},{3,2},{4,5},{5,4},{6,7},{7,6},{8,9},{9,8},{10,11... | collective-permute-start | bytes 165896 | tf_op jit(solution)/shard_map/ppermute | solution.py:39
  8.2 7.9 %collective-permute-start = (bf16[3,24,2,192]{3,2,1,0:T(2,128)(2,1)S(1)}, bf16[3,24,2,192]{3,2,1,0:T(2,128)(2,1)S(1)}, u32[]{:S(2)}, u32[]{:S(2)}) collective-permute-start(bf16[3,24,2,192]{3,2,1,0:T(2,128)(2,1)S(1)} %bitcast.25), channel_id=1, source_target_pairs={{1,2},{2,1},{5,6},{6,5},{9,10},{10,9},{13,14},{14,13},{17,18},{18,... | collective-permute-start | bytes 165896 | tf_op jit(solution)/shard_map/ppermute | solution.py:39
  12.9 0.7 %copy-start.10 = (bf16[192]{0:T(256)(128)(2,1)S(1)}, bf16[192]{0:T(256)(128)(2,1)}, u32[]{:S(2)}) copy-start(bf16[192]{0:T(256)(128)(2,1)} %param.22) | copy-start | bytes 1156
  13.6 0.7 %copy-start.11 = (bf16[192]{0:T(256)(128)(2,1)S(1)}, bf16[192]{0:T(256)(128)(2,1)}, u32[]{:S(2)}) copy-start(bf16[192]{0:T(256)(128)(2,1)} %param.25) | copy-start | bytes 1156
  14.2 1.0 %copy-start = (bf16[12,24,2,192]{3,2,1,0:T(2,128)(2,1)S(1)}, bf16[12,24,2,192]{3,2,1,0:T(2,128)(2,1)}, u32[]{:S(2)}) copy-start(bf16[12,24,2,192]{3,2,1,0:T(2,128)(2,1)} %back_ref.2) | copy-start | bytes 663556
  14.4 1.0 %copy-start.2 = (bf16[192,576]{1,0:T(8,128)(2,1)S(1)}, bf16[192,576]{1,0:T(8,128)(2,1)}, u32[]{:S(2)}) copy-start(bf16[192,576]{1,0:T(8,128)(2,1)} %attn_ref) | copy-start | bytes 663556
  15.3 0.7 %copy-start.5 = (bf16[8,192]{1,0:T(8,128)(2,1)S(1)}, bf16[8,192]{1,0:T(8,128)(2,1)}, u32[]{:S(2)}) copy-start(bf16[8,192]{1,0:T(8,128)(2,1)} %table_ref) | copy-start | bytes 9220
  16.2 3.1 %copy-start.1 = (bf16[192,768]{1,0:T(8,128)(2,1)S(1)}, bf16[192,768]{1,0:T(8,128)(2,1)}, u32[]{:S(2)}) copy-start(bf16[192,768]{1,0:T(8,128)(2,1)} %refs_3_.3) | copy-start | bytes 884740
  16.3 3.0 %copy-start.3 = (bf16[192,384]{1,0:T(8,128)(2,1)S(1)}, bf16[192,384]{1,0:T(8,128)(2,1)}, u32[]{:S(2)}) copy-start(bf16[192,384]{1,0:T(8,128)(2,1)} %lift_ref.1) | copy-start | bytes 442372
  16.3 3.0 %copy-start.4 = (bf16[192,192]{1,0:T(8,128)(2,1)S(1)}, bf16[192,192]{1,0:T(8,128)(2,1)}, u32[]{:S(2)}) copy-start(bf16[192,192]{1,0:T(8,128)(2,1)} %refs_1_.3) | copy-start | bytes 221188
  16.7 6.6 %collective-permute-start.2 = (bf16[18,6,2,192]{3,2,1,0:T(2,128)(2,1)S(1)}, bf16[18,6,2,192]{3,2,1,0:T(2,128)(2,1)S(1)}, u32[]{:S(2)}, u32[]{:S(2)}) collective-permute-start(bf16[18,6,2,192]{3,2,1,0:T(2,128)(2,1)S(1)} %get-tuple-element.46), channel_id=1, source_target_pairs={{0,4},{4,0},{8,12},{12,8},{16,20},{20,16},{24,28},{28,24},{1,5},{5... | collective-permute-start | bytes 248840 | tf_op jit(solution)/shard_map/ppermute | solution.py:39
  16.8 6.5 %collective-permute-start.3 = (bf16[18,6,2,192]{3,2,1,0:T(2,128)(2,1)S(1)}, bf16[18,6,2,192]{3,2,1,0:T(2,128)(2,1)S(1)}, u32[]{:S(2)}, u32[]{:S(2)}) collective-permute-start(bf16[18,6,2,192]{3,2,1,0:T(2,128)(2,1)S(1)} %get-tuple-element.45), channel_id=1, source_target_pairs={{4,8},{8,4},{12,16},{16,12},{20,24},{24,20},{28,0},{0,28},{5,9},{9... | collective-permute-start | bytes 248840 | tf_op jit(solution)/shard_map/ppermute | solution.py:39

commit v19 on v18

--- a/solution.py
+++ b/solution.py
@@ -228,12 +228,13 @@
     return beside + [(3 * i + j, 0) for i, j in windows if i != 1 and j != 1]
 
 
-def scattered(recv_ref, first_ref, lift_ref, plan, lon_cells):
+def scattered(recv_ref, first_ref, table_ref, lift_ref, plan, lon_cells):
     sources, _, capacity, _ = recv_ref.shape
     width = first_ref.shape[1]
     chunk = min(CHUNK, sources)
     slots = chunk * capacity
-    first, lift = first_ref[...], lift_ref[...]
+    table = below(*[table_ref[...].astype(F32)] * (LANES // INSTR)).astype(BF16)
+    first, lift = below(first_ref[...], table), lift_ref[...]
     lane = lax.broadcasted_iota(jnp.int32, (16, LANES), 1)
     sub = lax.broadcasted_iota(jnp.int32, (16, LANES), 0)
     weigh = jnp.where(lane == ROWS + sub, float(lon_cells * LEV), 0.0)
@@ -285,7 +286,7 @@
     return sums
 
 
-def prepare_kernel(plan, back_ref, first_ref, table_ref, attn_ref, rows_ref, both_ref, parts_ref):
+def prepare_kernel(plan, back_ref, attn_ref, rows_ref, parts_ref):
     width = back_ref.shape[3]
     pieces = []
     for top, high, left, wide in plan[4]:
@@ -295,14 +296,11 @@
             piece = below(piece, jnp.zeros((padded(count) - count, width), F32))
         pieces.append(piece)
     rows_ref[...] = below(*pieces)
-    table = below(*[table_ref[...].astype(F32)] * (LANES // INSTR)).astype(BF16)
-    both_ref[:LANES, :] = first_ref[...]
-    both_ref[LANES:, :] = table
     for n in range(3):
         parts_ref[n] = attn_ref[:, n * width : (n + 1) * width]
 
 
-def prepared(plan, background, input_weight, instrument_table, attn_weight):
+def prepared(plan, background, attn_weight):
     width = background.shape[3]
     rows = sum(padded(tokens_of(part)) for part in plan[4])
     vmem = pl.BlockSpec(memory_space=pltpu.VMEM)
@@ -310,14 +308,13 @@
         functools.partial(prepare_kernel, plan),
         out_shape=[
             jax.ShapeDtypeStruct((rows, width), F32),
-            jax.ShapeDtypeStruct((2 * LANES, width), BF16),
             jax.ShapeDtypeStruct((3, width, width), BF16),
         ],
-        in_specs=[vmem] * 4,
-        out_specs=[vmem] * 3,
+        in_specs=[vmem] * 2,
+        out_specs=[vmem] * 2,
         compiler_params=pltpu.CompilerParams(vmem_limit_bytes=LIMIT),
         cost_estimate=pl.CostEstimate(flops=10**9, bytes_accessed=10**6, transcendentals=0),
-    )(background, input_weight, instrument_table, attn_weight)
+    )(background, attn_weight)
 
 
 def normed_of(plan, entries, sums, borders, gain):
@@ -418,7 +415,7 @@
     mixed = below(*mixed).astype(BF16)
 
     after = (latent + dot(mixed, mix_ref[...])).astype(BF16).astype(F32)
-    normed_two = normalise(after, gain_ref[...].astype(F32)).astype(BF16)
+    normed_two = normalise(after, gain_ref[...].astype(F32).reshape(1, -1)).astype(BF16)
     hidden = gelu(dot(normed_two, up_ref[...]).astype(BF16))
     result = after + dot(hidden, down_ref[...])
     for begin, (i, j) in zip(begins, places):
@@ -444,13 +441,14 @@
     north_ref,
     south_ref,
     rows_ref,
-    both_ref,
+    first_ref,
+    table_ref,
     lift_ref,
     gain_one_ref,
     *refs,
 ):
     *weights, out_ref, rest_ref, latent_ref, normed_ref = refs
-    sums = scattered(recv_ref, both_ref, lift_ref, plan, lon_cells)
+    sums = scattered(recv_ref, first_ref, table_ref, lift_ref, plan, lon_cells)
 
     def sums_of(entries):
         pieces = []
@@ -460,7 +458,7 @@
         return below(*pieces)
 
     borders = (rows_ref, north_ref, south_ref, None, None, lat_cells)
-    gain = gain_one_ref[...].astype(F32)
+    gain = gain_one_ref[...].astype(F32).reshape(1, -1)
     entries = near_entries(MIDDLE)
     latent, normed, spans = normed_of(plan, entries, sums_of(entries), borders, gain)
 
@@ -501,7 +499,7 @@
         near[tile, number] = start
         start += padded(tokens_of(plan[tile][number]))
     borders = (None, None, None, west_ref, east_ref, lat_cells)
-    gain = gain_one_ref[...].astype(F32)
+    gain = gain_one_ref[...].astype(F32).reshape(1, -1)
     _, far, spans = normed_of(plan, far_entries(SIDES), rest_ref[...], borders, gain)
 
     def piece_of(tile, number):
@@ -553,8 +551,8 @@
     received = lax.all_to_all(sent, ("lon", "lat"), split_axis=0, concat_axis=0, tiled=True)
     north, south = before_and_after(swapped(up, down, "lat", wraps=False), "lat")
 
-    later, input_weight, instrument_table, attn_weight, down_weight, _ = lax.optimization_barrier(
-        (background, input_weight, instrument_table, attn_weight, down_weight, up)
+    later, input_weight, attn_weight, down_weight, _ = lax.optimization_barrier(
+        (background, input_weight, attn_weight, down_weight, up)
     )
 
     def columns(low, end):
@@ -563,15 +561,15 @@
     got = swapped(columns(0, HLON), columns(lon_cells - HLON, lon_cells), "lon", wraps=True)
 
     plan = rectangles(lat_cells, lon_cells)
-    rows, both, parts = prepared(plan, later, input_weight, instrument_table, attn_weight)
+    rows, parts = prepared(plan, later, attn_weight)
     lat = lax.axis_index("lat")
     scalars = jnp.stack([lat == 0, lat < 0, lat == tiles_lat - 1]).astype(jnp.int32)
 
     def rows_in(entries):
         return sum(padded(tokens_of(plan[tile][number])) for tile, number in entries)
 
-    gain_one = first_gain.reshape(1, width)
-    weights = [parts, mix_weight, second_gain.reshape(1, width), up_weight, down_weight]
+    gain_one = first_gain
+    weights = [parts, mix_weight, second_gain, up_weight, down_weight]
     smem = pl.BlockSpec(memory_space=pltpu.SMEM)
     vmem = pl.BlockSpec(memory_space=pltpu.VMEM)
     anywhere = pl.BlockSpec(memory_space=pl.ANY)
@@ -584,14 +582,26 @@
             jax.ShapeDtypeStruct((own_rows(plan, SIDES), width), F32),
             jax.ShapeDtypeStruct((rows_in(near_entries(SIDES)), width), F32),
         ],
-        in_specs=[smem] + [vmem] * (7 + len(weights)),
+        in_specs=[smem] + [vmem] * (8 + len(weights)),
         out_specs=[vmem] * 4,
         compiler_params=params,
         cost_estimate=pl.CostEstimate(
             flops=4 * 10**9, bytes_accessed=4 * 10**6, transcendentals=10**6
         ),
-    )(scalars, received, north, south, rows, both, lift_weight, gain_one, *weights)
-    rest, *got = lax.optimization_barrier((rest, *got))
+    )(
+        scalars,
+        received,
+        north,
+        south,
+        rows,
+        input_weight,
+        instrument_table,
+        lift_weight,
+        gain_one,
+        *weights,
+    )
+    rest, *got = lax.optimization_barrier((rest, *got[::-1]))
+    got = got[::-1]
     west, east = before_and_after(got, "lon")
     return pl.pallas_call(
         functools.partial(side_kernel, plan, lat_cells),

time: 27.8 us -> 27.4 us (0.986)
  the two profiles are of different devices: /device:TPU:8 before, /device:TPU:0 now
where the time goes in v19:
time: 27.4 us; the launch traced here: 27 us
  starting transfers between devices  11.5 us (42%)
  Pallas kernels  9.81 us (36%)
  waiting for transfers between devices  2.87 us (10%)
  local copies, waits for them, and re-layouts  1.89 us (7%)
  other arithmetic  0.66 us (2%)
    all_to_all x1, starting transfers between devices, local(): lax.all_to_all(sent, ('lon', 'lat'), split_axis=0, concat_axis=0, tiled=T...  7.3 us
    ppermute x4, starting transfers between devices, swapped(): got.append(lax.ppermute(mine, axis, pairs))  4.15 us
    pallas_call x1, Pallas kernels, local(): pl.pallas_call(functools.partial(side_kernel, plan, lat_cells), out_shape...  3.98 us
    pallas_call x1, Pallas kernels, local(): pl.pallas_call(functools.partial(middle_kernel, plan, lat_cells, lon_cell...  3.92 us
    ppermute x4, waiting for transfers between devices, swapped(): got.append(lax.ppermute(mine, axis, pairs))  2.87 us
    pallas_call x1, Pallas kernels, packed(): pl.pallas_call(pack_kernel, out_shape=[jax.ShapeDtypeStruct(shape, BF16),...  1.75 us
    unnamed x24, local copies, waits for them, and re-layouts  1.45 us
  transfers between devices with their start and end apart: 5, of which 2 were waited for; matrix products, arithmetic and copies ran while one was open for 3% of the time, Pallas kernels for 15%

profile of v19, /device:TPU:0, one launch (start us, length us, event | category | flops | bytes accessed | tf_op | source)
XLA Modules:
  0.0 27.0 jit_solution(17328015441071297584)
XLA Ops:
  0.0 1.8 %shard_map.136 = (bf16[8,4,10,2,128]{4,3,2,1,0:T(2,128)(2,1)}, bf16[3,24,2,192]{3,2,1,0:T(2,128)(2,1)}, bf16[3,24,2,192]{3,2,1,0:T(2,128)(2,1)}) custom-call(bf16[8,4,2,128]{3,2,1,0:T(2,128)(2,1)} %values_ref.1, s32[8,8]{1,0:T(8,128)} %bitcast.30, s32[8,8]{1,0:T(8,128)} %bitcast.31, s32[4,8]{1,0:T(4,128)} %bitcast.32, bf16[12,24,2,192]{3,2,1,0:T(2,128)(2,1)} %back_ref.2), custom_call_target="tpu_custom_call" | custom-call | flops 20000000000 | bytes 1000000 | tf_op jit(solution)/shard_map/pallas_call | solution.py:184
  1.8 0.0 copy-start.9
  1.8 0.0 copy-start.10
  1.8 7.3 %all-to-all-start = ((bf16[32,10,2,128]{3,2,1,0:T(2,128)(2,1)}), bf16[32,10,2,128]{3,2,1,0:T(2,128)(2,1)S(1)}, u32[]{:S(2)}, u32[]{:S(2)}) async-start(bf16[32,10,2,128]{3,2,1,0:T(2,128)(2,1)} %bitcast.23), calls=%async_computation | async-start | bytes 327680 | tf_op jit(solution)/shard_map/all_to_all | solution.py:551
  9.1 0.0 copy-start.8
  9.1 0.0 copy-done.9
  9.1 0.0 copy-done.10
  9.1 0.0 copy-start.11
  9.2 1.8 %collective-permute-start.1 = (bf16[3,24,2,192]{3,2,1,0:T(2,128)(2,1)S(1)}, bf16[3,24,2,192]{3,2,1,0:T(2,128)(2,1)S(1)}, u32[]{:S(2)}, u32[]{:S(2)}) collective-permute-start(bf16[3,24,2,192]{3,2,1,0:T(2,128)(2,1)S(1)} %bitcast.27), channel_id=1, source_target_pairs={{0,1},{1,0},{2,3},{3,2},{4,5},{5,4},{6,7},{7,6},{8,9},{9,8},{10,11... | collective-permute-start | bytes 165896 | tf_op jit(solution)/shard_map/ppermute | solution.py:39
  11.0 0.7 %collective-permute-start = (bf16[3,24,2,192]{3,2,1,0:T(2,128)(2,1)S(1)}, bf16[3,24,2,192]{3,2,1,0:T(2,128)(2,1)S(1)}, u32[]{:S(2)}, u32[]{:S(2)}) collective-permute-start(bf16[3,24,2,192]{3,2,1,0:T(2,128)(2,1)S(1)} %bitcast.25), channel_id=1, source_target_pairs={{1,2},{2,1},{5,6},{6,5},{9,10},{10,9},{13,14},{14,13},{17,18},{18,... | collective-permute-start | bytes 165896 | tf_op jit(solution)/shard_map/ppermute | solution.py:39
  11.7 0.0 copy-done.11
  11.7 0.1 copy.15.first_ref
  11.8 0.0 copy-done.8
  11.8 0.0 copy-start
  11.8 0.2 copy.16.refs_4_
  12.0 0.0 copy-start.2
  12.0 0.8 %copy-done = bf16[12,24,2,192]{3,2,1,0:T(2,128)(2,1)S(1)} copy-done((bf16[12,24,2,192]{3,2,1,0:T(2,128)(2,1)S(1)}, bf16[12,24,2,192]{3,2,1,0:T(2,128)(2,1)}, u32[]{:S(2)}) %copy-start) | copy-done | bytes 221208
  12.8 0.1 fusion
  12.9 0.1 add_convert_fusion.scalars_ref
  13.0 0.0 copy-done.2
  13.0 0.2 shard_map.137
  13.1 2.8 %collective-permute-done.1 = bf16[3,24,2,192]{3,2,1,0:T(2,128)(2,1)S(1)} collective-permute-done((bf16[3,24,2,192]{3,2,1,0:T(2,128)(2,1)S(1)}, bf16[3,24,2,192]{3,2,1,0:T(2,128)(2,1)S(1)}, u32[]{:S(2)}, u32[]{:S(2)}) %collective-permute-start.1) | collective-permute-done | bytes 55328 | tf_op jit(solution)/shard_map/ppermute | solution.py:39
  16.0 0.0 collective-permute-done
  16.0 0.0 copy-start.1
  16.0 0.1 fusion.1
  16.1 0.0 copy-start.3
  16.1 0.0 copy-start.4
  16.1 0.4 %broadcast_select_fusion.2 = (bf16[18,6,2,192]{3,2,1,0:T(2,128)(2,1)S(1)}, bf16[18,6,2,192]{3,2,1,0:T(2,128)(2,1)S(1)}) fusion(pred[]{:T(512)S(6)} %eq.22, bf16[3,6,2,192]{3,2,1,0:T(2,128)(2,1)S(1)} %get-tuple-element.51, bf16[12,6,2,192]{3,2,1,0:T(2,128)(2,1)S(1)} %get-tuple-element.38, bf16[3,6,2,192]{3,2,1,0:T(2,128)(2,1)S(1)} %get-tuple-element.48, ...), kind=kLoop, calls=%fused_computation.2 | loop fusion | flops 248832 | bytes 331777 | tf_op jit(solution)/shard_map/jit(_where)/select_n | solution.py:33
  16.5 0.0 copy-start.5
  16.5 1.2 %collective-permute-start.2 = (bf16[18,6,2,192]{3,2,1,0:T(2,128)(2,1)S(1)}, bf16[18,6,2,192]{3,2,1,0:T(2,128)(2,1)S(1)}, u32[]{:S(2)}, u32[]{:S(2)}) collective-permute-start(bf16[18,6,2,192]{3,2,1,0:T(2,128)(2,1)S(1)} %get-tuple-element.42), channel_id=1, source_target_pairs={{4,8},{8,4},{12,16},{16,12},{20,24},{24,20},{28,0},{0,28},{5,9},{9... | collective-permute-start | bytes 248840 | tf_op jit(solution)/shard_map/ppermute | solution.py:39
  17.7 0.4 %collective-permute-start.3 = (bf16[18,6,2,192]{3,2,1,0:T(2,128)(2,1)S(1)}, bf16[18,6,2,192]{3,2,1,0:T(2,128)(2,1)S(1)}, u32[]{:S(2)}, u32[]{:S(2)}) collective-permute-start(bf16[18,6,2,192]{3,2,1,0:T(2,128)(2,1)S(1)} %get-tuple-element.41), channel_id=1, source_target_pairs={{0,4},{4,0},{8,12},{12,8},{16,20},{20,16},{24,28},{28,24},{1,5},{5... | collective-permute-start | bytes 248840 | tf_op jit(solution)/shard_map/ppermute | solution.py:39
  18.1 0.0 all-to-all-done.recv_ref
  18.1 0.0 copy-start.6
  18.1 0.0 copy-start.7
  18.1 0.0 copy-done.1
  18.2 0.0 copy-done.3
  18.2 0.0 copy-done.4
  18.2 0.0 copy-done.5
  18.2 0.6 %copy-done.6 = bf16[192]{0:T(256)(128)(2,1)S(1)} copy-done((bf16[192]{0:T(256)(128)(2,1)S(1)}, bf16[192]{0:T(256)(128)(2,1)}, u32[]{:S(2)}) %copy-start.6) | copy-done | bytes 408
  18.8 0.0 copy-done.7
  18.8 3.9 %shard_map.138 = (bf16[12,12,2,192]{3,2,1,0:T(2,128)(2,1)S(1)}, f32[464,256]{1,0:T(8,128)S(1)}, f32[304,192]{1,0:T(8,128)S(1)}, f32[464,192]{1,0:T(8,128)S(1)}) custom-call(s32[3]{0:T(128)S(1)} %add_convert_fusion.scalars_ref, bf16[32,10,2,128]{3,2,1,0:T(2,128)(2,1)S(1)} %all-to-all-done.recv_ref, bf16[3,24,2,192]{3,2,1,0:T(2,128)(2,1)S(1)} %bitcast.22, ...), custom_call_target="tpu_custom_call" | custom-call | flops 4000000000 | bytes 4000000 | tf_op jit(solution)/shard_map/pallas_call | solution.py:577
  22.7 0.1 collective-permute-done.2
  22.8 0.0 collective-permute-done.3
  22.8 0.2 broadcast_select_fusion
  23.0 4.0 %shard_map.139 = bf16[12,24,2,192]{3,2,1,0:T(2,128)(2,1)} custom-call(s32[3]{0:T(128)S(1)} %add_convert_fusion.scalars_ref, f32[464,256]{1,0:T(8,128)S(1)} %get-tuple-element.31.rest_ref, f32[304,192]{1,0:T(8,128)S(1)} %get-tuple-element.32.latent_ref, f32[464,192]{1,0:T(8,128)S(1)} %get-tuple-element.33.normed_ref, ...), custom_call_target="tpu_custom_call" | custom-call | flops 3000000000 | bytes 4000000 | tf_op jit(solution)/shard_map/pallas_call | solution.py:606
  (2 shorter events, 0.0 us)
Async XLA Ops:
  1.8 7.4 %copy-start.9 = (bf16[3,24,2,192]{3,2,1,0:T(2,128)(2,1)S(1)}, bf16[3,24,2,192]{3,2,1,0:T(2,128)(2,1)}, u32[]{:S(2)}) copy-start(bf16[3,24,2,192]{3,2,1,0:T(2,128)(2,1)} %get-tuple-element.22) | copy-start | bytes 165892
  1.8 7.4 %copy-start.10 = (bf16[3,24,2,192]{3,2,1,0:T(2,128)(2,1)S(1)}, bf16[3,24,2,192]{3,2,1,0:T(2,128)(2,1)}, u32[]{:S(2)}) copy-start(bf16[3,24,2,192]{3,2,1,0:T(2,128)(2,1)} %get-tuple-element.23) | copy-start | bytes 165892
  1.8 16.4 %all-to-all-start = ((bf16[32,10,2,128]{3,2,1,0:T(2,128)(2,1)}), bf16[32,10,2,128]{3,2,1,0:T(2,128)(2,1)S(1)}, u32[]{:S(2)}, u32[]{:S(2)}) async-start(bf16[32,10,2,128]{3,2,1,0:T(2,128)(2,1)} %bitcast.23), calls=%async_computation | async-start | bytes 327680 | tf_op jit(solution)/shard_map/all_to_all | solution.py:551
  9.1 2.7 %copy-start.8 = (bf16[768,192]{0,1:T(8,128)(2,1)S(1)}, bf16[768,192]{0,1:T(8,128)(2,1)}, u32[]{:S(2)}) copy-start(bf16[768,192]{0,1:T(8,128)(2,1)} %param.27) | copy-start | bytes 884740
  9.1 2.6 %copy-start.11 = (bf16[128,192]{0,1:T(8,128)(2,1)S(1)}, bf16[128,192]{0,1:T(8,128)(2,1)}, u32[]{:S(2)}) copy-start(bf16[128,192]{0,1:T(8,128)(2,1)} %param.19) | copy-start | bytes 147460
  9.2 6.8 %collective-permute-start.1 = (bf16[3,24,2,192]{3,2,1,0:T(2,128)(2,1)S(1)}, bf16[3,24,2,192]{3,2,1,0:T(2,128)(2,1)S(1)}, u32[]{:S(2)}, u32[]{:S(2)}) collective-permute-start(bf16[3,24,2,192]{3,2,1,0:T(2,128)(2,1)S(1)} %bitcast.27), channel_id=1, source_target_pairs={{0,1},{1,0},{2,3},{3,2},{4,5},{5,4},{6,7},{7,6},{8,9},{9,8},{10,11... | collective-permute-start | bytes 165896 | tf_op jit(solution)/shard_map/ppermute | solution.py:39
  11.0 5.0 %collective-permute-start = (bf16[3,24,2,192]{3,2,1,0:T(2,128)(2,1)S(1)}, bf16[3,24,2,192]{3,2,1,0:T(2,128)(2,1)S(1)}, u32[]{:S(2)}, u32[]{:S(2)}) collective-permute-start(bf16[3,24,2,192]{3,2,1,0:T(2,128)(2,1)S(1)} %bitcast.25), channel_id=1, source_target_pairs={{1,2},{2,1},{5,6},{6,5},{9,10},{10,9},{13,14},{14,13},{17,18},{18,... | collective-permute-start | bytes 165896 | tf_op jit(solution)/shard_map/ppermute | solution.py:39
  11.8 1.0 %copy-start = (bf16[12,24,2,192]{3,2,1,0:T(2,128)(2,1)S(1)}, bf16[12,24,2,192]{3,2,1,0:T(2,128)(2,1)}, u32[]{:S(2)}) copy-start(bf16[12,24,2,192]{3,2,1,0:T(2,128)(2,1)} %back_ref.2) | copy-start | bytes 663556
  12.0 1.0 %copy-start.2 = (bf16[192,576]{1,0:T(8,128)(2,1)S(1)}, bf16[192,576]{1,0:T(8,128)(2,1)}, u32[]{:S(2)}) copy-start(bf16[192,576]{1,0:T(8,128)(2,1)} %attn_ref) | copy-start | bytes 663556
  16.0 2.2 %copy-start.1 = (bf16[192,768]{1,0:T(8,128)(2,1)S(1)}, bf16[192,768]{1,0:T(8,128)(2,1)}, u32[]{:S(2)}) copy-start(bf16[192,768]{1,0:T(8,128)(2,1)} %refs_3_.3) | copy-start | bytes 884740
  16.1 2.1 %copy-start.3 = (bf16[192,384]{1,0:T(8,128)(2,1)S(1)}, bf16[192,384]{1,0:T(8,128)(2,1)}, u32[]{:S(2)}) copy-start(bf16[192,384]{1,0:T(8,128)(2,1)} %lift_ref.1) | copy-start | bytes 442372
  16.1 2.1 %copy-start.4 = (bf16[192,192]{1,0:T(8,128)(2,1)S(1)}, bf16[192,192]{1,0:T(8,128)(2,1)}, u32[]{:S(2)}) copy-start(bf16[192,192]{1,0:T(8,128)(2,1)} %refs_1_.3) | copy-start | bytes 221188
  16.5 1.7 %copy-start.5 = (bf16[8,192]{1,0:T(8,128)(2,1)S(1)}, bf16[8,192]{1,0:T(8,128)(2,1)}, u32[]{:S(2)}) copy-start(bf16[8,192]{1,0:T(8,128)(2,1)} %table_ref.1) | copy-start | bytes 9220
  16.5 6.3 %collective-permute-start.2 = (bf16[18,6,2,192]{3,2,1,0:T(2,128)(2,1)S(1)}, bf16[18,6,2,192]{3,2,1,0:T(2,128)(2,1)S(1)}, u32[]{:S(2)}, u32[]{:S(2)}) collective-permute-start(bf16[18,6,2,192]{3,2,1,0:T(2,128)(2,1)S(1)} %get-tuple-element.42), channel_id=1, source_target_pairs={{4,8},{8,4},{12,16},{16,12},{20,24},{24,20},{28,0},{0,28},{5,9},{9... | collective-permute-start | bytes 248840 | tf_op jit(solution)/shard_map/ppermute | solution.py:39
  17.7 5.1 %collective-permute-start.3 = (bf16[18,6,2,192]{3,2,1,0:T(2,128)(2,1)S(1)}, bf16[18,6,2,192]{3,2,1,0:T(2,128)(2,1)S(1)}, u32[]{:S(2)}, u32[]{:S(2)}) collective-permute-start(bf16[18,6,2,192]{3,2,1,0:T(2,128)(2,1)S(1)} %get-tuple-element.41), channel_id=1, source_target_pairs={{0,4},{4,0},{8,12},{12,8},{16,20},{20,16},{24,28},{28,24},{1,5},{5... | collective-permute-start | bytes 248840 | tf_op jit(solution)/shard_map/ppermute | solution.py:39
  18.1 0.7 %copy-start.6 = (bf16[192]{0:T(256)(128)(2,1)S(1)}, bf16[192]{0:T(256)(128)(2,1)}, u32[]{:S(2)}) copy-start(bf16[192]{0:T(256)(128)(2,1)} %gain_one_ref.3) | copy-start | bytes 1156
  18.1 0.7 %copy-start.7 = (bf16[192]{0:T(256)(128)(2,1)S(1)}, bf16[192]{0:T(256)(128)(2,1)}, u32[]{:S(2)}) copy-start(bf16[192]{0:T(256)(128)(2,1)} %refs_2_.3) | copy-start | bytes 1156

commit v20 on v19

--- a/solution.py
+++ b/solution.py
@@ -185,7 +185,7 @@
         pack_kernel,
         out_shape=[jax.ShapeDtypeStruct(shape, BF16), across, across],
         in_specs=[anywhere] * 5,
-        out_specs=[pl.BlockSpec(memory_space=pltpu.VMEM)] * 3,
+        out_specs=[pl.BlockSpec(memory_space=pltpu.VMEM), anywhere, anywhere],
         scratch_shapes=[
             pltpu.VMEM(record_values.shape, BF16),
             ints,
@@ -286,7 +286,9 @@
     return sums
 
 
-def prepare_kernel(plan, back_ref, attn_ref, rows_ref, parts_ref):
+def prepare_kernel(
+    plan, back_ref, attn_ref, one_ref, two_ref, rows_ref, parts_ref, gain_one_ref, gain_two_ref
+):
     width = back_ref.shape[3]
     pieces = []
     for top, high, left, wide in plan[4]:
@@ -296,11 +298,13 @@
             piece = below(piece, jnp.zeros((padded(count) - count, width), F32))
         pieces.append(piece)
     rows_ref[...] = below(*pieces)
+    for gain, ref in ((one_ref, gain_one_ref), (two_ref, gain_two_ref)):
+        ref[...] = jnp.broadcast_to(gain[...].astype(F32).reshape(1, width), ref.shape)
     for n in range(3):
         parts_ref[n] = attn_ref[:, n * width : (n + 1) * width]
 
 
-def prepared(plan, background, attn_weight):
+def prepared(plan, background, attn_weight, first_gain, second_gain):
     width = background.shape[3]
     rows = sum(padded(tokens_of(part)) for part in plan[4])
     vmem = pl.BlockSpec(memory_space=pltpu.VMEM)
@@ -309,12 +313,14 @@
         out_shape=[
             jax.ShapeDtypeStruct((rows, width), F32),
             jax.ShapeDtypeStruct((3, width, width), BF16),
+            jax.ShapeDtypeStruct((8, width), F32),
+            jax.ShapeDtypeStruct((8, width), F32),
         ],
-        in_specs=[vmem] * 2,
-        out_specs=[vmem] * 2,
+        in_specs=[vmem] * 4,
+        out_specs=[vmem] * 4,
         compiler_params=pltpu.CompilerParams(vmem_limit_bytes=LIMIT),
         cost_estimate=pl.CostEstimate(flops=10**9, bytes_accessed=10**6, transcendentals=0),
-    )(background, attn_weight)
+    )(background, attn_weight, first_gain, second_gain)
 
 
 def normed_of(plan, entries, sums, borders, gain):
@@ -415,9 +421,12 @@
     mixed = below(*mixed).astype(BF16)
 
     after = (latent + dot(mixed, mix_ref[...])).astype(BF16).astype(F32)
-    normed_two = normalise(after, gain_ref[...].astype(F32).reshape(1, -1)).astype(BF16)
-    hidden = gelu(dot(normed_two, up_ref[...]).astype(BF16))
-    result = after + dot(hidden, down_ref[...])
+    normed_two = normalise(after, gain_ref[:1, :]).astype(BF16)
+    cuts = range(0, up_ref.shape[1], PAD)
+    hidden = [dot(normed_two, up_ref[:, at : at + PAD]).astype(BF16) for at in cuts]
+    result = after
+    for at, chunk in zip(cuts, hidden):
+        result = result + dot(gelu(chunk), down_ref[at : at + PAD, :])
     for begin, (i, j) in zip(begins, places):
         part = plan[4][3 * i + j]
         piece = result[begin : begin + tokens_of(part)].astype(BF16)
@@ -458,7 +467,7 @@
         return below(*pieces)
 
     borders = (rows_ref, north_ref, south_ref, None, None, lat_cells)
-    gain = gain_one_ref[...].astype(F32).reshape(1, -1)
+    gain = gain_one_ref[:1, :]
     entries = near_entries(MIDDLE)
     latent, normed, spans = normed_of(plan, entries, sums_of(entries), borders, gain)
 
@@ -499,7 +508,7 @@
         near[tile, number] = start
         start += padded(tokens_of(plan[tile][number]))
     borders = (None, None, None, west_ref, east_ref, lat_cells)
-    gain = gain_one_ref[...].astype(F32).reshape(1, -1)
+    gain = gain_one_ref[:1, :]
     _, far, spans = normed_of(plan, far_entries(SIDES), rest_ref[...], borders, gain)
 
     def piece_of(tile, number):
@@ -551,8 +560,10 @@
     received = lax.all_to_all(sent, ("lon", "lat"), split_axis=0, concat_axis=0, tiled=True)
     north, south = before_and_after(swapped(up, down, "lat", wraps=False), "lat")
 
-    later, input_weight, attn_weight, down_weight, _ = lax.optimization_barrier(
-        (background, input_weight, attn_weight, down_weight, up)
+    later, input_weight, attn_weight, down_weight, first_gain, second_gain, _ = (
+        lax.optimization_barrier(
+            (background, input_weight, attn_weight, down_weight, first_gain, second_gain, up)
+        )
     )
 
     def columns(low, end):
@@ -561,15 +572,16 @@
     got = swapped(columns(0, HLON), columns(lon_cells - HLON, lon_cells), "lon", wraps=True)
 
     plan = rectangles(lat_cells, lon_cells)
-    rows, parts = prepared(plan, later, attn_weight)
+    rows, parts, gain_one, gain_two = prepared(
+        plan, later, attn_weight, first_gain, second_gain
+    )
     lat = lax.axis_index("lat")
     scalars = jnp.stack([lat == 0, lat < 0, lat == tiles_lat - 1]).astype(jnp.int32)
 
     def rows_in(entries):
         return sum(padded(tokens_of(plan[tile][number])) for tile, number in entries)
 
-    gain_one = first_gain
-    weights = [parts, mix_weight, second_gain, up_weight, down_weight]
+    weights = [parts, mix_weight, gain_two, up_weight, down_weight]
     smem = pl.BlockSpec(memory_space=pltpu.SMEM)
     vmem = pl.BlockSpec(memory_space=pltpu.VMEM)
     anywhere = pl.BlockSpec(memory_space=pl.ANY)

time: 27.4 us -> 31.8 us (1.16)
  Pallas kernels: 9.81 us -> 14.4 us
    pallas_call x1, Pallas kernels: 1.75 us -> 6.29 us  [packed(): pl.pallas_call(pack_kernel, out_shape=[jax.ShapeDtypeStruct(shape, BF16),...]
  transfers between devices with their start and end apart: 5 -> 5, of which waited for: 2 -> 2; matrix products, arithmetic and copies ran while one was open for 3% -> 3% of each run, Pallas kernels for 15% -> 13%
where the time goes in v20:
time: 31.8 us; the launch traced here: 31.5 us
  Pallas kernels  14.4 us (45%)
  starting transfers between devices  11.5 us (36%)
  waiting for transfers between devices  2.68 us (8%)
  local copies, waits for them, and re-layouts  2.07 us (7%)
  other arithmetic  0.66 us (2%)
    all_to_all x1, starting transfers between devices, local(): lax.all_to_all(sent, ('lon', 'lat'), split_axis=0, concat_axis=0, tiled=T...  7.3 us
    pallas_call x1, Pallas kernels, packed(): pl.pallas_call(pack_kernel, out_shape=[jax.ShapeDtypeStruct(shape, BF16),...  6.29 us
    ppermute x4, starting transfers between devices, swapped(): got.append(lax.ppermute(mine, axis, pairs))  4.15 us
    pallas_call x1, Pallas kernels, local(): pl.pallas_call(functools.partial(side_kernel, plan, lat_cells), out_shape...  3.97 us
    pallas_call x1, Pallas kernels, local(): pl.pallas_call(functools.partial(middle_kernel, plan, lat_cells, lon_cell...  3.92 us
    ppermute x4, waiting for transfers between devices, swapped(): got.append(lax.ppermute(mine, axis, pairs))  2.68 us
    unnamed x24, local copies, waits for them, and re-layouts  1.63 us
  transfers between devices with their start and end apart: 5, of which 2 were waited for; matrix products, arithmetic and copies ran while one was open for 3% of the time, Pallas kernels for 13%

profile of v20, /device:TPU:0, one launch (start us, length us, event | category | flops | bytes accessed | tf_op | source)
XLA Modules:
  0.0 31.5 jit_solution(716847156360875486)
XLA Ops:
  0.0 6.3 %shard_map.136 = (bf16[8,4,10,2,128]{4,3,2,1,0:T(2,128)(2,1)}, bf16[3,24,2,192]{3,2,1,0:T(2,128)(2,1)}, bf16[3,24,2,192]{3,2,1,0:T(2,128)(2,1)}) custom-call(bf16[8,4,2,128]{3,2,1,0:T(2,128)(2,1)} %values_ref.1, s32[8,8]{1,0:T(8,128)} %bitcast.30, s32[8,8]{1,0:T(8,128)} %bitcast.31, s32[4,8]{1,0:T(4,128)} %bitcast.32, bf16[12,24,2,192]{3,2,1,0:T(2,128)(2,1)} %back_ref.2), custom_call_target="tpu_custom_call" | custom-call | flops 20000000000 | bytes 1000000 | tf_op jit(solution)/shard_map/pallas_call | solution.py:184
  6.3 0.0 copy-start.9
  6.3 0.0 copy-start.10
  6.3 7.3 %all-to-all-start = ((bf16[32,10,2,128]{3,2,1,0:T(2,128)(2,1)}), bf16[32,10,2,128]{3,2,1,0:T(2,128)(2,1)S(1)}, u32[]{:S(2)}, u32[]{:S(2)}) async-start(bf16[32,10,2,128]{3,2,1,0:T(2,128)(2,1)} %bitcast.23), calls=%async_computation | async-start | bytes 327680 | tf_op jit(solution)/shard_map/all_to_all | solution.py:560
  13.6 0.0 copy-start.8
  13.7 0.0 copy-done.9
  13.7 0.0 copy-done.10
  13.7 0.0 copy-start.11
  13.7 1.8 %collective-permute-start.1 = (bf16[3,24,2,192]{3,2,1,0:T(2,128)(2,1)S(1)}, bf16[3,24,2,192]{3,2,1,0:T(2,128)(2,1)S(1)}, u32[]{:S(2)}, u32[]{:S(2)}) collective-permute-start(bf16[3,24,2,192]{3,2,1,0:T(2,128)(2,1)S(1)} %bitcast.27), channel_id=1, source_target_pairs={{0,1},{1,0},{2,3},{3,2},{4,5},{5,4},{6,7},{7,6},{8,9},{9,8},{10,11... | collective-permute-start | bytes 165896 | tf_op jit(solution)/shard_map/ppermute | solution.py:39
  15.5 0.7 %collective-permute-start = (bf16[3,24,2,192]{3,2,1,0:T(2,128)(2,1)S(1)}, bf16[3,24,2,192]{3,2,1,0:T(2,128)(2,1)S(1)}, u32[]{:S(2)}, u32[]{:S(2)}) collective-permute-start(bf16[3,24,2,192]{3,2,1,0:T(2,128)(2,1)S(1)} %bitcast.25), channel_id=1, source_target_pairs={{1,2},{2,1},{5,6},{6,5},{9,10},{10,9},{13,14},{14,13},{17,18},{18,... | collective-permute-start | bytes 165896 | tf_op jit(solution)/shard_map/ppermute | solution.py:39
  16.2 0.0 copy-done.11
  16.2 0.1 copy.15.first_ref
  16.3 0.0 copy-done.8
  16.4 0.0 copy-start
  16.4 0.2 copy.16.refs_4_
  16.5 0.0 copy-start.2
  16.6 0.8 %copy-done = bf16[12,24,2,192]{3,2,1,0:T(2,128)(2,1)S(1)} copy-done((bf16[12,24,2,192]{3,2,1,0:T(2,128)(2,1)S(1)}, bf16[12,24,2,192]{3,2,1,0:T(2,128)(2,1)}, u32[]{:S(2)}) %copy-start) | copy-done | bytes 221208
  17.3 0.1 fusion
  17.4 0.0 copy-start.6
  17.4 0.0 copy-start.7
  17.5 0.1 add_convert_fusion.scalars_ref
  17.5 0.0 copy-done.2
  17.5 0.6 %copy-done.6 = bf16[192]{0:T(256)(128)(2,1)S(1)} copy-done((bf16[192]{0:T(256)(128)(2,1)S(1)}, bf16[192]{0:T(256)(128)(2,1)}, u32[]{:S(2)}) %copy-start.6) | copy-done | bytes 408
  18.1 0.0 copy-done.7
  18.1 0.2 shard_map.137
  18.3 2.2 %collective-permute-done.1 = bf16[3,24,2,192]{3,2,1,0:T(2,128)(2,1)S(1)} collective-permute-done((bf16[3,24,2,192]{3,2,1,0:T(2,128)(2,1)S(1)}, bf16[3,24,2,192]{3,2,1,0:T(2,128)(2,1)S(1)}, u32[]{:S(2)}, u32[]{:S(2)}) %collective-permute-start.1) | collective-permute-done | bytes 55328 | tf_op jit(solution)/shard_map/ppermute | solution.py:39
  20.5 0.0 collective-permute-done
  20.5 0.0 copy-start.1
  20.5 0.1 fusion.1
  20.6 0.0 copy-start.3
  20.6 0.0 copy-start.4
  20.6 0.4 %broadcast_select_fusion.2 = (bf16[18,6,2,192]{3,2,1,0:T(2,128)(2,1)S(1)}, bf16[18,6,2,192]{3,2,1,0:T(2,128)(2,1)S(1)}) fusion(pred[]{:T(512)S(6)} %eq.22, bf16[3,6,2,192]{3,2,1,0:T(2,128)(2,1)S(1)} %get-tuple-element.59, bf16[12,6,2,192]{3,2,1,0:T(2,128)(2,1)S(1)} %get-tuple-element.46, bf16[3,6,2,192]{3,2,1,0:T(2,128)(2,1)S(1)} %get-tuple-element.56, ...), kind=kLoop, calls=%fused_computation.2 | loop fusion | flops 248832 | bytes 331777 | tf_op jit(solution)/shard_map/jit(_where)/select_n | solution.py:33
  21.0 1.2 %collective-permute-start.2 = (bf16[18,6,2,192]{3,2,1,0:T(2,128)(2,1)S(1)}, bf16[18,6,2,192]{3,2,1,0:T(2,128)(2,1)S(1)}, u32[]{:S(2)}, u32[]{:S(2)}) collective-permute-start(bf16[18,6,2,192]{3,2,1,0:T(2,128)(2,1)S(1)} %get-tuple-element.50), channel_id=1, source_target_pairs={{4,8},{8,4},{12,16},{16,12},{20,24},{24,20},{28,0},{0,28},{5,9},{9... | collective-permute-start | bytes 248840 | tf_op jit(solution)/shard_map/ppermute | solution.py:39
  22.2 0.0 copy-start.5
  22.2 0.4 %collective-permute-start.3 = (bf16[18,6,2,192]{3,2,1,0:T(2,128)(2,1)S(1)}, bf16[18,6,2,192]{3,2,1,0:T(2,128)(2,1)S(1)}, u32[]{:S(2)}, u32[]{:S(2)}) collective-permute-start(bf16[18,6,2,192]{3,2,1,0:T(2,128)(2,1)S(1)} %get-tuple-element.49), channel_id=1, source_target_pairs={{0,4},{4,0},{8,12},{12,8},{16,20},{20,16},{24,28},{28,24},{1,5},{5... | collective-permute-start | bytes 248840 | tf_op jit(solution)/shard_map/ppermute | solution.py:39
  22.7 0.0 all-to-all-done.recv_ref
  22.7 0.0 copy-done.1
  22.7 0.0 copy-done.3
  22.7 0.0 copy-done.4
  22.7 0.2 copy-done.5
  22.9 3.9 %shard_map.138 = (bf16[12,12,2,192]{3,2,1,0:T(2,128)(2,1)S(1)}, f32[464,256]{1,0:T(8,128)S(1)}, f32[304,192]{1,0:T(8,128)S(1)}, f32[464,192]{1,0:T(8,128)S(1)}) custom-call(s32[3]{0:T(128)S(1)} %add_convert_fusion.scalars_ref, bf16[32,10,2,128]{3,2,1,0:T(2,128)(2,1)S(1)} %all-to-all-done.recv_ref, bf16[3,24,2,192]{3,2,1,0:T(2,128)(2,1)S(1)} %bitcast.22, ...), custom_call_target="tpu_custom_call" | custom-call | flops 4000000000 | bytes 4000000 | tf_op jit(solution)/shard_map/pallas_call | solution.py:589
  26.8 0.5 %collective-permute-done.2 = bf16[18,6,2,192]{3,2,1,0:T(2,128)(2,1)S(1)} collective-permute-done((bf16[18,6,2,192]{3,2,1,0:T(2,128)(2,1)S(1)}, bf16[18,6,2,192]{3,2,1,0:T(2,128)(2,1)S(1)}, u32[]{:S(2)}, u32[]{:S(2)}) %collective-permute-start.2) | collective-permute-done | bytes 82976 | tf_op jit(solution)/shard_map/ppermute | solution.py:39
  27.3 0.0 collective-permute-done.3
  27.3 0.2 broadcast_select_fusion
  27.5 4.0 %shard_map.139 = bf16[12,24,2,192]{3,2,1,0:T(2,128)(2,1)} custom-call(s32[3]{0:T(128)S(1)} %add_convert_fusion.scalars_ref, f32[464,256]{1,0:T(8,128)S(1)} %get-tuple-element.39.rest_ref, f32[304,192]{1,0:T(8,128)S(1)} %get-tuple-element.40.latent_ref, f32[464,192]{1,0:T(8,128)S(1)} %get-tuple-element.41.normed_ref, ...), custom_call_target="tpu_custom_call" | custom-call | flops 3000000000 | bytes 4000000 | tf_op jit(solution)/shard_map/pallas_call | solution.py:618
  (2 shorter events, 0.0 us)
Async XLA Ops:
  6.3 7.4 %copy-start.9 = (bf16[3,24,2,192]{3,2,1,0:T(2,128)(2,1)S(1)}, bf16[3,24,2,192]{3,2,1,0:T(2,128)(2,1)}, u32[]{:S(2)}) copy-start(bf16[3,24,2,192]{3,2,1,0:T(2,128)(2,1)} %get-tuple-element.26) | copy-start | bytes 165892
  6.3 7.4 %copy-start.10 = (bf16[3,24,2,192]{3,2,1,0:T(2,128)(2,1)S(1)}, bf16[3,24,2,192]{3,2,1,0:T(2,128)(2,1)}, u32[]{:S(2)}) copy-start(bf16[3,24,2,192]{3,2,1,0:T(2,128)(2,1)} %get-tuple-element.27) | copy-start | bytes 165892
  6.3 16.4 %all-to-all-start = ((bf16[32,10,2,128]{3,2,1,0:T(2,128)(2,1)}), bf16[32,10,2,128]{3,2,1,0:T(2,128)(2,1)S(1)}, u32[]{:S(2)}, u32[]{:S(2)}) async-start(bf16[32,10,2,128]{3,2,1,0:T(2,128)(2,1)} %bitcast.23), calls=%async_computation | async-start | bytes 327680 | tf_op jit(solution)/shard_map/all_to_all | solution.py:560
  13.6 2.7 %copy-start.8 = (bf16[768,192]{0,1:T(8,128)(2,1)S(1)}, bf16[768,192]{0,1:T(8,128)(2,1)}, u32[]{:S(2)}) copy-start(bf16[768,192]{0,1:T(8,128)(2,1)} %param.27) | copy-start | bytes 884740
  13.7 2.6 %copy-start.11 = (bf16[128,192]{0,1:T(8,128)(2,1)S(1)}, bf16[128,192]{0,1:T(8,128)(2,1)}, u32[]{:S(2)}) copy-start(bf16[128,192]{0,1:T(8,128)(2,1)} %param.19) | copy-start | bytes 147460
  13.7 6.8 %collective-permute-start.1 = (bf16[3,24,2,192]{3,2,1,0:T(2,128)(2,1)S(1)}, bf16[3,24,2,192]{3,2,1,0:T(2,128)(2,1)S(1)}, u32[]{:S(2)}, u32[]{:S(2)}) collective-permute-start(bf16[3,24,2,192]{3,2,1,0:T(2,128)(2,1)S(1)} %bitcast.27), channel_id=1, source_target_pairs={{0,1},{1,0},{2,3},{3,2},{4,5},{5,4},{6,7},{7,6},{8,9},{9,8},{10,11... | collective-permute-start | bytes 165896 | tf_op jit(solution)/shard_map/ppermute | solution.py:39
  15.5 5.0 %collective-permute-start = (bf16[3,24,2,192]{3,2,1,0:T(2,128)(2,1)S(1)}, bf16[3,24,2,192]{3,2,1,0:T(2,128)(2,1)S(1)}, u32[]{:S(2)}, u32[]{:S(2)}) collective-permute-start(bf16[3,24,2,192]{3,2,1,0:T(2,128)(2,1)S(1)} %bitcast.25), channel_id=1, source_target_pairs={{1,2},{2,1},{5,6},{6,5},{9,10},{10,9},{13,14},{14,13},{17,18},{18,... | collective-permute-start | bytes 165896 | tf_op jit(solution)/shard_map/ppermute | solution.py:39
  16.4 1.0 %copy-start = (bf16[12,24,2,192]{3,2,1,0:T(2,128)(2,1)S(1)}, bf16[12,24,2,192]{3,2,1,0:T(2,128)(2,1)}, u32[]{:S(2)}) copy-start(bf16[12,24,2,192]{3,2,1,0:T(2,128)(2,1)} %back_ref.2) | copy-start | bytes 663556
  16.5 1.0 %copy-start.2 = (bf16[192,576]{1,0:T(8,128)(2,1)S(1)}, bf16[192,576]{1,0:T(8,128)(2,1)}, u32[]{:S(2)}) copy-start(bf16[192,576]{1,0:T(8,128)(2,1)} %attn_ref) | copy-start | bytes 663556
  17.4 0.7 %copy-start.6 = (bf16[192]{0:T(256)(128)(2,1)S(1)}, bf16[192]{0:T(256)(128)(2,1)}, u32[]{:S(2)}) copy-start(bf16[192]{0:T(256)(128)(2,1)} %one_ref) | copy-start | bytes 1156
  17.4 0.7 %copy-start.7 = (bf16[192]{0:T(256)(128)(2,1)S(1)}, bf16[192]{0:T(256)(128)(2,1)}, u32[]{:S(2)}) copy-start(bf16[192]{0:T(256)(128)(2,1)} %two_ref) | copy-start | bytes 1156
  20.5 2.2 %copy-start.1 = (bf16[192,768]{1,0:T(8,128)(2,1)S(1)}, bf16[192,768]{1,0:T(8,128)(2,1)}, u32[]{:S(2)}) copy-start(bf16[192,768]{1,0:T(8,128)(2,1)} %refs_3_.3) | copy-start | bytes 884740
  20.6 2.1 %copy-start.3 = (bf16[192,384]{1,0:T(8,128)(2,1)S(1)}, bf16[192,384]{1,0:T(8,128)(2,1)}, u32[]{:S(2)}) copy-start(bf16[192,384]{1,0:T(8,128)(2,1)} %lift_ref.1) | copy-start | bytes 442372
  20.6 2.1 %copy-start.4 = (bf16[192,192]{1,0:T(8,128)(2,1)S(1)}, bf16[192,192]{1,0:T(8,128)(2,1)}, u32[]{:S(2)}) copy-start(bf16[192,192]{1,0:T(8,128)(2,1)} %refs_1_.3) | copy-start | bytes 221188
  21.0 6.3 %collective-permute-start.2 = (bf16[18,6,2,192]{3,2,1,0:T(2,128)(2,1)S(1)}, bf16[18,6,2,192]{3,2,1,0:T(2,128)(2,1)S(1)}, u32[]{:S(2)}, u32[]{:S(2)}) collective-permute-start(bf16[18,6,2,192]{3,2,1,0:T(2,128)(2,1)S(1)} %get-tuple-element.50), channel_id=1, source_target_pairs={{4,8},{8,4},{12,16},{16,12},{20,24},{24,20},{28,0},{0,28},{5,9},{9... | collective-permute-start | bytes 248840 | tf_op jit(solution)/shard_map/ppermute | solution.py:39
  22.2 0.7 %copy-start.5 = (bf16[8,192]{1,0:T(8,128)(2,1)S(1)}, bf16[8,192]{1,0:T(8,128)(2,1)}, u32[]{:S(2)}) copy-start(bf16[8,192]{1,0:T(8,128)(2,1)} %table_ref.1) | copy-start | bytes 9220
  22.2 5.1 %collective-permute-start.3 = (bf16[18,6,2,192]{3,2,1,0:T(2,128)(2,1)S(1)}, bf16[18,6,2,192]{3,2,1,0:T(2,128)(2,1)S(1)}, u32[]{:S(2)}, u32[]{:S(2)}) collective-permute-start(bf16[18,6,2,192]{3,2,1,0:T(2,128)(2,1)S(1)} %get-tuple-element.49), channel_id=1, source_target_pairs={{0,4},{4,0},{8,12},{12,8},{16,20},{20,16},{24,28},{28,24},{1,5},{5... | collective-permute-start | bytes 248840 | tf_op jit(solution)/shard_map/ppermute | solution.py:39

commit v21 on v20

--- a/solution.py
+++ b/solution.py
@@ -185,7 +185,7 @@
         pack_kernel,
         out_shape=[jax.ShapeDtypeStruct(shape, BF16), across, across],
         in_specs=[anywhere] * 5,
-        out_specs=[pl.BlockSpec(memory_space=pltpu.VMEM), anywhere, anywhere],
+        out_specs=[pl.BlockSpec(memory_space=pltpu.VMEM)] * 3,
         scratch_shapes=[
             pltpu.VMEM(record_values.shape, BF16),
             ints,
@@ -297,7 +297,7 @@
         if padded(count) > count:
             piece = below(piece, jnp.zeros((padded(count) - count, width), F32))
         pieces.append(piece)
-    rows_ref[...] = below(*pieces)
+    rows_ref[...] = below(*pieces).astype(BF16)
     for gain, ref in ((one_ref, gain_one_ref), (two_ref, gain_two_ref)):
         ref[...] = jnp.broadcast_to(gain[...].astype(F32).reshape(1, width), ref.shape)
     for n in range(3):
@@ -311,7 +311,7 @@
     return pl.pallas_call(
         functools.partial(prepare_kernel, plan),
         out_shape=[
-            jax.ShapeDtypeStruct((rows, width), F32),
+            jax.ShapeDtypeStruct((rows, width), BF16),
             jax.ShapeDtypeStruct((3, width, width), BF16),
             jax.ShapeDtypeStruct((8, width), F32),
             jax.ShapeDtypeStruct((8, width), F32),
@@ -324,7 +324,7 @@
 
 
 def normed_of(plan, entries, sums, borders, gain):
-    rows_ref, north_ref, south_ref, west_ref, east_ref, lat_cells = borders
+    rows, north_ref, south_ref, west_ref, east_ref, lat_cells = borders
     width = gain.shape[1]
     pieces, spans, start = [], {}, 0
     for tile, number in entries:
@@ -334,7 +334,7 @@
         full = padded(count)
         if tile == 4:
             begin = sum(padded(tokens_of(part)) for part in plan[4][:number])
-            piece = rows_ref[begin : begin + full, :]
+            piece = rows[begin : begin + full]
         else:
             if dx:
                 ref = west_ref if dx < 0 else east_ref
@@ -422,11 +422,8 @@
 
     after = (latent + dot(mixed, mix_ref[...])).astype(BF16).astype(F32)
     normed_two = normalise(after, gain_ref[:1, :]).astype(BF16)
-    cuts = range(0, up_ref.shape[1], PAD)
-    hidden = [dot(normed_two, up_ref[:, at : at + PAD]).astype(BF16) for at in cuts]
-    result = after
-    for at, chunk in zip(cuts, hidden):
-        result = result + dot(gelu(chunk), down_ref[at : at + PAD, :])
+    hidden = gelu(dot(normed_two, up_ref[...]).astype(BF16))
+    result = after + dot(hidden, down_ref[...])
     for begin, (i, j) in zip(begins, places):
         part = plan[4][3 * i + j]
         piece = result[begin : begin + tokens_of(part)].astype(BF16)
@@ -466,7 +463,7 @@
             pieces.append(sums[tile][start : start + padded(tokens_of(plan[tile][number]))])
         return below(*pieces)
 
-    borders = (rows_ref, north_ref, south_ref, None, None, lat_cells)
+    borders = (rows_ref[...].astype(F32), north_ref, south_ref, None, None, lat_cells)
     gain = gain_one_ref[:1, :]
     entries = near_entries(MIDDLE)
     latent, normed, spans = normed_of(plan, entries, sums_of(entries), borders, gain)

time: 31.8 us -> 27.2 us (0.86)
  Pallas kernels: 14.4 us -> 9.82 us
    pallas_call x1, Pallas kernels: 6.29 us -> 1.75 us  [packed(): pl.pallas_call(pack_kernel, out_shape=[jax.ShapeDtypeStruct(shape, BF16),...]
  transfers between devices with their start and end apart: 5 -> 5, of which waited for: 2 -> 2; matrix products, arithmetic and copies ran while one was open for 3% -> 3% of each run, Pallas kernels for 13% -> 15%
where the time goes in v21:
time: 27.2 us; the launch traced here: 26.9 us
  starting transfers between devices  11.5 us (42%)
  Pallas kernels  9.82 us (36%)
  waiting for transfers between devices  2.68 us (10%)
  local copies, waits for them, and re-layouts  2.07 us (8%)
  other arithmetic  0.66 us (2%)
    all_to_all x1, starting transfers between devices, local(): lax.all_to_all(sent, ('lon', 'lat'), split_axis=0, concat_axis=0, tiled=T...  7.3 us
    ppermute x4, starting transfers between devices, swapped(): got.append(lax.ppermute(mine, axis, pairs))  4.15 us
    pallas_call x1, Pallas kernels, local(): pl.pallas_call(functools.partial(side_kernel, plan, lat_cells), out_shape...  3.97 us
    pallas_call x1, Pallas kernels, local(): pl.pallas_call(functools.partial(middle_kernel, plan, lat_cells, lon_cell...  3.91 us
    ppermute x4, waiting for transfers between devices, swapped(): got.append(lax.ppermute(mine, axis, pairs))  2.68 us
    pallas_call x1, Pallas kernels, packed(): pl.pallas_call(pack_kernel, out_shape=[jax.ShapeDtypeStruct(shape, BF16),...  1.75 us
    unnamed x24, local copies, waits for them, and re-layouts  1.63 us
  transfers between devices with their start and end apart: 5, of which 2 were waited for; matrix products, arithmetic and copies ran while one was open for 3% of the time, Pallas kernels for 15%

profile of v21, /device:TPU:0, one launch (start us, length us, event | category | flops | bytes accessed | tf_op | source)
XLA Modules:
  0.0 26.9 jit_solution(912154752021996197)
XLA Ops:
  0.0 1.8 %shard_map.136 = (bf16[8,4,10,2,128]{4,3,2,1,0:T(2,128)(2,1)}, bf16[3,24,2,192]{3,2,1,0:T(2,128)(2,1)}, bf16[3,24,2,192]{3,2,1,0:T(2,128)(2,1)}) custom-call(bf16[8,4,2,128]{3,2,1,0:T(2,128)(2,1)} %values_ref.1, s32[8,8]{1,0:T(8,128)} %bitcast.30, s32[8,8]{1,0:T(8,128)} %bitcast.31, s32[4,8]{1,0:T(4,128)} %bitcast.32, bf16[12,24,2,192]{3,2,1,0:T(2,128)(2,1)} %back_ref.2), custom_call_target="tpu_custom_call" | custom-call | flops 20000000000 | bytes 1000000 | tf_op jit(solution)/shard_map/pallas_call | solution.py:184
  1.8 0.0 copy-start.9
  1.8 0.0 copy-start.10
  1.8 7.3 %all-to-all-start = ((bf16[32,10,2,128]{3,2,1,0:T(2,128)(2,1)}), bf16[32,10,2,128]{3,2,1,0:T(2,128)(2,1)S(1)}, u32[]{:S(2)}, u32[]{:S(2)}) async-start(bf16[32,10,2,128]{3,2,1,0:T(2,128)(2,1)} %bitcast.23), calls=%async_computation | async-start | bytes 327680 | tf_op jit(solution)/shard_map/all_to_all | solution.py:557
  9.1 0.0 copy-start.8
  9.1 0.0 copy-done.9
  9.1 0.0 copy-done.10
  9.1 0.0 copy-start.11
  9.2 1.8 %collective-permute-start.1 = (bf16[3,24,2,192]{3,2,1,0:T(2,128)(2,1)S(1)}, bf16[3,24,2,192]{3,2,1,0:T(2,128)(2,1)S(1)}, u32[]{:S(2)}, u32[]{:S(2)}) collective-permute-start(bf16[3,24,2,192]{3,2,1,0:T(2,128)(2,1)S(1)} %bitcast.27), channel_id=1, source_target_pairs={{0,1},{1,0},{2,3},{3,2},{4,5},{5,4},{6,7},{7,6},{8,9},{9,8},{10,11... | collective-permute-start | bytes 165896 | tf_op jit(solution)/shard_map/ppermute | solution.py:39
  11.0 0.7 %collective-permute-start = (bf16[3,24,2,192]{3,2,1,0:T(2,128)(2,1)S(1)}, bf16[3,24,2,192]{3,2,1,0:T(2,128)(2,1)S(1)}, u32[]{:S(2)}, u32[]{:S(2)}) collective-permute-start(bf16[3,24,2,192]{3,2,1,0:T(2,128)(2,1)S(1)} %bitcast.25), channel_id=1, source_target_pairs={{1,2},{2,1},{5,6},{6,5},{9,10},{10,9},{13,14},{14,13},{17,18},{18,... | collective-permute-start | bytes 165896 | tf_op jit(solution)/shard_map/ppermute | solution.py:39
  11.7 0.0 copy-done.11
  11.7 0.1 copy.15.first_ref
  11.8 0.0 copy-done.8
  11.8 0.0 copy-start
  11.8 0.2 copy.16.refs_4_
  12.0 0.0 copy-start.2
  12.0 0.8 %copy-done = bf16[12,24,2,192]{3,2,1,0:T(2,128)(2,1)S(1)} copy-done((bf16[12,24,2,192]{3,2,1,0:T(2,128)(2,1)S(1)}, bf16[12,24,2,192]{3,2,1,0:T(2,128)(2,1)}, u32[]{:S(2)}) %copy-start) | copy-done | bytes 221208
  12.8 0.1 fusion
  12.9 0.0 copy-start.6
  12.9 0.0 copy-start.7
  12.9 0.1 add_convert_fusion.scalars_ref
  13.0 0.0 copy-done.2
  13.0 0.6 %copy-done.6 = bf16[192]{0:T(256)(128)(2,1)S(1)} copy-done((bf16[192]{0:T(256)(128)(2,1)S(1)}, bf16[192]{0:T(256)(128)(2,1)}, u32[]{:S(2)}) %copy-start.6) | copy-done | bytes 408
  13.6 0.0 copy-done.7
  13.6 0.2 shard_map.137
  13.8 2.2 %collective-permute-done.1 = bf16[3,24,2,192]{3,2,1,0:T(2,128)(2,1)S(1)} collective-permute-done((bf16[3,24,2,192]{3,2,1,0:T(2,128)(2,1)S(1)}, bf16[3,24,2,192]{3,2,1,0:T(2,128)(2,1)S(1)}, u32[]{:S(2)}, u32[]{:S(2)}) %collective-permute-start.1) | collective-permute-done | bytes 55328 | tf_op jit(solution)/shard_map/ppermute | solution.py:39
  16.0 0.0 collective-permute-done
  16.0 0.0 copy-start.1
  16.0 0.1 fusion.1
  16.1 0.0 copy-start.3
  16.1 0.0 copy-start.4
  16.1 0.4 %broadcast_select_fusion.2 = (bf16[18,6,2,192]{3,2,1,0:T(2,128)(2,1)S(1)}, bf16[18,6,2,192]{3,2,1,0:T(2,128)(2,1)S(1)}) fusion(pred[]{:T(512)S(6)} %eq.22, bf16[3,6,2,192]{3,2,1,0:T(2,128)(2,1)S(1)} %get-tuple-element.59, bf16[12,6,2,192]{3,2,1,0:T(2,128)(2,1)S(1)} %get-tuple-element.46, bf16[3,6,2,192]{3,2,1,0:T(2,128)(2,1)S(1)} %get-tuple-element.56, ...), kind=kLoop, calls=%fused_computation.2 | loop fusion | flops 248832 | bytes 331777 | tf_op jit(solution)/shard_map/jit(_where)/select_n | solution.py:33
  16.5 1.2 %collective-permute-start.2 = (bf16[18,6,2,192]{3,2,1,0:T(2,128)(2,1)S(1)}, bf16[18,6,2,192]{3,2,1,0:T(2,128)(2,1)S(1)}, u32[]{:S(2)}, u32[]{:S(2)}) collective-permute-start(bf16[18,6,2,192]{3,2,1,0:T(2,128)(2,1)S(1)} %get-tuple-element.50), channel_id=1, source_target_pairs={{4,8},{8,4},{12,16},{16,12},{20,24},{24,20},{28,0},{0,28},{5,9},{9... | collective-permute-start | bytes 248840 | tf_op jit(solution)/shard_map/ppermute | solution.py:39
  17.7 0.0 copy-start.5
  17.7 0.4 %collective-permute-start.3 = (bf16[18,6,2,192]{3,2,1,0:T(2,128)(2,1)S(1)}, bf16[18,6,2,192]{3,2,1,0:T(2,128)(2,1)S(1)}, u32[]{:S(2)}, u32[]{:S(2)}) collective-permute-start(bf16[18,6,2,192]{3,2,1,0:T(2,128)(2,1)S(1)} %get-tuple-element.49), channel_id=1, source_target_pairs={{0,4},{4,0},{8,12},{12,8},{16,20},{20,16},{24,28},{28,24},{1,5},{5... | collective-permute-start | bytes 248840 | tf_op jit(solution)/shard_map/ppermute | solution.py:39
  18.1 0.0 all-to-all-done.recv_ref
  18.1 0.0 copy-done.1
  18.1 0.0 copy-done.3
  18.1 0.0 copy-done.4
  18.1 0.2 copy-done.5
  18.4 3.9 %shard_map.138 = (bf16[12,12,2,192]{3,2,1,0:T(2,128)(2,1)S(1)}, f32[464,256]{1,0:T(8,128)S(1)}, f32[304,192]{1,0:T(8,128)S(1)}, f32[464,192]{1,0:T(8,128)S(1)}) custom-call(s32[3]{0:T(128)S(1)} %add_convert_fusion.scalars_ref, bf16[32,10,2,128]{3,2,1,0:T(2,128)(2,1)S(1)} %all-to-all-done.recv_ref, bf16[3,24,2,192]{3,2,1,0:T(2,128)(2,1)S(1)} %bitcast.22, ...), custom_call_target="tpu_custom_call" | custom-call | flops 4000000000 | bytes 4000000 | tf_op jit(solution)/shard_map/pallas_call | solution.py:586
  22.3 0.5 %collective-permute-done.2 = bf16[18,6,2,192]{3,2,1,0:T(2,128)(2,1)S(1)} collective-permute-done((bf16[18,6,2,192]{3,2,1,0:T(2,128)(2,1)S(1)}, bf16[18,6,2,192]{3,2,1,0:T(2,128)(2,1)S(1)}, u32[]{:S(2)}, u32[]{:S(2)}) %collective-permute-start.2) | collective-permute-done | bytes 82976 | tf_op jit(solution)/shard_map/ppermute | solution.py:39
  22.8 0.0 collective-permute-done.3
  22.8 0.2 broadcast_select_fusion
  23.0 4.0 %shard_map.139 = bf16[12,24,2,192]{3,2,1,0:T(2,128)(2,1)} custom-call(s32[3]{0:T(128)S(1)} %add_convert_fusion.scalars_ref, f32[464,256]{1,0:T(8,128)S(1)} %get-tuple-element.39.rest_ref, f32[304,192]{1,0:T(8,128)S(1)} %get-tuple-element.40.latent_ref, f32[464,192]{1,0:T(8,128)S(1)} %get-tuple-element.41.normed_ref, ...), custom_call_target="tpu_custom_call" | custom-call | flops 3000000000 | bytes 4000000 | tf_op jit(solution)/shard_map/pallas_call | solution.py:615
  (2 shorter events, 0.0 us)
Async XLA Ops:
  1.8 7.4 %copy-start.9 = (bf16[3,24,2,192]{3,2,1,0:T(2,128)(2,1)S(1)}, bf16[3,24,2,192]{3,2,1,0:T(2,128)(2,1)}, u32[]{:S(2)}) copy-start(bf16[3,24,2,192]{3,2,1,0:T(2,128)(2,1)} %get-tuple-element.26) | copy-start | bytes 165892
  1.8 7.4 %copy-start.10 = (bf16[3,24,2,192]{3,2,1,0:T(2,128)(2,1)S(1)}, bf16[3,24,2,192]{3,2,1,0:T(2,128)(2,1)}, u32[]{:S(2)}) copy-start(bf16[3,24,2,192]{3,2,1,0:T(2,128)(2,1)} %get-tuple-element.27) | copy-start | bytes 165892
  1.8 16.4 %all-to-all-start = ((bf16[32,10,2,128]{3,2,1,0:T(2,128)(2,1)}), bf16[32,10,2,128]{3,2,1,0:T(2,128)(2,1)S(1)}, u32[]{:S(2)}, u32[]{:S(2)}) async-start(bf16[32,10,2,128]{3,2,1,0:T(2,128)(2,1)} %bitcast.23), calls=%async_computation | async-start | bytes 327680 | tf_op jit(solution)/shard_map/all_to_all | solution.py:557
  9.1 2.7 %copy-start.8 = (bf16[768,192]{0,1:T(8,128)(2,1)S(1)}, bf16[768,192]{0,1:T(8,128)(2,1)}, u32[]{:S(2)}) copy-start(bf16[768,192]{0,1:T(8,128)(2,1)} %param.27) | copy-start | bytes 884740
  9.1 2.6 %copy-start.11 = (bf16[128,192]{0,1:T(8,128)(2,1)S(1)}, bf16[128,192]{0,1:T(8,128)(2,1)}, u32[]{:S(2)}) copy-start(bf16[128,192]{0,1:T(8,128)(2,1)} %param.19) | copy-start | bytes 147460
  9.2 6.8 %collective-permute-start.1 = (bf16[3,24,2,192]{3,2,1,0:T(2,128)(2,1)S(1)}, bf16[3,24,2,192]{3,2,1,0:T(2,128)(2,1)S(1)}, u32[]{:S(2)}, u32[]{:S(2)}) collective-permute-start(bf16[3,24,2,192]{3,2,1,0:T(2,128)(2,1)S(1)} %bitcast.27), channel_id=1, source_target_pairs={{0,1},{1,0},{2,3},{3,2},{4,5},{5,4},{6,7},{7,6},{8,9},{9,8},{10,11... | collective-permute-start | bytes 165896 | tf_op jit(solution)/shard_map/ppermute | solution.py:39
  11.0 5.0 %collective-permute-start = (bf16[3,24,2,192]{3,2,1,0:T(2,128)(2,1)S(1)}, bf16[3,24,2,192]{3,2,1,0:T(2,128)(2,1)S(1)}, u32[]{:S(2)}, u32[]{:S(2)}) collective-permute-start(bf16[3,24,2,192]{3,2,1,0:T(2,128)(2,1)S(1)} %bitcast.25), channel_id=1, source_target_pairs={{1,2},{2,1},{5,6},{6,5},{9,10},{10,9},{13,14},{14,13},{17,18},{18,... | collective-permute-start | bytes 165896 | tf_op jit(solution)/shard_map/ppermute | solution.py:39
  11.8 1.0 %copy-start = (bf16[12,24,2,192]{3,2,1,0:T(2,128)(2,1)S(1)}, bf16[12,24,2,192]{3,2,1,0:T(2,128)(2,1)}, u32[]{:S(2)}) copy-start(bf16[12,24,2,192]{3,2,1,0:T(2,128)(2,1)} %back_ref.2) | copy-start | bytes 663556
  12.0 1.0 %copy-start.2 = (bf16[192,576]{1,0:T(8,128)(2,1)S(1)}, bf16[192,576]{1,0:T(8,128)(2,1)}, u32[]{:S(2)}) copy-start(bf16[192,576]{1,0:T(8,128)(2,1)} %attn_ref) | copy-start | bytes 663556
  12.9 0.7 %copy-start.6 = (bf16[192]{0:T(256)(128)(2,1)S(1)}, bf16[192]{0:T(256)(128)(2,1)}, u32[]{:S(2)}) copy-start(bf16[192]{0:T(256)(128)(2,1)} %one_ref) | copy-start | bytes 1156
  12.9 0.7 %copy-start.7 = (bf16[192]{0:T(256)(128)(2,1)S(1)}, bf16[192]{0:T(256)(128)(2,1)}, u32[]{:S(2)}) copy-start(bf16[192]{0:T(256)(128)(2,1)} %two_ref) | copy-start | bytes 1156
  16.0 2.2 %copy-start.1 = (bf16[192,768]{1,0:T(8,128)(2,1)S(1)}, bf16[192,768]{1,0:T(8,128)(2,1)}, u32[]{:S(2)}) copy-start(bf16[192,768]{1,0:T(8,128)(2,1)} %refs_3_.3) | copy-start | bytes 884740
  16.1 2.1 %copy-start.3 = (bf16[192,384]{1,0:T(8,128)(2,1)S(1)}, bf16[192,384]{1,0:T(8,128)(2,1)}, u32[]{:S(2)}) copy-start(bf16[192,384]{1,0:T(8,128)(2,1)} %lift_ref.1) | copy-start | bytes 442372
  16.1 2.1 %copy-start.4 = (bf16[192,192]{1,0:T(8,128)(2,1)S(1)}, bf16[192,192]{1,0:T(8,128)(2,1)}, u32[]{:S(2)}) copy-start(bf16[192,192]{1,0:T(8,128)(2,1)} %refs_1_.3) | copy-start | bytes 221188
  16.5 6.3 %collective-permute-start.2 = (bf16[18,6,2,192]{3,2,1,0:T(2,128)(2,1)S(1)}, bf16[18,6,2,192]{3,2,1,0:T(2,128)(2,1)S(1)}, u32[]{:S(2)}, u32[]{:S(2)}) collective-permute-start(bf16[18,6,2,192]{3,2,1,0:T(2,128)(2,1)S(1)} %get-tuple-element.50), channel_id=1, source_target_pairs={{4,8},{8,4},{12,16},{16,12},{20,24},{24,20},{28,0},{0,28},{5,9},{9... | collective-permute-start | bytes 248840 | tf_op jit(solution)/shard_map/ppermute | solution.py:39
  17.7 0.7 %copy-start.5 = (bf16[8,192]{1,0:T(8,128)(2,1)S(1)}, bf16[8,192]{1,0:T(8,128)(2,1)}, u32[]{:S(2)}) copy-start(bf16[8,192]{1,0:T(8,128)(2,1)} %table_ref.1) | copy-start | bytes 9220
  17.7 5.1 %collective-permute-start.3 = (bf16[18,6,2,192]{3,2,1,0:T(2,128)(2,1)S(1)}, bf16[18,6,2,192]{3,2,1,0:T(2,128)(2,1)S(1)}, u32[]{:S(2)}, u32[]{:S(2)}) collective-permute-start(bf16[18,6,2,192]{3,2,1,0:T(2,128)(2,1)S(1)} %get-tuple-element.49), channel_id=1, source_target_pairs={{0,4},{4,0},{8,12},{12,8},{16,20},{20,16},{24,28},{28,24},{1,5},{5... | collective-permute-start | bytes 248840 | tf_op jit(solution)/shard_map/ppermute | solution.py:39

commit v22 on v21

--- a/solution.py
+++ b/solution.py
@@ -90,7 +90,7 @@
 
 
 def with_ones(tensor):
-    ones = jnp.ones((tensor.shape[0], PAD - tensor.shape[1]), F32)
+    ones = jnp.ones((tensor.shape[0], PAD - tensor.shape[1]), tensor.dtype)
     return jnp.concatenate([tensor, ones], axis=1).astype(BF16)
 
 
@@ -233,8 +233,7 @@
     width = first_ref.shape[1]
     chunk = min(CHUNK, sources)
     slots = chunk * capacity
-    table = below(*[table_ref[...].astype(F32)] * (LANES // INSTR)).astype(BF16)
-    first, lift = below(first_ref[...], table), lift_ref[...]
+    first, lift = below(first_ref[...], table_ref[...]), lift_ref[...]
     lane = lax.broadcasted_iota(jnp.int32, (16, LANES), 1)
     sub = lax.broadcasted_iota(jnp.int32, (16, LANES), 0)
     weigh = jnp.where(lane == ROWS + sub, float(lon_cells * LEV), 0.0)
@@ -253,8 +252,8 @@
         wide = meta.astype(F32)
         chosen = below(*[jnp.where(lane == n, wide, 0.0) for n in range(len(AROUND))]).astype(BF16)
         both = jnp.concatenate([records, chosen], axis=1)
-        encoded = gelu(dot(both, first)).astype(BF16)
-        lifted = gelu(dot(encoded, lift))
+        encoded = gelu(dot(both, first).astype(BF16))
+        lifted = gelu(dot(encoded, lift).astype(BF16))
         tokens = dot_nt(weigh, meta)
         hots, parts = [], []
         for n in range(len(AROUND)):
@@ -287,7 +286,17 @@
 
 
 def prepare_kernel(
-    plan, back_ref, attn_ref, one_ref, two_ref, rows_ref, parts_ref, gain_one_ref, gain_two_ref
+    plan,
+    back_ref,
+    attn_ref,
+    table_ref,
+    one_ref,
+    two_ref,
+    rows_ref,
+    parts_ref,
+    tables_ref,
+    gain_one_ref,
+    gain_two_ref,
 ):
     width = back_ref.shape[3]
     pieces = []
@@ -298,13 +307,14 @@
             piece = below(piece, jnp.zeros((padded(count) - count, width), F32))
         pieces.append(piece)
     rows_ref[...] = below(*pieces).astype(BF16)
+    tables_ref[...] = below(*[table_ref[...].astype(F32)] * (LANES // INSTR)).astype(BF16)
     for gain, ref in ((one_ref, gain_one_ref), (two_ref, gain_two_ref)):
         ref[...] = jnp.broadcast_to(gain[...].astype(F32).reshape(1, width), ref.shape)
     for n in range(3):
         parts_ref[n] = attn_ref[:, n * width : (n + 1) * width]
 
 
-def prepared(plan, background, attn_weight, first_gain, second_gain):
+def prepared(plan, background, attn_weight, instrument_table, first_gain, second_gain):
     width = background.shape[3]
     rows = sum(padded(tokens_of(part)) for part in plan[4])
     vmem = pl.BlockSpec(memory_space=pltpu.VMEM)
@@ -313,14 +323,15 @@
         out_shape=[
             jax.ShapeDtypeStruct((rows, width), BF16),
             jax.ShapeDtypeStruct((3, width, width), BF16),
+            jax.ShapeDtypeStruct((LANES, width), BF16),
             jax.ShapeDtypeStruct((8, width), F32),
             jax.ShapeDtypeStruct((8, width), F32),
         ],
-        in_specs=[vmem] * 4,
-        out_specs=[vmem] * 4,
+        in_specs=[vmem] * 5,
+        out_specs=[vmem] * 5,
         compiler_params=pltpu.CompilerParams(vmem_limit_bytes=LIMIT),
         cost_estimate=pl.CostEstimate(flops=10**9, bytes_accessed=10**6, transcendentals=0),
-    )(background, attn_weight, first_gain, second_gain)
+    )(background, attn_weight, instrument_table, first_gain, second_gain)
 
 
 def normed_of(plan, entries, sums, borders, gain):
@@ -557,11 +568,10 @@
     received = lax.all_to_all(sent, ("lon", "lat"), split_axis=0, concat_axis=0, tiled=True)
     north, south = before_and_after(swapped(up, down, "lat", wraps=False), "lat")
 
-    later, input_weight, attn_weight, down_weight, first_gain, second_gain, _ = (
-        lax.optimization_barrier(
-            (background, input_weight, attn_weight, down_weight, first_gain, second_gain, up)
-        )
-    )
+    held = (background, input_weight, instrument_table, attn_weight, down_weight)
+    held = lax.optimization_barrier((*held, first_gain, second_gain, up))
+    later, input_weight, instrument_table, attn_weight, down_weight = held[:5]
+    first_gain, second_gain = held[5:7]
 
     def columns(low, end):
         return jnp.concatenate([north[:, low:end], later[:, low:end], south[:, low:end]], axis=0)
@@ -569,8 +579,8 @@
     got = swapped(columns(0, HLON), columns(lon_cells - HLON, lon_cells), "lon", wraps=True)
 
     plan = rectangles(lat_cells, lon_cells)
-    rows, parts, gain_one, gain_two = prepared(
-        plan, later, attn_weight, first_gain, second_gain
+    rows, parts, tables, gain_one, gain_two = prepared(
+        plan, later, attn_weight, instrument_table, first_gain, second_gain
     )
     lat = lax.axis_index("lat")
     scalars = jnp.stack([lat == 0, lat < 0, lat == tiles_lat - 1]).astype(jnp.int32)
@@ -604,7 +614,7 @@
         south,
         rows,
         input_weight,
-        instrument_table,
+        tables,
         lift_weight,
         gain_one,
         *weights,

time: 27.2 us -> 27.2 us (level)
  waiting for transfers between devices: 2.68 us -> 2.99 us
    ppermute x4, waiting for transfers between devices: 2.68 us -> 2.99 us  [swapped(): got.append(lax.ppermute(mine, axis, pairs))]
where the time goes in v22:
time: 27.2 us; the launch traced here: 26.9 us
  starting transfers between devices  11.5 us (42%)
  Pallas kernels  9.72 us (36%)
  waiting for transfers between devices  2.99 us (11%)
  local copies, waits for them, and re-layouts  1.86 us (7%)
  other arithmetic  0.66 us (2%)
    all_to_all x1, starting transfers between devices, local(): lax.all_to_all(sent, ('lon', 'lat'), split_axis=0, concat_axis=0, tiled=T...  7.3 us
    ppermute x4, starting transfers between devices, swapped(): got.append(lax.ppermute(mine, axis, pairs))  4.15 us
    pallas_call x1, Pallas kernels, local(): pl.pallas_call(functools.partial(side_kernel, plan, lat_cells), out_shape...  3.98 us
    pallas_call x1, Pallas kernels, local(): pl.pallas_call(functools.partial(middle_kernel, plan, lat_cells, lon_cell...  3.8 us
    ppermute x4, waiting for transfers between devices, swapped(): got.append(lax.ppermute(mine, axis, pairs))  2.99 us
    pallas_call x1, Pallas kernels, packed(): pl.pallas_call(pack_kernel, out_shape=[jax.ShapeDtypeStruct(shape, BF16),...  1.75 us
    unnamed x24, local copies, waits for them, and re-layouts  1.42 us
  transfers between devices with their start and end apart: 5, of which 2 were waited for; matrix products, arithmetic and copies ran while one was open for 3% of the time, Pallas kernels for 15%

profile of v22, /device:TPU:0, one launch (start us, length us, event | category | flops | bytes accessed | tf_op | source)
XLA Modules:
  0.0 26.9 jit_solution(157621793255842325)
XLA Ops:
  0.0 1.8 %shard_map.136 = (bf16[8,4,10,2,128]{4,3,2,1,0:T(2,128)(2,1)}, bf16[3,24,2,192]{3,2,1,0:T(2,128)(2,1)}, bf16[3,24,2,192]{3,2,1,0:T(2,128)(2,1)}) custom-call(bf16[8,4,2,128]{3,2,1,0:T(2,128)(2,1)} %values_ref.1, s32[8,8]{1,0:T(8,128)} %bitcast.30, s32[8,8]{1,0:T(8,128)} %bitcast.31, s32[4,8]{1,0:T(4,128)} %bitcast.32, bf16[12,24,2,192]{3,2,1,0:T(2,128)(2,1)} %back_ref.2), custom_call_target="tpu_custom_call" | custom-call | flops 20000000000 | bytes 1000000 | tf_op jit(solution)/shard_map/pallas_call | solution.py:184
  1.8 0.0 copy-start.9
  1.8 0.0 copy-start.10
  1.8 7.3 %all-to-all-start = ((bf16[32,10,2,128]{3,2,1,0:T(2,128)(2,1)}), bf16[32,10,2,128]{3,2,1,0:T(2,128)(2,1)S(1)}, u32[]{:S(2)}, u32[]{:S(2)}) async-start(bf16[32,10,2,128]{3,2,1,0:T(2,128)(2,1)} %bitcast.23), calls=%async_computation | async-start | bytes 327680 | tf_op jit(solution)/shard_map/all_to_all | solution.py:568
  9.1 0.0 copy-start.8
  9.1 0.0 copy-done.9
  9.1 0.0 copy-done.10
  9.1 0.0 copy-start.11
  9.2 1.8 %collective-permute-start.1 = (bf16[3,24,2,192]{3,2,1,0:T(2,128)(2,1)S(1)}, bf16[3,24,2,192]{3,2,1,0:T(2,128)(2,1)S(1)}, u32[]{:S(2)}, u32[]{:S(2)}) collective-permute-start(bf16[3,24,2,192]{3,2,1,0:T(2,128)(2,1)S(1)} %bitcast.27), channel_id=1, source_target_pairs={{0,1},{1,0},{2,3},{3,2},{4,5},{5,4},{6,7},{7,6},{8,9},{9,8},{10,11... | collective-permute-start | bytes 165896 | tf_op jit(solution)/shard_map/ppermute | solution.py:39
  11.0 0.7 %collective-permute-start = (bf16[3,24,2,192]{3,2,1,0:T(2,128)(2,1)S(1)}, bf16[3,24,2,192]{3,2,1,0:T(2,128)(2,1)S(1)}, u32[]{:S(2)}, u32[]{:S(2)}) collective-permute-start(bf16[3,24,2,192]{3,2,1,0:T(2,128)(2,1)S(1)} %bitcast.25), channel_id=1, source_target_pairs={{1,2},{2,1},{5,6},{6,5},{9,10},{10,9},{13,14},{14,13},{17,18},{18,... | collective-permute-start | bytes 165896 | tf_op jit(solution)/shard_map/ppermute | solution.py:39
  11.7 0.0 copy-done.11
  11.7 0.1 copy.15.first_ref
  11.8 0.0 copy-done.8
  11.8 0.0 copy-start
  11.8 0.2 copy.16.refs_4_
  12.0 0.0 copy-start.2
  12.0 0.8 %copy-done = bf16[12,24,2,192]{3,2,1,0:T(2,128)(2,1)S(1)} copy-done((bf16[12,24,2,192]{3,2,1,0:T(2,128)(2,1)S(1)}, bf16[12,24,2,192]{3,2,1,0:T(2,128)(2,1)}, u32[]{:S(2)}) %copy-start) | copy-done | bytes 221208
  12.8 0.1 fusion
  12.9 0.0 copy-start.5
  12.9 0.0 copy-start.6
  12.9 0.0 copy-start.7
  12.9 0.1 add_convert_fusion.scalars_ref
  13.0 0.0 copy-done.2
  13.0 0.6 %copy-done.5 = bf16[8,192]{1,0:T(8,128)(2,1)S(1)} copy-done((bf16[8,192]{1,0:T(8,128)(2,1)S(1)}, bf16[8,192]{1,0:T(8,128)(2,1)}, u32[]{:S(2)}) %copy-start.5) | copy-done | bytes 3096
  13.6 0.0 copy-done.6
  13.6 0.0 copy-done.7
  13.6 0.2 shard_map.137
  13.8 2.2 %collective-permute-done.1 = bf16[3,24,2,192]{3,2,1,0:T(2,128)(2,1)S(1)} collective-permute-done((bf16[3,24,2,192]{3,2,1,0:T(2,128)(2,1)S(1)}, bf16[3,24,2,192]{3,2,1,0:T(2,128)(2,1)S(1)}, u32[]{:S(2)}, u32[]{:S(2)}) %collective-permute-start.1) | collective-permute-done | bytes 55328 | tf_op jit(solution)/shard_map/ppermute | solution.py:39
  16.0 0.0 collective-permute-done
  16.0 0.0 copy-start.1
  16.0 0.1 fusion.1
  16.1 0.0 copy-start.3
  16.1 0.0 copy-start.4
  16.1 0.4 %broadcast_select_fusion.2 = (bf16[18,6,2,192]{3,2,1,0:T(2,128)(2,1)S(1)}, bf16[18,6,2,192]{3,2,1,0:T(2,128)(2,1)S(1)}) fusion(pred[]{:T(512)S(6)} %eq.22, bf16[3,6,2,192]{3,2,1,0:T(2,128)(2,1)S(1)} %get-tuple-element.63, bf16[12,6,2,192]{3,2,1,0:T(2,128)(2,1)S(1)} %get-tuple-element.50, bf16[3,6,2,192]{3,2,1,0:T(2,128)(2,1)S(1)} %get-tuple-element.60, ...), kind=kLoop, calls=%fused_computation.2 | loop fusion | flops 248832 | bytes 331777 | tf_op jit(solution)/shard_map/jit(_where)/select_n | solution.py:33
  16.5 1.2 %collective-permute-start.2 = (bf16[18,6,2,192]{3,2,1,0:T(2,128)(2,1)S(1)}, bf16[18,6,2,192]{3,2,1,0:T(2,128)(2,1)S(1)}, u32[]{:S(2)}, u32[]{:S(2)}) collective-permute-start(bf16[18,6,2,192]{3,2,1,0:T(2,128)(2,1)S(1)} %get-tuple-element.54), channel_id=1, source_target_pairs={{4,8},{8,4},{12,16},{16,12},{20,24},{24,20},{28,0},{0,28},{5,9},{9... | collective-permute-start | bytes 248840 | tf_op jit(solution)/shard_map/ppermute | solution.py:39
  17.7 0.4 %collective-permute-start.3 = (bf16[18,6,2,192]{3,2,1,0:T(2,128)(2,1)S(1)}, bf16[18,6,2,192]{3,2,1,0:T(2,128)(2,1)S(1)}, u32[]{:S(2)}, u32[]{:S(2)}) collective-permute-start(bf16[18,6,2,192]{3,2,1,0:T(2,128)(2,1)S(1)} %get-tuple-element.53), channel_id=1, source_target_pairs={{0,4},{4,0},{8,12},{12,8},{16,20},{20,16},{24,28},{28,24},{1,5},{5... | collective-permute-start | bytes 248840 | tf_op jit(solution)/shard_map/ppermute | solution.py:39
  18.1 0.0 all-to-all-done.recv_ref
  18.1 0.0 copy-done.1
  18.1 0.0 copy-done.3
  18.1 0.0 copy-done.4
  18.1 3.8 %shard_map.138 = (bf16[12,12,2,192]{3,2,1,0:T(2,128)(2,1)S(1)}, f32[464,256]{1,0:T(8,128)S(1)}, f32[304,192]{1,0:T(8,128)S(1)}, f32[464,192]{1,0:T(8,128)S(1)}) custom-call(s32[3]{0:T(128)S(1)} %add_convert_fusion.scalars_ref, bf16[32,10,2,128]{3,2,1,0:T(2,128)(2,1)S(1)} %all-to-all-done.recv_ref, bf16[3,24,2,192]{3,2,1,0:T(2,128)(2,1)S(1)} %bitcast.22, ...), custom_call_target="tpu_custom_call" | custom-call | flops 4000000000 | bytes 4000000 | tf_op jit(solution)/shard_map/pallas_call | solution.py:596
  22.0 0.8 %collective-permute-done.2 = bf16[18,6,2,192]{3,2,1,0:T(2,128)(2,1)S(1)} collective-permute-done((bf16[18,6,2,192]{3,2,1,0:T(2,128)(2,1)S(1)}, bf16[18,6,2,192]{3,2,1,0:T(2,128)(2,1)S(1)}, u32[]{:S(2)}, u32[]{:S(2)}) %collective-permute-start.2) | collective-permute-done | bytes 82976 | tf_op jit(solution)/shard_map/ppermute | solution.py:39
  22.8 0.0 collective-permute-done.3
  22.8 0.2 broadcast_select_fusion
  23.0 4.0 %shard_map.139 = bf16[12,24,2,192]{3,2,1,0:T(2,128)(2,1)} custom-call(s32[3]{0:T(128)S(1)} %add_convert_fusion.scalars_ref, f32[464,256]{1,0:T(8,128)S(1)} %get-tuple-element.43.rest_ref, f32[304,192]{1,0:T(8,128)S(1)} %get-tuple-element.44.latent_ref, f32[464,192]{1,0:T(8,128)S(1)} %get-tuple-element.45.normed_ref, ...), custom_call_target="tpu_custom_call" | custom-call | flops 3000000000 | bytes 4000000 | tf_op jit(solution)/shard_map/pallas_call | solution.py:625
  (2 shorter events, 0.0 us)
Async XLA Ops:
  1.8 7.4 %copy-start.9 = (bf16[3,24,2,192]{3,2,1,0:T(2,128)(2,1)S(1)}, bf16[3,24,2,192]{3,2,1,0:T(2,128)(2,1)}, u32[]{:S(2)}) copy-start(bf16[3,24,2,192]{3,2,1,0:T(2,128)(2,1)} %get-tuple-element.28) | copy-start | bytes 165892
  1.8 7.4 %copy-start.10 = (bf16[3,24,2,192]{3,2,1,0:T(2,128)(2,1)S(1)}, bf16[3,24,2,192]{3,2,1,0:T(2,128)(2,1)}, u32[]{:S(2)}) copy-start(bf16[3,24,2,192]{3,2,1,0:T(2,128)(2,1)} %get-tuple-element.29) | copy-start | bytes 165892
  1.8 16.3 %all-to-all-start = ((bf16[32,10,2,128]{3,2,1,0:T(2,128)(2,1)}), bf16[32,10,2,128]{3,2,1,0:T(2,128)(2,1)S(1)}, u32[]{:S(2)}, u32[]{:S(2)}) async-start(bf16[32,10,2,128]{3,2,1,0:T(2,128)(2,1)} %bitcast.23), calls=%async_computation | async-start | bytes 327680 | tf_op jit(solution)/shard_map/all_to_all | solution.py:568
  9.1 2.7 %copy-start.8 = (bf16[768,192]{0,1:T(8,128)(2,1)S(1)}, bf16[768,192]{0,1:T(8,128)(2,1)}, u32[]{:S(2)}) copy-start(bf16[768,192]{0,1:T(8,128)(2,1)} %param.27) | copy-start | bytes 884740
  9.1 2.6 %copy-start.11 = (bf16[128,192]{0,1:T(8,128)(2,1)S(1)}, bf16[128,192]{0,1:T(8,128)(2,1)}, u32[]{:S(2)}) copy-start(bf16[128,192]{0,1:T(8,128)(2,1)} %param.19) | copy-start | bytes 147460
  9.2 6.8 %collective-permute-start.1 = (bf16[3,24,2,192]{3,2,1,0:T(2,128)(2,1)S(1)}, bf16[3,24,2,192]{3,2,1,0:T(2,128)(2,1)S(1)}, u32[]{:S(2)}, u32[]{:S(2)}) collective-permute-start(bf16[3,24,2,192]{3,2,1,0:T(2,128)(2,1)S(1)} %bitcast.27), channel_id=1, source_target_pairs={{0,1},{1,0},{2,3},{3,2},{4,5},{5,4},{6,7},{7,6},{8,9},{9,8},{10,11... | collective-permute-start | bytes 165896 | tf_op jit(solution)/shard_map/ppermute | solution.py:39
  11.0 5.0 %collective-permute-start = (bf16[3,24,2,192]{3,2,1,0:T(2,128)(2,1)S(1)}, bf16[3,24,2,192]{3,2,1,0:T(2,128)(2,1)S(1)}, u32[]{:S(2)}, u32[]{:S(2)}) collective-permute-start(bf16[3,24,2,192]{3,2,1,0:T(2,128)(2,1)S(1)} %bitcast.25), channel_id=1, source_target_pairs={{1,2},{2,1},{5,6},{6,5},{9,10},{10,9},{13,14},{14,13},{17,18},{18,... | collective-permute-start | bytes 165896 | tf_op jit(solution)/shard_map/ppermute | solution.py:39
  11.8 1.0 %copy-start = (bf16[12,24,2,192]{3,2,1,0:T(2,128)(2,1)S(1)}, bf16[12,24,2,192]{3,2,1,0:T(2,128)(2,1)}, u32[]{:S(2)}) copy-start(bf16[12,24,2,192]{3,2,1,0:T(2,128)(2,1)} %back_ref.2) | copy-start | bytes 663556
  12.0 1.0 %copy-start.2 = (bf16[192,576]{1,0:T(8,128)(2,1)S(1)}, bf16[192,576]{1,0:T(8,128)(2,1)}, u32[]{:S(2)}) copy-start(bf16[192,576]{1,0:T(8,128)(2,1)} %attn_ref) | copy-start | bytes 663556
  12.9 0.7 %copy-start.5 = (bf16[8,192]{1,0:T(8,128)(2,1)S(1)}, bf16[8,192]{1,0:T(8,128)(2,1)}, u32[]{:S(2)}) copy-start(bf16[8,192]{1,0:T(8,128)(2,1)} %table_ref) | copy-start | bytes 9220
  12.9 0.7 %copy-start.6 = (bf16[192]{0:T(256)(128)(2,1)S(1)}, bf16[192]{0:T(256)(128)(2,1)}, u32[]{:S(2)}) copy-start(bf16[192]{0:T(256)(128)(2,1)} %one_ref) | copy-start | bytes 1156
  12.9 0.7 %copy-start.7 = (bf16[192]{0:T(256)(128)(2,1)S(1)}, bf16[192]{0:T(256)(128)(2,1)}, u32[]{:S(2)}) copy-start(bf16[192]{0:T(256)(128)(2,1)} %two_ref) | copy-start | bytes 1156
  16.0 2.1 %copy-start.1 = (bf16[192,768]{1,0:T(8,128)(2,1)S(1)}, bf16[192,768]{1,0:T(8,128)(2,1)}, u32[]{:S(2)}) copy-start(bf16[192,768]{1,0:T(8,128)(2,1)} %refs_3_.3) | copy-start | bytes 884740
  16.1 2.1 %copy-start.3 = (bf16[192,384]{1,0:T(8,128)(2,1)S(1)}, bf16[192,384]{1,0:T(8,128)(2,1)}, u32[]{:S(2)}) copy-start(bf16[192,384]{1,0:T(8,128)(2,1)} %lift_ref.1) | copy-start | bytes 442372
  16.1 2.1 %copy-start.4 = (bf16[192,192]{1,0:T(8,128)(2,1)S(1)}, bf16[192,192]{1,0:T(8,128)(2,1)}, u32[]{:S(2)}) copy-start(bf16[192,192]{1,0:T(8,128)(2,1)} %refs_1_.3) | copy-start | bytes 221188
  16.5 6.3 %collective-permute-start.2 = (bf16[18,6,2,192]{3,2,1,0:T(2,128)(2,1)S(1)}, bf16[18,6,2,192]{3,2,1,0:T(2,128)(2,1)S(1)}, u32[]{:S(2)}, u32[]{:S(2)}) collective-permute-start(bf16[18,6,2,192]{3,2,1,0:T(2,128)(2,1)S(1)} %get-tuple-element.54), channel_id=1, source_target_pairs={{4,8},{8,4},{12,16},{16,12},{20,24},{24,20},{28,0},{0,28},{5,9},{9... | collective-permute-start | bytes 248840 | tf_op jit(solution)/shard_map/ppermute | solution.py:39
  17.7 5.1 %collective-permute-start.3 = (bf16[18,6,2,192]{3,2,1,0:T(2,128)(2,1)S(1)}, bf16[18,6,2,192]{3,2,1,0:T(2,128)(2,1)S(1)}, u32[]{:S(2)}, u32[]{:S(2)}) collective-permute-start(bf16[18,6,2,192]{3,2,1,0:T(2,128)(2,1)S(1)} %get-tuple-element.53), channel_id=1, source_target_pairs={{0,4},{4,0},{8,12},{12,8},{16,20},{20,16},{24,28},{28,24},{1,5},{5... | collective-permute-start | bytes 248840 | tf_op jit(solution)/shard_map/ppermute | solution.py:39

commit v23 on v22

--- a/solution.py
+++ b/solution.py
@@ -365,27 +365,30 @@
     return latent, normalise(latent, gain), spans
 
 
-def worked(plan, places, piece_of, own_normed, latent, weights, scalars_ref, put):
-    parts_ref, mix_ref, gain_ref, up_ref, down_ref = weights
+def stacks_of(plan, places, own_normed, weight):
+    width = weight.shape[0]
+    head = width // HEADS
+    query = dot(own_normed.astype(BF16), weight) * head ** (-0.5)
+    query = jnp.concatenate([query, jnp.ones((query.shape[0], PAD - width), F32)], axis=1)
+    lane = lax.broadcasted_iota(jnp.int32, (1, PAD), 1)
+    stacks, begin = [], 0
+    for i, j in places:
+        rows = padded(tokens_of(plan[4][3 * i + j]))
+        part = query[begin : begin + rows]
+        begin += rows
+        stacks.append(
+            below(
+                *[jnp.where((lane // head == h) | (lane >= width), part, 0.0) for h in range(HEADS)]
+            ).astype(BF16)
+        )
+    return stacks
+
+
+def worked(plan, places, stacks, keys, values, latent, weights, scalars_ref, put):
+    mix_ref, gain_ref, up_ref, down_ref = weights
     width = mix_ref.shape[0]
+    head = width // HEADS
     groups = [padded(tokens_of(plan[4][3 * i + j])) for i, j in places]
-    windows = []
-    for i, j in places:
-        window = [piece_of(4, 3 * i + j)]
-        if i != 1:
-            window.append(piece_of(3 * i + 1, j))
-        if j != 1:
-            window.append(piece_of(3 + j, i))
-        if i != 1 and j != 1:
-            window.append(piece_of(3 * i + j, 0))
-        windows.append(window)
-    tokens = below(*[piece for window in windows for piece in window]).astype(BF16)
-    head = width // HEADS
-    query = dot(own_normed.astype(BF16), parts_ref[0]) * head ** (-0.5)
-    query = jnp.concatenate([query, jnp.ones((query.shape[0], PAD - width), F32)], axis=1)
-    keys = dot(tokens, parts_ref[1])
-    values = with_ones(dot(tokens, parts_ref[2]))
-
     lane = lax.broadcasted_iota(jnp.int32, (1, PAD), 1)
     many = WLAT * WLON * LEV
     corner = HLAT * HLON * LEV
@@ -403,22 +406,15 @@
             else:
                 inside = (key < corner) | ((key >= 2 * corner) & (key < 3 * corner))
             bias = jnp.where(inside | (spare > 0), 0.0, -3e38) * scalars_ref[i].astype(F32)
-        here = jnp.concatenate([keys[w * many : (w + 1) * many], bias], axis=1)
+        here = jnp.concatenate([keys[w], bias], axis=1)
         return below(here.astype(BF16), unused)
 
     begins = [sum(groups[:w]) for w in range(len(groups))]
-    parts = [query[begin : begin + rows] for begin, rows in zip(begins, groups)]
-    stacks = [
-        below(
-            *[jnp.where((lane // head == h) | (lane >= width), part, 0.0) for h in range(HEADS)]
-        ).astype(BF16)
-        for part in parts
-    ]
     held = [keys_of(w, i, j) for w, (i, j) in enumerate(places)]
     scores = [dot_nt(stack, here) for stack, here in zip(stacks, held)]
     largest = [jnp.max(score, axis=-1, keepdims=True) for score in scores]
     raised = [jnp.exp((score - most).astype(BF16)) for score, most in zip(scores, largest)]
-    held = [below(values[w * many : (w + 1) * many], nothing) for w in range(len(places))]
+    held = [below(with_ones(value).astype(BF16), nothing) for value in values]
     products = [dot(one, here) for one, here in zip(raised, held)]
     shares = [about_one_over(product[:, width : width + 1]) for product in products]
     products = [product[:, :width] * share for product, share in zip(products, shares)]
@@ -464,7 +460,7 @@
     gain_one_ref,
     *refs,
 ):
-    *weights, out_ref, rest_ref, latent_ref, normed_ref = refs
+    parts_ref, *weights, out_ref, rest_ref, latent_ref, keys_ref, values_ref, stacks_ref = refs
     sums = scattered(recv_ref, first_ref, table_ref, lift_ref, plan, lon_cells)
 
     def sums_of(entries):
@@ -487,12 +483,42 @@
         out_ref[part[0] : part[0] + part[1]] = piece
 
     end = own_rows(plan, MIDDLE)
-    worked(plan, MIDDLE, piece_of, normed[:end], latent[:end], weights, scalars_ref, put)
+    many = WLAT * WLON * LEV
+    tokens = []
+    for i, j in MIDDLE:
+        tokens.append(piece_of(4, 3 * i + j))
+        if i != 1:
+            tokens.append(piece_of(3 * i + 1, j))
+    tokens = below(*tokens).astype(BF16)
+    keys, values = dot(tokens, parts_ref[1]), dot(tokens, parts_ref[2])
+    spots = [slice(w * many, (w + 1) * many) for w in range(len(MIDDLE))]
+    worked(
+        plan,
+        MIDDLE,
+        stacks_of(plan, MIDDLE, normed[:end], parts_ref[0]),
+        [keys[spot] for spot in spots],
+        [values[spot] for spot in spots],
+        latent[:end],
+        weights,
+        scalars_ref,
+        put,
+    )
     rest_ref[...] = sums_of(far_entries(SIDES))
     entries = near_entries(SIDES)
-    latent, normed, _ = normed_of(plan, entries, sums_of(entries), borders, gain)
-    latent_ref[...] = latent[: latent_ref.shape[0]]
-    normed_ref[...] = normed
+    latent, normed, spans = normed_of(plan, entries, sums_of(entries), borders, gain)
+    end = latent_ref.shape[0]
+    latent_ref[...] = latent[:end]
+    tokens = []
+    for i, j in SIDES:
+        start, count = spans[4, 3 * i + j]
+        tokens.append(normed[start : start + count])
+        if i != 1:
+            start, count = spans[3 * i + 1, j]
+            tokens.append(normed[start : start + count])
+    tokens = below(*tokens).astype(BF16)
+    keys_ref[...] = dot(tokens, parts_ref[1])
+    values_ref[...] = dot(tokens, parts_ref[2])
+    stacks_ref[...] = below(*stacks_of(plan, SIDES, normed[:end], parts_ref[0]))
 
 
 def side_kernel(
@@ -501,37 +527,50 @@
     scalars_ref,
     rest_ref,
     latent_ref,
-    normed_ref,
+    keys_ref,
+    values_ref,
+    stacks_ref,
     west_ref,
     east_ref,
     gain_one_ref,
     *refs,
 ):
-    *weights, middle_ref, out_ref, held_ref, sem = refs
+    parts_ref, *weights, middle_ref, out_ref, held_ref, sem = refs
     left, wide = plan[4][4][2:]
     copies = [pltpu.make_async_copy(middle_ref, out_ref.at[:, left : left + wide], sem.at[2])]
     copies[0].start()
-    near, start = {}, 0
-    for tile, number in near_entries(SIDES):
-        near[tile, number] = start
-        start += padded(tokens_of(plan[tile][number]))
     borders = (None, None, None, west_ref, east_ref, lat_cells)
     gain = gain_one_ref[:1, :]
     _, far, spans = normed_of(plan, far_entries(SIDES), rest_ref[...], borders, gain)
 
-    def piece_of(tile, number):
-        if (tile, number) in spans:
-            start, count = spans[tile, number]
-            return far[start : start + count]
-        start = near[tile, number]
-        return normed_ref[start : start + tokens_of(plan[tile][number]), :]
+    tokens = []
+    for i, j in SIDES:
+        for entry in [(3 + j, i)] + ([(3 * i + j, 0)] if i != 1 else []):
+            start, count = spans[entry]
+            tokens.append(far[start : start + count])
+    tokens = below(*tokens).astype(BF16)
+    keys, values = dot(tokens, parts_ref[1]), dot(tokens, parts_ref[2])
+    half = WLAT * HLON * LEV
+    spots = [slice(w * half, (w + 1) * half) for w in range(len(SIDES))]
+    stacks, start = [], 0
+    for i, j in SIDES:
+        rows = HEADS * padded(tokens_of(plan[4][3 * i + j]))
+        stacks.append(stacks_ref[start : start + rows, :])
+        start += rows
 
     def put(part, j, piece):
         held_ref[j // 2, part[0] : part[0] + part[1]] = piece
 
-    end = own_rows(plan, SIDES)
     worked(
-        plan, SIDES, piece_of, normed_ref[:end, :], latent_ref[...], weights, scalars_ref, put
+        plan,
+        SIDES,
+        stacks,
+        [below(keys_ref[spot, :], keys[spot]) for spot in spots],
+        [below(values_ref[spot, :], values[spot]) for spot in spots],
+        latent_ref[...],
+        weights,
+        scalars_ref,
+        put,
     )
     for n, number in enumerate((0, 2)):
         left, wide = plan[4][number][2:]
@@ -593,16 +632,19 @@
     vmem = pl.BlockSpec(memory_space=pltpu.VMEM)
     anywhere = pl.BlockSpec(memory_space=pl.ANY)
     params = pltpu.CompilerParams(vmem_limit_bytes=LIMIT)
-    middle, rest, latent, normed = pl.pallas_call(
+    half = WLAT * HLON * LEV * len(SIDES)
+    middle, rest, latent, *near = pl.pallas_call(
         functools.partial(middle_kernel, plan, lat_cells, lon_cells),
         out_shape=[
             jax.ShapeDtypeStruct((lat_cells, lon_cells - WLON, LEV, width), BF16),
             jax.ShapeDtypeStruct((rows_in(far_entries(SIDES)), PAD), F32),
             jax.ShapeDtypeStruct((own_rows(plan, SIDES), width), F32),
-            jax.ShapeDtypeStruct((rows_in(near_entries(SIDES)), width), F32),
+            jax.ShapeDtypeStruct((half, width), F32),
+            jax.ShapeDtypeStruct((half, width), F32),
+            jax.ShapeDtypeStruct((HEADS * own_rows(plan, SIDES), PAD), BF16),
         ],
         in_specs=[smem] + [vmem] * (8 + len(weights)),
-        out_specs=[vmem] * 4,
+        out_specs=[vmem] * 6,
         compiler_params=params,
         cost_estimate=pl.CostEstimate(
             flops=4 * 10**9, bytes_accessed=4 * 10**6, transcendentals=10**6
@@ -625,7 +667,7 @@
     return pl.pallas_call(
         functools.partial(side_kernel, plan, lat_cells),
         out_shape=jax.ShapeDtypeStruct(background.shape, BF16),
-        in_specs=[smem] + [vmem] * (7 + len(weights)),
+        in_specs=[smem] + [vmem] * (9 + len(weights)),
         out_specs=anywhere,
         scratch_shapes=[
             pltpu.VMEM((2, lat_cells, HLON, LEV, width), BF16),
@@ -635,7 +677,7 @@
         cost_estimate=pl.CostEstimate(
             flops=3 * 10**9, bytes_accessed=4 * 10**6, transcendentals=10**6
         ),
-    )(scalars, rest, latent, normed, west, east, gain_one, *weights, middle)
+    )(scalars, rest, latent, *near, west, east, gain_one, *weights, middle)
 
 
 def solution(mesh):

time: 27.2 us -> 27 us (level)
  transfers between devices with their start and end apart: 5 -> 5, of which waited for: 2 -> 2; matrix products, arithmetic and copies ran while one was open for 3% -> 3% of each run, Pallas kernels for 15% -> 16%
where the time goes in v23:
time: 27 us; the launch traced here: 26.7 us
  starting transfers between devices  11.5 us (43%)
  Pallas kernels  9.75 us (36%)
  waiting for transfers between devices  2.74 us (10%)
  local copies, waits for them, and re-layouts  1.86 us (7%)
  other arithmetic  0.66 us (2%)
    all_to_all x1, starting transfers between devices, local(): lax.all_to_all(sent, ('lon', 'lat'), split_axis=0, concat_axis=0, tiled=T...  7.3 us
    ppermute x4, starting transfers between devices, swapped(): got.append(lax.ppermute(mine, axis, pairs))  4.15 us
    pallas_call x1, Pallas kernels, local(): pl.pallas_call(functools.partial(middle_kernel, plan, lat_cells, lon_cell...  4.05 us
    pallas_call x1, Pallas kernels, local(): pl.pallas_call(functools.partial(side_kernel, plan, lat_cells), out_shape...  3.76 us
    ppermute x4, waiting for transfers between devices, swapped(): got.append(lax.ppermute(mine, axis, pairs))  2.74 us
    pallas_call x1, Pallas kernels, packed(): pl.pallas_call(pack_kernel, out_shape=[jax.ShapeDtypeStruct(shape, BF16),...  1.75 us
    unnamed x24, local copies, waits for them, and re-layouts  1.42 us
  transfers between devices with their start and end apart: 5, of which 2 were waited for; matrix products, arithmetic and copies ran while one was open for 3% of the time, Pallas kernels for 16%

profile of v23, /device:TPU:0, one launch (start us, length us, event | category | flops | bytes accessed | tf_op | source)
XLA Modules:
  0.0 26.7 jit_solution(14985444156095071742)
XLA Ops:
  0.0 1.8 %shard_map.136 = (bf16[8,4,10,2,128]{4,3,2,1,0:T(2,128)(2,1)}, bf16[3,24,2,192]{3,2,1,0:T(2,128)(2,1)}, bf16[3,24,2,192]{3,2,1,0:T(2,128)(2,1)}) custom-call(bf16[8,4,2,128]{3,2,1,0:T(2,128)(2,1)} %values_ref.1, s32[8,8]{1,0:T(8,128)} %bitcast.30, s32[8,8]{1,0:T(8,128)} %bitcast.31, s32[4,8]{1,0:T(4,128)} %bitcast.32, bf16[12,24,2,192]{3,2,1,0:T(2,128)(2,1)} %back_ref.2), custom_call_target="tpu_custom_call" | custom-call | flops 20000000000 | bytes 1000000 | tf_op jit(solution)/shard_map/pallas_call | solution.py:184
  1.8 0.0 copy-start.9
  1.8 0.0 copy-start.10
  1.8 7.3 %all-to-all-start = ((bf16[32,10,2,128]{3,2,1,0:T(2,128)(2,1)}), bf16[32,10,2,128]{3,2,1,0:T(2,128)(2,1)S(1)}, u32[]{:S(2)}, u32[]{:S(2)}) async-start(bf16[32,10,2,128]{3,2,1,0:T(2,128)(2,1)} %bitcast.23), calls=%async_computation | async-start | bytes 327680 | tf_op jit(solution)/shard_map/all_to_all | solution.py:607
  9.1 0.0 copy-start.8
  9.1 0.0 copy-done.9
  9.1 0.0 copy-done.10
  9.1 0.0 copy-start.11
  9.2 1.8 %collective-permute-start.1 = (bf16[3,24,2,192]{3,2,1,0:T(2,128)(2,1)S(1)}, bf16[3,24,2,192]{3,2,1,0:T(2,128)(2,1)S(1)}, u32[]{:S(2)}, u32[]{:S(2)}) collective-permute-start(bf16[3,24,2,192]{3,2,1,0:T(2,128)(2,1)S(1)} %bitcast.27), channel_id=1, source_target_pairs={{0,1},{1,0},{2,3},{3,2},{4,5},{5,4},{6,7},{7,6},{8,9},{9,8},{10,11... | collective-permute-start | bytes 165896 | tf_op jit(solution)/shard_map/ppermute | solution.py:39
  11.0 0.7 %collective-permute-start = (bf16[3,24,2,192]{3,2,1,0:T(2,128)(2,1)S(1)}, bf16[3,24,2,192]{3,2,1,0:T(2,128)(2,1)S(1)}, u32[]{:S(2)}, u32[]{:S(2)}) collective-permute-start(bf16[3,24,2,192]{3,2,1,0:T(2,128)(2,1)S(1)} %bitcast.25), channel_id=1, source_target_pairs={{1,2},{2,1},{5,6},{6,5},{9,10},{10,9},{13,14},{14,13},{17,18},{18,... | collective-permute-start | bytes 165896 | tf_op jit(solution)/shard_map/ppermute | solution.py:39
  11.7 0.0 copy-done.11
  11.7 0.1 copy.15.first_ref
  11.8 0.0 copy-done.8
  11.8 0.0 copy-start
  11.8 0.2 copy.16.refs_4_
  12.0 0.0 copy-start.2
  12.0 0.8 %copy-done = bf16[12,24,2,192]{3,2,1,0:T(2,128)(2,1)S(1)} copy-done((bf16[12,24,2,192]{3,2,1,0:T(2,128)(2,1)S(1)}, bf16[12,24,2,192]{3,2,1,0:T(2,128)(2,1)}, u32[]{:S(2)}) %copy-start) | copy-done | bytes 221208
  12.8 0.1 fusion
  12.9 0.0 copy-start.5
  12.9 0.0 copy-start.6
  12.9 0.0 copy-start.7
  12.9 0.1 add_convert_fusion.scalars_ref
  13.0 0.0 copy-done.2
  13.0 0.6 %copy-done.5 = bf16[8,192]{1,0:T(8,128)(2,1)S(1)} copy-done((bf16[8,192]{1,0:T(8,128)(2,1)S(1)}, bf16[8,192]{1,0:T(8,128)(2,1)}, u32[]{:S(2)}) %copy-start.5) | copy-done | bytes 3096
  13.6 0.0 copy-done.6
  13.6 0.0 copy-done.7
  13.6 0.2 shard_map.137
  13.8 2.2 %collective-permute-done.1 = bf16[3,24,2,192]{3,2,1,0:T(2,128)(2,1)S(1)} collective-permute-done((bf16[3,24,2,192]{3,2,1,0:T(2,128)(2,1)S(1)}, bf16[3,24,2,192]{3,2,1,0:T(2,128)(2,1)S(1)}, u32[]{:S(2)}, u32[]{:S(2)}) %collective-permute-start.1) | collective-permute-done | bytes 55328 | tf_op jit(solution)/shard_map/ppermute | solution.py:39
  16.0 0.0 collective-permute-done
  16.0 0.0 copy-start.1
  16.0 0.1 fusion.1
  16.1 0.0 copy-start.3
  16.1 0.0 copy-start.4
  16.1 0.4 %broadcast_select_fusion.2 = (bf16[18,6,2,192]{3,2,1,0:T(2,128)(2,1)S(1)}, bf16[18,6,2,192]{3,2,1,0:T(2,128)(2,1)S(1)}) fusion(pred[]{:T(512)S(6)} %eq.22, bf16[3,6,2,192]{3,2,1,0:T(2,128)(2,1)S(1)} %get-tuple-element.67, bf16[12,6,2,192]{3,2,1,0:T(2,128)(2,1)S(1)} %get-tuple-element.54, bf16[3,6,2,192]{3,2,1,0:T(2,128)(2,1)S(1)} %get-tuple-element.64, ...), kind=kLoop, calls=%fused_computation.2 | loop fusion | flops 248832 | bytes 331777 | tf_op jit(solution)/shard_map/jit(_where)/select_n | solution.py:33
  16.5 1.2 %collective-permute-start.2 = (bf16[18,6,2,192]{3,2,1,0:T(2,128)(2,1)S(1)}, bf16[18,6,2,192]{3,2,1,0:T(2,128)(2,1)S(1)}, u32[]{:S(2)}, u32[]{:S(2)}) collective-permute-start(bf16[18,6,2,192]{3,2,1,0:T(2,128)(2,1)S(1)} %get-tuple-element.58), channel_id=1, source_target_pairs={{4,8},{8,4},{12,16},{16,12},{20,24},{24,20},{28,0},{0,28},{5,9},{9... | collective-permute-start | bytes 248840 | tf_op jit(solution)/shard_map/ppermute | solution.py:39
  17.7 0.4 %collective-permute-start.3 = (bf16[18,6,2,192]{3,2,1,0:T(2,128)(2,1)S(1)}, bf16[18,6,2,192]{3,2,1,0:T(2,128)(2,1)S(1)}, u32[]{:S(2)}, u32[]{:S(2)}) collective-permute-start(bf16[18,6,2,192]{3,2,1,0:T(2,128)(2,1)S(1)} %get-tuple-element.57), channel_id=1, source_target_pairs={{0,4},{4,0},{8,12},{12,8},{16,20},{20,16},{24,28},{28,24},{1,5},{5... | collective-permute-start | bytes 248840 | tf_op jit(solution)/shard_map/ppermute | solution.py:39
  18.1 0.0 all-to-all-done.recv_ref
  18.1 0.0 copy-done.1
  18.1 0.0 copy-done.3
  18.1 0.0 copy-done.4
  18.1 4.1 %shard_map.138 = (bf16[12,12,2,192]{3,2,1,0:T(2,128)(2,1)S(1)}, f32[464,256]{1,0:T(8,128)S(1)}, f32[304,192]{1,0:T(8,128)S(1)}, f32[432,192]{1,0:T(8,128)S(1)}, ...) custom-call(s32[3]{0:T(128)S(1)} %add_convert_fusion.scalars_ref, ...), custom_call_target="tpu_custom_call" | custom-call | flops 4000000000 | bytes 4000000 | tf_op jit(solution)/shard_map/pallas_call | solution.py:636
  22.2 0.6 %collective-permute-done.2 = bf16[18,6,2,192]{3,2,1,0:T(2,128)(2,1)S(1)} collective-permute-done((bf16[18,6,2,192]{3,2,1,0:T(2,128)(2,1)S(1)}, bf16[18,6,2,192]{3,2,1,0:T(2,128)(2,1)S(1)}, u32[]{:S(2)}, u32[]{:S(2)}) %collective-permute-start.2) | collective-permute-done | bytes 82976 | tf_op jit(solution)/shard_map/ppermute | solution.py:39
  22.8 0.0 collective-permute-done.3
  22.8 0.2 broadcast_select_fusion
  23.0 3.8 %shard_map.139 = bf16[12,24,2,192]{3,2,1,0:T(2,128)(2,1)} custom-call(s32[3]{0:T(128)S(1)} %add_convert_fusion.scalars_ref, f32[464,256]{1,0:T(8,128)S(1)} %get-tuple-element.45.rest_ref, f32[304,192]{1,0:T(8,128)S(1)} %get-tuple-element.46.latent_ref, f32[432,192]{1,0:T(8,128)S(1)} %get-tuple-element.47.keys_ref, ...), custom_call_target="tpu_custom_call" | custom-call | flops 3000000000 | bytes 4000000 | tf_op jit(solution)/shard_map/pallas_call | solution.py:667
  (2 shorter events, 0.0 us)
Async XLA Ops:
  1.8 7.4 %copy-start.9 = (bf16[3,24,2,192]{3,2,1,0:T(2,128)(2,1)S(1)}, bf16[3,24,2,192]{3,2,1,0:T(2,128)(2,1)}, u32[]{:S(2)}) copy-start(bf16[3,24,2,192]{3,2,1,0:T(2,128)(2,1)} %get-tuple-element.30) | copy-start | bytes 165892
  1.8 7.4 %copy-start.10 = (bf16[3,24,2,192]{3,2,1,0:T(2,128)(2,1)S(1)}, bf16[3,24,2,192]{3,2,1,0:T(2,128)(2,1)}, u32[]{:S(2)}) copy-start(bf16[3,24,2,192]{3,2,1,0:T(2,128)(2,1)} %get-tuple-element.31) | copy-start | bytes 165892
  1.8 16.3 %all-to-all-start = ((bf16[32,10,2,128]{3,2,1,0:T(2,128)(2,1)}), bf16[32,10,2,128]{3,2,1,0:T(2,128)(2,1)S(1)}, u32[]{:S(2)}, u32[]{:S(2)}) async-start(bf16[32,10,2,128]{3,2,1,0:T(2,128)(2,1)} %bitcast.23), calls=%async_computation | async-start | bytes 327680 | tf_op jit(solution)/shard_map/all_to_all | solution.py:607
  9.1 2.7 %copy-start.8 = (bf16[768,192]{0,1:T(8,128)(2,1)S(1)}, bf16[768,192]{0,1:T(8,128)(2,1)}, u32[]{:S(2)}) copy-start(bf16[768,192]{0,1:T(8,128)(2,1)} %param.27) | copy-start | bytes 884740
  9.1 2.6 %copy-start.11 = (bf16[128,192]{0,1:T(8,128)(2,1)S(1)}, bf16[128,192]{0,1:T(8,128)(2,1)}, u32[]{:S(2)}) copy-start(bf16[128,192]{0,1:T(8,128)(2,1)} %param.19) | copy-start | bytes 147460
  9.2 6.8 %collective-permute-start.1 = (bf16[3,24,2,192]{3,2,1,0:T(2,128)(2,1)S(1)}, bf16[3,24,2,192]{3,2,1,0:T(2,128)(2,1)S(1)}, u32[]{:S(2)}, u32[]{:S(2)}) collective-permute-start(bf16[3,24,2,192]{3,2,1,0:T(2,128)(2,1)S(1)} %bitcast.27), channel_id=1, source_target_pairs={{0,1},{1,0},{2,3},{3,2},{4,5},{5,4},{6,7},{7,6},{8,9},{9,8},{10,11... | collective-permute-start | bytes 165896 | tf_op jit(solution)/shard_map/ppermute | solution.py:39
  11.0 5.0 %collective-permute-start = (bf16[3,24,2,192]{3,2,1,0:T(2,128)(2,1)S(1)}, bf16[3,24,2,192]{3,2,1,0:T(2,128)(2,1)S(1)}, u32[]{:S(2)}, u32[]{:S(2)}) collective-permute-start(bf16[3,24,2,192]{3,2,1,0:T(2,128)(2,1)S(1)} %bitcast.25), channel_id=1, source_target_pairs={{1,2},{2,1},{5,6},{6,5},{9,10},{10,9},{13,14},{14,13},{17,18},{18,... | collective-permute-start | bytes 165896 | tf_op jit(solution)/shard_map/ppermute | solution.py:39
  11.8 1.0 %copy-start = (bf16[12,24,2,192]{3,2,1,0:T(2,128)(2,1)S(1)}, bf16[12,24,2,192]{3,2,1,0:T(2,128)(2,1)}, u32[]{:S(2)}) copy-start(bf16[12,24,2,192]{3,2,1,0:T(2,128)(2,1)} %back_ref.2) | copy-start | bytes 663556
  12.0 1.0 %copy-start.2 = (bf16[192,576]{1,0:T(8,128)(2,1)S(1)}, bf16[192,576]{1,0:T(8,128)(2,1)}, u32[]{:S(2)}) copy-start(bf16[192,576]{1,0:T(8,128)(2,1)} %attn_ref) | copy-start | bytes 663556
  12.9 0.7 %copy-start.5 = (bf16[8,192]{1,0:T(8,128)(2,1)S(1)}, bf16[8,192]{1,0:T(8,128)(2,1)}, u32[]{:S(2)}) copy-start(bf16[8,192]{1,0:T(8,128)(2,1)} %table_ref) | copy-start | bytes 9220
  12.9 0.7 %copy-start.6 = (bf16[192]{0:T(256)(128)(2,1)S(1)}, bf16[192]{0:T(256)(128)(2,1)}, u32[]{:S(2)}) copy-start(bf16[192]{0:T(256)(128)(2,1)} %one_ref) | copy-start | bytes 1156
  12.9 0.7 %copy-start.7 = (bf16[192]{0:T(256)(128)(2,1)S(1)}, bf16[192]{0:T(256)(128)(2,1)}, u32[]{:S(2)}) copy-start(bf16[192]{0:T(256)(128)(2,1)} %two_ref) | copy-start | bytes 1156
  16.0 2.1 %copy-start.1 = (bf16[192,768]{1,0:T(8,128)(2,1)S(1)}, bf16[192,768]{1,0:T(8,128)(2,1)}, u32[]{:S(2)}) copy-start(bf16[192,768]{1,0:T(8,128)(2,1)} %refs_3_.3) | copy-start | bytes 884740
  16.1 2.1 %copy-start.3 = (bf16[192,384]{1,0:T(8,128)(2,1)S(1)}, bf16[192,384]{1,0:T(8,128)(2,1)}, u32[]{:S(2)}) copy-start(bf16[192,384]{1,0:T(8,128)(2,1)} %lift_ref.1) | copy-start | bytes 442372
  16.1 2.1 %copy-start.4 = (bf16[192,192]{1,0:T(8,128)(2,1)S(1)}, bf16[192,192]{1,0:T(8,128)(2,1)}, u32[]{:S(2)}) copy-start(bf16[192,192]{1,0:T(8,128)(2,1)} %refs_1_.3) | copy-start | bytes 221188
  16.5 6.3 %collective-permute-start.2 = (bf16[18,6,2,192]{3,2,1,0:T(2,128)(2,1)S(1)}, bf16[18,6,2,192]{3,2,1,0:T(2,128)(2,1)S(1)}, u32[]{:S(2)}, u32[]{:S(2)}) collective-permute-start(bf16[18,6,2,192]{3,2,1,0:T(2,128)(2,1)S(1)} %get-tuple-element.58), channel_id=1, source_target_pairs={{4,8},{8,4},{12,16},{16,12},{20,24},{24,20},{28,0},{0,28},{5,9},{9... | collective-permute-start | bytes 248840 | tf_op jit(solution)/shard_map/ppermute | solution.py:39
  17.7 5.1 %collective-permute-start.3 = (bf16[18,6,2,192]{3,2,1,0:T(2,128)(2,1)S(1)}, bf16[18,6,2,192]{3,2,1,0:T(2,128)(2,1)S(1)}, u32[]{:S(2)}, u32[]{:S(2)}) collective-permute-start(bf16[18,6,2,192]{3,2,1,0:T(2,128)(2,1)S(1)} %get-tuple-element.57), channel_id=1, source_target_pairs={{0,4},{4,0},{8,12},{12,8},{16,20},{20,16},{24,28},{28,24},{1,5},{5... | collective-permute-start | bytes 248840 | tf_op jit(solution)/shard_map/ppermute | solution.py:39

commit v24 on v23

--- a/solution.py
+++ b/solution.py
@@ -352,7 +352,8 @@
                 top, left = {-1: 0, 0: top + HLAT, 1: lat_cells + HLAT}[dy], 0
             else:
                 ref, top = (north_ref, 0) if dy < 0 else (south_ref, 0)
-            piece = ref[top : top + high, left : left + wide].reshape(count, width).astype(F32)
+            block = ref(top, high) if dx else ref[top : top + high, left : left + wide]
+            piece = block.reshape(count, width).astype(F32)
             if full > count:
                 piece = below(piece, jnp.zeros((full - count, width), F32))
         pieces.append(piece)
@@ -530,8 +531,8 @@
     keys_ref,
     values_ref,
     stacks_ref,
-    west_ref,
-    east_ref,
+    one_ref,
+    two_ref,
     gain_one_ref,
     *refs,
 ):
@@ -539,7 +540,15 @@
     left, wide = plan[4][4][2:]
     copies = [pltpu.make_async_copy(middle_ref, out_ref.at[:, left : left + wide], sem.at[2])]
     copies[0].start()
-    borders = (None, None, None, west_ref, east_ref, lat_cells)
+    even = scalars_ref[3] == 1
+
+    def west(top, high):
+        return jnp.where(even, two_ref[top : top + high], one_ref[top : top + high])
+
+    def east(top, high):
+        return jnp.where(even, one_ref[top : top + high], two_ref[top : top + high])
+
+    borders = (None, None, None, west, east, lat_cells)
     gain = gain_one_ref[:1, :]
     _, far, spans = normed_of(plan, far_entries(SIDES), rest_ref[...], borders, gain)
 
@@ -622,7 +631,8 @@
         plan, later, attn_weight, instrument_table, first_gain, second_gain
     )
     lat = lax.axis_index("lat")
-    scalars = jnp.stack([lat == 0, lat < 0, lat == tiles_lat - 1]).astype(jnp.int32)
+    even = lax.axis_index("lon") % 2 == 0
+    scalars = jnp.stack([lat == 0, lat < 0, lat == tiles_lat - 1, even]).astype(jnp.int32)
 
     def rows_in(entries):
         return sum(padded(tokens_of(plan[tile][number])) for tile, number in entries)
@@ -663,7 +673,6 @@
     )
     rest, *got = lax.optimization_barrier((rest, *got[::-1]))
     got = got[::-1]
-    west, east = before_and_after(got, "lon")
     return pl.pallas_call(
         functools.partial(side_kernel, plan, lat_cells),
         out_shape=jax.ShapeDtypeStruct(background.shape, BF16),
@@ -677,7 +686,7 @@
         cost_estimate=pl.CostEstimate(
             flops=3 * 10**9, bytes_accessed=4 * 10**6, transcendentals=10**6
         ),
-    )(scalars, rest, latent, *near, west, east, gain_one, *weights, middle)
+    )(scalars, rest, latent, *near, *got, gain_one, *weights, middle)
 
 
 def solution(mesh):

time: 27 us -> 26.8 us (level)
  no operation moved by 1% of the time
where the time goes in v24:
time: 26.8 us; the launch traced here: 26.5 us
  starting transfers between devices  11.5 us (43%)
  Pallas kernels  9.75 us (36%)
  waiting for transfers between devices  2.59 us (10%)
  local copies, waits for them, and re-layouts  2 us (7%)
  other arithmetic  0.48 us (2%)
    all_to_all x1, starting transfers between devices, local(): lax.all_to_all(sent, ('lon', 'lat'), split_axis=0, concat_axis=0, tiled=T...  7.3 us
    ppermute x4, starting transfers between devices, swapped(): got.append(lax.ppermute(mine, axis, pairs))  4.15 us
    pallas_call x1, Pallas kernels, local(): pl.pallas_call(functools.partial(middle_kernel, plan, lat_cells, lon_cell...  4.06 us
    pallas_call x1, Pallas kernels, local(): pl.pallas_call(functools.partial(side_kernel, plan, lat_cells), out_shape...  3.76 us
    ppermute x4, waiting for transfers between devices, swapped(): got.append(lax.ppermute(mine, axis, pairs))  2.59 us
    pallas_call x1, Pallas kernels, packed(): pl.pallas_call(pack_kernel, out_shape=[jax.ShapeDtypeStruct(shape, BF16),...  1.74 us
    unnamed x24, local copies, waits for them, and re-layouts  1.56 us
  transfers between devices with their start and end apart: 5, of which 2 were waited for; matrix products, arithmetic and copies ran while one was open for 3% of the time, Pallas kernels for 16%

profile of v24, /device:TPU:0, one launch (start us, length us, event | category | flops | bytes accessed | tf_op | source)
XLA Modules:
  0.0 26.5 jit_solution(3219055759980645586)
XLA Ops:
  0.0 1.7 %shard_map.136 = (bf16[8,4,10,2,128]{4,3,2,1,0:T(2,128)(2,1)}, bf16[3,24,2,192]{3,2,1,0:T(2,128)(2,1)}, bf16[3,24,2,192]{3,2,1,0:T(2,128)(2,1)}) custom-call(bf16[8,4,2,128]{3,2,1,0:T(2,128)(2,1)} %values_ref.1, s32[8,8]{1,0:T(8,128)} %bitcast.31, s32[8,8]{1,0:T(8,128)} %bitcast.32, s32[4,8]{1,0:T(4,128)} %bitcast.33, bf16[12,24,2,192]{3,2,1,0:T(2,128)(2,1)} %back_ref.2), custom_call_target="tpu_custom_call" | custom-call | flops 20000000000 | bytes 1000000 | tf_op jit(solution)/shard_map/pallas_call | solution.py:184
  1.7 0.0 copy-start.9
  1.8 0.0 copy-start.10
  1.8 7.3 %all-to-all-start = ((bf16[32,10,2,128]{3,2,1,0:T(2,128)(2,1)}), bf16[32,10,2,128]{3,2,1,0:T(2,128)(2,1)S(1)}, u32[]{:S(2)}, u32[]{:S(2)}) async-start(bf16[32,10,2,128]{3,2,1,0:T(2,128)(2,1)} %bitcast.24), calls=%async_computation | async-start | bytes 327680 | tf_op jit(solution)/shard_map/all_to_all | solution.py:616
  9.1 0.0 copy-start.8
  9.1 0.0 copy-done.9
  9.1 0.0 copy-done.10
  9.1 0.0 copy-start.11
  9.2 1.8 %collective-permute-start.1 = (bf16[3,24,2,192]{3,2,1,0:T(2,128)(2,1)S(1)}, bf16[3,24,2,192]{3,2,1,0:T(2,128)(2,1)S(1)}, u32[]{:S(2)}, u32[]{:S(2)}) collective-permute-start(bf16[3,24,2,192]{3,2,1,0:T(2,128)(2,1)S(1)} %bitcast.28), channel_id=1, source_target_pairs={{0,1},{1,0},{2,3},{3,2},{4,5},{5,4},{6,7},{7,6},{8,9},{9,8},{10,11... | collective-permute-start | bytes 165896 | tf_op jit(solution)/shard_map/ppermute | solution.py:39
  11.0 0.7 %collective-permute-start = (bf16[3,24,2,192]{3,2,1,0:T(2,128)(2,1)S(1)}, bf16[3,24,2,192]{3,2,1,0:T(2,128)(2,1)S(1)}, u32[]{:S(2)}, u32[]{:S(2)}) collective-permute-start(bf16[3,24,2,192]{3,2,1,0:T(2,128)(2,1)S(1)} %bitcast.26), channel_id=1, source_target_pairs={{1,2},{2,1},{5,6},{6,5},{9,10},{10,9},{13,14},{14,13},{17,18},{18,... | collective-permute-start | bytes 165896 | tf_op jit(solution)/shard_map/ppermute | solution.py:39
  11.7 0.0 copy-done.11
  11.7 0.1 copy.15.first_ref
  11.8 0.0 copy-done.8
  11.8 0.0 copy-start
  11.8 0.2 copy.16.refs_4_
  12.0 0.8 %copy-done = bf16[12,24,2,192]{3,2,1,0:T(2,128)(2,1)S(1)} copy-done((bf16[12,24,2,192]{3,2,1,0:T(2,128)(2,1)S(1)}, bf16[12,24,2,192]{3,2,1,0:T(2,128)(2,1)}, u32[]{:S(2)}) %copy-start) | copy-done | bytes 221208
  12.8 0.0 copy-start.2
  12.8 0.1 fusion
  12.9 0.0 copy-start.5
  12.9 0.0 copy-start.6
  12.9 0.0 copy-start.7
  12.9 0.1 add_convert_fusion.scalars_ref
  13.0 0.7 %copy-done.2 = bf16[192,576]{1,0:T(8,128)(2,1)S(1)} copy-done((bf16[192,576]{1,0:T(8,128)(2,1)S(1)}, bf16[192,576]{1,0:T(8,128)(2,1)}, u32[]{:S(2)}) %copy-start.2) | copy-done | bytes 221208
  13.7 0.0 copy-done.5
  13.7 0.0 copy-done.6
  13.7 0.0 copy-done.7
  13.7 0.2 shard_map.137
  13.9 2.0 %collective-permute-done.1 = bf16[3,24,2,192]{3,2,1,0:T(2,128)(2,1)S(1)} collective-permute-done((bf16[3,24,2,192]{3,2,1,0:T(2,128)(2,1)S(1)}, bf16[3,24,2,192]{3,2,1,0:T(2,128)(2,1)S(1)}, u32[]{:S(2)}, u32[]{:S(2)}) %collective-permute-start.1) | collective-permute-done | bytes 55328 | tf_op jit(solution)/shard_map/ppermute | solution.py:39
  15.9 0.0 collective-permute-done
  16.0 0.0 copy-start.1
  16.0 0.1 fusion.1
  16.0 0.0 copy-start.3
  16.1 0.0 copy-start.4
  16.1 0.4 %broadcast_select_fusion = (bf16[18,6,2,192]{3,2,1,0:T(2,128)(2,1)S(1)}, bf16[18,6,2,192]{3,2,1,0:T(2,128)(2,1)S(1)}) fusion(pred[]{:T(512)} %eq.21, bf16[3,6,2,192]{3,2,1,0:T(2,128)(2,1)S(1)} %get-tuple-element.65, bf16[12,6,2,192]{3,2,1,0:T(2,128)(2,1)S(1)} %get-tuple-element.54, bf16[3,6,2,192]{3,2,1,0:T(2,128)(2,1)S(1)} %get-tuple-element.62, ...), kind=kLoop, calls=%fused_computation | loop fusion | flops 248832 | bytes 331777 | tf_op jit(solution)/shard_map/jit(_where)/select_n | solution.py:33
  16.5 1.2 %collective-permute-start.2 = (bf16[18,6,2,192]{3,2,1,0:T(2,128)(2,1)S(1)}, bf16[18,6,2,192]{3,2,1,0:T(2,128)(2,1)S(1)}, u32[]{:S(2)}, u32[]{:S(2)}) collective-permute-start(bf16[18,6,2,192]{3,2,1,0:T(2,128)(2,1)S(1)} %get-tuple-element.56), channel_id=1, source_target_pairs={{4,8},{8,4},{12,16},{16,12},{20,24},{24,20},{28,0},{0,28},{5,9},{9... | collective-permute-start | bytes 248840 | tf_op jit(solution)/shard_map/ppermute | solution.py:39
  17.7 0.4 %collective-permute-start.3 = (bf16[18,6,2,192]{3,2,1,0:T(2,128)(2,1)S(1)}, bf16[18,6,2,192]{3,2,1,0:T(2,128)(2,1)S(1)}, u32[]{:S(2)}, u32[]{:S(2)}) collective-permute-start(bf16[18,6,2,192]{3,2,1,0:T(2,128)(2,1)S(1)} %get-tuple-element.55), channel_id=1, source_target_pairs={{0,4},{4,0},{8,12},{12,8},{16,20},{20,16},{24,28},{28,24},{1,5},{5... | collective-permute-start | bytes 248840 | tf_op jit(solution)/shard_map/ppermute | solution.py:39
  18.1 0.0 all-to-all-done.recv_ref
  18.1 0.0 copy-done.1
  18.1 0.0 copy-done.3
  18.1 0.0 copy-done.4
  18.1 4.1 %shard_map.138 = (bf16[12,12,2,192]{3,2,1,0:T(2,128)(2,1)S(1)}, f32[464,256]{1,0:T(8,128)S(1)}, f32[304,192]{1,0:T(8,128)S(1)}, f32[432,192]{1,0:T(8,128)S(1)}, ...) custom-call(s32[4]{0:T(128)S(1)} %add_convert_fusion.scalars_ref, ...), custom_call_target="tpu_custom_call" | custom-call | flops 4000000000 | bytes 4000000 | tf_op jit(solution)/shard_map/pallas_call | solution.py:646
  22.2 0.6 %collective-permute-done.2.two_ref = bf16[18,6,2,192]{3,2,1,0:T(2,128)(2,1)S(1)} collective-permute-done((bf16[18,6,2,192]{3,2,1,0:T(2,128)(2,1)S(1)}, bf16[18,6,2,192]{3,2,1,0:T(2,128)(2,1)S(1)}, u32[]{:S(2)}, u32[]{:S(2)}) %collective-permute-start.2) | collective-permute-done | bytes 82976 | tf_op jit(solution)/shard_map/ppermute | solution.py:39
  22.8 0.0 collective-permute-done.3.one_ref
  22.8 3.8 %shard_map.139 = bf16[12,24,2,192]{3,2,1,0:T(2,128)(2,1)} custom-call(s32[4]{0:T(128)S(1)} %add_convert_fusion.scalars_ref, f32[464,256]{1,0:T(8,128)S(1)} %get-tuple-element.45.rest_ref, f32[304,192]{1,0:T(8,128)S(1)} %get-tuple-element.46.latent_ref, f32[432,192]{1,0:T(8,128)S(1)} %get-tuple-element.47.keys_ref, ...), custom_call_target="tpu_custom_call" | custom-call | flops 3000000000 | bytes 4000000 | tf_op jit(solution)/shard_map/pallas_call | solution.py:676
  (2 shorter events, 0.0 us)
Async XLA Ops:
  1.7 7.4 %copy-start.9 = (bf16[3,24,2,192]{3,2,1,0:T(2,128)(2,1)S(1)}, bf16[3,24,2,192]{3,2,1,0:T(2,128)(2,1)}, u32[]{:S(2)}) copy-start(bf16[3,24,2,192]{3,2,1,0:T(2,128)(2,1)} %get-tuple-element.30) | copy-start | bytes 165892
  1.8 7.4 %copy-start.10 = (bf16[3,24,2,192]{3,2,1,0:T(2,128)(2,1)S(1)}, bf16[3,24,2,192]{3,2,1,0:T(2,128)(2,1)}, u32[]{:S(2)}) copy-start(bf16[3,24,2,192]{3,2,1,0:T(2,128)(2,1)} %get-tuple-element.31) | copy-start | bytes 165892
  1.8 16.3 %all-to-all-start = ((bf16[32,10,2,128]{3,2,1,0:T(2,128)(2,1)}), bf16[32,10,2,128]{3,2,1,0:T(2,128)(2,1)S(1)}, u32[]{:S(2)}, u32[]{:S(2)}) async-start(bf16[32,10,2,128]{3,2,1,0:T(2,128)(2,1)} %bitcast.24), calls=%async_computation | async-start | bytes 327680 | tf_op jit(solution)/shard_map/all_to_all | solution.py:616
  9.1 2.7 %copy-start.8 = (bf16[768,192]{0,1:T(8,128)(2,1)S(1)}, bf16[768,192]{0,1:T(8,128)(2,1)}, u32[]{:S(2)}) copy-start(bf16[768,192]{0,1:T(8,128)(2,1)} %param.27) | copy-start | bytes 884740
  9.1 2.6 %copy-start.11 = (bf16[128,192]{0,1:T(8,128)(2,1)S(1)}, bf16[128,192]{0,1:T(8,128)(2,1)}, u32[]{:S(2)}) copy-start(bf16[128,192]{0,1:T(8,128)(2,1)} %param.19) | copy-start | bytes 147460
  9.2 6.8 %collective-permute-start.1 = (bf16[3,24,2,192]{3,2,1,0:T(2,128)(2,1)S(1)}, bf16[3,24,2,192]{3,2,1,0:T(2,128)(2,1)S(1)}, u32[]{:S(2)}, u32[]{:S(2)}) collective-permute-start(bf16[3,24,2,192]{3,2,1,0:T(2,128)(2,1)S(1)} %bitcast.28), channel_id=1, source_target_pairs={{0,1},{1,0},{2,3},{3,2},{4,5},{5,4},{6,7},{7,6},{8,9},{9,8},{10,11... | collective-permute-start | bytes 165896 | tf_op jit(solution)/shard_map/ppermute | solution.py:39
  11.0 5.0 %collective-permute-start = (bf16[3,24,2,192]{3,2,1,0:T(2,128)(2,1)S(1)}, bf16[3,24,2,192]{3,2,1,0:T(2,128)(2,1)S(1)}, u32[]{:S(2)}, u32[]{:S(2)}) collective-permute-start(bf16[3,24,2,192]{3,2,1,0:T(2,128)(2,1)S(1)} %bitcast.26), channel_id=1, source_target_pairs={{1,2},{2,1},{5,6},{6,5},{9,10},{10,9},{13,14},{14,13},{17,18},{18,... | collective-permute-start | bytes 165896 | tf_op jit(solution)/shard_map/ppermute | solution.py:39
  11.8 1.0 %copy-start = (bf16[12,24,2,192]{3,2,1,0:T(2,128)(2,1)S(1)}, bf16[12,24,2,192]{3,2,1,0:T(2,128)(2,1)}, u32[]{:S(2)}) copy-start(bf16[12,24,2,192]{3,2,1,0:T(2,128)(2,1)} %back_ref.2) | copy-start | bytes 663556
  12.8 0.9 %copy-start.2 = (bf16[192,576]{1,0:T(8,128)(2,1)S(1)}, bf16[192,576]{1,0:T(8,128)(2,1)}, u32[]{:S(2)}) copy-start(bf16[192,576]{1,0:T(8,128)(2,1)} %attn_ref) | copy-start | bytes 663556
  12.9 0.8 %copy-start.5 = (bf16[8,192]{1,0:T(8,128)(2,1)S(1)}, bf16[8,192]{1,0:T(8,128)(2,1)}, u32[]{:S(2)}) copy-start(bf16[8,192]{1,0:T(8,128)(2,1)} %table_ref) | copy-start | bytes 9220
  12.9 0.8 %copy-start.6 = (bf16[192]{0:T(256)(128)(2,1)S(1)}, bf16[192]{0:T(256)(128)(2,1)}, u32[]{:S(2)}) copy-start(bf16[192]{0:T(256)(128)(2,1)} %one_ref) | copy-start | bytes 1156
  12.9 0.8 %copy-start.7 = (bf16[192]{0:T(256)(128)(2,1)S(1)}, bf16[192]{0:T(256)(128)(2,1)}, u32[]{:S(2)}) copy-start(bf16[192]{0:T(256)(128)(2,1)} %two_ref) | copy-start | bytes 1156
  16.0 2.1 %copy-start.1 = (bf16[192,768]{1,0:T(8,128)(2,1)S(1)}, bf16[192,768]{1,0:T(8,128)(2,1)}, u32[]{:S(2)}) copy-start(bf16[192,768]{1,0:T(8,128)(2,1)} %refs_3_.3) | copy-start | bytes 884740
  16.0 2.1 %copy-start.3 = (bf16[192,384]{1,0:T(8,128)(2,1)S(1)}, bf16[192,384]{1,0:T(8,128)(2,1)}, u32[]{:S(2)}) copy-start(bf16[192,384]{1,0:T(8,128)(2,1)} %lift_ref.1) | copy-start | bytes 442372
  16.1 2.1 %copy-start.4 = (bf16[192,192]{1,0:T(8,128)(2,1)S(1)}, bf16[192,192]{1,0:T(8,128)(2,1)}, u32[]{:S(2)}) copy-start(bf16[192,192]{1,0:T(8,128)(2,1)} %refs_1_.3) | copy-start | bytes 221188
  16.5 6.3 %collective-permute-start.2 = (bf16[18,6,2,192]{3,2,1,0:T(2,128)(2,1)S(1)}, bf16[18,6,2,192]{3,2,1,0:T(2,128)(2,1)S(1)}, u32[]{:S(2)}, u32[]{:S(2)}) collective-permute-start(bf16[18,6,2,192]{3,2,1,0:T(2,128)(2,1)S(1)} %get-tuple-element.56), channel_id=1, source_target_pairs={{4,8},{8,4},{12,16},{16,12},{20,24},{24,20},{28,0},{0,28},{5,9},{9... | collective-permute-start | bytes 248840 | tf_op jit(solution)/shard_map/ppermute | solution.py:39
  17.7 5.1 %collective-permute-start.3 = (bf16[18,6,2,192]{3,2,1,0:T(2,128)(2,1)S(1)}, bf16[18,6,2,192]{3,2,1,0:T(2,128)(2,1)S(1)}, u32[]{:S(2)}, u32[]{:S(2)}) collective-permute-start(bf16[18,6,2,192]{3,2,1,0:T(2,128)(2,1)S(1)} %get-tuple-element.55), channel_id=1, source_target_pairs={{0,4},{4,0},{8,12},{12,8},{16,20},{20,16},{24,28},{28,24},{1,5},{5... | collective-permute-start | bytes 248840 | tf_op jit(solution)/shard_map/ppermute | solution.py:39

commit v25 on v24

--- a/solution.py
+++ b/solution.py
@@ -26,23 +26,22 @@
 COLS = ROWS + len(AROUND)
 
 
-def swapped(up, down, axis, wraps):
+def swapped_as(mine, axis, wraps):
     count = lax.axis_size(axis)
-    even = lax.axis_index(axis) % 2 == 0
     got = []
-    for first, mine in ((0, jnp.where(even, down, up)), (1, jnp.where(even, up, down))):
+    for first, one in enumerate(mine):
         pairs = []
         for low in range(first, count, 2):
             high = (low + 1) % count
             if high > low or wraps:
                 pairs += [(low, high), (high, low)]
-        got.append(lax.ppermute(mine, axis, pairs))
+        got.append(lax.ppermute(one, axis, pairs))
     return got
 
 
-def before_and_after(got, axis):
+def swapped(up, down, axis, wraps):
     even = lax.axis_index(axis) % 2 == 0
-    return jnp.where(even, got[1], got[0]), jnp.where(even, got[0], got[1])
+    return swapped_as((jnp.where(even, down, up), jnp.where(even, up, down)), axis, wraps)
 
 
 def rectangles(lat_cells, lon_cells):
@@ -287,6 +286,7 @@
 
 def prepare_kernel(
     plan,
+    even_ref,
     back_ref,
     attn_ref,
     table_ref,
@@ -297,8 +297,14 @@
     tables_ref,
     gain_one_ref,
     gain_two_ref,
+    mine_ref,
+    other_ref,
 ):
-    width = back_ref.shape[3]
+    lon_cells, _, width = back_ref.shape[1:]
+    even = even_ref[1] == 1
+    left, right = back_ref[:, :HLON], back_ref[:, lon_cells - HLON :]
+    mine_ref[...] = jnp.where(even, right, left)
+    other_ref[...] = jnp.where(even, left, right)
     pieces = []
     for top, high, left, wide in plan[4]:
         count = high * wide * LEV
@@ -314,8 +320,8 @@
         parts_ref[n] = attn_ref[:, n * width : (n + 1) * width]
 
 
-def prepared(plan, background, attn_weight, instrument_table, first_gain, second_gain):
-    width = background.shape[3]
+def prepared(plan, even, background, attn_weight, instrument_table, first_gain, second_gain):
+    lat_cells, _, levels, width = background.shape
     rows = sum(padded(tokens_of(part)) for part in plan[4])
     vmem = pl.BlockSpec(memory_space=pltpu.VMEM)
     return pl.pallas_call(
@@ -326,12 +332,37 @@
             jax.ShapeDtypeStruct((LANES, width), BF16),
             jax.ShapeDtypeStruct((8, width), F32),
             jax.ShapeDtypeStruct((8, width), F32),
+            *[jax.ShapeDtypeStruct((lat_cells, HLON, levels, width), BF16)] * 2,
         ],
-        in_specs=[vmem] * 5,
-        out_specs=[vmem] * 5,
+        in_specs=[pl.BlockSpec(memory_space=pltpu.SMEM)] + [vmem] * 5,
+        out_specs=[vmem] * 7,
         compiler_params=pltpu.CompilerParams(vmem_limit_bytes=LIMIT),
         cost_estimate=pl.CostEstimate(flops=10**9, bytes_accessed=10**6, transcendentals=0),
-    )(background, attn_weight, instrument_table, first_gain, second_gain)
+    )(even, background, attn_weight, instrument_table, first_gain, second_gain)
+
+
+def join_kernel(even_ref, one_ref, two_ref, mine_ref, other_ref, first_ref, second_ref):
+    lon_cells, lat_cells = one_ref.shape[1], mine_ref.shape[0]
+    lat_even, lon_even = even_ref[0] == 1, even_ref[1] == 1
+    for ref, strip, same in ((first_ref, mine_ref, True), (second_ref, other_ref, False)):
+        ref[HLAT : HLAT + lat_cells] = strip[...]
+        low, high = slice(0, HLON), slice(lon_cells - HLON, lon_cells)
+        spots = (high, low) if same else (low, high)
+        ends = [jnp.where(lon_even, got[:, spots[0]], got[:, spots[1]]) for got in (one_ref, two_ref)]
+        ref[:HLAT] = jnp.where(lat_even, ends[1], ends[0])
+        ref[HLAT + lat_cells :] = jnp.where(lat_even, ends[0], ends[1])
+
+
+def joined(even, got, mine):
+    lat_cells, _, levels, width = mine[0].shape
+    vmem = pl.BlockSpec(memory_space=pltpu.VMEM)
+    return pl.pallas_call(
+        join_kernel,
+        out_shape=[jax.ShapeDtypeStruct((lat_cells + WLAT, HLON, levels, width), BF16)] * 2,
+        in_specs=[pl.BlockSpec(memory_space=pltpu.SMEM)] + [vmem] * 4,
+        out_specs=[vmem] * 2,
+        compiler_params=pltpu.CompilerParams(vmem_limit_bytes=LIMIT),
+    )(even, *got, *mine)
 
 
 def normed_of(plan, entries, sums, borders, gain):
@@ -351,8 +382,8 @@
                 ref = west_ref if dx < 0 else east_ref
                 top, left = {-1: 0, 0: top + HLAT, 1: lat_cells + HLAT}[dy], 0
             else:
-                ref, top = (north_ref, 0) if dy < 0 else (south_ref, 0)
-            block = ref(top, high) if dx else ref[top : top + high, left : left + wide]
+                ref = north_ref if dy < 0 else south_ref
+            block = ref(top, high) if dx else ref(left, wide)
             piece = block.reshape(count, width).astype(F32)
             if full > count:
                 piece = below(piece, jnp.zeros((full - count, width), F32))
@@ -452,8 +483,8 @@
     lon_cells,
     scalars_ref,
     recv_ref,
-    north_ref,
-    south_ref,
+    one_ref,
+    two_ref,
     rows_ref,
     first_ref,
     table_ref,
@@ -471,7 +502,15 @@
             pieces.append(sums[tile][start : start + padded(tokens_of(plan[tile][number]))])
         return below(*pieces)
 
-    borders = (rows_ref[...].astype(F32), north_ref, south_ref, None, None, lat_cells)
+    even = scalars_ref[4] == 1
+
+    def north(left, wide):
+        return jnp.where(even, two_ref[:, left : left + wide], one_ref[:, left : left + wide])
+
+    def south(left, wide):
+        return jnp.where(even, one_ref[:, left : left + wide], two_ref[:, left : left + wide])
+
+    borders = (rows_ref[...].astype(F32), north, south, None, None, lat_cells)
     gain = gain_one_ref[:1, :]
     entries = near_entries(MIDDLE)
     latent, normed, spans = normed_of(plan, entries, sums_of(entries), borders, gain)
@@ -614,25 +653,22 @@
         record_values, record_cell, record_instrument, block_counts, background
     )
     received = lax.all_to_all(sent, ("lon", "lat"), split_axis=0, concat_axis=0, tiled=True)
-    north, south = before_and_after(swapped(up, down, "lat", wraps=False), "lat")
+    borders = swapped(up, down, "lat", wraps=False)
 
     held = (background, input_weight, instrument_table, attn_weight, down_weight)
     held = lax.optimization_barrier((*held, first_gain, second_gain, up))
     later, input_weight, instrument_table, attn_weight, down_weight = held[:5]
     first_gain, second_gain = held[5:7]
 
-    def columns(low, end):
-        return jnp.concatenate([north[:, low:end], later[:, low:end], south[:, low:end]], axis=0)
-
-    got = swapped(columns(0, HLON), columns(lon_cells - HLON, lon_cells), "lon", wraps=True)
-
     plan = rectangles(lat_cells, lon_cells)
-    rows, parts, tables, gain_one, gain_two = prepared(
-        plan, later, attn_weight, instrument_table, first_gain, second_gain
+    even = [lax.axis_index(axis) % 2 == 0 for axis in ("lat", "lon")]
+    evens = jnp.stack(even).astype(jnp.int32)
+    rows, parts, tables, gain_one, gain_two, *mine = prepared(
+        plan, evens, later, attn_weight, instrument_table, first_gain, second_gain
     )
+    got = swapped_as(joined(evens, borders, mine), "lon", wraps=True)
     lat = lax.axis_index("lat")
-    even = lax.axis_index("lon") % 2 == 0
-    scalars = jnp.stack([lat == 0, lat < 0, lat == tiles_lat - 1, even]).astype(jnp.int32)
+    scalars = jnp.stack([lat == 0, lat < 0, lat == tiles_lat - 1, even[1], even[0]]).astype(jnp.int32)
 
     def rows_in(entries):
         return sum(padded(tokens_of(plan[tile][number])) for tile, number in entries)
@@ -662,8 +698,7 @@
     )(
         scalars,
         received,
-        north,
-        south,
+        *borders,
         rows,
         input_weight,
         tables,

time: 26.8 us -> 26.9 us (level)
  Pallas kernels: 9.75 us -> 11 us
  other arithmetic: 0.48 us -> 0.1 us
  local copies, waits for them, and re-layouts: 2 us -> 1.64 us
  waiting for transfers between devices: 2.59 us -> 2.27 us
    pallas_call x0 -> x1, Pallas kernels: none -> 0.63 us  [joined(): pl.pallas_call(join_kernel, out_shape=[jax.ShapeDtypeStruct((lat_cells +...]
    pallas_call x1, Pallas kernels: 0.19 us -> 0.82 us  [prepared(): pl.pallas_call(functools.partial(prepare_kernel, plan), out_shape=[jax.Sh...]
    select_n x3 -> x1, other arithmetic: 0.41 us -> 0.02 us  [swapped(): jnp.where(even, up, down)]
    ppermute x4, waiting for transfers between devices: 2.59 us -> 2.27 us  [swapped_as(): got.append(lax.ppermute(one, axis, pairs))]
    unnamed x24, local copies, waits for them, and re-layouts: 1.56 us -> 1.26 us
  transfers between devices with their start and end apart: 5 -> 5, of which waited for: 2 -> 2; matrix products, arithmetic and copies ran while one was open for 3% -> 2% of each run, Pallas kernels for 16% -> 21%
where the time goes in v25:
time: 26.9 us; the launch traced here: 26.7 us
  starting transfers between devices  11.5 us (43%)
  Pallas kernels  11 us (41%)
  waiting for transfers between devices  2.27 us (8%)
  local copies, waits for them, and re-layouts  1.64 us (6%)
    all_to_all x1, starting transfers between devices, local(): lax.all_to_all(sent, ('lon', 'lat'), split_axis=0, concat_axis=0, tiled=T...  7.3 us
    ppermute x4, starting transfers between devices, swapped_as(): got.append(lax.ppermute(one, axis, pairs))  4.15 us
    pallas_call x1, Pallas kernels, local(): pl.pallas_call(functools.partial(middle_kernel, plan, lat_cells, lon_cell...  4.06 us
    pallas_call x1, Pallas kernels, local(): pl.pallas_call(functools.partial(side_kernel, plan, lat_cells), out_shape...  3.75 us
    ppermute x4, waiting for transfers between devices, swapped_as(): got.append(lax.ppermute(one, axis, pairs))  2.27 us
    pallas_call x1, Pallas kernels, packed(): pl.pallas_call(pack_kernel, out_shape=[jax.ShapeDtypeStruct(shape, BF16),...  1.73 us
    unnamed x24, local copies, waits for them, and re-layouts  1.26 us
    pallas_call x1, Pallas kernels, prepared(): pl.pallas_call(functools.partial(prepare_kernel, plan), out_shape=[jax.Sh...  0.82 us
  transfers between devices with their start and end apart: 5, of which 2 were waited for; matrix products, arithmetic and copies ran while one was open for 2% of the time, Pallas kernels for 21%

profile of v25, /device:TPU:0, one launch (start us, length us, event | category | flops | bytes accessed | tf_op | source)
XLA Modules:
  0.0 26.7 jit_solution(10755452254695348836)
XLA Ops:
  0.0 1.7 %shard_map.136 = (bf16[8,4,10,2,128]{4,3,2,1,0:T(2,128)(2,1)}, bf16[3,24,2,192]{3,2,1,0:T(2,128)(2,1)}, bf16[3,24,2,192]{3,2,1,0:T(2,128)(2,1)}) custom-call(bf16[8,4,2,128]{3,2,1,0:T(2,128)(2,1)} %values_ref.1, s32[8,8]{1,0:T(8,128)} %bitcast.22, s32[8,8]{1,0:T(8,128)} %bitcast.23, s32[4,8]{1,0:T(4,128)} %bitcast.24, bf16[12,24,2,192]{3,2,1,0:T(2,128)(2,1)} %back_ref.2), custom_call_target="tpu_custom_call" | custom-call | flops 20000000000 | bytes 1000000 | tf_op jit(solution)/shard_map/pallas_call | solution.py:183
  1.7 0.0 copy-start.9
  1.8 0.0 copy-start.10
  1.8 0.0 copy-start.8
  1.8 7.3 %all-to-all-start = ((bf16[32,10,2,128]{3,2,1,0:T(2,128)(2,1)}), bf16[32,10,2,128]{3,2,1,0:T(2,128)(2,1)S(1)}, u32[]{:S(2)}, u32[]{:S(2)}) async-start(bf16[32,10,2,128]{3,2,1,0:T(2,128)(2,1)} %bitcast.17), calls=%async_computation | async-start | bytes 327680 | tf_op jit(solution)/shard_map/all_to_all | solution.py:655
  9.1 0.0 copy-done.9
  9.1 0.0 copy-done.10
  9.1 1.8 %collective-permute-start = (bf16[3,24,2,192]{3,2,1,0:T(2,128)(2,1)S(1)}, bf16[3,24,2,192]{3,2,1,0:T(2,128)(2,1)S(1)}, u32[]{:S(2)}, u32[]{:S(2)}) collective-permute-start(bf16[3,24,2,192]{3,2,1,0:T(2,128)(2,1)S(1)} %bitcast.19), channel_id=1, source_target_pairs={{0,1},{1,0},{2,3},{3,2},{4,5},{5,4},{6,7},{7,6},{8,9},{9,8},{10,11... | collective-permute-start | bytes 165896 | tf_op jit(solution)/shard_map/ppermute | solution.py:38
  11.0 0.7 %collective-permute-start.1 = (bf16[3,24,2,192]{3,2,1,0:T(2,128)(2,1)S(1)}, bf16[3,24,2,192]{3,2,1,0:T(2,128)(2,1)S(1)}, u32[]{:S(2)}, u32[]{:S(2)}) collective-permute-start(bf16[3,24,2,192]{3,2,1,0:T(2,128)(2,1)S(1)} %bitcast.18), channel_id=1, source_target_pairs={{1,2},{2,1},{5,6},{6,5},{9,10},{10,9},{13,14},{14,13},{17,18},{18,... | collective-permute-start | bytes 165896 | tf_op jit(solution)/shard_map/ppermute | solution.py:38
  11.7 0.1 stack.28
  11.8 0.0 copy-done.8
  11.8 0.0 copy-start.11
  11.8 0.0 copy-start
  11.8 0.0 copy-start.2
  11.8 0.2 copy.16.refs_4_
  12.0 0.6 %copy-done.11 = bf16[128,192]{0,1:T(8,128)(2,1)S(1)} copy-done((bf16[128,192]{0,1:T(8,128)(2,1)S(1)}, bf16[128,192]{0,1:T(8,128)(2,1)}, u32[]{:S(2)}) %copy-start.11) | copy-done | bytes 49176
  12.6 0.0 copy-start.5
  12.6 0.1 copy.15.first_ref
  12.7 0.0 copy-start.6
  12.7 0.0 copy-start.7
  12.7 0.1 add_convert_fusion.even_ref
  12.8 0.0 copy-done
  12.8 0.0 copy-done.2
  12.8 0.5 %copy-done.5 = bf16[8,192]{1,0:T(8,128)(2,1)S(1)} copy-done((bf16[8,192]{1,0:T(8,128)(2,1)S(1)}, bf16[8,192]{1,0:T(8,128)(2,1)}, u32[]{:S(2)}) %copy-start.5) | copy-done | bytes 3096
  13.3 0.1 copy-done.6
  13.4 0.0 copy-done.7
  13.4 0.0 copy-start.3
  13.4 0.0 copy-start.4
  13.4 0.8 %shard_map.137 = (bf16[592,192]{1,0:T(8,128)(2,1)S(1)}, bf16[3,192,192]{2,1,0:T(8,128)(2,1)S(1)}, bf16[128,192]{1,0:T(8,128)(2,1)S(1)}, f32[8,192]{1,0:T(8,128)S...) custom-call(s32[2]{0:T(128)S(1)} %add_convert_fusion.even_ref, ...), custom_call_target="tpu_custom_call" | custom-call | flops 1000000000 | bytes 1000000 | tf_op jit(solution)/shard_map/pallas_call | solution.py:327
  14.2 0.0 copy-start.1
  14.3 1.7 %collective-permute-done.one_ref = bf16[3,24,2,192]{3,2,1,0:T(2,128)(2,1)S(1)} collective-permute-done((bf16[3,24,2,192]{3,2,1,0:T(2,128)(2,1)S(1)}, bf16[3,24,2,192]{3,2,1,0:T(2,128)(2,1)S(1)}, u32[]{:S(2)}, u32[]{:S(2)}) %collective-permute-start) | collective-permute-done | bytes 55328 | tf_op jit(solution)/shard_map/ppermute | solution.py:38
  16.0 0.0 collective-permute-done.1.two_ref
  16.0 0.6 %shard_map.139 = (bf16[18,6,2,192]{3,2,1,0:T(2,128)(2,1)S(1)}, bf16[18,6,2,192]{3,2,1,0:T(2,128)(2,1)S(1)}) custom-call(s32[2]{0:T(128)S(1)} %add_convert_fusion.even_ref, bf16[3,24,2,192]{3,2,1,0:T(2,128)(2,1)S(1)} %collective-permute-done.one_ref, bf16[3,24,2,192]{3,2,1,0:T(2,128)(2,1)S(1)} %collective-permute-done.1.two_ref, ...), custom_call_target="tpu_custom_call" | custom-call | tf_op jit(solution)/shard_map/pallas_call | solution.py:359
  16.6 1.2 %collective-permute-start.2 = (bf16[18,6,2,192]{3,2,1,0:T(2,128)(2,1)S(1)}, bf16[18,6,2,192]{3,2,1,0:T(2,128)(2,1)S(1)}, u32[]{:S(2)}, u32[]{:S(2)}) collective-permute-start(bf16[18,6,2,192]{3,2,1,0:T(2,128)(2,1)S(1)} %get-tuple-element.51), channel_id=1, source_target_pairs={{4,8},{8,4},{12,16},{16,12},{20,24},{24,20},{28,0},{0,28},{5,9},{9... | collective-permute-start | bytes 248840 | tf_op jit(solution)/shard_map/ppermute | solution.py:38
  17.8 0.4 %collective-permute-start.3 = (bf16[18,6,2,192]{3,2,1,0:T(2,128)(2,1)S(1)}, bf16[18,6,2,192]{3,2,1,0:T(2,128)(2,1)S(1)}, u32[]{:S(2)}, u32[]{:S(2)}) collective-permute-start(bf16[18,6,2,192]{3,2,1,0:T(2,128)(2,1)S(1)} %get-tuple-element.52), channel_id=1, source_target_pairs={{0,4},{4,0},{8,12},{12,8},{16,20},{20,16},{24,28},{28,24},{1,5},{5... | collective-permute-start | bytes 248840 | tf_op jit(solution)/shard_map/ppermute | solution.py:38
  18.3 0.0 all-to-all-done.recv_ref
  18.3 0.0 copy-done.3
  18.3 0.0 copy-done.4
  18.3 0.0 copy-done.1
  18.3 4.1 %shard_map.138 = (bf16[12,12,2,192]{3,2,1,0:T(2,128)(2,1)S(1)}, f32[464,256]{1,0:T(8,128)S(1)}, f32[304,192]{1,0:T(8,128)S(1)}, f32[432,192]{1,0:T(8,128)S(1)}, ...) custom-call(s32[5]{0:T(128)S(1)} %convert_element_type.6.scalars_ref, ...), custom_call_target="tpu_custom_call" | custom-call | flops 4000000000 | bytes 4000000 | tf_op jit(solution)/shard_map/pallas_call | solution.py:682
  22.3 0.6 %collective-permute-done.2.two_ref = bf16[18,6,2,192]{3,2,1,0:T(2,128)(2,1)S(1)} collective-permute-done((bf16[18,6,2,192]{3,2,1,0:T(2,128)(2,1)S(1)}, bf16[18,6,2,192]{3,2,1,0:T(2,128)(2,1)S(1)}, u32[]{:S(2)}, u32[]{:S(2)}) %collective-permute-start.2) | collective-permute-done | bytes 82976 | tf_op jit(solution)/shard_map/ppermute | solution.py:38
  22.9 0.0 collective-permute-done.3.one_ref
  22.9 3.8 %shard_map.140 = bf16[12,24,2,192]{3,2,1,0:T(2,128)(2,1)} custom-call(s32[5]{0:T(128)S(1)} %convert_element_type.6.scalars_ref, f32[464,256]{1,0:T(8,128)S(1)} %get-tuple-element.53.rest_ref, f32[304,192]{1,0:T(8,128)S(1)} %get-tuple-element.54.latent_ref, f32[432,192]{1,0:T(8,128)S(1)} %get-tuple-element.55.keys_ref, ...), custom_call_target="tpu_custom_call" | custom-call | flops 3000000000 | bytes 4000000 | tf_op jit(solution)/shard_map/pallas_call | solution.py:711
  (2 shorter events, 0.0 us)
Async XLA Ops:
  1.7 7.4 %copy-start.9 = (bf16[3,24,2,192]{3,2,1,0:T(2,128)(2,1)S(1)}, bf16[3,24,2,192]{3,2,1,0:T(2,128)(2,1)}, u32[]{:S(2)}) copy-start(bf16[3,24,2,192]{3,2,1,0:T(2,128)(2,1)} %get-tuple-element.35) | copy-start | bytes 165892
  1.8 7.4 %copy-start.10 = (bf16[3,24,2,192]{3,2,1,0:T(2,128)(2,1)S(1)}, bf16[3,24,2,192]{3,2,1,0:T(2,128)(2,1)}, u32[]{:S(2)}) copy-start(bf16[3,24,2,192]{3,2,1,0:T(2,128)(2,1)} %get-tuple-element.34) | copy-start | bytes 165892
  1.8 10.0 %copy-start.8 = (bf16[768,192]{0,1:T(8,128)(2,1)S(1)}, bf16[768,192]{0,1:T(8,128)(2,1)}, u32[]{:S(2)}) copy-start(bf16[768,192]{0,1:T(8,128)(2,1)} %param.27) | copy-start | bytes 884740
  1.8 16.5 %all-to-all-start = ((bf16[32,10,2,128]{3,2,1,0:T(2,128)(2,1)}), bf16[32,10,2,128]{3,2,1,0:T(2,128)(2,1)S(1)}, u32[]{:S(2)}, u32[]{:S(2)}) async-start(bf16[32,10,2,128]{3,2,1,0:T(2,128)(2,1)} %bitcast.17), calls=%async_computation | async-start | bytes 327680 | tf_op jit(solution)/shard_map/all_to_all | solution.py:655
  9.1 6.8 %collective-permute-start = (bf16[3,24,2,192]{3,2,1,0:T(2,128)(2,1)S(1)}, bf16[3,24,2,192]{3,2,1,0:T(2,128)(2,1)S(1)}, u32[]{:S(2)}, u32[]{:S(2)}) collective-permute-start(bf16[3,24,2,192]{3,2,1,0:T(2,128)(2,1)S(1)} %bitcast.19), channel_id=1, source_target_pairs={{0,1},{1,0},{2,3},{3,2},{4,5},{5,4},{6,7},{7,6},{8,9},{9,8},{10,11... | collective-permute-start | bytes 165896 | tf_op jit(solution)/shard_map/ppermute | solution.py:38
  11.0 5.0 %collective-permute-start.1 = (bf16[3,24,2,192]{3,2,1,0:T(2,128)(2,1)S(1)}, bf16[3,24,2,192]{3,2,1,0:T(2,128)(2,1)S(1)}, u32[]{:S(2)}, u32[]{:S(2)}) collective-permute-start(bf16[3,24,2,192]{3,2,1,0:T(2,128)(2,1)S(1)} %bitcast.18), channel_id=1, source_target_pairs={{1,2},{2,1},{5,6},{6,5},{9,10},{10,9},{13,14},{14,13},{17,18},{18,... | collective-permute-start | bytes 165896 | tf_op jit(solution)/shard_map/ppermute | solution.py:38
  11.8 0.8 %copy-start.11 = (bf16[128,192]{0,1:T(8,128)(2,1)S(1)}, bf16[128,192]{0,1:T(8,128)(2,1)}, u32[]{:S(2)}) copy-start(bf16[128,192]{0,1:T(8,128)(2,1)} %param.19) | copy-start | bytes 147460
  11.8 1.0 %copy-start = (bf16[12,24,2,192]{3,2,1,0:T(2,128)(2,1)S(1)}, bf16[12,24,2,192]{3,2,1,0:T(2,128)(2,1)}, u32[]{:S(2)}) copy-start(bf16[12,24,2,192]{3,2,1,0:T(2,128)(2,1)} %back_ref.2) | copy-start | bytes 663556
  11.8 1.0 %copy-start.2 = (bf16[192,576]{1,0:T(8,128)(2,1)S(1)}, bf16[192,576]{1,0:T(8,128)(2,1)}, u32[]{:S(2)}) copy-start(bf16[192,576]{1,0:T(8,128)(2,1)} %attn_ref) | copy-start | bytes 663556
  12.6 0.7 %copy-start.5 = (bf16[8,192]{1,0:T(8,128)(2,1)S(1)}, bf16[8,192]{1,0:T(8,128)(2,1)}, u32[]{:S(2)}) copy-start(bf16[8,192]{1,0:T(8,128)(2,1)} %table_ref) | copy-start | bytes 9220
  12.7 0.7 %copy-start.6 = (bf16[192]{0:T(256)(128)(2,1)S(1)}, bf16[192]{0:T(256)(128)(2,1)}, u32[]{:S(2)}) copy-start(bf16[192]{0:T(256)(128)(2,1)} %one_ref) | copy-start | bytes 1156
  12.7 0.7 %copy-start.7 = (bf16[192]{0:T(256)(128)(2,1)S(1)}, bf16[192]{0:T(256)(128)(2,1)}, u32[]{:S(2)}) copy-start(bf16[192]{0:T(256)(128)(2,1)} %two_ref) | copy-start | bytes 1156
  13.4 4.9 %copy-start.3 = (bf16[192,384]{1,0:T(8,128)(2,1)S(1)}, bf16[192,384]{1,0:T(8,128)(2,1)}, u32[]{:S(2)}) copy-start(bf16[192,384]{1,0:T(8,128)(2,1)} %lift_ref.1) | copy-start | bytes 442372
  13.4 4.9 %copy-start.4 = (bf16[192,192]{1,0:T(8,128)(2,1)S(1)}, bf16[192,192]{1,0:T(8,128)(2,1)}, u32[]{:S(2)}) copy-start(bf16[192,192]{1,0:T(8,128)(2,1)} %refs_1_.3) | copy-start | bytes 221188
  14.2 4.0 %copy-start.1 = (bf16[192,768]{1,0:T(8,128)(2,1)S(1)}, bf16[192,768]{1,0:T(8,128)(2,1)}, u32[]{:S(2)}) copy-start(bf16[192,768]{1,0:T(8,128)(2,1)} %refs_3_.3) | copy-start | bytes 884740
  16.6 6.3 %collective-permute-start.2 = (bf16[18,6,2,192]{3,2,1,0:T(2,128)(2,1)S(1)}, bf16[18,6,2,192]{3,2,1,0:T(2,128)(2,1)S(1)}, u32[]{:S(2)}, u32[]{:S(2)}) collective-permute-start(bf16[18,6,2,192]{3,2,1,0:T(2,128)(2,1)S(1)} %get-tuple-element.51), channel_id=1, source_target_pairs={{4,8},{8,4},{12,16},{16,12},{20,24},{24,20},{28,0},{0,28},{5,9},{9... | collective-permute-start | bytes 248840 | tf_op jit(solution)/shard_map/ppermute | solution.py:38
  17.8 5.1 %collective-permute-start.3 = (bf16[18,6,2,192]{3,2,1,0:T(2,128)(2,1)S(1)}, bf16[18,6,2,192]{3,2,1,0:T(2,128)(2,1)S(1)}, u32[]{:S(2)}, u32[]{:S(2)}) collective-permute-start(bf16[18,6,2,192]{3,2,1,0:T(2,128)(2,1)S(1)} %get-tuple-element.52), channel_id=1, source_target_pairs={{0,4},{4,0},{8,12},{12,8},{16,20},{20,16},{24,28},{28,24},{1,5},{5... | collective-permute-start | bytes 248840 | tf_op jit(solution)/shard_map/ppermute | solution.py:38

commit v26 on v25

--- a/solution.py
+++ b/solution.py
@@ -341,28 +341,16 @@
     )(even, background, attn_weight, instrument_table, first_gain, second_gain)
 
 
-def join_kernel(even_ref, one_ref, two_ref, mine_ref, other_ref, first_ref, second_ref):
-    lon_cells, lat_cells = one_ref.shape[1], mine_ref.shape[0]
-    lat_even, lon_even = even_ref[0] == 1, even_ref[1] == 1
-    for ref, strip, same in ((first_ref, mine_ref, True), (second_ref, other_ref, False)):
-        ref[HLAT : HLAT + lat_cells] = strip[...]
-        low, high = slice(0, HLON), slice(lon_cells - HLON, lon_cells)
-        spots = (high, low) if same else (low, high)
-        ends = [jnp.where(lon_even, got[:, spots[0]], got[:, spots[1]]) for got in (one_ref, two_ref)]
-        ref[:HLAT] = jnp.where(lat_even, ends[1], ends[0])
-        ref[HLAT + lat_cells :] = jnp.where(lat_even, ends[0], ends[1])
-
-
 def joined(even, got, mine):
-    lat_cells, _, levels, width = mine[0].shape
-    vmem = pl.BlockSpec(memory_space=pltpu.VMEM)
-    return pl.pallas_call(
-        join_kernel,
-        out_shape=[jax.ShapeDtypeStruct((lat_cells + WLAT, HLON, levels, width), BF16)] * 2,
-        in_specs=[pl.BlockSpec(memory_space=pltpu.SMEM)] + [vmem] * 4,
-        out_specs=[vmem] * 2,
-        compiler_params=pltpu.CompilerParams(vmem_limit_bytes=LIMIT),
-    )(even, *got, *mine)
+    lon_cells = got[0].shape[1]
+    low, high = slice(0, HLON), slice(lon_cells - HLON, lon_cells)
+    strips = []
+    for own, spots in zip(mine, ((high, low), (low, high))):
+        ends = [jnp.where(even[1], one[:, spots[0]], one[:, spots[1]]) for one in got]
+        north = jnp.where(even[0], ends[1], ends[0])
+        south = jnp.where(even[0], ends[0], ends[1])
+        strips.append(jnp.concatenate([north, own, south], axis=0))
+    return strips
 
 
 def normed_of(plan, entries, sums, borders, gain):
@@ -666,7 +654,7 @@
     rows, parts, tables, gain_one, gain_two, *mine = prepared(
         plan, evens, later, attn_weight, instrument_table, first_gain, second_gain
     )
-    got = swapped_as(joined(evens, borders, mine), "lon", wraps=True)
+    got = swapped_as(joined(even, borders, mine), "lon", wraps=True)
     lat = lax.axis_index("lat")
     scalars = jnp.stack([lat == 0, lat < 0, lat == tiles_lat - 1, even[1], even[0]]).astype(jnp.int32)
 

time: 26.9 us -> 30.2 us (1.12)
  starting transfers between devices: 11.5 us -> 13 us
  other arithmetic: 0.1 us -> 1.49 us
  waiting for transfers between devices: 2.27 us -> 3.24 us
  Pallas kernels: 11 us -> 10.4 us
    all_to_all x1, waiting for transfers between devices: 0.01 us -> 3.23 us  [local(): lax.all_to_all(sent, ('lon', 'lat'), split_axis=0, concat_axis=0, tiled=T...]
    ppermute x4, waiting for transfers between devices: 2.27 us -> 0.01 us  [swapped_as(): got.append(lax.ppermute(one, axis, pairs))]
    ppermute x4, starting transfers between devices: 4.15 us -> 6.3 us  [swapped_as(): got.append(lax.ppermute(one, axis, pairs))]
    select_n x1, other arithmetic: 0.02 us -> 0.98 us  [swapped(): jnp.where(even, up, down)]
    all_to_all x1, starting transfers between devices: 7.3 us -> 6.65 us  [local(): lax.all_to_all(sent, ('lon', 'lat'), split_axis=0, concat_axis=0, tiled=T...]
    pallas_call x1 -> x0, Pallas kernels: 0.63 us -> none  [joined(): pl.pallas_call(join_kernel, out_shape=[jax.ShapeDtypeStruct((lat_cells +...]
    concatenate x0 -> x2, other arithmetic: none -> 0.35 us  [joined(): strips.append(jnp.concatenate([north, own, south], axis=0))]
    unnamed x24 -> x20, local copies, waits for them, and re-layouts: 1.26 us -> 1.26 us
  transfers between devices with their start and end apart: 5 -> 5, of which waited for: 2 -> 1; matrix products, arithmetic and copies ran while one was open for 2% -> 3% of each run, Pallas kernels for 21% -> 16%
where the time goes in v26:
time: 30.2 us; the launch traced here: 29.9 us
  starting transfers between devices  13 us (43%)
  Pallas kernels  10.4 us (34%)
  waiting for transfers between devices  3.24 us (11%)
  local copies, waits for them, and re-layouts  1.64 us (5%)
  other arithmetic  1.49 us (5%)
    all_to_all x1, starting transfers between devices, local(): lax.all_to_all(sent, ('lon', 'lat'), split_axis=0, concat_axis=0, tiled=T...  6.65 us
    ppermute x4, starting transfers between devices, swapped_as(): got.append(lax.ppermute(one, axis, pairs))  6.3 us
    pallas_call x1, Pallas kernels, local(): pl.pallas_call(functools.partial(middle_kernel, plan, lat_cells, lon_cell...  4.06 us
    pallas_call x1, Pallas kernels, local(): pl.pallas_call(functools.partial(side_kernel, plan, lat_cells), out_shape...  3.79 us
    all_to_all x1, waiting for transfers between devices, local(): lax.all_to_all(sent, ('lon', 'lat'), split_axis=0, concat_axis=0, tiled=T...  3.23 us
    pallas_call x1, Pallas kernels, packed(): pl.pallas_call(pack_kernel, out_shape=[jax.ShapeDtypeStruct(shape, BF16),...  1.73 us
    unnamed x20, local copies, waits for them, and re-layouts  1.26 us
    select_n x1, other arithmetic, swapped(): jnp.where(even, up, down)  0.98 us
  transfers between devices with their start and end apart: 5, of which 1 were waited for; matrix products, arithmetic and copies ran while one was open for 3% of the time, Pallas kernels for 16%

profile of v26, /device:TPU:0, one launch (start us, length us, event | category | flops | bytes accessed | tf_op | source)
XLA Modules:
  0.0 29.9 jit_solution(1836654846078838037)
XLA Ops:
  0.0 1.7 %shard_map.136 = (bf16[8,4,10,2,128]{4,3,2,1,0:T(2,128)(2,1)}, bf16[3,24,2,192]{3,2,1,0:T(2,128)(2,1)}, bf16[3,24,2,192]{3,2,1,0:T(2,128)(2,1)}) custom-call(bf16[8,4,2,128]{3,2,1,0:T(2,128)(2,1)} %values_ref.1, s32[8,8]{1,0:T(8,128)} %bitcast.21, s32[8,8]{1,0:T(8,128)} %bitcast.22, s32[4,8]{1,0:T(4,128)} %bitcast.23, bf16[12,24,2,192]{3,2,1,0:T(2,128)(2,1)} %back_ref.2), custom_call_target="tpu_custom_call" | custom-call | flops 20000000000 | bytes 1000000 | tf_op jit(solution)/shard_map/pallas_call | solution.py:183
  1.7 0.0 copy-start.8
  1.8 1.0 %broadcast_select_fusion = (bf16[3,6,8,192]{3,2,1,0:T(8,128)(2,1)S(1)}, bf16[3,6,8,192]{3,2,1,0:T(8,128)(2,1)S(1)}) fusion(bf16[3,6,8,192]{3,2,1,0:T(8,128)(2,1)} %bitcast.19, bf16[3,6,8,192]{3,2,1,0:T(8,128)(2,1)} %bitcast.20, pred[]{:T(512)} %eq.20), kind=kLoop, calls=%fused_computation | loop fusion | flops 55296 | bytes 221185 | tf_op jit(solution)/shard_map/jit(_where)/select_n | solution.py:44
  2.7 3.1 %collective-permute-start = (bf16[3,24,2,192]{3,2,1,0:T(2,128)(2,1)S(1)}, bf16[3,24,2,192]{3,2,1,0:T(2,128)(2,1)S(1)}, u32[]{:S(2)}, u32[]{:S(2)}) collective-permute-start(bf16[3,24,2,192]{3,2,1,0:T(2,128)(2,1)S(1)} %bitcast.18), channel_id=1, source_target_pairs={{0,1},{1,0},{2,3},{3,2},{4,5},{5,4},{6,7},{7,6},{8,9},{9,8},{10,11... | collective-permute-start | bytes 165896 | tf_op jit(solution)/shard_map/ppermute | solution.py:38
  5.8 0.7 %collective-permute-start.1 = (bf16[3,24,2,192]{3,2,1,0:T(2,128)(2,1)S(1)}, bf16[3,24,2,192]{3,2,1,0:T(2,128)(2,1)S(1)}, u32[]{:S(2)}, u32[]{:S(2)}) collective-permute-start(bf16[3,24,2,192]{3,2,1,0:T(2,128)(2,1)S(1)} %bitcast.17), channel_id=1, source_target_pairs={{1,2},{2,1},{5,6},{6,5},{9,10},{10,9},{13,14},{14,13},{17,18},{18,... | collective-permute-start | bytes 165896 | tf_op jit(solution)/shard_map/ppermute | solution.py:38
  6.5 6.7 %all-to-all-start = ((bf16[32,10,2,128]{3,2,1,0:T(2,128)(2,1)}), bf16[32,10,2,128]{3,2,1,0:T(2,128)(2,1)S(1)}, u32[]{:S(2)}, u32[]{:S(2)}) async-start(bf16[32,10,2,128]{3,2,1,0:T(2,128)(2,1)} %bitcast.10), calls=%async_computation | async-start | bytes 327680 | tf_op jit(solution)/shard_map/all_to_all | solution.py:643
  13.2 0.1 add_convert_fusion.even_ref
  13.2 0.1 stack.28
  13.4 0.0 copy-done.8
  13.4 0.0 copy-start.9
  13.4 0.0 copy-start
  13.4 0.0 copy-start.2
  13.4 0.2 copy.16.refs_4_
  13.6 0.6 %copy-done.9 = bf16[128,192]{0,1:T(8,128)(2,1)S(1)} copy-done((bf16[128,192]{0,1:T(8,128)(2,1)S(1)}, bf16[128,192]{0,1:T(8,128)(2,1)}, u32[]{:S(2)}) %copy-start.9) | copy-done | bytes 49176
  14.2 0.0 copy-start.5
  14.2 0.0 copy-start.6
  14.2 0.0 copy-start.7
  14.2 0.1 copy.15.first_ref
  14.3 0.1 copy-done
  14.3 0.1 copy-done.2
  14.4 0.5 %copy-done.5 = bf16[8,192]{1,0:T(8,128)(2,1)S(1)} copy-done((bf16[8,192]{1,0:T(8,128)(2,1)S(1)}, bf16[8,192]{1,0:T(8,128)(2,1)}, u32[]{:S(2)}) %copy-start.5) | copy-done | bytes 3096
  14.9 0.0 copy-done.6
  14.9 0.0 copy-done.7
  14.9 0.0 copy-start.4
  14.9 0.8 %shard_map.137 = (bf16[592,192]{1,0:T(8,128)(2,1)S(1)}, bf16[3,192,192]{2,1,0:T(8,128)(2,1)S(1)}, bf16[128,192]{1,0:T(8,128)(2,1)S(1)}, f32[8,192]{1,0:T(8,128)S...) custom-call(s32[2]{0:T(128)S(1)} %add_convert_fusion.even_ref, ...), custom_call_target="tpu_custom_call" | custom-call | flops 1000000000 | bytes 1000000 | tf_op jit(solution)/shard_map/pallas_call | solution.py:327
  15.7 0.0 copy-start.1
  15.7 0.0 collective-permute-done.one_ref
  15.8 0.0 collective-permute-done.1.two_ref
  15.8 0.1 broadcast_select_fusion.7
  15.9 0.2 pad_maximum_fusion
  16.0 0.0 copy-start.3
  16.0 2.5 %collective-permute-start.2 = (bf16[18,6,2,192]{3,2,1,0:T(2,128)(2,1)S(1)}, bf16[18,6,2,192]{3,2,1,0:T(2,128)(2,1)S(1)}, u32[]{:S(2)}, u32[]{:S(2)}) collective-permute-start(bf16[18,6,2,192]{3,2,1,0:T(2,128)(2,1)S(1)} %pad_maximum_fusion), channel_id=1, source_target_pairs={{4,8},{8,4},{12,16},{16,12},{20,24},{24,20},{28,0},{0,28},{5,9},{9... | collective-permute-start | bytes 248840 | tf_op jit(solution)/shard_map/ppermute | solution.py:38
  18.5 0.2 pad_maximum_fusion.1
  18.7 0.1 collective-permute-start.3
  18.8 3.2 %all-to-all-done.recv_ref = bf16[32,10,2,128]{3,2,1,0:T(2,128)(2,1)S(1)} async-done(((bf16[32,10,2,128]{3,2,1,0:T(2,128)(2,1)}), bf16[32,10,2,128]{3,2,1,0:T(2,128)(2,1)S(1)}, u32[]{:S(2)}, u32[]{:S(2)}) %all-to-all-start) | async-done | bytes 163872 | tf_op jit(solution)/shard_map/all_to_all | solution.py:643
  22.0 0.0 copy-done.4
  22.0 0.0 copy-done.1
  22.0 0.0 copy-done.3
  22.0 4.1 %shard_map.138 = (bf16[12,12,2,192]{3,2,1,0:T(2,128)(2,1)S(1)}, f32[464,256]{1,0:T(8,128)S(1)}, f32[304,192]{1,0:T(8,128)S(1)}, f32[432,192]{1,0:T(8,128)S(1)}, ...) custom-call(s32[5]{0:T(128)S(1)} %convert_element_type.6.scalars_ref, ...), custom_call_target="tpu_custom_call" | custom-call | flops 4000000000 | bytes 4000000 | tf_op jit(solution)/shard_map/pallas_call | solution.py:670
  26.1 0.0 collective-permute-done.2.two_ref
  26.1 0.0 collective-permute-done.3.one_ref
  26.1 3.8 %shard_map.139 = bf16[12,24,2,192]{3,2,1,0:T(2,128)(2,1)} custom-call(s32[5]{0:T(128)S(1)} %convert_element_type.6.scalars_ref, f32[464,256]{1,0:T(8,128)S(1)} %get-tuple-element.49.rest_ref, f32[304,192]{1,0:T(8,128)S(1)} %get-tuple-element.50.latent_ref, f32[432,192]{1,0:T(8,128)S(1)} %get-tuple-element.51.keys_ref, ...), custom_call_target="tpu_custom_call" | custom-call | flops 3000000000 | bytes 4000000 | tf_op jit(solution)/shard_map/pallas_call | solution.py:699
  (1 shorter events, 0.0 us)
Async XLA Ops:
  1.7 11.6 %copy-start.8 = (bf16[768,192]{0,1:T(8,128)(2,1)S(1)}, bf16[768,192]{0,1:T(8,128)(2,1)}, u32[]{:S(2)}) copy-start(bf16[768,192]{0,1:T(8,128)(2,1)} %param.27) | copy-start | bytes 884740
  2.7 13.0 %collective-permute-start = (bf16[3,24,2,192]{3,2,1,0:T(2,128)(2,1)S(1)}, bf16[3,24,2,192]{3,2,1,0:T(2,128)(2,1)S(1)}, u32[]{:S(2)}, u32[]{:S(2)}) collective-permute-start(bf16[3,24,2,192]{3,2,1,0:T(2,128)(2,1)S(1)} %bitcast.18), channel_id=1, source_target_pairs={{0,1},{1,0},{2,3},{3,2},{4,5},{5,4},{6,7},{7,6},{8,9},{9,8},{10,11... | collective-permute-start | bytes 165896 | tf_op jit(solution)/shard_map/ppermute | solution.py:38
  5.8 9.9 %collective-permute-start.1 = (bf16[3,24,2,192]{3,2,1,0:T(2,128)(2,1)S(1)}, bf16[3,24,2,192]{3,2,1,0:T(2,128)(2,1)S(1)}, u32[]{:S(2)}, u32[]{:S(2)}) collective-permute-start(bf16[3,24,2,192]{3,2,1,0:T(2,128)(2,1)S(1)} %bitcast.17), channel_id=1, source_target_pairs={{1,2},{2,1},{5,6},{6,5},{9,10},{10,9},{13,14},{14,13},{17,18},{18,... | collective-permute-start | bytes 165896 | tf_op jit(solution)/shard_map/ppermute | solution.py:38
  6.5 15.5 %all-to-all-start = ((bf16[32,10,2,128]{3,2,1,0:T(2,128)(2,1)}), bf16[32,10,2,128]{3,2,1,0:T(2,128)(2,1)S(1)}, u32[]{:S(2)}, u32[]{:S(2)}) async-start(bf16[32,10,2,128]{3,2,1,0:T(2,128)(2,1)} %bitcast.10), calls=%async_computation | async-start | bytes 327680 | tf_op jit(solution)/shard_map/all_to_all | solution.py:643
  13.4 0.8 %copy-start.9 = (bf16[128,192]{0,1:T(8,128)(2,1)S(1)}, bf16[128,192]{0,1:T(8,128)(2,1)}, u32[]{:S(2)}) copy-start(bf16[128,192]{0,1:T(8,128)(2,1)} %param.19) | copy-start | bytes 147460
  13.4 1.0 %copy-start = (bf16[12,24,2,192]{3,2,1,0:T(2,128)(2,1)S(1)}, bf16[12,24,2,192]{3,2,1,0:T(2,128)(2,1)}, u32[]{:S(2)}) copy-start(bf16[12,24,2,192]{3,2,1,0:T(2,128)(2,1)} %back_ref.2) | copy-start | bytes 663556
  13.4 1.0 %copy-start.2 = (bf16[192,576]{1,0:T(8,128)(2,1)S(1)}, bf16[192,576]{1,0:T(8,128)(2,1)}, u32[]{:S(2)}) copy-start(bf16[192,576]{1,0:T(8,128)(2,1)} %attn_ref) | copy-start | bytes 663556
  14.2 0.7 %copy-start.5 = (bf16[8,192]{1,0:T(8,128)(2,1)S(1)}, bf16[8,192]{1,0:T(8,128)(2,1)}, u32[]{:S(2)}) copy-start(bf16[8,192]{1,0:T(8,128)(2,1)} %table_ref) | copy-start | bytes 9220
  14.2 0.7 %copy-start.6 = (bf16[192]{0:T(256)(128)(2,1)S(1)}, bf16[192]{0:T(256)(128)(2,1)}, u32[]{:S(2)}) copy-start(bf16[192]{0:T(256)(128)(2,1)} %one_ref) | copy-start | bytes 1156
  14.2 0.7 %copy-start.7 = (bf16[192]{0:T(256)(128)(2,1)S(1)}, bf16[192]{0:T(256)(128)(2,1)}, u32[]{:S(2)}) copy-start(bf16[192]{0:T(256)(128)(2,1)} %two_ref) | copy-start | bytes 1156
  14.9 7.1 %copy-start.4 = (bf16[192,192]{1,0:T(8,128)(2,1)S(1)}, bf16[192,192]{1,0:T(8,128)(2,1)}, u32[]{:S(2)}) copy-start(bf16[192,192]{1,0:T(8,128)(2,1)} %refs_1_.3) | copy-start | bytes 221188
  15.7 6.3 %copy-start.1 = (bf16[192,768]{1,0:T(8,128)(2,1)S(1)}, bf16[192,768]{1,0:T(8,128)(2,1)}, u32[]{:S(2)}) copy-start(bf16[192,768]{1,0:T(8,128)(2,1)} %refs_3_.3) | copy-start | bytes 884740
  16.0 6.0 %copy-start.3 = (bf16[192,384]{1,0:T(8,128)(2,1)S(1)}, bf16[192,384]{1,0:T(8,128)(2,1)}, u32[]{:S(2)}) copy-start(bf16[192,384]{1,0:T(8,128)(2,1)} %lift_ref.1) | copy-start | bytes 442372
  16.0 10.1 %collective-permute-start.2 = (bf16[18,6,2,192]{3,2,1,0:T(2,128)(2,1)S(1)}, bf16[18,6,2,192]{3,2,1,0:T(2,128)(2,1)S(1)}, u32[]{:S(2)}, u32[]{:S(2)}) collective-permute-start(bf16[18,6,2,192]{3,2,1,0:T(2,128)(2,1)S(1)} %pad_maximum_fusion), channel_id=1, source_target_pairs={{4,8},{8,4},{12,16},{16,12},{20,24},{24,20},{28,0},{0,28},{5,9},{9... | collective-permute-start | bytes 248840 | tf_op jit(solution)/shard_map/ppermute | solution.py:38
  18.7 7.4 %collective-permute-start.3 = (bf16[18,6,2,192]{3,2,1,0:T(2,128)(2,1)S(1)}, bf16[18,6,2,192]{3,2,1,0:T(2,128)(2,1)S(1)}, u32[]{:S(2)}, u32[]{:S(2)}) collective-permute-start(bf16[18,6,2,192]{3,2,1,0:T(2,128)(2,1)S(1)} %pad_maximum_fusion.1), channel_id=1, source_target_pairs={{0,4},{4,0},{8,12},{12,8},{16,20},{20,16},{24,28},{28,24},{1,5},{5... | collective-permute-start | bytes 248840 | tf_op jit(solution)/shard_map/ppermute | solution.py:38

commit v27 on v24

--- a/solution.py
+++ b/solution.py
@@ -439,7 +439,7 @@
 
 
 MIDDLE = [(0, 1), (1, 1), (2, 1)]
-SIDES = [(0, 0), (0, 2), (2, 0), (2, 2), (1, 0), (1, 2)]
+SIDES = [(1, 0), (1, 2), (0, 0), (0, 2), (2, 0), (2, 2)]
 
 
 def own_rows(plan, places):

time: 26.8 us -> 26.6 us (level)
  transfers between devices with their start and end apart: 5 -> 5, of which waited for: 2 -> 2; matrix products, arithmetic and copies ran while one was open for 3% -> 4% of each run, Pallas kernels for 16% -> 16%
where the time goes in v27:
time: 26.6 us; the launch traced here: 26.3 us
  starting transfers between devices  11.5 us (43%)
  Pallas kernels  9.51 us (36%)
  waiting for transfers between devices  2.6 us (10%)
  local copies, waits for them, and re-layouts  2 us (8%)
  other arithmetic  0.48 us (2%)
    all_to_all x1, starting transfers between devices, local(): lax.all_to_all(sent, ('lon', 'lat'), split_axis=0, concat_axis=0, tiled=T...  7.3 us
    ppermute x4, starting transfers between devices, swapped(): got.append(lax.ppermute(mine, axis, pairs))  4.15 us
    pallas_call x1, Pallas kernels, local(): pl.pallas_call(functools.partial(middle_kernel, plan, lat_cells, lon_cell...  4.05 us
    pallas_call x1, Pallas kernels, local(): pl.pallas_call(functools.partial(side_kernel, plan, lat_cells), out_shape...  3.53 us
    ppermute x4, waiting for transfers between devices, swapped(): got.append(lax.ppermute(mine, axis, pairs))  2.59 us
    pallas_call x1, Pallas kernels, packed(): pl.pallas_call(pack_kernel, out_shape=[jax.ShapeDtypeStruct(shape, BF16),...  1.74 us
    unnamed x24, local copies, waits for them, and re-layouts  1.56 us
  transfers between devices with their start and end apart: 5, of which 2 were waited for; matrix products, arithmetic and copies ran while one was open for 4% of the time, Pallas kernels for 16%

profile of v27, /device:TPU:0, one launch (start us, length us, event | category | flops | bytes accessed | tf_op | source)
XLA Modules:
  0.0 26.3 jit_solution(12477897851748807576)
XLA Ops:
  0.0 1.7 %shard_map.136 = (bf16[8,4,10,2,128]{4,3,2,1,0:T(2,128)(2,1)}, bf16[3,24,2,192]{3,2,1,0:T(2,128)(2,1)}, bf16[3,24,2,192]{3,2,1,0:T(2,128)(2,1)}) custom-call(bf16[8,4,2,128]{3,2,1,0:T(2,128)(2,1)} %values_ref.1, s32[8,8]{1,0:T(8,128)} %bitcast.31, s32[8,8]{1,0:T(8,128)} %bitcast.32, s32[4,8]{1,0:T(4,128)} %bitcast.33, bf16[12,24,2,192]{3,2,1,0:T(2,128)(2,1)} %back_ref.2), custom_call_target="tpu_custom_call" | custom-call | flops 20000000000 | bytes 1000000 | tf_op jit(solution)/shard_map/pallas_call | solution.py:184
  1.7 0.0 copy-start.9
  1.8 0.0 copy-start.10
  1.8 7.3 %all-to-all-start = ((bf16[32,10,2,128]{3,2,1,0:T(2,128)(2,1)}), bf16[32,10,2,128]{3,2,1,0:T(2,128)(2,1)S(1)}, u32[]{:S(2)}, u32[]{:S(2)}) async-start(bf16[32,10,2,128]{3,2,1,0:T(2,128)(2,1)} %bitcast.24), calls=%async_computation | async-start | bytes 327680 | tf_op jit(solution)/shard_map/all_to_all | solution.py:616
  9.1 0.0 copy-start.8
  9.1 0.0 copy-done.9
  9.1 0.0 copy-done.10
  9.1 0.0 copy-start.11
  9.2 1.8 %collective-permute-start.1 = (bf16[3,24,2,192]{3,2,1,0:T(2,128)(2,1)S(1)}, bf16[3,24,2,192]{3,2,1,0:T(2,128)(2,1)S(1)}, u32[]{:S(2)}, u32[]{:S(2)}) collective-permute-start(bf16[3,24,2,192]{3,2,1,0:T(2,128)(2,1)S(1)} %bitcast.28), channel_id=1, source_target_pairs={{0,1},{1,0},{2,3},{3,2},{4,5},{5,4},{6,7},{7,6},{8,9},{9,8},{10,11... | collective-permute-start | bytes 165896 | tf_op jit(solution)/shard_map/ppermute | solution.py:39
  11.0 0.7 %collective-permute-start = (bf16[3,24,2,192]{3,2,1,0:T(2,128)(2,1)S(1)}, bf16[3,24,2,192]{3,2,1,0:T(2,128)(2,1)S(1)}, u32[]{:S(2)}, u32[]{:S(2)}) collective-permute-start(bf16[3,24,2,192]{3,2,1,0:T(2,128)(2,1)S(1)} %bitcast.26), channel_id=1, source_target_pairs={{1,2},{2,1},{5,6},{6,5},{9,10},{10,9},{13,14},{14,13},{17,18},{18,... | collective-permute-start | bytes 165896 | tf_op jit(solution)/shard_map/ppermute | solution.py:39
  11.7 0.0 copy-done.11
  11.7 0.1 copy.15.first_ref
  11.8 0.0 copy-done.8
  11.8 0.0 copy-start
  11.8 0.2 copy.16.refs_4_
  12.0 0.8 %copy-done = bf16[12,24,2,192]{3,2,1,0:T(2,128)(2,1)S(1)} copy-done((bf16[12,24,2,192]{3,2,1,0:T(2,128)(2,1)S(1)}, bf16[12,24,2,192]{3,2,1,0:T(2,128)(2,1)}, u32[]{:S(2)}) %copy-start) | copy-done | bytes 221208
  12.8 0.0 copy-start.2
  12.8 0.1 fusion
  12.9 0.0 copy-start.5
  12.9 0.0 copy-start.6
  12.9 0.0 copy-start.7
  12.9 0.1 add_convert_fusion.scalars_ref
  13.0 0.7 %copy-done.2 = bf16[192,576]{1,0:T(8,128)(2,1)S(1)} copy-done((bf16[192,576]{1,0:T(8,128)(2,1)S(1)}, bf16[192,576]{1,0:T(8,128)(2,1)}, u32[]{:S(2)}) %copy-start.2) | copy-done | bytes 221208
  13.7 0.0 copy-done.5
  13.7 0.0 copy-done.6
  13.7 0.0 copy-done.7
  13.7 0.2 shard_map.137
  13.9 2.0 %collective-permute-done.1 = bf16[3,24,2,192]{3,2,1,0:T(2,128)(2,1)S(1)} collective-permute-done((bf16[3,24,2,192]{3,2,1,0:T(2,128)(2,1)S(1)}, bf16[3,24,2,192]{3,2,1,0:T(2,128)(2,1)S(1)}, u32[]{:S(2)}, u32[]{:S(2)}) %collective-permute-start.1) | collective-permute-done | bytes 55328 | tf_op jit(solution)/shard_map/ppermute | solution.py:39
  15.9 0.0 collective-permute-done
  16.0 0.0 copy-start.1
  16.0 0.1 fusion.1
  16.0 0.0 copy-start.3
  16.1 0.0 copy-start.4
  16.1 0.4 %broadcast_select_fusion = (bf16[18,6,2,192]{3,2,1,0:T(2,128)(2,1)S(1)}, bf16[18,6,2,192]{3,2,1,0:T(2,128)(2,1)S(1)}) fusion(pred[]{:T(512)} %eq.21, bf16[3,6,2,192]{3,2,1,0:T(2,128)(2,1)S(1)} %get-tuple-element.65, bf16[12,6,2,192]{3,2,1,0:T(2,128)(2,1)S(1)} %get-tuple-element.54, bf16[3,6,2,192]{3,2,1,0:T(2,128)(2,1)S(1)} %get-tuple-element.62, ...), kind=kLoop, calls=%fused_computation | loop fusion | flops 248832 | bytes 331777 | tf_op jit(solution)/shard_map/jit(_where)/select_n | solution.py:33
  16.5 1.2 %collective-permute-start.2 = (bf16[18,6,2,192]{3,2,1,0:T(2,128)(2,1)S(1)}, bf16[18,6,2,192]{3,2,1,0:T(2,128)(2,1)S(1)}, u32[]{:S(2)}, u32[]{:S(2)}) collective-permute-start(bf16[18,6,2,192]{3,2,1,0:T(2,128)(2,1)S(1)} %get-tuple-element.56), channel_id=1, source_target_pairs={{4,8},{8,4},{12,16},{16,12},{20,24},{24,20},{28,0},{0,28},{5,9},{9... | collective-permute-start | bytes 248840 | tf_op jit(solution)/shard_map/ppermute | solution.py:39
  17.7 0.4 %collective-permute-start.3 = (bf16[18,6,2,192]{3,2,1,0:T(2,128)(2,1)S(1)}, bf16[18,6,2,192]{3,2,1,0:T(2,128)(2,1)S(1)}, u32[]{:S(2)}, u32[]{:S(2)}) collective-permute-start(bf16[18,6,2,192]{3,2,1,0:T(2,128)(2,1)S(1)} %get-tuple-element.55), channel_id=1, source_target_pairs={{0,4},{4,0},{8,12},{12,8},{16,20},{20,16},{24,28},{28,24},{1,5},{5... | collective-permute-start | bytes 248840 | tf_op jit(solution)/shard_map/ppermute | solution.py:39
  18.1 0.0 all-to-all-done.recv_ref
  18.1 0.0 copy-done.1
  18.1 0.0 copy-done.3
  18.1 0.0 copy-done.4
  18.1 4.1 %shard_map.138 = (bf16[12,12,2,192]{3,2,1,0:T(2,128)(2,1)S(1)}, f32[464,256]{1,0:T(8,128)S(1)}, f32[304,192]{1,0:T(8,128)S(1)}, f32[432,192]{1,0:T(8,128)S(1)}, ...) custom-call(s32[4]{0:T(128)S(1)} %add_convert_fusion.scalars_ref, ...), custom_call_target="tpu_custom_call" | custom-call | flops 4000000000 | bytes 4000000 | tf_op jit(solution)/shard_map/pallas_call | solution.py:646
  22.2 0.6 %collective-permute-done.2.two_ref = bf16[18,6,2,192]{3,2,1,0:T(2,128)(2,1)S(1)} collective-permute-done((bf16[18,6,2,192]{3,2,1,0:T(2,128)(2,1)S(1)}, bf16[18,6,2,192]{3,2,1,0:T(2,128)(2,1)S(1)}, u32[]{:S(2)}, u32[]{:S(2)}) %collective-permute-start.2) | collective-permute-done | bytes 82976 | tf_op jit(solution)/shard_map/ppermute | solution.py:39
  22.8 0.0 collective-permute-done.3.one_ref
  22.8 3.5 %shard_map.139 = bf16[12,24,2,192]{3,2,1,0:T(2,128)(2,1)} custom-call(s32[4]{0:T(128)S(1)} %add_convert_fusion.scalars_ref, f32[464,256]{1,0:T(8,128)S(1)} %get-tuple-element.45.rest_ref, f32[304,192]{1,0:T(8,128)S(1)} %get-tuple-element.46.latent_ref, f32[432,192]{1,0:T(8,128)S(1)} %get-tuple-element.47.keys_ref, ...), custom_call_target="tpu_custom_call" | custom-call | flops 3000000000 | bytes 4000000 | tf_op jit(solution)/shard_map/pallas_call | solution.py:676
  (2 shorter events, 0.0 us)
Async XLA Ops:
  1.7 7.4 %copy-start.9 = (bf16[3,24,2,192]{3,2,1,0:T(2,128)(2,1)S(1)}, bf16[3,24,2,192]{3,2,1,0:T(2,128)(2,1)}, u32[]{:S(2)}) copy-start(bf16[3,24,2,192]{3,2,1,0:T(2,128)(2,1)} %get-tuple-element.30) | copy-start | bytes 165892
  1.8 7.4 %copy-start.10 = (bf16[3,24,2,192]{3,2,1,0:T(2,128)(2,1)S(1)}, bf16[3,24,2,192]{3,2,1,0:T(2,128)(2,1)}, u32[]{:S(2)}) copy-start(bf16[3,24,2,192]{3,2,1,0:T(2,128)(2,1)} %get-tuple-element.31) | copy-start | bytes 165892
  1.8 16.3 %all-to-all-start = ((bf16[32,10,2,128]{3,2,1,0:T(2,128)(2,1)}), bf16[32,10,2,128]{3,2,1,0:T(2,128)(2,1)S(1)}, u32[]{:S(2)}, u32[]{:S(2)}) async-start(bf16[32,10,2,128]{3,2,1,0:T(2,128)(2,1)} %bitcast.24), calls=%async_computation | async-start | bytes 327680 | tf_op jit(solution)/shard_map/all_to_all | solution.py:616
  9.1 2.7 %copy-start.8 = (bf16[768,192]{0,1:T(8,128)(2,1)S(1)}, bf16[768,192]{0,1:T(8,128)(2,1)}, u32[]{:S(2)}) copy-start(bf16[768,192]{0,1:T(8,128)(2,1)} %param.27) | copy-start | bytes 884740
  9.1 2.6 %copy-start.11 = (bf16[128,192]{0,1:T(8,128)(2,1)S(1)}, bf16[128,192]{0,1:T(8,128)(2,1)}, u32[]{:S(2)}) copy-start(bf16[128,192]{0,1:T(8,128)(2,1)} %param.19) | copy-start | bytes 147460
  9.2 6.8 %collective-permute-start.1 = (bf16[3,24,2,192]{3,2,1,0:T(2,128)(2,1)S(1)}, bf16[3,24,2,192]{3,2,1,0:T(2,128)(2,1)S(1)}, u32[]{:S(2)}, u32[]{:S(2)}) collective-permute-start(bf16[3,24,2,192]{3,2,1,0:T(2,128)(2,1)S(1)} %bitcast.28), channel_id=1, source_target_pairs={{0,1},{1,0},{2,3},{3,2},{4,5},{5,4},{6,7},{7,6},{8,9},{9,8},{10,11... | collective-permute-start | bytes 165896 | tf_op jit(solution)/shard_map/ppermute | solution.py:39
  11.0 5.0 %collective-permute-start = (bf16[3,24,2,192]{3,2,1,0:T(2,128)(2,1)S(1)}, bf16[3,24,2,192]{3,2,1,0:T(2,128)(2,1)S(1)}, u32[]{:S(2)}, u32[]{:S(2)}) collective-permute-start(bf16[3,24,2,192]{3,2,1,0:T(2,128)(2,1)S(1)} %bitcast.26), channel_id=1, source_target_pairs={{1,2},{2,1},{5,6},{6,5},{9,10},{10,9},{13,14},{14,13},{17,18},{18,... | collective-permute-start | bytes 165896 | tf_op jit(solution)/shard_map/ppermute | solution.py:39
  11.8 1.0 %copy-start = (bf16[12,24,2,192]{3,2,1,0:T(2,128)(2,1)S(1)}, bf16[12,24,2,192]{3,2,1,0:T(2,128)(2,1)}, u32[]{:S(2)}) copy-start(bf16[12,24,2,192]{3,2,1,0:T(2,128)(2,1)} %back_ref.2) | copy-start | bytes 663556
  12.8 0.9 %copy-start.2 = (bf16[192,576]{1,0:T(8,128)(2,1)S(1)}, bf16[192,576]{1,0:T(8,128)(2,1)}, u32[]{:S(2)}) copy-start(bf16[192,576]{1,0:T(8,128)(2,1)} %attn_ref) | copy-start | bytes 663556
  12.9 0.8 %copy-start.5 = (bf16[8,192]{1,0:T(8,128)(2,1)S(1)}, bf16[8,192]{1,0:T(8,128)(2,1)}, u32[]{:S(2)}) copy-start(bf16[8,192]{1,0:T(8,128)(2,1)} %table_ref) | copy-start | bytes 9220
  12.9 0.8 %copy-start.6 = (bf16[192]{0:T(256)(128)(2,1)S(1)}, bf16[192]{0:T(256)(128)(2,1)}, u32[]{:S(2)}) copy-start(bf16[192]{0:T(256)(128)(2,1)} %one_ref) | copy-start | bytes 1156
  12.9 0.8 %copy-start.7 = (bf16[192]{0:T(256)(128)(2,1)S(1)}, bf16[192]{0:T(256)(128)(2,1)}, u32[]{:S(2)}) copy-start(bf16[192]{0:T(256)(128)(2,1)} %two_ref) | copy-start | bytes 1156
  16.0 2.1 %copy-start.1 = (bf16[192,768]{1,0:T(8,128)(2,1)S(1)}, bf16[192,768]{1,0:T(8,128)(2,1)}, u32[]{:S(2)}) copy-start(bf16[192,768]{1,0:T(8,128)(2,1)} %refs_3_.3) | copy-start | bytes 884740
  16.0 2.1 %copy-start.3 = (bf16[192,384]{1,0:T(8,128)(2,1)S(1)}, bf16[192,384]{1,0:T(8,128)(2,1)}, u32[]{:S(2)}) copy-start(bf16[192,384]{1,0:T(8,128)(2,1)} %lift_ref.1) | copy-start | bytes 442372
  16.1 2.1 %copy-start.4 = (bf16[192,192]{1,0:T(8,128)(2,1)S(1)}, bf16[192,192]{1,0:T(8,128)(2,1)}, u32[]{:S(2)}) copy-start(bf16[192,192]{1,0:T(8,128)(2,1)} %refs_1_.3) | copy-start | bytes 221188
  16.5 6.3 %collective-permute-start.2 = (bf16[18,6,2,192]{3,2,1,0:T(2,128)(2,1)S(1)}, bf16[18,6,2,192]{3,2,1,0:T(2,128)(2,1)S(1)}, u32[]{:S(2)}, u32[]{:S(2)}) collective-permute-start(bf16[18,6,2,192]{3,2,1,0:T(2,128)(2,1)S(1)} %get-tuple-element.56), channel_id=1, source_target_pairs={{4,8},{8,4},{12,16},{16,12},{20,24},{24,20},{28,0},{0,28},{5,9},{9... | collective-permute-start | bytes 248840 | tf_op jit(solution)/shard_map/ppermute | solution.py:39
  17.7 5.1 %collective-permute-start.3 = (bf16[18,6,2,192]{3,2,1,0:T(2,128)(2,1)S(1)}, bf16[18,6,2,192]{3,2,1,0:T(2,128)(2,1)S(1)}, u32[]{:S(2)}, u32[]{:S(2)}) collective-permute-start(bf16[18,6,2,192]{3,2,1,0:T(2,128)(2,1)S(1)} %get-tuple-element.55), channel_id=1, source_target_pairs={{0,4},{4,0},{8,12},{12,8},{16,20},{20,16},{24,28},{28,24},{1,5},{5... | collective-permute-start | bytes 248840 | tf_op jit(solution)/shard_map/ppermute | solution.py:39
